TPU v7x, 256 devices: a whole 4x4x8 slice. The times are simulated.
256 devices in a mesh: fsdp: 4 (over y_lo, core), ctx: 64 (over z, y_hi, x).
Axes of the slice: x: 4, y: 4 (y_hi: 2, y_lo: 2; y = y_hi * 2 + y_lo), z: 8, core: 2. Of those that a mesh axis runs over, the one named last changes fastest.
Arguments:
- tokens: bfloat16 [4, 8192, 2048], P('fsdp', 'ctx'), may hold values from -6 to 6
- norm_gain: float32 [2048], replicated, may hold values from 0.5 to 1.5
- in_weight: bfloat16 [2048, 6144], P(('fsdp', 'ctx')), may hold values from -0.125 to 0.125
- short_filter: float32 [3, 6144], replicated, may hold values from -3.5 to 3.5
- rates: float32 [2048, 16], P('ctx'), may hold values from 3.0517578e-05 to 0.033333335
- residues: float32 [2048, 16], P('ctx'), may hold values from -1.5 to 1.5
- skip: float32 [2048], P('ctx'), may hold values from 0.5 to 2
Outputs:
- mixed: bfloat16 [4, 2048, 8192], P('fsdp', None, 'ctx')
All inputs are finite; a program needn't handle non-finite values.
Results may differ from a plain program's by a relative error of at most 0.0092.
Values may be sent and summed in bfloat16 or wider, within the bound.
No kernel may reach another device: no remote copies, remote signals or barrier semaphores. Data moves between devices by JAX's collectives and lax.ppermute only.
A program may use at most 128 MiB of HBM per device.

v0:
```python
import math

import jax
import jax.numpy as jnp
from jax import lax
from jax.sharding import PartitionSpec as P


def shifted(block, axis, distance):
    devices = range(lax.axis_size(axis))
    route = [(i - distance, i) for i in devices if i - distance in devices]
    return lax.ppermute(block, axis, route)


def settle(values):
    return lax.optimization_barrier(values.astype(jnp.bfloat16))


def long_conv(signal, rates, residues, skip):
    seq_count, channels_here, length = signal.shape
    rows_all = seq_count * channels_here
    padded_len = 2 * length
    inner = 128
    outer = padded_len // inner
    half_outer = outer // 2
    highest = lax.Precision.HIGHEST
    two_pi = 2.0 * math.pi
    values = signal.astype(jnp.float32)
    blocks = values.reshape(rows_all, half_outer, inner)
    outer_idx = jnp.arange(outer, dtype=jnp.int32)
    half_idx = jnp.arange(half_outer, dtype=jnp.int32)
    inner_idx = jnp.arange(inner, dtype=jnp.int32)
    outer_angle = (
        two_pi * (outer_idx[:, None] * half_idx[None, :] % outer).astype(jnp.float32) / outer
    )
    outer_cos = jnp.cos(outer_angle)
    outer_sin = jnp.sin(outer_angle)
    twist_angle = (
        two_pi
        * (outer_idx[:, None] * inner_idx[None, :] % padded_len).astype(jnp.float32)
        / padded_len
    )
    twist_cos = jnp.cos(twist_angle)
    twist_sin = jnp.sin(twist_angle)
    inner_angle = (
        two_pi * (inner_idx[:, None] * inner_idx[None, :] % inner).astype(jnp.float32) / inner
    )
    inner_cos = jnp.cos(inner_angle)
    inner_sin = jnp.sin(inner_angle)
    first_re = jnp.einsum("fa,cab->cfb", outer_cos, blocks, precision=highest)
    first_im = -jnp.einsum("fa,cab->cfb", outer_sin, blocks, precision=highest)
    turned_re = first_re * twist_cos + first_im * twist_sin
    turned_im = first_im * twist_cos - first_re * twist_sin
    spec_re = jnp.einsum("cfb,bg->cfg", turned_re, inner_cos, precision=highest) + jnp.einsum(
        "cfb,bg->cfg", turned_im, inner_sin, precision=highest
    )
    spec_im = jnp.einsum("cfb,bg->cfg", turned_im, inner_cos, precision=highest) - jnp.einsum(
        "cfb,bg->cfg", turned_re, inner_sin, precision=highest
    )
    freq = outer_idx[:, None] + outer * inner_idx[None, :]
    full_angle = two_pi * freq.astype(jnp.float32) / padded_len
    full_cos = jnp.cos(full_angle)
    full_sin = jnp.sin(full_angle)
    half_sin = jnp.sin(math.pi * freq.astype(jnp.float32) / padded_len)
    parity_sign = 1.0 - 2.0 * (freq % 2).astype(jnp.float32)
    resp_re = jnp.zeros((channels_here, outer, inner), jnp.float32)
    resp_im = jnp.zeros((channels_here, outer, inner), jnp.float32)
    for pole_index in range(rates.shape[1]):
        decay = rates[:, pole_index][:, None, None]
        weight_col = residues[:, pole_index][:, None, None]
        factor = jnp.exp(-decay)
        gap = -jnp.expm1(-decay)
        tail = jnp.exp(-decay * length)
        numer = weight_col * jnp.sqrt(2.0 * decay) * (1.0 - tail * parity_sign)
        denom = gap * gap + 4.0 * factor * half_sin * half_sin
        resp_re = resp_re + numer * (1.0 - factor * full_cos) / denom
        resp_im = resp_im + numer * (-factor * full_sin) / denom
    spec_re = spec_re.reshape(seq_count, channels_here, outer, inner)
    spec_im = spec_im.reshape(seq_count, channels_here, outer, inner)
    prod_re = (spec_re * resp_re[None] - spec_im * resp_im[None]).reshape(rows_all, outer, inner)
    prod_im = (spec_re * resp_im[None] + spec_im * resp_re[None]).reshape(rows_all, outer, inner)
    back_re = jnp.einsum("cfg,gb->cfb", prod_re, inner_cos, precision=highest) - jnp.einsum(
        "cfg,gb->cfb", prod_im, inner_sin, precision=highest
    )
    back_im = jnp.einsum("cfg,gb->cfb", prod_im, inner_cos, precision=highest) + jnp.einsum(
        "cfg,gb->cfb", prod_re, inner_sin, precision=highest
    )
    untw_re = back_re * twist_cos - back_im * twist_sin
    untw_im = back_im * twist_cos + back_re * twist_sin
    result_rows = jnp.einsum("fa,cfb->cab", outer_cos, untw_re, precision=highest) - jnp.einsum(
        "fa,cfb->cab", outer_sin, untw_im, precision=highest
    )
    filtered = result_rows.reshape(seq_count, channels_here, length) / padded_len
    return filtered + skip[None, :, None] * values


def featurize(projected, taps, share):
    earlier = shifted(projected[:, :, -2:], "ctx", 1)
    padded = jnp.concatenate([earlier, projected], axis=2).astype(jnp.float32)
    length = projected.shape[2]
    featured = (
        taps[0][None, :, None] * padded[:, :, 2:]
        + taps[1][None, :, None] * padded[:, :, 1 : length + 1]
        + taps[2][None, :, None] * padded[:, :, :length]
    )
    carried = settle(featured[:, share : 2 * share] * featured[:, 2 * share :])
    gate = settle(featured[:, :share])
    return (carried, gate)


def convolve(local_carried, rate_rows, residue_rows, skip_rows):
    response = long_conv(local_carried, rate_rows, residue_rows, skip_rows)
    return settle(response)


def mix_channels(carried, gate, rate_rows, residue_rows, skip_rows):
    local_carried, local_gate = (
        lax.all_to_all(carried, "ctx", split_axis=1, concat_axis=2, tiled=True),
        lax.all_to_all(gate, "ctx", split_axis=1, concat_axis=2, tiled=True),
    )
    response = convolve(local_carried, rate_rows, residue_rows, skip_rows)
    product = (local_gate.astype(jnp.float32) * response.astype(jnp.float32)).astype(jnp.bfloat16)
    result = lax.all_to_all(product, "ctx", split_axis=2, concat_axis=1, tiled=True)
    return result


def body(tokens, norm_gain, in_weight, short_filter, rates, residues, skip):
    token_rows = tokens[0].astype(jnp.float32)
    inv_rms = lax.rsqrt(jnp.mean(token_rows * token_rows, axis=1, keepdims=True) + 1e-06)
    normed = (token_rows * inv_rms * norm_gain[None, :]).astype(jnp.bfloat16)
    channels = skip.shape[0] * lax.axis_size("ctx")
    projected_acc = lax.dot_general(
        lax.all_gather(in_weight, ("fsdp", "ctx"), axis=0, tiled=True),
        normed,
        (((0,), (1,)), ((), ())),
        preferred_element_type=jnp.float32,
    )
    projected = projected_acc.astype(jnp.bfloat16)[None]
    carried, gate = featurize(projected, short_filter, channels)
    return mix_channels(carried, gate, rates, residues, skip)


def solution(mesh):
    in_specs = (
        P("fsdp", "ctx", None),
        P(),
        P(("fsdp", "ctx"), None),
        P(),
        P("ctx", None),
        P("ctx", None),
        P("ctx"),
    )
    out_specs = P("fsdp", None, "ctx")
    return jax.shard_map(body, mesh=mesh, in_specs=in_specs, out_specs=out_specs, check_vma=False)
```

profile of v0, /device:TPU:2, one launch (start us, length us, event | category | flops | bytes accessed | tf_op | source)
XLA Modules:
  0.0 1026.5 jit_solution(6290357354320460975)
XLA Ops:
  8.5 1.5 exponential_bitcast_fusion.13
  10.0 1.7 broadcast_multiply_fusion.15
  12.9 741.4 %all-gather.2.cloned.1.call-done = bf16[2048,6144]{1,0:T(8,128)(2,1)} async-done(((bf16[8,6144]{1,0:T(8,128)(2,1)}), bf16[2048,6144]{1,0:T(8,128)(2,1)}) %all-gather.2.cloned.1.call-update) | async-done | bytes 25165840 | tf_op jit(solution)/shard_map/all_gather | solution.py:133
  754.4 11.9 %fusion = bf16[1,6144,128]{1,2,0:T(8,128)(2,1)S(1)} fusion(bf16[2048,6144]{1,0:T(8,128)(2,1)} %all-gather.2.cloned.1.call-done, bf16[1,128,2048]{2,1,0:T(8,128)(2,1)} %param.7, f32[2048]{0:T(1024)} %param.8, f32[128]{0:T(128)S(1)} %add_rsqrt_fusion), kind=kOutput, calls=%fused_computation.1 | convolution fusion | flops 3223060480 | bytes 27271680 | tf_op jit(solution)/shard_map/dot_general | solution.py:132
  766.3 1.9 collective-permute-start
  768.5 4.3 collective-permute-done
  775.1 3.6 copy.125
  779.2 13.3 %reduce.1 = bf16[2048,128]{1,0:T(8,128)(2,1)} reduce(bf16[2048,1,128]{2,1,0:T(2,128)(2,1)} %bitcast.259, bf16[]{:T(256)} %broadcast.616), dimensions={1}, to_apply=%bitcast.220.reduce_sub_computation | reduce | bytes 1048578
  792.6 2.0 reshape.1251
  794.6 17.8 %all-to-all-start.1 = ((bf16[64,2,2048]{2,1,0:T(2,128)(2,1)}), bf16[64,2,2048]{2,1,0:T(2,128)(2,1)}, u32[]{:S(2)}, u32[]{:S(2)}) async-start(bf16[64,2,2048]{2,1,0:T(2,128)(2,1)} %reshape.1251), calls=%async_computation.1 | async-start | bytes 1048576 | tf_op jit(solution)/shard_map/all_to_all | solution.py:118
  824.9 2.3 copy.122
  827.3 11.5 %reduce = bf16[2048,128]{1,0:T(8,128)(2,1)S(1)} reduce(bf16[2048,1,128]{2,1,0:T(2,128)(2,1)S(1)} %bitcast.261, bf16[]{:T(256)} %broadcast.616), dimensions={1}, to_apply=%bitcast.218.reduce_sub_computation | reduce | bytes 1048578
  839.7 12.9 %all-to-all-start = ((bf16[64,2,2048]{2,1,0:T(2,128)(2,1)}), bf16[64,2,2048]{2,1,0:T(2,128)(2,1)}, u32[]{:S(2)}, u32[]{:S(2)}) async-start(bf16[64,2,2048]{2,1,0:T(2,128)(2,1)} %reshape.1249), calls=%async_computation | async-start | bytes 1048576 | tf_op jit(solution)/shard_map/all_to_all | solution.py:119
  852.6 3.8 reshape.1252
  857.9 1.3 fusion.34
  859.2 3.8 fusion.43
  863.0 3.7 fusion.39
  867.3 4.2 convolution_add_fusion.1
  872.0 24.7 %multiply_add_fusion = (f32[32,128,128]{2,1,0:T(8,128)S(1)}, f32[32,128,128]{2,1,0:T(8,128)S(1)}, f32[32,128,128]{2,1,0:T(8,128)S(1)}, f32[32,128,128]{2,1,0:T(8,128)S(1)}) fusion(f32[32,128,128]{2,1,0:T(8,128)S(1)} %convolution_add_fusion.1, f32[32]{0:T(128)S(1)} %copy-done.9, f32[32]{0:T(128)} %get-tuple-element.59, f32[32]{0:T(128)S(1)} %copy-done.11, ...), kind=kOutput, calls=%fused_computation.21 | convolution fusion | flops 934510592 | bytes 17182720 | tf_op jit(solution)/shard_map/cfb,bg->cfg/dot_general | solution.py:57
  896.6 2.3 fusion.59
  899.9 2.3 fusion.61
  902.1 2.3 convolution_add_fusion
  904.4 2.3 convolution_subtract_fusion
  906.7 2.8 fusion.5
  909.4 3.0 fusion.19
  914.0 3.6 reshape.1250
  919.4 6.7 copy.140
  926.1 45.2 %reduce.2 = bf16[8192,32]{1,0:T(8,128)(2,1)S(1)} reduce(bf16[8192,1,32]{2,1,0:T(2,128)(2,1)} %bitcast.252, bf16[]{:T(256)} %broadcast.616), dimensions={1}, to_apply=%bitcast.222.reduce_sub_computation | reduce | bytes 1048578
  971.3 2.1 reshape.1253
  973.4 29.4 %all_to_all.42 = bf16[64,2,2048]{2,1,0:T(2,128)(2,1)S(1)} all-to-all(bf16[64,2,2048]{2,1,0:T(2,128)(2,1)S(1)} %reshape.1253), channel_id=1, replica_groups=mesh['fsdp'=4,'ctx'=64] {'ctx'}, dimensions={0} | all-to-all | bytes 1048576 | tf_op jit(solution)/shard_map/all_to_all | solution.py:123
  1002.8 7.2 reshape.1254
  1010.0 8.0 copy.141
  (173 shorter events, 26.9 us)
Async XLA Ops:
  6.5 747.8 %all-gather.2.cloned.1.call-start = ((), (), s32[]{:S(2)}) async-start(), calls=%async_computation.3 | async-start | bytes 25264128 | tf_op jit(solution)/shard_map/all_gather | solution.py:133
  11.7 801.2 %copy-start.7 = (f32[32]{0:T(128)}, f32[32]{0:T(128)S(1)}, u32[]{:S(2)}) copy-start(f32[32]{0:T(128)S(1)} %get-tuple-element.9) | copy-start | bytes 388
  11.7 801.7 %copy-start.52 = (f32[32]{0:T(128)}, f32[32]{0:T(128)S(1)}, u32[]{:S(2)}) copy-start(f32[32]{0:T(128)S(1)} %get-tuple-element.108) | copy-start | bytes 388
  11.7 802.3 %copy-start.49 = (f32[32]{0:T(128)}, f32[32]{0:T(128)S(1)}, u32[]{:S(2)}) copy-start(f32[32]{0:T(128)S(1)} %get-tuple-element.106) | copy-start | bytes 388
  11.7 802.9 %copy-start.46 = (f32[32]{0:T(128)}, f32[32]{0:T(128)S(1)}, u32[]{:S(2)}) copy-start(f32[32]{0:T(128)S(1)} %get-tuple-element.104) | copy-start | bytes 388
  11.7 803.4 %copy-start.43 = (f32[32]{0:T(128)}, f32[32]{0:T(128)S(1)}, u32[]{:S(2)}) copy-start(f32[32]{0:T(128)S(1)} %get-tuple-element.102) | copy-start | bytes 388
  11.7 804.0 %copy-start.40 = (f32[32]{0:T(128)}, f32[32]{0:T(128)S(1)}, u32[]{:S(2)}) copy-start(f32[32]{0:T(128)S(1)} %get-tuple-element.100) | copy-start | bytes 388
  11.7 804.5 %copy-start.37 = (f32[32]{0:T(128)}, f32[32]{0:T(128)S(1)}, u32[]{:S(2)}) copy-start(f32[32]{0:T(128)S(1)} %get-tuple-element.98) | copy-start | bytes 388
  11.7 805.0 %copy-start.34 = (f32[32]{0:T(128)}, f32[32]{0:T(128)S(1)}, u32[]{:S(2)}) copy-start(f32[32]{0:T(128)S(1)} %get-tuple-element.96) | copy-start | bytes 388
  11.7 805.5 %copy-start.31 = (f32[32]{0:T(128)}, f32[32]{0:T(128)S(1)}, u32[]{:S(2)}) copy-start(f32[32]{0:T(128)S(1)} %get-tuple-element.94) | copy-start | bytes 388
  11.7 806.1 %copy-start.28 = (f32[32]{0:T(128)}, f32[32]{0:T(128)S(1)}, u32[]{:S(2)}) copy-start(f32[32]{0:T(128)S(1)} %get-tuple-element.92) | copy-start | bytes 388
  11.8 806.6 %copy-start.25 = (f32[32]{0:T(128)}, f32[32]{0:T(128)S(1)}, u32[]{:S(2)}) copy-start(f32[32]{0:T(128)S(1)} %get-tuple-element.90) | copy-start | bytes 388
  11.8 807.1 %copy-start.22 = (f32[32]{0:T(128)}, f32[32]{0:T(128)S(1)}, u32[]{:S(2)}) copy-start(f32[32]{0:T(128)S(1)} %get-tuple-element.88) | copy-start | bytes 388
  11.8 807.7 %copy-start.19 = (f32[32]{0:T(128)}, f32[32]{0:T(128)S(1)}, u32[]{:S(2)}) copy-start(f32[32]{0:T(128)S(1)} %get-tuple-element.86) | copy-start | bytes 388
  11.8 808.2 %copy-start.16 = (f32[32]{0:T(128)}, f32[32]{0:T(128)S(1)}, u32[]{:S(2)}) copy-start(f32[32]{0:T(128)S(1)} %get-tuple-element.84) | copy-start | bytes 388
  11.8 808.7 %copy-start.13 = (f32[32]{0:T(128)}, f32[32]{0:T(128)S(1)}, u32[]{:S(2)}) copy-start(f32[32]{0:T(128)S(1)} %get-tuple-element.82) | copy-start | bytes 388
  11.8 809.2 %copy-start.10 = (f32[32]{0:T(128)}, f32[32]{0:T(128)S(1)}, u32[]{:S(2)}) copy-start(f32[32]{0:T(128)S(1)} %get-tuple-element.80) | copy-start | bytes 388
  766.3 6.5 collective-permute-start
  778.7 43.0 %copy-start.1 = (f32[32,16]{0,1:T(8,128)S(1)}, f32[32,16]{0,1:T(8,128)}, u32[]{:S(2)}) copy-start(f32[32,16]{0,1:T(8,128)} %param.11) | copy-start | bytes 6148
  778.7 43.0 %copy-start.2 = (f32[32,16]{0,1:T(8,128)S(1)}, f32[32,16]{0,1:T(8,128)}, u32[]{:S(2)}) copy-start(f32[32,16]{0,1:T(8,128)} %param.12) | copy-start | bytes 6148
  794.6 45.2 %all-to-all-start.1 = ((bf16[64,2,2048]{2,1,0:T(2,128)(2,1)}), bf16[64,2,2048]{2,1,0:T(2,128)(2,1)}, u32[]{:S(2)}, u32[]{:S(2)}) async-start(bf16[64,2,2048]{2,1,0:T(2,128)(2,1)} %reshape.1251), calls=%async_computation.1 | async-start | bytes 1048576 | tf_op jit(solution)/shard_map/all_to_all | solution.py:118
  839.7 74.3 %all-to-all-start = ((bf16[64,2,2048]{2,1,0:T(2,128)(2,1)}), bf16[64,2,2048]{2,1,0:T(2,128)(2,1)}, u32[]{:S(2)}, u32[]{:S(2)}) async-start(bf16[64,2,2048]{2,1,0:T(2,128)(2,1)} %reshape.1249), calls=%async_computation | async-start | bytes 1048576 | tf_op jit(solution)/shard_map/all_to_all | solution.py:119
  866.9 4.6 copy-start.3
  866.9 4.6 copy-start.4
  867.0 4.6 copy-start.5
  867.0 4.6 copy-start.6
  867.0 4.6 copy-start.8
  867.0 4.6 copy-start.9
  867.0 4.6 copy-start.11
  867.0 4.6 copy-start.12
  867.0 4.6 copy-start.14
  867.0 4.6 copy-start.15
  (32 other events, 140.8 us)
Sparse Core Ops, SparseCore 0:
  9.2 745.0 all-gather.1
where the time goes:
time: 1040 us; the launch traced here: 1030 us
  waiting for transfers between devices  746 us (72%)
  other arithmetic  91.2 us (9%)
  matrix products  65.7 us (6%)
  local copies, waits for them, and re-layouts  46.1 us (4%)
  starting transfers between devices  32.6 us (3%)
  blocking collectives  29.4 us (3%)
  between operations  14.9 us (1%)
    all_gather x1, waiting for transfers between devices, body(): lax.all_gather(in_weight, ('fsdp', 'ctx'), axis=0, tiled=True)  741 us
    unnamed x3, other arithmetic  70.1 us
    all_to_all x1, blocking collectives, mix_channels(): lax.all_to_all(product, 'ctx', split_axis=2, concat_axis=1, tiled=True)  29.4 us
    dot_general x1, matrix products, long_conv(): jnp.einsum('cfb,bg->cfg', turned_re, inner_sin, precision=highest)  24.7 us
    unnamed x129, local copies, waits for them, and re-layouts  21.1 us
  transfers between devices with their start and end apart: 4, of which 2 were waited for; matrix products, arithmetic and copies ran while one was open for 9% of the time, Pallas kernels for 0%

commit v1 on v0

v1 whole, which is shorter than its diff:
```python
import functools

import jax
import jax.numpy as jnp
from jax import lax
from jax.experimental import pallas as pl
from jax.experimental.pallas import tpu as pltpu
from jax.sharding import Mesh, PartitionSpec as P

F32 = jnp.float32
BF16 = jnp.bfloat16
NX, NY, NZ = 4, 4, 8
GROUPS = 16
POLES = 16
HERE = 128
CHUNK = 16
LANES = 128
CH = 512
HALO = 16
ROWS = HALO + NX * HERE
D = 2048
COLS = 3 * CH
VMEM_LIMIT = 50 * 1024 * 1024


def params(**kw):
    return pltpu.CompilerParams(vmem_limit_bytes=VMEM_LIMIT, **kw)


def norm_kernel(tok_ref, gain_ref, out_ref, scr):
    x = tok_ref[...].astype(F32)
    inv = lax.rsqrt(jnp.mean(x * x, axis=1, keepdims=True) + 1e-6)
    for k in range(D // LANES):
        lanes = slice(k * LANES, (k + 1) * LANES)
        scr[k] = x[:, lanes] * inv * gain_ref[:, lanes]
    for k in range(D // LANES):
        for j in range(0, CHUNK, 2):
            pair = [scr[k, pl.ds(j + i, 8, stride=CHUNK), :] for i in range(2)]
            out_ref[8 * j : 8 * j + 16, k * LANES : (k + 1) * LANES] = jnp.concatenate(
                pair, axis=0
            ).astype(BF16)


def normalise(tokens, gain):
    return pl.pallas_call(
        norm_kernel,
        out_shape=jax.ShapeDtypeStruct((HERE, D), BF16),
        scratch_shapes=[pltpu.VMEM((D // LANES, HERE, LANES), F32)],
        compiler_params=params(),
    )(tokens, gain)


def rounded(v):
    return v.astype(BF16).astype(F32)


def project_kernel(
    n0, n1, n2, n3, halo,
    w00, w01, w02, w03, w10, w11, w12, w13,
    taps, rates, residues, skip,
    gate_ref, local_ref, chunk_ref, state_ref,
    lhs, w, proj, decay_s, taps_s, carry, sems,
):
    x = lax.axis_index("x")
    z = lax.axis_index("z")
    y = lax.axis_index("yh") * 2 + lax.axis_index("yl")
    core = lax.axis_index("co")
    copies = []

    def copy(src, dst):
        c = pltpu.make_async_copy(src, dst, sems.at[len(copies)])
        c.start()
        copies.append(c)

    copy(halo, lhs.at[pl.ds(0, HALO)])
    for d, piece in enumerate((n0, n1, n2, n3)):
        row = pl.multiple_of(HALO + lax.rem(x + NX - d, NX) * HERE, 16)
        copy(piece, lhs.at[pl.ds(row, HERE)])
    for r, pieces in enumerate(((w00, w01, w02, w03), (w10, w11, w12, w13))):
        for e, piece in enumerate(pieces):
            yy = lax.rem(y + NY - e, NY)
            base = lax.rem(yy, 2) * 1024 + lax.rem(core + r, 2) * 512 + (yy // 2) * 32
            for d in range(NZ):
                row = pl.multiple_of(base + lax.rem(z + NZ - d, NZ) * 64, 32)
                copy(piece.at[d], w.at[pl.ds(row, 32)])

    rate = rates[...]
    weight = residues[...] * jnp.sqrt(2.0 * rate)
    decay = jnp.exp(-rate)
    decay_s[...] = decay
    power = weight
    for i in range(CHUNK):
        row = jnp.sum(power, axis=0, keepdims=True)
        taps_s[i : i + 1, :] = row + skip[...] if i == 0 else row
        power = power * decay

    for c in copies:
        c.wait()

    @pl.loop(0, COLS // 256)
    def _(n):
        cols = pl.ds(pl.multiple_of(n * 256, 256), 256)
        proj[:, cols] = rounded(jnp.dot(lhs[...], w[:, cols], preferred_element_type=F32))

    sub = lax.broadcasted_iota(jnp.int32, (8, LANES), 0)

    def down(v, by):
        return jnp.where(sub >= by, pltpu.roll(v, by, 0), 0.0)

    @pl.loop(0, CH // LANES)
    def _(l):
        lane0 = pl.multiple_of(l * LANES, LANES)
        here = pl.ds(lane0, LANES)
        carry[...] = jnp.zeros_like(carry)

        @pl.loop(0, NX)
        def _(p):
            row0 = pl.multiple_of(p * HERE, 16)

            def featured(s):
                lanes = pl.ds(pl.multiple_of(s * CH + lane0, LANES), LANES)
                before = [proj[pl.ds(row0 + 8 * i, 8), lanes] for i in range(2)]
                rows = [proj[pl.ds(row0 + HALO + 8 * j, 8), lanes] for j in range(CHUNK)]
                t = [taps[i : i + 1, lanes] for i in range(3)]
                prev = [
                    jnp.where(sub == 0, pltpu.roll(before[i], 1, 0), pltpu.roll(rows[14 + i], 1, 0))
                    for i in range(2)
                ]
                ext = prev + rows
                return [
                    t[0] * ext[j + 2] + t[1] * ext[j + 1] + t[2] * ext[j] for j in range(CHUNK)
                ]

            queries = featured(0)
            for j in range(0, CHUNK, 2):
                gate_ref[pl.ds(pl.multiple_of(row0 + 8 * j, 16), 16), here] = jnp.concatenate(
                    queries[j : j + 2], axis=0
                ).astype(BF16)
            keys, values = featured(1), featured(2)
            carried = [rounded(a * b) for a, b in zip(keys, values)]

            k = [taps_s[i : i + 1, here] for i in range(CHUNK)]
            for j in range(CHUNK):
                acc = k[0] * carried[j]
                for i in range(j):
                    acc = acc + k[j - i] * carried[i]
                local_ref[pl.ds(row0 + 8 * j, 8), here] = acc

            for m in range(POLES):
                e = decay_s[m : m + 1, here]
                s = carried[0]
                for j in range(1, CHUNK):
                    s = s * e + carried[j]
                a1 = jnp.exp(-float(CHUNK) * rates[m : m + 1, here])
                a2 = a1 * a1
                a4 = a2 * a2
                s = s + a1 * down(s, 1)
                s = s + a2 * down(s, 2)
                s = s + a4 * down(s, 4)
                start = carry[m]
                s = s + jnp.exp(
                    -float(CHUNK) * rates[m : m + 1, here] * (sub + 1).astype(F32)
                ) * start
                chunk_ref[m, pl.ds(pl.multiple_of(p * 8, 8), 8), here] = jnp.where(
                    sub == 0, start, pltpu.roll(s, 1, 0)
                )
                carry[m] = jnp.broadcast_to(s[7:8, :], (8, LANES))

        for m in range(POLES):
            state_ref[m : m + 1, here] = carry[m, 0:1, :]


def project(normed, halo, weights, taps, rates, residues, skip):
    any_spec = pl.BlockSpec(memory_space=pl.ANY)
    vmem = pl.BlockSpec(memory_space=pltpu.VMEM)
    return pl.pallas_call(
        project_kernel,
        in_specs=[any_spec] * 13 + [vmem] * 4,
        out_specs=[vmem] * 4,
        out_shape=[
            jax.ShapeDtypeStruct((NX * HERE, CH), BF16),
            jax.ShapeDtypeStruct((NX * HERE, CH), F32),
            jax.ShapeDtypeStruct((POLES, NX * HERE // CHUNK, CH), F32),
            jax.ShapeDtypeStruct((POLES, CH), F32),
        ],
        scratch_shapes=[
            pltpu.VMEM((ROWS, D), BF16),
            pltpu.VMEM((D, COLS), BF16),
            pltpu.VMEM((ROWS, COLS), F32),
            pltpu.VMEM((POLES, CH), F32),
            pltpu.VMEM((CHUNK, CH), F32),
            pltpu.VMEM((POLES, 8, LANES), F32),
            pltpu.SemaphoreType.DMA((69,)),
        ],
        compiler_params=params(),
        cost_estimate=pl.CostEstimate(
            flops=2 * ROWS * D * COLS, bytes_accessed=12_000_000, transcendentals=0
        ),
    )(*normed, halo, *weights, taps, rates, residues, skip)


def finish_kernel(
    states, rates, residues, local, chunk, gate, o0, o1, o2, o3, scr, start_s, decay_s, weight_s
):
    x = lax.axis_index("x")
    g = lax.axis_index("z") * 2 + lax.axis_index("yh")
    rate = rates[...]
    span = jnp.exp(-float(NX * HERE) * rate)
    total = jnp.zeros((POLES, CH), F32)
    for i in range(GROUPS - 1):
        total = jnp.where(i < g, total * span + states[i], total)
    start_s[...] = total
    decay = jnp.exp(-rate)
    decay_s[...] = decay
    weight_s[...] = residues[...] * jnp.sqrt(2.0 * rate) * decay
    sub = lax.broadcasted_iota(jnp.int32, (8, LANES), 0)
    for d, out in enumerate((o0, o1, o2, o3)):
        p = lax.rem(x + d, NX)

        @pl.loop(0, CH // LANES)
        def _(l, p=p, out=out):
            here = pl.ds(pl.multiple_of(l * LANES, LANES), LANES)
            row0 = pl.multiple_of(p * HERE, 16)
            age = -float(CHUNK) * (p * 8 + sub).astype(F32)
            v, e = [], []
            for m in range(POLES):
                fade = jnp.exp(rates[m : m + 1, here] * age)
                at = chunk[m, pl.ds(pl.multiple_of(p * 8, 8), 8), here]
                v.append((at + fade * start_s[m : m + 1, here]) * weight_s[m : m + 1, here])
                e.append(decay_s[m : m + 1, here])
            for j in range(0, CHUNK, 2):
                gates = gate[pl.ds(pl.multiple_of(row0 + 8 * j, 16), 16), here].astype(F32)
                for i in range(2):
                    parts = list(v)
                    while len(parts) > 1:
                        parts = [a + b for a, b in zip(parts[::2], parts[1::2])]
                    response = rounded(local[pl.ds(row0 + 8 * (j + i), 8), here] + parts[0])
                    scr[pl.ds(j + i, 8, stride=CHUNK), :] = gates[8 * i : 8 * i + 8] * response
                    v = [a * b for a, b in zip(v, e)]
            out[here, :] = scr[...].T.astype(BF16)


def finish(states, rates, residues, local, chunk, gate):
    vmem = pl.BlockSpec(memory_space=pltpu.VMEM)
    return pl.pallas_call(
        finish_kernel,
        in_specs=[vmem] * 6,
        out_specs=[vmem] * NX,
        out_shape=[jax.ShapeDtypeStruct((CH, HERE), BF16)] * NX,
        scratch_shapes=[
            pltpu.VMEM((HERE, LANES), F32),
            pltpu.VMEM((POLES, CH), F32),
            pltpu.VMEM((POLES, CH), F32),
            pltpu.VMEM((POLES, CH), F32),
        ],
        compiler_params=params(),
    )(states, rates, residues, local, chunk, gate)


def place_kernel(p0, p1, p2, p3, out):
    x = lax.axis_index("x")
    for d, piece in enumerate((p0, p1, p2, p3)):
        at = lax.rem(x + NX - d, NX)
        for i in range(GROUPS):
            out[i, at] = piece[32 * i : 32 * i + 32, :]


def place(pieces):
    out = pl.pallas_call(
        place_kernel,
        out_shape=jax.ShapeDtypeStruct((GROUPS, NX, 32, HERE), BF16),
        compiler_params=params(),
    )(*pieces)
    return out.reshape(1, GROUPS * NX * 32, HERE)


def ring(size, by):
    return [(i, (i + by) % size) for i in range(size)]


def along_y(value, by):
    def flat(y):
        return (y % 2) * 2 + y // 2

    return lax.ppermute(value, ("yl", "yh"), [(flat(a), flat(b)) for a, b in ring(NY, by)])


def body(tokens, norm_gain, in_weight, short_filter, rates, residues, skip):
    x = lax.axis_index("x")
    own = normalise(tokens[0], norm_gain[None, :])
    others = {d: lax.ppermute(own, "x", ring(NX, d)) for d in (2, 1, 3)}
    normed = [own] + [others[d] for d in (1, 2, 3)]

    tails = jnp.stack([piece[HERE - HALO :] for piece in normed])
    tail = lax.dynamic_index_in_dim(tails, lax.rem(x + 1, NX), 0, keepdims=False)
    halo = lax.ppermute(tail, ("z", "yh"), [(i, i + 1) for i in range(GROUPS - 1)])

    blocks = in_weight.reshape(8, 3, GROUPS, NX, 32).transpose(3, 0, 1, 2, 4).reshape(NX, 8, COLS)
    unit = lax.all_to_all(blocks, "x", split_axis=0, concat_axis=0, tiled=True).reshape(32, COLS)
    along_z = {d: lax.ppermute(unit, "z", ring(NZ, d)) for d in (4, 3, 5, 2, 6, 1, 7)}
    plane = jnp.stack([unit] + [along_z[d] for d in range(1, NZ)])
    swap = [(0, 1), (1, 0)]
    planes = {0: plane}
    for e in (2, 1, 3):
        planes[e] = along_y(plane, e)
    sibling = {e: lax.ppermute(planes[e], "co", swap) for e in (0, 1, 3, 2)}
    weights = [planes[e] for e in range(NY)] + [sibling[e] for e in range(NY)]

    mine = jnp.concatenate(
        [
            rates.T.reshape(4, LANES),
            residues.T.reshape(4, LANES),
            jnp.pad(skip, (0, LANES - 32)).reshape(1, LANES),
        ]
    )
    table = lax.all_to_all(
        jnp.broadcast_to(mine[None], (GROUPS,) + mine.shape),
        ("z", "yh"),
        split_axis=0,
        concat_axis=0,
        tiled=True,
    )
    rate_table = table[:, 0:4].reshape(GROUPS, POLES, 32).transpose(1, 0, 2).reshape(POLES, CH)
    residue_table = table[:, 4:8].reshape(GROUPS, POLES, 32).transpose(1, 0, 2).reshape(POLES, CH)
    skip_row = table[:, 8, :32].reshape(1, CH)
    taps = short_filter.reshape(3, 3, GROUPS, NX, 32)
    taps = lax.dynamic_index_in_dim(taps, x, 3, keepdims=False).reshape(3, COLS)

    gate, local, chunk, state = project(
        normed, halo, weights, taps, rate_table, residue_table, skip_row
    )
    states = lax.all_to_all(
        jnp.broadcast_to(state[None], (GROUPS,) + state.shape),
        ("z", "yh"),
        split_axis=0,
        concat_axis=0,
        tiled=True,
    )
    pieces = finish(states, rate_table, residue_table, local, chunk, gate)
    arrived = {d: lax.ppermute(pieces[d], "x", ring(NX, d)) for d in (2, 1, 3)}
    return place([pieces[0]] + [arrived[d] for d in (1, 2, 3)])


def solution(mesh):
    fine = Mesh(mesh.devices.reshape(2, 2, NZ, 2, NX), ("yl", "co", "z", "yh", "x"))
    fsdp, ctx = ("yl", "co"), ("z", "yh", "x")
    in_specs = (
        P(fsdp, ctx, None),
        P(),
        P(fsdp + ctx, None),
        P(),
        P(ctx, None),
        P(ctx, None),
        P(ctx),
    )
    return jax.shard_map(
        body, mesh=fine, in_specs=in_specs, out_specs=P(fsdp, None, ctx), check_vma=False
    )
```

time: 1040 us -> 190 us (0.18); the launches traced: 1030 us -> 188 us
  waiting for transfers between devices: 746 us -> 89 us
  other arithmetic: 91.2 us -> 0.08 us
  matrix products: 65.7 us -> 0 us
  local copies, waits for them, and re-layouts: 46.1 us -> 7.44 us
  Pallas kernels: 0 us -> 19.3 us
  between operations: 14.9 us -> 0.25 us
  starting transfers between devices: 32.6 us -> 45.3 us
    all_gather x1 -> x0, waiting for transfers between devices: 741 us -> none  [body(): lax.all_gather(in_weight, ('fsdp', 'ctx'), axis=0, tiled=True)]
    unnamed x3 -> x0, other arithmetic: 70.1 us -> none
    dot_general x13 -> x0, matrix products: 65.7 us -> none  [the longest x1 24.7 us: long_conv(): jnp.einsum('cfb,bg->cfg', turned_re, inner_sin, precision=highest)]
    ppermute x1 -> x21, waiting for transfers between devices: 4.31 us -> 66.1 us  [the longest x7 30.4 us: body(): lax.ppermute(unit, 'z', ring(NZ, d))]
    ppermute x1 -> x21, starting transfers between devices: 1.92 us -> 29.2 us  [the longest x7 11.5 us: body(): lax.ppermute(unit, 'z', ring(NZ, d))]
    all_to_all x2, waiting for transfers between devices: 0.01 us -> 22.9 us  [the longest x1 14.7 us: body(): lax.all_to_all(blocks, 'x', split_axis=0, concat_axis=0, tiled=True)]
    pallas_call x0 -> x4, Pallas kernels: none -> 19.3 us  [the longest x1 14.5 us: project(): pl.pallas_call(project_kernel, in_specs=[any_spec] * 13 + [vmem] * 4, out...]
    unnamed x129 -> x25, local copies, waits for them, and re-layouts: 21.1 us -> 4.32 us
  transfers between devices with their start and end apart: 4 -> 23, of which waited for: 2 -> 14; matrix products, arithmetic and copies ran while one was open for 9% -> 2% of each run, Pallas kernels for 0% -> 0%
where the time goes in v1:
time: 190 us; the launch traced here: 188 us
  waiting for transfers between devices  89 us (47%)
  starting transfers between devices  45.3 us (24%)
  blocking collectives  27.1 us (14%)
  Pallas kernels  19.3 us (10%)
  local copies, waits for them, and re-layouts  7.44 us (4%)
    ppermute x7, waiting for transfers between devices, body(): lax.ppermute(unit, 'z', ring(NZ, d))  30.4 us
    ppermute x3, waiting for transfers between devices, along_y(): lax.ppermute(value, ('yl', 'yh'), [(flat(a), flat(b)) for a, b in ring(NY...  29.3 us
    all_to_all x1, blocking collectives, body(): lax.all_to_all(jnp.broadcast_to(state[None], (GROUPS,) + state.shape), ('...  27.1 us
    all_to_all x1, waiting for transfers between devices, body(): lax.all_to_all(blocks, 'x', split_axis=0, concat_axis=0, tiled=True)  14.7 us
    pallas_call x1, Pallas kernels, project(): pl.pallas_call(project_kernel, in_specs=[any_spec] * 13 + [vmem] * 4, out...  14.5 us
    ppermute x7, starting transfers between devices, body(): lax.ppermute(unit, 'z', ring(NZ, d))  11.5 us
    all_to_all x1, starting transfers between devices, body(): lax.all_to_all(jnp.broadcast_to(mine[None], (GROUPS,) + mine.shape), ('z'...  11.2 us
    all_to_all x1, waiting for transfers between devices, body(): lax.all_to_all(jnp.broadcast_to(mine[None], (GROUPS,) + mine.shape), ('z'...  8.26 us
  transfers between devices with their start and end apart: 23, of which 14 were waited for; matrix products, arithmetic and copies ran while one was open for 2% of the time, Pallas kernels for 0%

profile of v1, /device:TPU:2, one launch (start us, length us, event | category | flops | bytes accessed | tf_op | source)
XLA Modules:
  0.0 188.5 jit_solution(3999634535991485016)
XLA Ops:
  0.0 1.0 copy-done.2
  2.3 2.3 %collective-permute-start.2 = (bf16[128,2048]{1,0:T(8,128)(2,1)S(1)}, bf16[128,2048]{1,0:T(8,128)(2,1)S(1)}, u32[]{:S(2)}, u32[]{:S(2)}) collective-permute-start(bf16[128,2048]{1,0:T(8,128)(2,1)S(1)} %shard_map.73.n0), channel_id=1, source_target_pairs={{0,3},{1,0},{2,1},{3,2},{4,7},{5,4},{6,5},{7,6},{8,11},{9,8},{10,9... | collective-permute-start | bytes 1572872 | tf_op jit(solution)/shard_map/ppermute | solution.py:291
  5.3 1.8 collective-permute-start
  7.5 0.9 reshape.43
  8.4 4.9 %all-to-all-start = ((bf16[4,8,1536]{2,1,0:T(8,128)(2,1)}), bf16[4,8,1536]{2,1,0:T(8,128)(2,1)S(1)}, u32[]{:S(2)}, u32[]{:S(2)}) async-start(bf16[4,8,1536]{2,1,0:T(8,128)(2,1)} %reshape.43), calls=%async_computation | async-start | bytes 196608 | tf_op jit(solution)/shard_map/all_to_all | solution.py:299
  15.2 14.7 %all-to-all-done = bf16[4,8,1536]{2,1,0:T(8,128)(2,1)S(1)} async-done(((bf16[4,8,1536]{2,1,0:T(8,128)(2,1)}), bf16[4,8,1536]{2,1,0:T(8,128)(2,1)S(1)}, u32[]{:S(2)}, u32[]{:S(2)}) %all-to-all-start) | async-done | bytes 98336 | tf_op jit(solution)/shard_map/all_to_all | solution.py:299
  30.6 11.2 %all-to-all-start.1 = ((f32[16,9,128]{2,1,0:T(8,128)}), f32[16,9,128]{2,1,0:T(8,128)S(1)}, u32[]{:S(2)}, u32[]{:S(2)}) async-start(f32[16,9,128]{2,1,0:T(8,128)} %broadcast_in_dim.7), calls=%async_computation.1 | async-start | bytes 262144 | tf_op jit(solution)/shard_map/all_to_all | solution.py:316
  41.8 3.1 %collective-permute-start.10 = (bf16[32,1536]{1,0:T(8,128)(2,1)S(1)}, bf16[32,1536]{1,0:T(8,128)(2,1)S(1)}, u32[]{:S(2)}, u32[]{:S(2)}) collective-permute-start(bf16[32,1536]{1,0:T(8,128)(2,1)S(1)} %bitcast.49), channel_id=1, source_target_pairs={{0,56},{8,0},{16,8},{24,16},{32,24},{40,32},{48,40},{56,48},{1,57}... | collective-permute-start | bytes 294920 | tf_op jit(solution)/shard_map/ppermute | solution.py:300
  44.9 8.3 %all-to-all-done.1 = f32[16,9,128]{2,1,0:T(8,128)S(1)} async-done(((f32[16,9,128]{2,1,0:T(8,128)}), f32[16,9,128]{2,1,0:T(8,128)S(1)}, u32[]{:S(2)}, u32[]{:S(2)}) %all-to-all-start.1) | async-done | bytes 73760 | tf_op jit(solution)/shard_map/all_to_all | solution.py:316
  53.8 6.7 %collective-permute-done.5 = bf16[32,1536]{1,0:T(8,128)(2,1)S(1)} collective-permute-done((bf16[32,1536]{1,0:T(8,128)(2,1)S(1)}, bf16[32,1536]{1,0:T(8,128)(2,1)S(1)}, u32[]{:S(2)}, u32[]{:S(2)}) %collective-permute-start.5) | collective-permute-done | bytes 98336 | tf_op jit(solution)/shard_map/ppermute | solution.py:300
  60.7 8.2 %collective-permute-done.6 = bf16[32,1536]{1,0:T(8,128)(2,1)S(1)} collective-permute-done((bf16[32,1536]{1,0:T(8,128)(2,1)S(1)}, bf16[32,1536]{1,0:T(8,128)(2,1)S(1)}, u32[]{:S(2)}, u32[]{:S(2)}) %collective-permute-start.6) | collective-permute-done | bytes 98336 | tf_op jit(solution)/shard_map/ppermute | solution.py:300
  68.9 2.5 %collective-permute-start.7 = (bf16[32,1536]{1,0:T(8,128)(2,1)S(1)}, bf16[32,1536]{1,0:T(8,128)(2,1)S(1)}, u32[]{:S(2)}, u32[]{:S(2)}) collective-permute-start(bf16[32,1536]{1,0:T(8,128)(2,1)S(1)} %bitcast.53), channel_id=1, source_target_pairs={{0,32},{8,40},{16,48},{24,56},{32,0},{40,8},{48,16},{56,24},{1,33}... | collective-permute-start | bytes 294920 | tf_op jit(solution)/shard_map/ppermute | solution.py:300
  71.4 6.4 %collective-permute-done.7 = bf16[32,1536]{1,0:T(8,128)(2,1)S(1)} collective-permute-done((bf16[32,1536]{1,0:T(8,128)(2,1)S(1)}, bf16[32,1536]{1,0:T(8,128)(2,1)S(1)}, u32[]{:S(2)}, u32[]{:S(2)}) %collective-permute-start.7) | collective-permute-done | bytes 98336 | tf_op jit(solution)/shard_map/ppermute | solution.py:300
  77.7 0.9 collective-permute-start.8
  78.6 6.8 %collective-permute-done.8 = bf16[32,1536]{1,0:T(8,128)(2,1)S(1)} collective-permute-done((bf16[32,1536]{1,0:T(8,128)(2,1)S(1)}, bf16[32,1536]{1,0:T(8,128)(2,1)S(1)}, u32[]{:S(2)}, u32[]{:S(2)}) %collective-permute-start.8) | collective-permute-done | bytes 98336 | tf_op jit(solution)/shard_map/ppermute | solution.py:300
  85.4 4.3 %collective-permute-start.9 = (bf16[32,1536]{1,0:T(8,128)(2,1)S(1)}, bf16[32,1536]{1,0:T(8,128)(2,1)S(1)}, u32[]{:S(2)}, u32[]{:S(2)}) collective-permute-start(bf16[32,1536]{1,0:T(8,128)(2,1)S(1)} %bitcast.55), channel_id=1, source_target_pairs={{0,48},{8,56},{16,0},{24,8},{32,16},{40,24},{48,32},{56,40},{1,49}... | collective-permute-start | bytes 294920 | tf_op jit(solution)/shard_map/ppermute | solution.py:300
  89.8 2.3 %collective-permute-done.9 = bf16[32,1536]{1,0:T(8,128)(2,1)S(1)} collective-permute-done((bf16[32,1536]{1,0:T(8,128)(2,1)S(1)}, bf16[32,1536]{1,0:T(8,128)(2,1)S(1)}, u32[]{:S(2)}, u32[]{:S(2)}) %collective-permute-start.9) | collective-permute-done | bytes 98336 | tf_op jit(solution)/shard_map/ppermute | solution.py:300
  92.3 2.6 %collective-permute-start.12 = (bf16[8,32,1536]{2,1,0:T(8,128)(2,1)S(1)}, bf16[8,32,1536]{2,1,0:T(8,128)(2,1)}, u32[]{:S(2)}, u32[]{:S(2)}) collective-permute-start(bf16[8,32,1536]{2,1,0:T(8,128)(2,1)S(1)} %bitcast_dynamic-update-slice_fusion.w00), channel_id=1, source_target_pairs={{0,4},{128,132},{4,0},{132,128},{1,5},{129,133},{5,1},{133,129},{2... | collective-permute-start | bytes 2359304 | tf_op jit(solution)/shard_map/ppermute | solution.py:285
  95.1 17.7 %collective-permute-done.13.w03 = bf16[8,32,1536]{2,1,0:T(8,128)(2,1)} collective-permute-done((bf16[8,32,1536]{2,1,0:T(8,128)(2,1)S(1)}, bf16[8,32,1536]{2,1,0:T(8,128)(2,1)}, u32[]{:S(2)}, u32[]{:S(2)}) %collective-permute-start.13) | collective-permute-done | bytes 786464 | tf_op jit(solution)/shard_map/ppermute | solution.py:285
  112.8 1.6 collective-permute-done.12.w02
  114.4 10.0 %collective-permute-done.11.w01 = bf16[8,32,1536]{2,1,0:T(8,128)(2,1)} collective-permute-done((bf16[8,32,1536]{2,1,0:T(8,128)(2,1)S(1)}, bf16[8,32,1536]{2,1,0:T(8,128)(2,1)}, u32[]{:S(2)}, u32[]{:S(2)}) %collective-permute-start.11) | collective-permute-done | bytes 786464 | tf_op jit(solution)/shard_map/ppermute | solution.py:285
  124.5 3.5 %collective-permute-start.3 = (bf16[16,2048]{1,0:T(8,128)(2,1)S(1)}, bf16[16,2048]{1,0:T(8,128)(2,1)S(1)}, u32[]{:S(2)}, u32[]{:S(2)}) collective-permute-start(bf16[16,2048]{1,0:T(8,128)(2,1)S(1)} %fusion.3), channel_id=1, source_target_pairs={{0,4},{4,8},{8,12},{12,16},{16,20},{20,24},{24,28},{28,32},{32,36}... | collective-permute-start | bytes 196616 | tf_op jit(solution)/shard_map/ppermute | solution.py:296
  128.7 1.4 collective-permute-done.3.halo
  130.0 14.5 %shard_map.74 = (bf16[512,512]{1,0:T(8,128)(2,1)S(1)}, f32[512,512]{1,0:T(8,128)}, f32[16,32,512]{2,1,0:T(8,128)}, f32[16,512]{1,0:T(8,128)S(1)}) custom-call(bf16[128,2048]{1,0:T(8,128)(2,1)S(1)} %shard_map.73.n0, bf16[128,2048]{1,0:T(8,128)(2,1)S(1)} %collective-permute-done.n1, bf16[128,2048]{1,0:T(8,128)(2,1)S(1)} %collective-permute-done.1.n2, ...), custom_call_target="tpu_custom_call" | custom-call | flops 3321888768 | bytes 12000000 | tf_op jit(solution)/shard_map/pallas_call | solution.py:176
  144.6 27.1 %all_to_all.15.states = f32[16,16,512]{2,1,0:T(8,128)S(1)} all-to-all(f32[16,16,512]{2,1,0:T(8,128)S(1)} %broadcast_in_dim.8), channel_id=1, replica_groups=mesh['yl'=2,'co'=2,'z'=8,'yh'=2,'x'=4] {'z','yh'}, dimensions={0} | all-to-all | bytes 1048576 | tf_op jit(solution)/shard_map/all_to_all | solution.py:332
  171.7 1.2 copy-done.1
  172.9 3.4 %shard_map.75 = (bf16[512,128]{1,0:T(8,128)(2,1)S(1)}, bf16[512,128]{1,0:T(8,128)(2,1)S(1)}, bf16[512,128]{1,0:T(8,128)(2,1)S(1)}, bf16[512,128]{1,0:T(8,128)(2,1)S(1)}) custom-call(f32[16,16,512]{2,1,0:T(8,128)S(1)} %all_to_all.15.states, f32[16,512]{1,0:T(8,128)S(1)} %reshape.51.rates, f32[16,512]{1,0:T(8,128)S(1)} %reshape.53.residues, ...), custom_call_target="tpu_custom_call" | custom-call | tf_op jit(solution)/shard_map/pallas_call | solution.py:245
  176.3 3.0 %collective-permute-start.18 = (bf16[512,128]{1,0:T(8,128)(2,1)S(1)}, bf16[512,128]{1,0:T(8,128)(2,1)S(1)}, u32[]{:S(2)}, u32[]{:S(2)}) collective-permute-start(bf16[512,128]{1,0:T(8,128)(2,1)S(1)} %get-tuple-element.18), channel_id=1, source_target_pairs={{0,1},{1,2},{2,3},{3,0},{4,5},{5,6},{6,7},{7,4},{8,9},{9,10},{10,1... | collective-permute-start | bytes 393224 | tf_op jit(solution)/shard_map/ppermute | solution.py:340
  179.4 3.3 %collective-permute-start.19 = (bf16[512,128]{1,0:T(8,128)(2,1)S(1)}, bf16[512,128]{1,0:T(8,128)(2,1)S(1)}, u32[]{:S(2)}, u32[]{:S(2)}) collective-permute-start(bf16[512,128]{1,0:T(8,128)(2,1)S(1)} %get-tuple-element.19), channel_id=1, source_target_pairs={{0,2},{1,3},{2,0},{3,1},{4,6},{5,7},{6,4},{7,5},{8,10},{9,11},{10,... | collective-permute-start | bytes 393224 | tf_op jit(solution)/shard_map/ppermute | solution.py:340
  182.7 1.0 collective-permute-done.18.p1
  183.7 2.1 %collective-permute-done.19.p2 = bf16[512,128]{1,0:T(8,128)(2,1)S(1)} collective-permute-done((bf16[512,128]{1,0:T(8,128)(2,1)S(1)}, bf16[512,128]{1,0:T(8,128)(2,1)S(1)}, u32[]{:S(2)}, u32[]{:S(2)}) %collective-permute-start.19) | collective-permute-done | bytes 131104 | tf_op jit(solution)/shard_map/ppermute | solution.py:340
  185.8 1.8 collective-permute-done.20.p3
  (71 shorter events, 7.4 us)
Async XLA Ops:
  0.0 1.0 copy-start.2
  1.0 0.7 copy-start.3
  1.7 5.4 %copy-start.5 = (bf16[8,6144]{1,0:T(8,128)(2,1)S(1)}, bf16[8,6144]{1,0:T(8,128)(2,1)}, u32[]{:S(2)}) copy-start(bf16[8,6144]{1,0:T(8,128)(2,1)} %param.9) | copy-start | bytes 294916
  2.3 92.6 %collective-permute-start.2 = (bf16[128,2048]{1,0:T(8,128)(2,1)S(1)}, bf16[128,2048]{1,0:T(8,128)(2,1)S(1)}, u32[]{:S(2)}, u32[]{:S(2)}) collective-permute-start(bf16[128,2048]{1,0:T(8,128)(2,1)S(1)} %shard_map.73.n0), channel_id=1, source_target_pairs={{0,3},{1,0},{2,1},{3,2},{4,7},{5,4},{6,5},{7,6},{8,11},{9,8},{10,9... | collective-permute-start | bytes 1572872 | tf_op jit(solution)/shard_map/ppermute | solution.py:291
  4.7 90.3 %collective-permute-start.1 = (bf16[128,2048]{1,0:T(8,128)(2,1)S(1)}, bf16[128,2048]{1,0:T(8,128)(2,1)S(1)}, u32[]{:S(2)}, u32[]{:S(2)}) collective-permute-start(bf16[128,2048]{1,0:T(8,128)(2,1)S(1)} %shard_map.73.n0), channel_id=1, source_target_pairs={{0,2},{1,3},{2,0},{3,1},{4,6},{5,7},{6,4},{7,5},{8,10},{9,11},{10,... | collective-permute-start | bytes 1572872 | tf_op jit(solution)/shard_map/ppermute | solution.py:291
  5.3 119.1 %collective-permute-start = (bf16[128,2048]{1,0:T(8,128)(2,1)S(1)}, bf16[128,2048]{1,0:T(8,128)(2,1)S(1)}, u32[]{:S(2)}, u32[]{:S(2)}) collective-permute-start(bf16[128,2048]{1,0:T(8,128)(2,1)S(1)} %shard_map.73.n0), channel_id=1, source_target_pairs={{0,1},{1,2},{2,3},{3,0},{4,5},{5,6},{6,7},{7,4},{8,9},{9,10},{10,1... | collective-permute-start | bytes 1572872 | tf_op jit(solution)/shard_map/ppermute | solution.py:291
  8.4 21.5 %all-to-all-start = ((bf16[4,8,1536]{2,1,0:T(8,128)(2,1)}), bf16[4,8,1536]{2,1,0:T(8,128)(2,1)S(1)}, u32[]{:S(2)}, u32[]{:S(2)}) async-start(bf16[4,8,1536]{2,1,0:T(8,128)(2,1)} %reshape.43), calls=%async_computation | async-start | bytes 196608 | tf_op jit(solution)/shard_map/all_to_all | solution.py:299
  13.4 1.5 copy-start.4
  13.4 0.7 copy-start.8
  13.4 0.7 copy-start.6
  14.0 0.7 copy-start.7
  30.6 22.6 %all-to-all-start.1 = ((f32[16,9,128]{2,1,0:T(8,128)}), f32[16,9,128]{2,1,0:T(8,128)S(1)}, u32[]{:S(2)}, u32[]{:S(2)}) async-start(f32[16,9,128]{2,1,0:T(8,128)} %broadcast_in_dim.7), calls=%async_computation.1 | async-start | bytes 262144 | tf_op jit(solution)/shard_map/all_to_all | solution.py:316
  41.8 50.3 %collective-permute-start.10 = (bf16[32,1536]{1,0:T(8,128)(2,1)S(1)}, bf16[32,1536]{1,0:T(8,128)(2,1)S(1)}, u32[]{:S(2)}, u32[]{:S(2)}) collective-permute-start(bf16[32,1536]{1,0:T(8,128)(2,1)S(1)} %bitcast.49), channel_id=1, source_target_pairs={{0,56},{8,0},{16,8},{24,16},{32,24},{40,32},{48,40},{56,48},{1,57}... | collective-permute-start | bytes 294920 | tf_op jit(solution)/shard_map/ppermute | solution.py:300
  44.9 8.3 %collective-permute-start.4 = (bf16[32,1536]{1,0:T(8,128)(2,1)S(1)}, bf16[32,1536]{1,0:T(8,128)(2,1)S(1)}, u32[]{:S(2)}, u32[]{:S(2)}) collective-permute-start(bf16[32,1536]{1,0:T(8,128)(2,1)S(1)} %bitcast.50), channel_id=1, source_target_pairs={{0,8},{8,16},{16,24},{24,32},{32,40},{40,48},{48,56},{56,0},{1,9},... | collective-permute-start | bytes 294920 | tf_op jit(solution)/shard_map/ppermute | solution.py:300
  53.2 7.4 %collective-permute-start.5 = (bf16[32,1536]{1,0:T(8,128)(2,1)S(1)}, bf16[32,1536]{1,0:T(8,128)(2,1)S(1)}, u32[]{:S(2)}, u32[]{:S(2)}) collective-permute-start(bf16[32,1536]{1,0:T(8,128)(2,1)S(1)} %bitcast.51), channel_id=1, source_target_pairs={{0,16},{8,24},{16,32},{24,40},{32,48},{40,56},{48,0},{56,8},{1,17}... | collective-permute-start | bytes 294920 | tf_op jit(solution)/shard_map/ppermute | solution.py:300
  60.6 8.3 %collective-permute-start.6 = (bf16[32,1536]{1,0:T(8,128)(2,1)S(1)}, bf16[32,1536]{1,0:T(8,128)(2,1)S(1)}, u32[]{:S(2)}, u32[]{:S(2)}) collective-permute-start(bf16[32,1536]{1,0:T(8,128)(2,1)S(1)} %bitcast.52), channel_id=1, source_target_pairs={{0,24},{8,32},{16,40},{24,48},{32,56},{40,0},{48,8},{56,16},{1,25}... | collective-permute-start | bytes 294920 | tf_op jit(solution)/shard_map/ppermute | solution.py:300
  68.9 8.8 %collective-permute-start.7 = (bf16[32,1536]{1,0:T(8,128)(2,1)S(1)}, bf16[32,1536]{1,0:T(8,128)(2,1)S(1)}, u32[]{:S(2)}, u32[]{:S(2)}) collective-permute-start(bf16[32,1536]{1,0:T(8,128)(2,1)S(1)} %bitcast.53), channel_id=1, source_target_pairs={{0,32},{8,40},{16,48},{24,56},{32,0},{40,8},{48,16},{56,24},{1,33}... | collective-permute-start | bytes 294920 | tf_op jit(solution)/shard_map/ppermute | solution.py:300
  77.7 7.7 %collective-permute-start.8 = (bf16[32,1536]{1,0:T(8,128)(2,1)S(1)}, bf16[32,1536]{1,0:T(8,128)(2,1)S(1)}, u32[]{:S(2)}, u32[]{:S(2)}) collective-permute-start(bf16[32,1536]{1,0:T(8,128)(2,1)S(1)} %bitcast.54), channel_id=1, source_target_pairs={{0,40},{8,48},{16,56},{24,0},{32,8},{40,16},{48,24},{56,32},{1,41}... | collective-permute-start | bytes 294920 | tf_op jit(solution)/shard_map/ppermute | solution.py:300
  85.4 6.6 %collective-permute-start.9 = (bf16[32,1536]{1,0:T(8,128)(2,1)S(1)}, bf16[32,1536]{1,0:T(8,128)(2,1)S(1)}, u32[]{:S(2)}, u32[]{:S(2)}) collective-permute-start(bf16[32,1536]{1,0:T(8,128)(2,1)S(1)} %bitcast.55), channel_id=1, source_target_pairs={{0,48},{8,56},{16,0},{24,8},{32,16},{40,24},{48,32},{56,40},{1,49}... | collective-permute-start | bytes 294920 | tf_op jit(solution)/shard_map/ppermute | solution.py:300
  92.1 20.7 %collective-permute-start.13 = (bf16[8,32,1536]{2,1,0:T(8,128)(2,1)S(1)}, bf16[8,32,1536]{2,1,0:T(8,128)(2,1)}, u32[]{:S(2)}, u32[]{:S(2)}) collective-permute-start(bf16[8,32,1536]{2,1,0:T(8,128)(2,1)S(1)} %bitcast_dynamic-update-slice_fusion.w00), channel_id=1, source_target_pairs={{0,132},{128,0},{4,128},{132,4},{1,133},{129,1},{5,129},{133,5},{2... | collective-permute-start | bytes 2359304 | tf_op jit(solution)/shard_map/ppermute | solution.py:285
  92.3 22.1 %collective-permute-start.12 = (bf16[8,32,1536]{2,1,0:T(8,128)(2,1)S(1)}, bf16[8,32,1536]{2,1,0:T(8,128)(2,1)}, u32[]{:S(2)}, u32[]{:S(2)}) collective-permute-start(bf16[8,32,1536]{2,1,0:T(8,128)(2,1)S(1)} %bitcast_dynamic-update-slice_fusion.w00), channel_id=1, source_target_pairs={{0,4},{128,132},{4,0},{132,128},{1,5},{129,133},{5,1},{133,129},{2... | collective-permute-start | bytes 2359304 | tf_op jit(solution)/shard_map/ppermute | solution.py:285
  94.9 29.5 %collective-permute-start.11 = (bf16[8,32,1536]{2,1,0:T(8,128)(2,1)S(1)}, bf16[8,32,1536]{2,1,0:T(8,128)(2,1)}, u32[]{:S(2)}, u32[]{:S(2)}) collective-permute-start(bf16[8,32,1536]{2,1,0:T(8,128)(2,1)S(1)} %bitcast_dynamic-update-slice_fusion.w00), channel_id=1, source_target_pairs={{0,128},{128,4},{4,132},{132,0},{1,129},{129,5},{5,133},{133,1},{2... | collective-permute-start | bytes 2359304 | tf_op jit(solution)/shard_map/ppermute | solution.py:285
  94.9 35.1 %collective-permute-start.14 = (bf16[8,32,1536]{2,1,0:T(8,128)(2,1)S(1)}, bf16[8,32,1536]{2,1,0:T(8,128)(2,1)}, u32[]{:S(2)}, u32[]{:S(2)}) collective-permute-start(bf16[8,32,1536]{2,1,0:T(8,128)(2,1)S(1)} %bitcast_dynamic-update-slice_fusion.w00), channel_id=1, source_target_pairs={{0,64},{64,0},{1,65},{65,1},{2,66},{66,2},{3,67},{67,3},{4,68},{68... | collective-permute-start | bytes 2359304 | tf_op jit(solution)/shard_map/ppermute | solution.py:306
  112.8 17.3 %collective-permute-start.17 = (bf16[8,32,1536]{2,1,0:T(8,128)(2,1)}, bf16[8,32,1536]{2,1,0:T(8,128)(2,1)}, u32[]{:S(2)}, u32[]{:S(2)}) collective-permute-start(bf16[8,32,1536]{2,1,0:T(8,128)(2,1)} %collective-permute-done.13.w03), channel_id=1, source_target_pairs={{0,64},{64,0},{1,65},{65,1},{2,66},{66,2},{3,67},{67,3},{4,68},{68... | collective-permute-start | bytes 2359304 | tf_op jit(solution)/shard_map/ppermute | solution.py:306
  114.4 15.7 %collective-permute-start.16 = (bf16[8,32,1536]{2,1,0:T(8,128)(2,1)}, bf16[8,32,1536]{2,1,0:T(8,128)(2,1)}, u32[]{:S(2)}, u32[]{:S(2)}) collective-permute-start(bf16[8,32,1536]{2,1,0:T(8,128)(2,1)} %collective-permute-done.12.w02), channel_id=1, source_target_pairs={{0,64},{64,0},{1,65},{65,1},{2,66},{66,2},{3,67},{67,3},{4,68},{68... | collective-permute-start | bytes 2359304 | tf_op jit(solution)/shard_map/ppermute | solution.py:306
  124.4 5.7 %collective-permute-start.15 = (bf16[8,32,1536]{2,1,0:T(8,128)(2,1)}, bf16[8,32,1536]{2,1,0:T(8,128)(2,1)}, u32[]{:S(2)}, u32[]{:S(2)}) collective-permute-start(bf16[8,32,1536]{2,1,0:T(8,128)(2,1)} %collective-permute-done.11.w01), channel_id=1, source_target_pairs={{0,64},{64,0},{1,65},{65,1},{2,66},{66,2},{3,67},{67,3},{4,68},{68... | collective-permute-start | bytes 2359304 | tf_op jit(solution)/shard_map/ppermute | solution.py:306
  124.5 5.5 %collective-permute-start.3 = (bf16[16,2048]{1,0:T(8,128)(2,1)S(1)}, bf16[16,2048]{1,0:T(8,128)(2,1)S(1)}, u32[]{:S(2)}, u32[]{:S(2)}) collective-permute-start(bf16[16,2048]{1,0:T(8,128)(2,1)S(1)} %fusion.3), channel_id=1, source_target_pairs={{0,4},{4,8},{8,12},{12,16},{16,20},{20,24},{24,28},{28,32},{32,36}... | collective-permute-start | bytes 196616 | tf_op jit(solution)/shard_map/ppermute | solution.py:296
  144.5 27.1 %copy-start = (f32[512,512]{1,0:T(8,128)S(1)}, f32[512,512]{1,0:T(8,128)}, u32[]{:S(2)}) copy-start(f32[512,512]{1,0:T(8,128)} %get-tuple-element.14.local) | copy-start | bytes 3145732
  171.7 1.2 copy-start.1
  176.3 7.4 %collective-permute-start.18 = (bf16[512,128]{1,0:T(8,128)(2,1)S(1)}, bf16[512,128]{1,0:T(8,128)(2,1)S(1)}, u32[]{:S(2)}, u32[]{:S(2)}) collective-permute-start(bf16[512,128]{1,0:T(8,128)(2,1)S(1)} %get-tuple-element.18), channel_id=1, source_target_pairs={{0,1},{1,2},{2,3},{3,0},{4,5},{5,6},{6,7},{7,4},{8,9},{9,10},{10,1... | collective-permute-start | bytes 393224 | tf_op jit(solution)/shard_map/ppermute | solution.py:340
  179.4 6.5 %collective-permute-start.19 = (bf16[512,128]{1,0:T(8,128)(2,1)S(1)}, bf16[512,128]{1,0:T(8,128)(2,1)S(1)}, u32[]{:S(2)}, u32[]{:S(2)}) collective-permute-start(bf16[512,128]{1,0:T(8,128)(2,1)S(1)} %get-tuple-element.19), channel_id=1, source_target_pairs={{0,2},{1,3},{2,0},{3,1},{4,6},{5,7},{6,4},{7,5},{8,10},{9,11},{10,... | collective-permute-start | bytes 393224 | tf_op jit(solution)/shard_map/ppermute | solution.py:340
  182.7 5.0 %collective-permute-start.20 = (bf16[512,128]{1,0:T(8,128)(2,1)S(1)}, bf16[512,128]{1,0:T(8,128)(2,1)S(1)}, u32[]{:S(2)}, u32[]{:S(2)}) collective-permute-start(bf16[512,128]{1,0:T(8,128)(2,1)S(1)} %get-tuple-element.20), channel_id=1, source_target_pairs={{0,3},{1,0},{2,1},{3,2},{4,7},{5,4},{6,5},{7,6},{8,11},{9,8},{10,9... | collective-permute-start | bytes 393224 | tf_op jit(solution)/shard_map/ppermute | solution.py:340

commit v2 on v1

--- a/solution.py
+++ b/solution.py
@@ -9,15 +9,16 @@
 
 F32 = jnp.float32
 BF16 = jnp.bfloat16
-NX, NY, NZ = 4, 4, 8
-GROUPS = 16
+NX, NZ = 4, 8
+PIECES = 8
 POLES = 16
 HERE = 128
 CHUNK = 16
 LANES = 128
-CH = 512
+CH = 256
 HALO = 16
-ROWS = HALO + NX * HERE
+SPAN = PIECES * HERE
+ROWS = HALO + SPAN
 D = 2048
 COLS = 3 * CH
 VMEM_LIMIT = 50 * 1024 * 1024
@@ -55,15 +56,14 @@
 
 
 def project_kernel(
-    n0, n1, n2, n3, halo,
-    w00, w01, w02, w03, w10, w11, w12, w13,
+    a0, a1, a2, a3, b0, b1, b2, b3, halo, w00, w01, w10, w11,
     taps, rates, residues, skip,
     gate_ref, local_ref, chunk_ref, state_ref,
     lhs, w, proj, decay_s, taps_s, carry, sems,
 ):
     x = lax.axis_index("x")
-    z = lax.axis_index("z")
-    y = lax.axis_index("yh") * 2 + lax.axis_index("yl")
+    yh = lax.axis_index("yh")
+    yl = lax.axis_index("yl")
     core = lax.axis_index("co")
     copies = []
 
@@ -72,17 +72,15 @@
         c.start()
         copies.append(c)
 
+    for r, pieces in enumerate(((w00, w01), (w10, w11))):
+        for e, piece in enumerate(pieces):
+            row = lax.rem(yl + e, 2) * 1024 + lax.rem(core + r, 2) * 512
+            copy(piece, w.at[pl.ds(pl.multiple_of(row, 512), 512)])
     copy(halo, lhs.at[pl.ds(0, HALO)])
-    for d, piece in enumerate((n0, n1, n2, n3)):
-        row = pl.multiple_of(HALO + lax.rem(x + NX - d, NX) * HERE, 16)
-        copy(piece, lhs.at[pl.ds(row, HERE)])
-    for r, pieces in enumerate(((w00, w01, w02, w03), (w10, w11, w12, w13))):
-        for e, piece in enumerate(pieces):
-            yy = lax.rem(y + NY - e, NY)
-            base = lax.rem(yy, 2) * 1024 + lax.rem(core + r, 2) * 512 + (yy // 2) * 32
-            for d in range(NZ):
-                row = pl.multiple_of(base + lax.rem(z + NZ - d, NZ) * 64, 32)
-                copy(piece.at[d], w.at[pl.ds(row, 32)])
+    for e, pieces in enumerate(((a0, a1, a2, a3), (b0, b1, b2, b3))):
+        for d, piece in enumerate(pieces):
+            at = lax.rem(yh + e, 2) * NX + lax.rem(x + NX - d, NX)
+            copy(piece, lhs.at[pl.ds(pl.multiple_of(HALO + at * HERE, 16), HERE)])
 
     rate = rates[...]
     weight = residues[...] * jnp.sqrt(2.0 * rate)
@@ -113,7 +111,7 @@
         here = pl.ds(lane0, LANES)
         carry[...] = jnp.zeros_like(carry)
 
-        @pl.loop(0, NX)
+        @pl.loop(0, PIECES)
         def _(p):
             row0 = pl.multiple_of(p * HERE, 16)
 
@@ -178,9 +176,9 @@
         in_specs=[any_spec] * 13 + [vmem] * 4,
         out_specs=[vmem] * 4,
         out_shape=[
-            jax.ShapeDtypeStruct((NX * HERE, CH), BF16),
-            jax.ShapeDtypeStruct((NX * HERE, CH), F32),
-            jax.ShapeDtypeStruct((POLES, NX * HERE // CHUNK, CH), F32),
+            jax.ShapeDtypeStruct((SPAN, CH), BF16),
+            jax.ShapeDtypeStruct((SPAN, CH), F32),
+            jax.ShapeDtypeStruct((POLES, SPAN // CHUNK, CH), F32),
             jax.ShapeDtypeStruct((POLES, CH), F32),
         ],
         scratch_shapes=[
@@ -190,7 +188,7 @@
             pltpu.VMEM((POLES, CH), F32),
             pltpu.VMEM((CHUNK, CH), F32),
             pltpu.VMEM((POLES, 8, LANES), F32),
-            pltpu.SemaphoreType.DMA((69,)),
+            pltpu.SemaphoreType.DMA((13,)),
         ],
         compiler_params=params(),
         cost_estimate=pl.CostEstimate(
@@ -200,25 +198,24 @@
 
 
 def finish_kernel(
-    states, rates, residues, local, chunk, gate, o0, o1, o2, o3, scr, start_s, decay_s, weight_s
+    states, rates, residues, local, chunk, gate, out, scr, start_s, decay_s, weight_s
 ):
-    x = lax.axis_index("x")
-    g = lax.axis_index("z") * 2 + lax.axis_index("yh")
+    z = lax.axis_index("z")
     rate = rates[...]
-    span = jnp.exp(-float(NX * HERE) * rate)
+    span = jnp.exp(-float(SPAN) * rate)
     total = jnp.zeros((POLES, CH), F32)
-    for i in range(GROUPS - 1):
-        total = jnp.where(i < g, total * span + states[i], total)
+    for i in range(NZ - 1):
+        total = jnp.where(i < z, total * span + states[i], total)
     start_s[...] = total
     decay = jnp.exp(-rate)
     decay_s[...] = decay
     weight_s[...] = residues[...] * jnp.sqrt(2.0 * rate) * decay
     sub = lax.broadcasted_iota(jnp.int32, (8, LANES), 0)
-    for d, out in enumerate((o0, o1, o2, o3)):
-        p = lax.rem(x + d, NX)
-
+
+    @pl.loop(0, PIECES)
+    def _(p):
         @pl.loop(0, CH // LANES)
-        def _(l, p=p, out=out):
+        def _(l):
             here = pl.ds(pl.multiple_of(l * LANES, LANES), LANES)
             row0 = pl.multiple_of(p * HERE, 16)
             age = -float(CHUNK) * (p * 8 + sub).astype(F32)
@@ -237,7 +234,7 @@
                     response = rounded(local[pl.ds(row0 + 8 * (j + i), 8), here] + parts[0])
                     scr[pl.ds(j + i, 8, stride=CHUNK), :] = gates[8 * i : 8 * i + 8] * response
                     v = [a * b for a, b in zip(v, e)]
-            out[here, :] = scr[...].T.astype(BF16)
+            out[p, here, :] = scr[...].T.astype(BF16)
 
 
 def finish(states, rates, residues, local, chunk, gate):
@@ -245,8 +242,8 @@
     return pl.pallas_call(
         finish_kernel,
         in_specs=[vmem] * 6,
-        out_specs=[vmem] * NX,
-        out_shape=[jax.ShapeDtypeStruct((CH, HERE), BF16)] * NX,
+        out_specs=vmem,
+        out_shape=jax.ShapeDtypeStruct((PIECES, CH, HERE), BF16),
         scratch_shapes=[
             pltpu.VMEM((HERE, LANES), F32),
             pltpu.VMEM((POLES, CH), F32),
@@ -257,55 +254,62 @@
     )(states, rates, residues, local, chunk, gate)
 
 
-def place_kernel(p0, p1, p2, p3, out):
-    x = lax.axis_index("x")
-    for d, piece in enumerate((p0, p1, p2, p3)):
-        at = lax.rem(x + NX - d, NX)
-        for i in range(GROUPS):
-            out[i, at] = piece[32 * i : 32 * i + 32, :]
+def place_kernel(pieces, out):
+    for g in range(PIECES):
+        for i in range(NZ):
+            out[i, g] = pieces[g, 32 * i : 32 * i + 32, :]
 
 
 def place(pieces):
     out = pl.pallas_call(
         place_kernel,
-        out_shape=jax.ShapeDtypeStruct((GROUPS, NX, 32, HERE), BF16),
+        out_shape=jax.ShapeDtypeStruct((NZ, PIECES, 32, HERE), BF16),
         compiler_params=params(),
-    )(*pieces)
-    return out.reshape(1, GROUPS * NX * 32, HERE)
+    )(pieces)
+    return out.reshape(1, NZ * PIECES * 32, HERE)
 
 
 def ring(size, by):
     return [(i, (i + by) % size) for i in range(size)]
 
 
-def along_y(value, by):
-    def flat(y):
-        return (y % 2) * 2 + y // 2
-
-    return lax.ppermute(value, ("yl", "yh"), [(flat(a), flat(b)) for a, b in ring(NY, by)])
+def along_x(value):
+    got = {d: lax.ppermute(value, "x", ring(NX, d)) for d in (2, 1, 3)}
+    return [value] + [got[d] for d in (1, 2, 3)]
+
+
+def spread(value):
+    return jnp.broadcast_to(value[None], (NZ,) + value.shape)
+
+
+def swap(value, axes):
+    return lax.all_to_all(value, axes, split_axis=0, concat_axis=0, tiled=True)
 
 
 def body(tokens, norm_gain, in_weight, short_filter, rates, residues, skip):
-    x = lax.axis_index("x")
+    x, yh = lax.axis_index("x"), lax.axis_index("yh")
     own = normalise(tokens[0], norm_gain[None, :])
-    others = {d: lax.ppermute(own, "x", ring(NX, d)) for d in (2, 1, 3)}
-    normed = [own] + [others[d] for d in (1, 2, 3)]
+    own_row = along_x(own)
+    partner = lax.ppermute(own, "yh", ring(2, 1))
+
+    blocks = in_weight.reshape(8, 3, NZ, PIECES, 32).transpose(3, 0, 1, 2, 4)
+    blocks = spread(blocks.reshape(PIECES, 8, COLS)).reshape(NZ * PIECES, 8, COLS)
+    plane = swap(blocks, ("z", "yh", "x")).reshape(512, COLS)
+    partner, plane = lax.optimization_barrier((partner, plane))
+
+    other_plane = lax.ppermute(plane, "yl", ring(2, 1))
+    partner_row = along_x(partner)
+    sibling = lax.ppermute(plane, "co", ring(2, 1))
+    other_sibling = lax.ppermute(other_plane, "co", ring(2, 1))
+    weights = [plane, other_plane, sibling, other_sibling]
+    normed = own_row + partner_row
 
     tails = jnp.stack([piece[HERE - HALO :] for piece in normed])
-    tail = lax.dynamic_index_in_dim(tails, lax.rem(x + 1, NX), 0, keepdims=False)
-    halo = lax.ppermute(tail, ("z", "yh"), [(i, i + 1) for i in range(GROUPS - 1)])
-
-    blocks = in_weight.reshape(8, 3, GROUPS, NX, 32).transpose(3, 0, 1, 2, 4).reshape(NX, 8, COLS)
-    unit = lax.all_to_all(blocks, "x", split_axis=0, concat_axis=0, tiled=True).reshape(32, COLS)
-    along_z = {d: lax.ppermute(unit, "z", ring(NZ, d)) for d in (4, 3, 5, 2, 6, 1, 7)}
-    plane = jnp.stack([unit] + [along_z[d] for d in range(1, NZ)])
-    swap = [(0, 1), (1, 0)]
-    planes = {0: plane}
-    for e in (2, 1, 3):
-        planes[e] = along_y(plane, e)
-    sibling = {e: lax.ppermute(planes[e], "co", swap) for e in (0, 1, 3, 2)}
-    weights = [planes[e] for e in range(NY)] + [sibling[e] for e in range(NY)]
-
+    last = (1 - yh) * NX + lax.rem(x + 1, NX)
+    tail = lax.dynamic_index_in_dim(tails, last, 0, keepdims=False)
+    halo = lax.ppermute(tail, "z", [(i, i + 1) for i in range(NZ - 1)])
+
+    rates, residues, skip, plane = lax.optimization_barrier((rates, residues, skip, plane))
     mine = jnp.concatenate(
         [
             rates.T.reshape(4, LANES),
@@ -313,32 +317,19 @@
             jnp.pad(skip, (0, LANES - 32)).reshape(1, LANES),
         ]
     )
-    table = lax.all_to_all(
-        jnp.broadcast_to(mine[None], (GROUPS,) + mine.shape),
-        ("z", "yh"),
-        split_axis=0,
-        concat_axis=0,
-        tiled=True,
-    )
-    rate_table = table[:, 0:4].reshape(GROUPS, POLES, 32).transpose(1, 0, 2).reshape(POLES, CH)
-    residue_table = table[:, 4:8].reshape(GROUPS, POLES, 32).transpose(1, 0, 2).reshape(POLES, CH)
+    table = swap(spread(mine), "z")
+    rate_table = table[:, 0:4].reshape(NZ, POLES, 32).transpose(1, 0, 2).reshape(POLES, CH)
+    residue_table = table[:, 4:8].reshape(NZ, POLES, 32).transpose(1, 0, 2).reshape(POLES, CH)
     skip_row = table[:, 8, :32].reshape(1, CH)
-    taps = short_filter.reshape(3, 3, GROUPS, NX, 32)
-    taps = lax.dynamic_index_in_dim(taps, x, 3, keepdims=False).reshape(3, COLS)
+    taps = short_filter.reshape(3, 3, NZ, PIECES, 32)
+    taps = lax.dynamic_index_in_dim(taps, yh * NX + x, 3, keepdims=False).reshape(3, COLS)
 
     gate, local, chunk, state = project(
         normed, halo, weights, taps, rate_table, residue_table, skip_row
     )
-    states = lax.all_to_all(
-        jnp.broadcast_to(state[None], (GROUPS,) + state.shape),
-        ("z", "yh"),
-        split_axis=0,
-        concat_axis=0,
-        tiled=True,
-    )
+    states = swap(spread(state), "z")
     pieces = finish(states, rate_table, residue_table, local, chunk, gate)
-    arrived = {d: lax.ppermute(pieces[d], "x", ring(NX, d)) for d in (2, 1, 3)}
-    return place([pieces[0]] + [arrived[d] for d in (1, 2, 3)])
+    return place(swap(pieces, ("yh", "x")))
 
 
 def solution(mesh):

time: 190 us -> 132 us (0.69)
  waiting for transfers between devices: 89 us -> 29.9 us
  starting transfers between devices: 45.3 us -> 34.1 us
  local copies, waits for them, and re-layouts: 7.44 us -> 16.8 us
  blocking collectives: 27.1 us -> 34.1 us
  Pallas kernels: 19.3 us -> 16.3 us
    ppermute x21 -> x11, waiting for transfers between devices: 66.1 us -> 18.5 us  [the longest x6 16.9 us: along_x(): got = {d: lax.ppermute(value, 'x', ring(NX, d)) for d in (2, 1, 3)}]
    all_to_all x2, waiting for transfers between devices: 22.9 us -> 11.4 us  [swap(): return lax.all_to_all(value, axes, split_axis=0, concat_axis=0, tiled=True)]
    ppermute x21 -> x11, starting transfers between devices: 29.2 us -> 18.9 us  [the longest x6 10.3 us: along_x(): got = {d: lax.ppermute(value, 'x', ring(NX, d)) for d in (2, 1, 3)}]
    all_to_all x1 -> x2, blocking collectives: 27.1 us -> 34.1 us  [swap(): return lax.all_to_all(value, axes, split_axis=0, concat_axis=0, tiled=True)]
    unnamed x25 -> x27, local copies, waits for them, and re-layouts: 4.32 us -> 9.76 us
    pallas_call x1, Pallas kernels: 14.5 us -> 11.6 us  [project(): pl.pallas_call(project_kernel, in_specs=[any_spec] * 13 + [vmem] * 4, out...]
  transfers between devices with their start and end apart: 23 -> 13, of which waited for: 14 -> 6; matrix products, arithmetic and copies ran while one was open for 2% -> 9% of each run, Pallas kernels for 0% -> 0%
where the time goes in v2:
time: 132 us; the launch traced here: 131 us
  starting transfers between devices  34.1 us (26%)
  blocking collectives  34.1 us (26%)
  waiting for transfers between devices  29.9 us (23%)
  local copies, waits for them, and re-layouts  16.8 us (13%)
  Pallas kernels  16.3 us (12%)
    all_to_all x2, blocking collectives, swap(): return lax.all_to_all(value, axes, split_axis=0, concat_axis=0, tiled=True)  34.1 us
    ppermute x6, waiting for transfers between devices, along_x(): got = {d: lax.ppermute(value, 'x', ring(NX, d)) for d in (2, 1, 3)}  16.9 us
    all_to_all x2, starting transfers between devices, swap(): return lax.all_to_all(value, axes, split_axis=0, concat_axis=0, tiled=True)  15.2 us
    pallas_call x1, Pallas kernels, project(): pl.pallas_call(project_kernel, in_specs=[any_spec] * 13 + [vmem] * 4, out...  11.6 us
    all_to_all x2, waiting for transfers between devices, swap(): return lax.all_to_all(value, axes, split_axis=0, concat_axis=0, tiled=True)  11.4 us
    ppermute x6, starting transfers between devices, along_x(): got = {d: lax.ppermute(value, 'x', ring(NX, d)) for d in (2, 1, 3)}  10.3 us
    unnamed x27, local copies, waits for them, and re-layouts  9.76 us
    ppermute x1, starting transfers between devices, body(): halo = lax.ppermute(tail, 'z', [(i, i + 1) for i in range(NZ - 1)])  3.99 us
  transfers between devices with their start and end apart: 13, of which 6 were waited for; matrix products, arithmetic and copies ran while one was open for 9% of the time, Pallas kernels for 0%

profile of v2, /device:TPU:2, one launch (start us, length us, event | category | flops | bytes accessed | tf_op | source)
XLA Modules:
  0.0 131.3 jit_solution(3384088029258495813)
XLA Ops:
  0.0 1.0 copy-done.2
  1.0 0.7 copy-done.3
  2.3 3.3 %collective-permute-start.3 = (bf16[128,2048]{1,0:T(8,128)(2,1)S(1)}, bf16[128,2048]{1,0:T(8,128)(2,1)S(1)}, u32[]{:S(2)}, u32[]{:S(2)}) collective-permute-start(bf16[128,2048]{1,0:T(8,128)(2,1)S(1)} %shard_map.73.a0), channel_id=1, source_target_pairs={{0,4},{4,0},{1,5},{5,1},{2,6},{6,2},{3,7},{7,3},{8,12},{12,8},{9,1... | collective-permute-start | bytes 1572872 | tf_op jit(solution)/shard_map/ppermute | solution.py:293
  6.1 2.4 %collective-permute-start.1 = (bf16[128,2048]{1,0:T(8,128)(2,1)S(1)}, bf16[128,2048]{1,0:T(8,128)(2,1)S(1)}, u32[]{:S(2)}, u32[]{:S(2)}) collective-permute-start(bf16[128,2048]{1,0:T(8,128)(2,1)S(1)} %shard_map.73.a0), channel_id=1, source_target_pairs={{0,2},{1,3},{2,0},{3,1},{4,6},{5,7},{6,4},{7,5},{8,10},{9,11},{10,... | collective-permute-start | bytes 1572872 | tf_op jit(solution)/shard_map/ppermute | solution.py:277
  8.5 1.8 %collective-permute-start = (bf16[128,2048]{1,0:T(8,128)(2,1)S(1)}, bf16[128,2048]{1,0:T(8,128)(2,1)S(1)}, u32[]{:S(2)}, u32[]{:S(2)}) collective-permute-start(bf16[128,2048]{1,0:T(8,128)(2,1)S(1)} %shard_map.73.a0), channel_id=1, source_target_pairs={{0,1},{1,2},{2,3},{3,0},{4,5},{5,6},{6,7},{7,4},{8,9},{9,10},{10,1... | collective-permute-start | bytes 1572872 | tf_op jit(solution)/shard_map/ppermute | solution.py:277
  10.9 0.9 broadcast_in_dim.24
  11.8 11.0 %all-to-all-start = ((bf16[64,8,768]{2,1,0:T(8,128)(2,1)}), bf16[64,8,768]{2,1,0:T(8,128)(2,1)S(1)}, u32[]{:S(2)}, u32[]{:S(2)}) async-start(bf16[64,8,768]{2,1,0:T(8,128)(2,1)} %bitcast.3), calls=%async_computation | async-start | bytes 1572864 | tf_op jit(solution)/shard_map/all_to_all | solution.py:286
  22.9 0.6 fusion.6
  23.8 0.9 reshape.46
  24.7 1.0 constant_dynamic-slice_fusion
  25.7 13.5 %collective-permute-done.a1 = bf16[128,2048]{1,0:T(8,128)(2,1)S(1)} collective-permute-done((bf16[128,2048]{1,0:T(8,128)(2,1)S(1)}, bf16[128,2048]{1,0:T(8,128)(2,1)S(1)}, u32[]{:S(2)}, u32[]{:S(2)}) %collective-permute-start) | collective-permute-done | bytes 524320 | tf_op jit(solution)/shard_map/ppermute | solution.py:277
  40.6 0.6 fusion.3
  41.2 3.6 %all-to-all-done = bf16[64,8,768]{2,1,0:T(8,128)(2,1)S(1)} async-done(((bf16[64,8,768]{2,1,0:T(8,128)(2,1)}), bf16[64,8,768]{2,1,0:T(8,128)(2,1)S(1)}, u32[]{:S(2)}, u32[]{:S(2)}) %all-to-all-start) | async-done | bytes 786464 | tf_op jit(solution)/shard_map/all_to_all | solution.py:286
  44.8 1.5 %collective-permute-start.6 = (bf16[128,2048]{1,0:T(8,128)(2,1)S(1)}, bf16[128,2048]{1,0:T(8,128)(2,1)}, u32[]{:S(2)}, u32[]{:S(2)}) collective-permute-start(bf16[128,2048]{1,0:T(8,128)(2,1)S(1)} %collective-permute-done.3.b0), channel_id=1, source_target_pairs={{0,3},{1,0},{2,1},{3,2},{4,7},{5,4},{6,5},{7,6},{8,11},{9,8},{10,9... | collective-permute-start | bytes 1572872 | tf_op jit(solution)/shard_map/ppermute | solution.py:277
  46.3 2.3 %collective-permute-start.5 = (bf16[128,2048]{1,0:T(8,128)(2,1)S(1)}, bf16[128,2048]{1,0:T(8,128)(2,1)}, u32[]{:S(2)}, u32[]{:S(2)}) collective-permute-start(bf16[128,2048]{1,0:T(8,128)(2,1)S(1)} %collective-permute-done.3.b0), channel_id=1, source_target_pairs={{0,2},{1,3},{2,0},{3,1},{4,6},{5,7},{6,4},{7,5},{8,10},{9,11},{10,... | collective-permute-start | bytes 1572872 | tf_op jit(solution)/shard_map/ppermute | solution.py:277
  48.6 1.8 %collective-permute-start.4 = (bf16[128,2048]{1,0:T(8,128)(2,1)S(1)}, bf16[128,2048]{1,0:T(8,128)(2,1)S(1)}, u32[]{:S(2)}, u32[]{:S(2)}) collective-permute-start(bf16[128,2048]{1,0:T(8,128)(2,1)S(1)} %collective-permute-done.3.b0), channel_id=1, source_target_pairs={{0,1},{1,2},{2,3},{3,0},{4,5},{5,6},{6,7},{7,4},{8,9},{9,10},{10,1... | collective-permute-start | bytes 1572872 | tf_op jit(solution)/shard_map/ppermute | solution.py:277
  50.4 1.3 %collective-permute-start.8 = (bf16[512,768]{1,0:T(8,128)(2,1)}, bf16[512,768]{1,0:T(8,128)(2,1)}, u32[]{:S(2)}, u32[]{:S(2)}) collective-permute-start(bf16[512,768]{1,0:T(8,128)(2,1)} %bitcast.57), channel_id=1, source_target_pairs={{0,128},{128,0},{1,129},{129,1},{2,130},{130,2},{3,131},{131,3},{4... | collective-permute-start | bytes 2359304 | tf_op jit(solution)/shard_map/ppermute | solution.py:300
  52.6 4.1 %all-to-all-start.1 = ((f32[8,9,128]{2,1,0:T(8,128)}), f32[8,9,128]{2,1,0:T(8,128)S(1)}, u32[]{:S(2)}, u32[]{:S(2)}) async-start(f32[8,9,128]{2,1,0:T(8,128)} %broadcast_in_dim.25), calls=%async_computation.1 | async-start | bytes 131072 | tf_op jit(solution)/shard_map/all_to_all | solution.py:286
  57.3 7.7 %all-to-all-done.1 = f32[8,9,128]{2,1,0:T(8,128)S(1)} async-done(((f32[8,9,128]{2,1,0:T(8,128)}), f32[8,9,128]{2,1,0:T(8,128)S(1)}, u32[]{:S(2)}, u32[]{:S(2)}) %all-to-all-start.1) | async-done | bytes 36896 | tf_op jit(solution)/shard_map/all_to_all | solution.py:286
  65.1 3.3 %collective-permute-done.4.b1 = bf16[128,2048]{1,0:T(8,128)(2,1)S(1)} collective-permute-done((bf16[128,2048]{1,0:T(8,128)(2,1)S(1)}, bf16[128,2048]{1,0:T(8,128)(2,1)S(1)}, u32[]{:S(2)}, u32[]{:S(2)}) %collective-permute-start.4) | collective-permute-done | bytes 524320 | tf_op jit(solution)/shard_map/ppermute | solution.py:277
  69.0 1.5 %fusion.1 = bf16[8,16,2048]{2,1,0:T(8,128)(2,1)} fusion(bf16[8,16,2048]{2,1,0:T(8,128)(2,1)} %fusion.2, bf16[128,2048]{1,0:T(8,128)(2,1)} %collective-permute-done.5.b2), kind=kLoop, calls=%fused_computation.4 | loop fusion | bytes 131072
  70.7 1.5 %fusion = bf16[8,16,2048]{2,1,0:T(8,128)(2,1)} fusion(bf16[8,16,2048]{2,1,0:T(8,128)(2,1)} %fusion.1, bf16[128,2048]{1,0:T(8,128)(2,1)} %collective-permute-done.6.b3), kind=kLoop, calls=%fused_computation.2 | loop fusion | bytes 131072 | tf_op jit(solution)/shard_map/stack | solution.py:307
  72.2 0.8 dynamic-slice_bitcast_fusion
  73.0 4.0 %collective-permute-start.7 = (bf16[16,2048]{1,0:T(8,128)(2,1)S(1)}, bf16[16,2048]{1,0:T(8,128)(2,1)S(1)}, u32[]{:S(2)}, u32[]{:S(2)}) collective-permute-start(bf16[16,2048]{1,0:T(8,128)(2,1)S(1)} %dynamic-slice_bitcast_fusion), channel_id=1, source_target_pairs={{0,8},{8,16},{16,24},{24,32},{32,40},{40,48},{48,56},{1,9},{9,17},... | collective-permute-start | bytes 196616 | tf_op jit(solution)/shard_map/ppermute | solution.py:310
  77.5 1.5 %collective-permute-done.7.halo = bf16[16,2048]{1,0:T(8,128)(2,1)S(1)} collective-permute-done((bf16[16,2048]{1,0:T(8,128)(2,1)S(1)}, bf16[16,2048]{1,0:T(8,128)(2,1)S(1)}, u32[]{:S(2)}, u32[]{:S(2)}) %collective-permute-start.7) | collective-permute-done | bytes 65568 | tf_op jit(solution)/shard_map/ppermute | solution.py:310
  79.0 11.6 %shard_map.74 = (bf16[1024,256]{1,0:T(8,128)(2,1)S(1)}, f32[1024,256]{1,0:T(8,128)}, f32[16,64,256]{2,1,0:T(8,128)}, f32[16,256]{1,0:T(8,128)S(1)}) custom-call(bf16[128,2048]{1,0:T(8,128)(2,1)S(1)} %shard_map.73.a0, bf16[128,2048]{1,0:T(8,128)(2,1)S(1)} %collective-permute-done.a1, bf16[128,2048]{1,0:T(8,128)(2,1)S(1)} %collective-permute-done.1.a2, ...), custom_call_target="tpu_custom_call" | custom-call | flops 3271557120 | bytes 12000000 | tf_op jit(solution)/shard_map/pallas_call | solution.py:174
  90.6 19.5 %all_to_all.20.states = f32[8,16,256]{2,1,0:T(8,128)S(1)} all-to-all(f32[8,16,256]{2,1,0:T(8,128)S(1)} %broadcast_in_dim.26), channel_id=1, replica_groups=mesh['yl'=2,'co'=2,'z'=8,'yh'=2,'x'=4] {'z'}, dimensions={0} | all-to-all | bytes 262144 | tf_op jit(solution)/shard_map/all_to_all | solution.py:286
  110.1 1.2 copy-done
  111.3 1.2 copy-done.1
  112.5 3.4 %shard_map.75 = bf16[8,256,128]{2,1,0:T(8,128)(2,1)S(1)} custom-call(f32[8,16,256]{2,1,0:T(8,128)S(1)} %all_to_all.20.states, f32[16,256]{1,0:T(8,128)S(1)} %reshape.52.rates, f32[16,256]{1,0:T(8,128)S(1)} %reshape.54.residues, f32[1024,256]{1,0:T(8,128)S(1)} %copy-done, f32[16,64,256]{2,1,0:T(8,128)S(1)} %copy-done.1, ...), custom_call_target="tpu_custom_call" | custom-call | tf_op jit(solution)/shard_map/pallas_call | solution.py:242
  115.9 14.6 %all_to_all.21.pieces = bf16[8,256,128]{2,1,0:T(8,128)(2,1)S(1)} all-to-all(bf16[8,256,128]{2,1,0:T(8,128)(2,1)S(1)} %shard_map.75), channel_id=1, replica_groups=mesh['yl'=2,'co'=2,'z'=8,'yh'=2,'x'=4] {'yh','x'}, dimensions={0} | all-to-all | bytes 1048576 | tf_op jit(solution)/shard_map/all_to_all | solution.py:286
  130.5 0.8 shard_map.76
  (51 shorter events, 6.1 us)
Async XLA Ops:
  0.0 1.0 copy-start.2
  1.0 0.7 copy-start.3
  1.7 8.6 %copy-start.6 = (bf16[8,6144]{1,0:T(8,128)(2,1)S(1)}, bf16[8,6144]{1,0:T(8,128)(2,1)}, u32[]{:S(2)}) copy-start(bf16[8,6144]{1,0:T(8,128)(2,1)} %param.9) | copy-start | bytes 294916
  2.3 38.9 %collective-permute-start.3 = (bf16[128,2048]{1,0:T(8,128)(2,1)S(1)}, bf16[128,2048]{1,0:T(8,128)(2,1)S(1)}, u32[]{:S(2)}, u32[]{:S(2)}) collective-permute-start(bf16[128,2048]{1,0:T(8,128)(2,1)S(1)} %shard_map.73.a0), channel_id=1, source_target_pairs={{0,4},{4,0},{1,5},{5,1},{2,6},{6,2},{3,7},{7,3},{8,12},{12,8},{9,1... | collective-permute-start | bytes 1572872 | tf_op jit(solution)/shard_map/ppermute | solution.py:293
  5.6 35.0 %collective-permute-start.2 = (bf16[128,2048]{1,0:T(8,128)(2,1)S(1)}, bf16[128,2048]{1,0:T(8,128)(2,1)S(1)}, u32[]{:S(2)}, u32[]{:S(2)}) collective-permute-start(bf16[128,2048]{1,0:T(8,128)(2,1)S(1)} %shard_map.73.a0), channel_id=1, source_target_pairs={{0,3},{1,0},{2,1},{3,2},{4,7},{5,4},{6,5},{7,6},{8,11},{9,8},{10,9... | collective-permute-start | bytes 1572872 | tf_op jit(solution)/shard_map/ppermute | solution.py:277
  6.1 33.8 %collective-permute-start.1 = (bf16[128,2048]{1,0:T(8,128)(2,1)S(1)}, bf16[128,2048]{1,0:T(8,128)(2,1)S(1)}, u32[]{:S(2)}, u32[]{:S(2)}) collective-permute-start(bf16[128,2048]{1,0:T(8,128)(2,1)S(1)} %shard_map.73.a0), channel_id=1, source_target_pairs={{0,2},{1,3},{2,0},{3,1},{4,6},{5,7},{6,4},{7,5},{8,10},{9,11},{10,... | collective-permute-start | bytes 1572872 | tf_op jit(solution)/shard_map/ppermute | solution.py:277
  8.5 30.7 %collective-permute-start = (bf16[128,2048]{1,0:T(8,128)(2,1)S(1)}, bf16[128,2048]{1,0:T(8,128)(2,1)S(1)}, u32[]{:S(2)}, u32[]{:S(2)}) collective-permute-start(bf16[128,2048]{1,0:T(8,128)(2,1)S(1)} %shard_map.73.a0), channel_id=1, source_target_pairs={{0,1},{1,2},{2,3},{3,0},{4,5},{5,6},{6,7},{7,4},{8,9},{9,10},{10,1... | collective-permute-start | bytes 1572872 | tf_op jit(solution)/shard_map/ppermute | solution.py:277
  11.8 33.0 %all-to-all-start = ((bf16[64,8,768]{2,1,0:T(8,128)(2,1)}), bf16[64,8,768]{2,1,0:T(8,128)(2,1)S(1)}, u32[]{:S(2)}, u32[]{:S(2)}) async-start(bf16[64,8,768]{2,1,0:T(8,128)(2,1)} %bitcast.3), calls=%async_computation | async-start | bytes 1572864 | tf_op jit(solution)/shard_map/all_to_all | solution.py:286
  22.9 0.9 copy-start.5
  40.6 11.2 %copy-start.7 = (f32[32,16]{0,1:T(8,128)S(1)}, f32[32,16]{0,1:T(8,128)}, u32[]{:S(2)}) copy-start(f32[32,16]{0,1:T(8,128)} %param.12) | copy-start | bytes 6148
  41.2 10.6 %copy-start.9 = (f32[32]{0:T(128)S(1)}, f32[32]{0:T(128)}, u32[]{:S(2)}) copy-start(f32[32]{0:T(128)} %param.13) | copy-start | bytes 388
  44.8 1.5 %copy-start.4 = (bf16[64,8,768]{2,1,0:T(8,128)(2,1)}, bf16[64,8,768]{2,1,0:T(8,128)(2,1)S(1)}, u32[]{:S(2)}) copy-start(bf16[64,8,768]{2,1,0:T(8,128)(2,1)S(1)} %all-to-all-done) | copy-start | bytes 2359300
  44.8 7.0 %copy-start.8 = (f32[32,16]{0,1:T(8,128)S(1)}, f32[32,16]{0,1:T(8,128)}, u32[]{:S(2)}) copy-start(f32[32,16]{0,1:T(8,128)} %param.11) | copy-start | bytes 6148
  44.8 25.8 %collective-permute-start.6 = (bf16[128,2048]{1,0:T(8,128)(2,1)S(1)}, bf16[128,2048]{1,0:T(8,128)(2,1)}, u32[]{:S(2)}, u32[]{:S(2)}) collective-permute-start(bf16[128,2048]{1,0:T(8,128)(2,1)S(1)} %collective-permute-done.3.b0), channel_id=1, source_target_pairs={{0,3},{1,0},{2,1},{3,2},{4,7},{5,4},{6,5},{7,6},{8,11},{9,8},{10,9... | collective-permute-start | bytes 1572872 | tf_op jit(solution)/shard_map/ppermute | solution.py:277
  46.3 22.7 %collective-permute-start.5 = (bf16[128,2048]{1,0:T(8,128)(2,1)S(1)}, bf16[128,2048]{1,0:T(8,128)(2,1)}, u32[]{:S(2)}, u32[]{:S(2)}) collective-permute-start(bf16[128,2048]{1,0:T(8,128)(2,1)S(1)} %collective-permute-done.3.b0), channel_id=1, source_target_pairs={{0,2},{1,3},{2,0},{3,1},{4,6},{5,7},{6,4},{7,5},{8,10},{9,11},{10,... | collective-permute-start | bytes 1572872 | tf_op jit(solution)/shard_map/ppermute | solution.py:277
  48.6 19.7 %collective-permute-start.4 = (bf16[128,2048]{1,0:T(8,128)(2,1)S(1)}, bf16[128,2048]{1,0:T(8,128)(2,1)S(1)}, u32[]{:S(2)}, u32[]{:S(2)}) collective-permute-start(bf16[128,2048]{1,0:T(8,128)(2,1)S(1)} %collective-permute-done.3.b0), channel_id=1, source_target_pairs={{0,1},{1,2},{2,3},{3,0},{4,5},{5,6},{6,7},{7,4},{8,9},{9,10},{10,1... | collective-permute-start | bytes 1572872 | tf_op jit(solution)/shard_map/ppermute | solution.py:277
  50.4 28.6 %collective-permute-start.9 = (bf16[512,768]{1,0:T(8,128)(2,1)}, bf16[512,768]{1,0:T(8,128)(2,1)}, u32[]{:S(2)}, u32[]{:S(2)}) collective-permute-start(bf16[512,768]{1,0:T(8,128)(2,1)} %bitcast.56), channel_id=1, source_target_pairs={{0,64},{64,0},{1,65},{65,1},{2,66},{66,2},{3,67},{67,3},{4,68},{68... | collective-permute-start | bytes 2359304 | tf_op jit(solution)/shard_map/ppermute | solution.py:302
  50.4 20.3 %collective-permute-start.8 = (bf16[512,768]{1,0:T(8,128)(2,1)}, bf16[512,768]{1,0:T(8,128)(2,1)}, u32[]{:S(2)}, u32[]{:S(2)}) collective-permute-start(bf16[512,768]{1,0:T(8,128)(2,1)} %bitcast.57), channel_id=1, source_target_pairs={{0,128},{128,0},{1,129},{129,1},{2,130},{130,2},{3,131},{131,3},{4... | collective-permute-start | bytes 2359304 | tf_op jit(solution)/shard_map/ppermute | solution.py:300
  52.6 12.5 %all-to-all-start.1 = ((f32[8,9,128]{2,1,0:T(8,128)}), f32[8,9,128]{2,1,0:T(8,128)S(1)}, u32[]{:S(2)}, u32[]{:S(2)}) async-start(f32[8,9,128]{2,1,0:T(8,128)} %broadcast_in_dim.25), calls=%async_computation.1 | async-start | bytes 131072 | tf_op jit(solution)/shard_map/all_to_all | solution.py:286
  70.7 8.3 %collective-permute-start.10 = (bf16[512,768]{1,0:T(8,128)(2,1)}, bf16[512,768]{1,0:T(8,128)(2,1)}, u32[]{:S(2)}, u32[]{:S(2)}) collective-permute-start(bf16[512,768]{1,0:T(8,128)(2,1)} %collective-permute-done.8.w01), channel_id=1, source_target_pairs={{0,64},{64,0},{1,65},{65,1},{2,66},{66,2},{3,67},{67,3},{4,68},{68... | collective-permute-start | bytes 2359304 | tf_op jit(solution)/shard_map/ppermute | solution.py:303
  73.0 6.0 %collective-permute-start.7 = (bf16[16,2048]{1,0:T(8,128)(2,1)S(1)}, bf16[16,2048]{1,0:T(8,128)(2,1)S(1)}, u32[]{:S(2)}, u32[]{:S(2)}) collective-permute-start(bf16[16,2048]{1,0:T(8,128)(2,1)S(1)} %dynamic-slice_bitcast_fusion), channel_id=1, source_target_pairs={{0,8},{8,16},{16,24},{24,32},{32,40},{40,48},{48,56},{1,9},{9,17},... | collective-permute-start | bytes 196616 | tf_op jit(solution)/shard_map/ppermute | solution.py:310
  110.1 1.2 copy-start
  111.3 1.2 copy-start.1

commit v3 on v2

--- a/solution.py
+++ b/solution.py
@@ -21,11 +21,11 @@
 ROWS = HALO + SPAN
 D = 2048
 COLS = 3 * CH
-VMEM_LIMIT = 50 * 1024 * 1024
-
-
-def params(**kw):
-    return pltpu.CompilerParams(vmem_limit_bytes=VMEM_LIMIT, **kw)
+MIB = 1024 * 1024
+
+
+def params(mib):
+    return pltpu.CompilerParams(vmem_limit_bytes=mib * MIB)
 
 
 def norm_kernel(tok_ref, gain_ref, out_ref, scr):
@@ -47,7 +47,7 @@
         norm_kernel,
         out_shape=jax.ShapeDtypeStruct((HERE, D), BF16),
         scratch_shapes=[pltpu.VMEM((D // LANES, HERE, LANES), F32)],
-        compiler_params=params(),
+        compiler_params=params(10),
     )(tokens, gain)
 
 
@@ -55,11 +55,20 @@
     return v.astype(BF16).astype(F32)
 
 
+def filtered(ext, t, sub):
+    prev = [
+        jnp.where(sub == 0, pltpu.roll(ext[i], 1, 0), pltpu.roll(ext[CHUNK + i], 1, 0))
+        for i in range(2)
+    ]
+    ext = prev + ext[2:]
+    return [t[0] * ext[j + 2] + t[1] * ext[j + 1] + t[2] * ext[j] for j in range(CHUNK)]
+
+
 def project_kernel(
     a0, a1, a2, a3, b0, b1, b2, b3, halo, w00, w01, w10, w11,
-    taps, rates, residues, skip,
-    gate_ref, local_ref, chunk_ref, state_ref,
-    lhs, w, proj, decay_s, taps_s, carry, sems,
+    taps, rates,
+    query_ref, carried_ref, chunk_ref, state_ref,
+    lhs, w, proj, decay_s, carry, sems,
 ):
     x = lax.axis_index("x")
     yh = lax.axis_index("yh")
@@ -82,23 +91,17 @@
             at = lax.rem(yh + e, 2) * NX + lax.rem(x + NX - d, NX)
             copy(piece, lhs.at[pl.ds(pl.multiple_of(HALO + at * HERE, 16), HERE)])
 
-    rate = rates[...]
-    weight = residues[...] * jnp.sqrt(2.0 * rate)
-    decay = jnp.exp(-rate)
-    decay_s[...] = decay
-    power = weight
-    for i in range(CHUNK):
-        row = jnp.sum(power, axis=0, keepdims=True)
-        taps_s[i : i + 1, :] = row + skip[...] if i == 0 else row
-        power = power * decay
-
+    decay_s[...] = jnp.exp(-rates[...])
     for c in copies:
         c.wait()
 
-    @pl.loop(0, COLS // 256)
-    def _(n):
-        cols = pl.ds(pl.multiple_of(n * 256, 256), 256)
-        proj[:, cols] = rounded(jnp.dot(lhs[...], w[:, cols], preferred_element_type=F32))
+    for s in (1, 2, 0):
+        cols = slice(s * CH, (s + 1) * CH)
+        product = jnp.dot(lhs[...], w[:, cols], preferred_element_type=F32).astype(BF16)
+        if s == 0:
+            query_ref[...] = product
+        else:
+            proj[:, (s - 1) * CH : s * CH] = product.astype(F32)
 
     sub = lax.broadcasted_iota(jnp.int32, (8, LANES), 0)
 
@@ -117,32 +120,17 @@
 
             def featured(s):
                 lanes = pl.ds(pl.multiple_of(s * CH + lane0, LANES), LANES)
-                before = [proj[pl.ds(row0 + 8 * i, 8), lanes] for i in range(2)]
-                rows = [proj[pl.ds(row0 + HALO + 8 * j, 8), lanes] for j in range(CHUNK)]
-                t = [taps[i : i + 1, lanes] for i in range(3)]
-                prev = [
-                    jnp.where(sub == 0, pltpu.roll(before[i], 1, 0), pltpu.roll(rows[14 + i], 1, 0))
-                    for i in range(2)
-                ]
-                ext = prev + rows
-                return [
-                    t[0] * ext[j + 2] + t[1] * ext[j + 1] + t[2] * ext[j] for j in range(CHUNK)
-                ]
-
-            queries = featured(0)
+                first = pl.ds(pl.multiple_of((s + 1) * CH + lane0, LANES), LANES)
+                ext = [proj[pl.ds(row0 + 8 * i, 8), lanes] for i in range(2 + CHUNK)]
+                return filtered(ext, [taps[i : i + 1, first] for i in range(3)], sub)
+
+            keys, values = featured(0), featured(1)
+            pairs = [(a * b).astype(BF16) for a, b in zip(keys, values)]
             for j in range(0, CHUNK, 2):
-                gate_ref[pl.ds(pl.multiple_of(row0 + 8 * j, 16), 16), here] = jnp.concatenate(
-                    queries[j : j + 2], axis=0
-                ).astype(BF16)
-            keys, values = featured(1), featured(2)
-            carried = [rounded(a * b) for a, b in zip(keys, values)]
-
-            k = [taps_s[i : i + 1, here] for i in range(CHUNK)]
-            for j in range(CHUNK):
-                acc = k[0] * carried[j]
-                for i in range(j):
-                    acc = acc + k[j - i] * carried[i]
-                local_ref[pl.ds(row0 + 8 * j, 8), here] = acc
+                carried_ref[pl.ds(pl.multiple_of(row0 + 8 * j, 16), 16), here] = jnp.concatenate(
+                    pairs[j : j + 2], axis=0
+                )
+            carried = [a.astype(F32) for a in pairs]
 
             for m in range(POLES):
                 e = decay_s[m : m + 1, here]
@@ -168,33 +156,89 @@
             state_ref[m : m + 1, here] = carry[m, 0:1, :]
 
 
-def project(normed, halo, weights, taps, rates, residues, skip):
+def project(normed, halo, weights, taps, rates):
     any_spec = pl.BlockSpec(memory_space=pl.ANY)
     vmem = pl.BlockSpec(memory_space=pltpu.VMEM)
     return pl.pallas_call(
         project_kernel,
-        in_specs=[any_spec] * 13 + [vmem] * 4,
+        in_specs=[any_spec] * 13 + [vmem] * 2,
         out_specs=[vmem] * 4,
         out_shape=[
+            jax.ShapeDtypeStruct((ROWS, CH), BF16),
             jax.ShapeDtypeStruct((SPAN, CH), BF16),
-            jax.ShapeDtypeStruct((SPAN, CH), F32),
             jax.ShapeDtypeStruct((POLES, SPAN // CHUNK, CH), F32),
             jax.ShapeDtypeStruct((POLES, CH), F32),
         ],
         scratch_shapes=[
             pltpu.VMEM((ROWS, D), BF16),
             pltpu.VMEM((D, COLS), BF16),
-            pltpu.VMEM((ROWS, COLS), F32),
+            pltpu.VMEM((ROWS, 2 * CH), F32),
             pltpu.VMEM((POLES, CH), F32),
-            pltpu.VMEM((CHUNK, CH), F32),
             pltpu.VMEM((POLES, 8, LANES), F32),
             pltpu.SemaphoreType.DMA((13,)),
         ],
-        compiler_params=params(),
+        compiler_params=params(28),
         cost_estimate=pl.CostEstimate(
-            flops=2 * ROWS * D * COLS, bytes_accessed=12_000_000, transcendentals=0
+            flops=2 * ROWS * D * COLS, bytes_accessed=10_000_000, transcendentals=0
         ),
-    )(*normed, halo, *weights, taps, rates, residues, skip)
+    )(*normed, halo, *weights, taps, rates)
+
+
+def direct_kernel(query, carried, taps, rates, residues, skip, gate_ref, local_ref, taps_s):
+    decay = jnp.exp(-rates[...])
+    power = residues[...] * jnp.sqrt(2.0 * rates[...])
+    for i in range(CHUNK):
+        row = jnp.sum(power, axis=0, keepdims=True)
+        taps_s[i : i + 1, :] = row + skip[...] if i == 0 else row
+        power = power * decay
+    sub = lax.broadcasted_iota(jnp.int32, (8, LANES), 0)
+
+    @pl.loop(0, CH // LANES)
+    def _(l):
+        here = pl.ds(pl.multiple_of(l * LANES, LANES), LANES)
+
+        @pl.loop(0, PIECES)
+        def _(p):
+            row0 = pl.multiple_of(p * HERE, 16)
+
+            def rows(ref, count):
+                pairs = [
+                    ref[pl.ds(pl.multiple_of(row0 + 16 * i, 16), 16), here].astype(F32)
+                    for i in range(count)
+                ]
+                return [half for pair in pairs for half in (pair[:8], pair[8:])]
+
+            t = [taps[i : i + 1, here] for i in range(3)]
+            queries = filtered(rows(query, 9), t, sub)
+            for j in range(0, CHUNK, 2):
+                gate_ref[pl.ds(pl.multiple_of(row0 + 8 * j, 16), 16), here] = jnp.concatenate(
+                    queries[j : j + 2], axis=0
+                ).astype(BF16)
+            x = rows(carried, 8)
+            k = [taps_s[i : i + 1, here] for i in range(CHUNK)]
+            for j in range(CHUNK):
+                acc = k[0] * x[j]
+                for i in range(j):
+                    acc = acc + k[j - i] * x[i]
+                local_ref[pl.ds(row0 + 8 * j, 8), here] = acc
+
+
+def direct(query, carried, taps, rates, residues, skip):
+    vmem = pl.BlockSpec(memory_space=pltpu.VMEM)
+    return pl.pallas_call(
+        direct_kernel,
+        in_specs=[vmem] * 6,
+        out_specs=[vmem] * 2,
+        out_shape=[
+            jax.ShapeDtypeStruct((SPAN, CH), BF16),
+            jax.ShapeDtypeStruct((SPAN, CH), F32),
+        ],
+        scratch_shapes=[pltpu.VMEM((CHUNK, CH), F32)],
+        compiler_params=params(10),
+        cost_estimate=pl.CostEstimate(
+            flops=40 * SPAN * CH, bytes_accessed=3_000_000, transcendentals=0
+        ),
+    )(query, carried, taps, rates, residues, skip)
 
 
 def finish_kernel(
@@ -250,7 +294,7 @@
             pltpu.VMEM((POLES, CH), F32),
             pltpu.VMEM((POLES, CH), F32),
         ],
-        compiler_params=params(),
+        compiler_params=params(10),
     )(states, rates, residues, local, chunk, gate)
 
 
@@ -264,7 +308,7 @@
     out = pl.pallas_call(
         place_kernel,
         out_shape=jax.ShapeDtypeStruct((NZ, PIECES, 32, HERE), BF16),
-        compiler_params=params(),
+        compiler_params=params(10),
     )(pieces)
     return out.reshape(1, NZ * PIECES * 32, HERE)
 
@@ -286,30 +330,52 @@
     return lax.all_to_all(value, axes, split_axis=0, concat_axis=0, tiled=True)
 
 
+def tail_kernel(a0, a1, a2, a3, out, sem):
+    which = lax.rem(lax.axis_index("x") + 1, NX)
+    for d, piece in enumerate((a0, a1, a2, a3)):
+
+        @pl.when(which == d)
+        def _(piece=piece):
+            copy = pltpu.make_async_copy(piece.at[pl.ds(HERE - HALO, HALO)], out, sem)
+            copy.start()
+            copy.wait()
+
+
+def last_rows(row):
+    any_spec = pl.BlockSpec(memory_space=pl.ANY)
+    return pl.pallas_call(
+        tail_kernel,
+        in_specs=[any_spec] * NX,
+        out_specs=any_spec,
+        out_shape=jax.ShapeDtypeStruct((HALO, D), BF16),
+        scratch_shapes=[pltpu.SemaphoreType.DMA],
+        compiler_params=params(10),
+    )(*row)
+
+
 def body(tokens, norm_gain, in_weight, short_filter, rates, residues, skip):
     x, yh = lax.axis_index("x"), lax.axis_index("yh")
     own = normalise(tokens[0], norm_gain[None, :])
+    partner = lax.ppermute(own, "yh", ring(2, 1))
     own_row = along_x(own)
-    partner = lax.ppermute(own, "yh", ring(2, 1))
 
     blocks = in_weight.reshape(8, 3, NZ, PIECES, 32).transpose(3, 0, 1, 2, 4)
     blocks = spread(blocks.reshape(PIECES, 8, COLS)).reshape(NZ * PIECES, 8, COLS)
     plane = swap(blocks, ("z", "yh", "x")).reshape(512, COLS)
-    partner, plane = lax.optimization_barrier((partner, plane))
 
     other_plane = lax.ppermute(plane, "yl", ring(2, 1))
     partner_row = along_x(partner)
     sibling = lax.ppermute(plane, "co", ring(2, 1))
     other_sibling = lax.ppermute(other_plane, "co", ring(2, 1))
     weights = [plane, other_plane, sibling, other_sibling]
-    normed = own_row + partner_row
-
-    tails = jnp.stack([piece[HERE - HALO :] for piece in normed])
-    last = (1 - yh) * NX + lax.rem(x + 1, NX)
-    tail = lax.dynamic_index_in_dim(tails, last, 0, keepdims=False)
-    halo = lax.ppermute(tail, "z", [(i, i + 1) for i in range(NZ - 1)])
-
-    rates, residues, skip, plane = lax.optimization_barrier((rates, residues, skip, plane))
+
+    tail = last_rows(own_row)
+    halo = 0
+    for to in range(2):
+        pairs = [(2 * z + 1, 2 * z + 2 + to) for z in range(NZ - 1)]
+        halo = halo + lax.ppermute(tail, ("z", "yh"), pairs)
+
+    rates, residues, skip, _ = lax.optimization_barrier((rates, residues, skip, plane))
     mine = jnp.concatenate(
         [
             rates.T.reshape(4, LANES),
@@ -324,10 +390,9 @@
     taps = short_filter.reshape(3, 3, NZ, PIECES, 32)
     taps = lax.dynamic_index_in_dim(taps, yh * NX + x, 3, keepdims=False).reshape(3, COLS)
 
-    gate, local, chunk, state = project(
-        normed, halo, weights, taps, rate_table, residue_table, skip_row
-    )
+    query, carried, chunk, state = project(own_row + partner_row, halo, weights, taps, rate_table)
     states = swap(spread(state), "z")
+    gate, local = direct(query, carried, taps, rate_table, residue_table, skip_row)
     pieces = finish(states, rate_table, residue_table, local, chunk, gate)
     return place(swap(pieces, ("yh", "x")))
 

time: 132 us -> 149 us (1.13)
  blocking collectives: 34.1 us -> 55.7 us
  starting transfers between devices: 34.1 us -> 27.5 us
  waiting for transfers between devices: 29.9 us -> 35.9 us
  local copies, waits for them, and re-layouts: 16.8 us -> 14.2 us
    all_to_all x2, blocking collectives: 34.1 us -> 55.7 us  [swap(): return lax.all_to_all(value, axes, split_axis=0, concat_axis=0, tiled=True)]
    ppermute x1, waiting for transfers between devices: 0.18 us -> 5.27 us  [body(): other_plane = lax.ppermute(plane, 'yl', ring(2, 1))]
    ppermute x6, waiting for transfers between devices: 16.9 us -> 13.9 us  [along_x(): got = {d: lax.ppermute(value, 'x', ring(NX, d)) for d in (2, 1, 3)}]
    all_to_all x2, waiting for transfers between devices: 11.4 us -> 14.2 us  [swap(): return lax.all_to_all(value, axes, split_axis=0, concat_axis=0, tiled=True)]
    ppermute x1 -> x2, starting transfers between devices: 3.99 us -> 1.32 us  [body(): halo = halo + lax.ppermute(tail, ('z', 'yh'), pairs)]
    ppermute x1, waiting for transfers between devices: 0.01 us -> 2.62 us  [body(): partner = lax.ppermute(own, 'yh', ring(2, 1))]
    all_to_all x2, starting transfers between devices: 15.2 us -> 13 us  [swap(): return lax.all_to_all(value, axes, split_axis=0, concat_axis=0, tiled=True)]
    pallas_call x1 -> x3, Pallas kernels: 11.6 us -> 10.1 us  [the longest x1 8.92 us: project(): pl.pallas_call(project_kernel, in_specs=[any_spec] * 13 + [vmem] * 2, out...]
  transfers between devices with their start and end apart: 13 -> 14, of which waited for: 6 -> 9; matrix products, arithmetic and copies ran while one was open for 9% -> 1% of each run, Pallas kernels for 0% -> 1%
where the time goes in v3:
time: 149 us; the launch traced here: 148 us
  blocking collectives  55.7 us (37%)
  waiting for transfers between devices  35.9 us (24%)
  starting transfers between devices  27.5 us (18%)
  Pallas kernels  14.9 us (10%)
  local copies, waits for them, and re-layouts  14.2 us (10%)
    all_to_all x2, blocking collectives, swap(): return lax.all_to_all(value, axes, split_axis=0, concat_axis=0, tiled=True)  55.7 us
    all_to_all x2, waiting for transfers between devices, swap(): return lax.all_to_all(value, axes, split_axis=0, concat_axis=0, tiled=True)  14.2 us
    ppermute x6, waiting for transfers between devices, along_x(): got = {d: lax.ppermute(value, 'x', ring(NX, d)) for d in (2, 1, 3)}  13.9 us
    all_to_all x2, starting transfers between devices, swap(): return lax.all_to_all(value, axes, split_axis=0, concat_axis=0, tiled=True)  13 us
    unnamed x40, local copies, waits for them, and re-layouts  10.4 us
    ppermute x6, starting transfers between devices, along_x(): got = {d: lax.ppermute(value, 'x', ring(NX, d)) for d in (2, 1, 3)}  10.4 us
    pallas_call x1, Pallas kernels, project(): pl.pallas_call(project_kernel, in_specs=[any_spec] * 13 + [vmem] * 2, out...  8.92 us
    ppermute x1, waiting for transfers between devices, body(): other_plane = lax.ppermute(plane, 'yl', ring(2, 1))  5.27 us
  transfers between devices with their start and end apart: 14, of which 9 were waited for; matrix products, arithmetic and copies ran while one was open for 1% of the time, Pallas kernels for 1%

profile of v3, /device:TPU:2, one launch (start us, length us, event | category | flops | bytes accessed | tf_op | source)
XLA Modules:
  0.0 148.4 jit_solution(12303743001683314691)
XLA Ops:
  0.0 1.2 reshape.43
  1.6 37.6 %all_to_all.20 = bf16[64,8,768]{2,1,0:T(8,128)(2,1)S(1)} all-to-all(bf16[64,8,768]{2,1,0:T(8,128)(2,1)S(1)} %bitcast.26), channel_id=1, replica_groups=mesh['yl'=2,'co'=2,'z'=8,'yh'=2,'x'=4] {'z','yh','x'}, dimensions={0} | all-to-all | bytes 1572864 | tf_op jit(solution)/shard_map/all_to_all | solution.py:330
  40.5 1.6 %collective-permute-start.2 = (bf16[128,2048]{1,0:T(8,128)(2,1)S(1)}, bf16[128,2048]{1,0:T(8,128)(2,1)S(1)}, u32[]{:S(2)}, u32[]{:S(2)}) collective-permute-start(bf16[128,2048]{1,0:T(8,128)(2,1)S(1)} %shard_map.73.a0), channel_id=1, source_target_pairs={{0,3},{1,0},{2,1},{3,2},{4,7},{5,4},{6,5},{7,6},{8,11},{9,8},{10,9... | collective-permute-start | bytes 1572872 | tf_op jit(solution)/shard_map/ppermute | solution.py:321
  42.0 1.5 collective-permute-start.1
  43.5 2.5 %collective-permute-start = (bf16[128,2048]{1,0:T(8,128)(2,1)S(1)}, bf16[128,2048]{1,0:T(8,128)(2,1)S(1)}, u32[]{:S(2)}, u32[]{:S(2)}) collective-permute-start(bf16[128,2048]{1,0:T(8,128)(2,1)S(1)} %shard_map.73.a0), channel_id=1, source_target_pairs={{0,1},{1,2},{2,3},{3,0},{4,5},{5,6},{6,7},{7,4},{8,9},{9,10},{10,1... | collective-permute-start | bytes 1572872 | tf_op jit(solution)/shard_map/ppermute | solution.py:321
  46.0 2.1 %collective-permute-start.3 = (bf16[128,2048]{1,0:T(8,128)(2,1)S(1)}, bf16[128,2048]{1,0:T(8,128)(2,1)}, u32[]{:S(2)}, u32[]{:S(2)}) collective-permute-start(bf16[128,2048]{1,0:T(8,128)(2,1)S(1)} %shard_map.73.a0), channel_id=1, source_target_pairs={{0,4},{4,0},{1,5},{5,1},{2,6},{6,2},{3,7},{7,3},{8,12},{12,8},{9,1... | collective-permute-start | bytes 1572872 | tf_op jit(solution)/shard_map/ppermute | solution.py:359
  48.1 6.3 %collective-permute-done.2.a3 = bf16[128,2048]{1,0:T(8,128)(2,1)S(1)} collective-permute-done((bf16[128,2048]{1,0:T(8,128)(2,1)S(1)}, bf16[128,2048]{1,0:T(8,128)(2,1)S(1)}, u32[]{:S(2)}, u32[]{:S(2)}) %collective-permute-start.2) | collective-permute-done | bytes 524320 | tf_op jit(solution)/shard_map/ppermute | solution.py:321
  54.4 5.3 %collective-permute-done.9.w01 = bf16[512,768]{1,0:T(8,128)(2,1)S(1)} collective-permute-done((bf16[512,768]{1,0:T(8,128)(2,1)S(1)}, bf16[512,768]{1,0:T(8,128)(2,1)S(1)}, u32[]{:S(2)}, u32[]{:S(2)}) %collective-permute-start.9) | collective-permute-done | bytes 786464 | tf_op jit(solution)/shard_map/ppermute | solution.py:366
  59.7 0.9 copy-done.10
  60.6 2.9 %collective-permute-done.1.a2 = bf16[128,2048]{1,0:T(8,128)(2,1)S(1)} collective-permute-done((bf16[128,2048]{1,0:T(8,128)(2,1)S(1)}, bf16[128,2048]{1,0:T(8,128)(2,1)S(1)}, u32[]{:S(2)}, u32[]{:S(2)}) %collective-permute-start.1) | collective-permute-done | bytes 524320 | tf_op jit(solution)/shard_map/ppermute | solution.py:321
  63.5 0.9 collective-permute-done.a1
  66.7 2.6 %collective-permute-done.3.b0 = bf16[128,2048]{1,0:T(8,128)(2,1)} collective-permute-done((bf16[128,2048]{1,0:T(8,128)(2,1)S(1)}, bf16[128,2048]{1,0:T(8,128)(2,1)}, u32[]{:S(2)}, u32[]{:S(2)}) %collective-permute-start.3) | collective-permute-done | bytes 524320 | tf_op jit(solution)/shard_map/ppermute | solution.py:359
  70.2 2.7 %collective-permute-start.5 = (bf16[128,2048]{1,0:T(8,128)(2,1)}, bf16[128,2048]{1,0:T(8,128)(2,1)}, u32[]{:S(2)}, u32[]{:S(2)}) collective-permute-start(bf16[128,2048]{1,0:T(8,128)(2,1)} %collective-permute-done.3.b0), channel_id=1, source_target_pairs={{0,2},{1,3},{2,0},{3,1},{4,6},{5,7},{6,4},{7,5},{8,10},{9,11},{10,... | collective-permute-start | bytes 1572872 | tf_op jit(solution)/shard_map/ppermute | solution.py:321
  72.8 1.5 %collective-permute-start.4 = (bf16[128,2048]{1,0:T(8,128)(2,1)}, bf16[128,2048]{1,0:T(8,128)(2,1)}, u32[]{:S(2)}, u32[]{:S(2)}) collective-permute-start(bf16[128,2048]{1,0:T(8,128)(2,1)} %collective-permute-done.3.b0), channel_id=1, source_target_pairs={{0,1},{1,2},{2,3},{3,0},{4,5},{5,6},{6,7},{7,4},{8,9},{9,10},{10,1... | collective-permute-start | bytes 1572872 | tf_op jit(solution)/shard_map/ppermute | solution.py:321
  75.0 7.9 %all-to-all-start.1 = ((f32[8,9,128]{2,1,0:T(8,128)}), f32[8,9,128]{2,1,0:T(8,128)S(1)}, u32[]{:S(2)}, u32[]{:S(2)}) async-start(f32[8,9,128]{2,1,0:T(8,128)} %broadcast_in_dim.25), calls=%async_computation.1 | async-start | bytes 131072 | tf_op jit(solution)/shard_map/all_to_all | solution.py:330
  83.7 7.5 %all-to-all-done.1 = f32[8,9,128]{2,1,0:T(8,128)S(1)} async-done(((f32[8,9,128]{2,1,0:T(8,128)}), f32[8,9,128]{2,1,0:T(8,128)S(1)}, u32[]{:S(2)}, u32[]{:S(2)}) %all-to-all-start.1) | async-done | bytes 36896 | tf_op jit(solution)/shard_map/all_to_all | solution.py:330
  91.5 2.7 %collective-permute-done.5.b2 = bf16[128,2048]{1,0:T(8,128)(2,1)} collective-permute-done((bf16[128,2048]{1,0:T(8,128)(2,1)}, bf16[128,2048]{1,0:T(8,128)(2,1)}, u32[]{:S(2)}, u32[]{:S(2)}) %collective-permute-start.5) | collective-permute-done | bytes 524320 | tf_op jit(solution)/shard_map/ppermute | solution.py:321
  94.1 1.1 collective-permute-done.4.b1
  95.2 0.9 copy-done.12
  96.1 1.0 copy-done.4
  97.2 1.0 copy-done.6
  98.2 1.0 copy-done.8
  99.3 1.1 copy-done.11
  100.4 1.1 copy-done.13
  101.5 8.9 %shard_map.75 = (bf16[1040,256]{1,0:T(8,128)(2,1)S(1)}, bf16[1024,256]{1,0:T(8,128)(2,1)S(1)}, f32[16,64,256]{2,1,0:T(8,128)S(1)}, f32[16,256]{1,0:T(8,128)S(1)}) custom-call(bf16[128,2048]{1,0:T(8,128)(2,1)S(1)} %shard_map.73.a0, bf16[128,2048]{1,0:T(8,128)(2,1)S(1)} %copy-done.8, bf16[128,2048]{1,0:T(8,128)(2,1)S(1)} %copy-done.6, ...), custom_call_target="tpu_custom_call" | custom-call | flops 3271557120 | bytes 10000000 | tf_op jit(solution)/shard_map/pallas_call | solution.py:162
  111.9 5.1 %all-to-all-start.2 = ((f32[8,16,256]{2,1,0:T(8,128)}), f32[8,16,256]{2,1,0:T(8,128)S(1)}, u32[]{:S(2)}, u32[]{:S(2)}) async-start(f32[8,16,256]{2,1,0:T(8,128)} %broadcast_in_dim.26), calls=%async_computation.2 | async-start | bytes 262144 | tf_op jit(solution)/shard_map/all_to_all | solution.py:330
  117.4 1.0 copy-done.1
  118.4 1.1 shard_map.76
  119.5 6.7 %all-to-all-done.2.states = f32[8,16,256]{2,1,0:T(8,128)S(1)} async-done(((f32[8,16,256]{2,1,0:T(8,128)}), f32[8,16,256]{2,1,0:T(8,128)S(1)}, u32[]{:S(2)}, u32[]{:S(2)}) %all-to-all-start.2) | async-done | bytes 131104 | tf_op jit(solution)/shard_map/all_to_all | solution.py:330
  126.1 3.4 %shard_map.77 = bf16[8,256,128]{2,1,0:T(8,128)(2,1)S(1)} custom-call(f32[8,16,256]{2,1,0:T(8,128)S(1)} %all-to-all-done.2.states, f32[16,256]{1,0:T(8,128)S(1)} %reshape.52.rates, f32[16,256]{1,0:T(8,128)S(1)} %reshape.54.residues, f32[1024,256]{1,0:T(8,128)S(1)} %get-tuple-element.20.local, f32[16,64,256]{2,1,0:T(8,128)S(1)} %get-tuple-element.21.chunk, ...), custom_call_target="tpu_custom_call" | custom-call | tf_op jit(solution)/shard_map/pallas_call | solution.py:286
  129.5 18.0 %all_to_all.21.pieces = bf16[8,256,128]{2,1,0:T(8,128)(2,1)S(1)} all-to-all(bf16[8,256,128]{2,1,0:T(8,128)(2,1)S(1)} %shard_map.77), channel_id=1, replica_groups=mesh['yl'=2,'co'=2,'z'=8,'yh'=2,'x'=4] {'yh','x'}, dimensions={0} | all-to-all | bytes 1048576 | tf_op jit(solution)/shard_map/all_to_all | solution.py:330
  147.6 0.8 shard_map.78
  (67 shorter events, 8.2 us)
Async XLA Ops:
  1.6 38.3 %copy-start.2 = (bf16[1,128,2048]{2,1,0:T(8,128)(2,1)S(1)}, bf16[1,128,2048]{2,1,0:T(8,128)(2,1)}, u32[]{:S(2)}) copy-start(bf16[1,128,2048]{2,1,0:T(8,128)(2,1)} %param.7) | copy-start | bytes 1572868
  1.6 38.3 %copy-start.9 = (f32[2048]{0:T(1024)S(1)}, f32[2048]{0:T(1024)}, u32[]{:S(2)}) copy-start(f32[2048]{0:T(1024)} %param.8) | copy-start | bytes 24580
  39.2 20.5 %collective-permute-start.9 = (bf16[512,768]{1,0:T(8,128)(2,1)S(1)}, bf16[512,768]{1,0:T(8,128)(2,1)S(1)}, u32[]{:S(2)}, u32[]{:S(2)}) collective-permute-start(bf16[512,768]{1,0:T(8,128)(2,1)S(1)} %bitcast.21), channel_id=1, source_target_pairs={{0,128},{128,0},{1,129},{129,1},{2,130},{130,2},{3,131},{131,3},{4... | collective-permute-start | bytes 2359304 | tf_op jit(solution)/shard_map/ppermute | solution.py:366
  40.5 26.1 %copy-start.14 = (f32[3,6144]{1,0:T(4,128)S(1)}, f32[3,6144]{1,0:T(4,128)}, u32[]{:S(2)}) copy-start(f32[3,6144]{1,0:T(4,128)} %param.10) | copy-start | bytes 221188
  40.5 13.9 %collective-permute-start.2 = (bf16[128,2048]{1,0:T(8,128)(2,1)S(1)}, bf16[128,2048]{1,0:T(8,128)(2,1)S(1)}, u32[]{:S(2)}, u32[]{:S(2)}) collective-permute-start(bf16[128,2048]{1,0:T(8,128)(2,1)S(1)} %shard_map.73.a0), channel_id=1, source_target_pairs={{0,3},{1,0},{2,1},{3,2},{4,7},{5,4},{6,5},{7,6},{8,11},{9,8},{10,9... | collective-permute-start | bytes 1572872 | tf_op jit(solution)/shard_map/ppermute | solution.py:321
  42.0 21.4 %collective-permute-start.1 = (bf16[128,2048]{1,0:T(8,128)(2,1)S(1)}, bf16[128,2048]{1,0:T(8,128)(2,1)S(1)}, u32[]{:S(2)}, u32[]{:S(2)}) collective-permute-start(bf16[128,2048]{1,0:T(8,128)(2,1)S(1)} %shard_map.73.a0), channel_id=1, source_target_pairs={{0,2},{1,3},{2,0},{3,1},{4,6},{5,7},{6,4},{7,5},{8,10},{9,11},{10,... | collective-permute-start | bytes 1572872 | tf_op jit(solution)/shard_map/ppermute | solution.py:321
  43.5 20.9 %collective-permute-start = (bf16[128,2048]{1,0:T(8,128)(2,1)S(1)}, bf16[128,2048]{1,0:T(8,128)(2,1)S(1)}, u32[]{:S(2)}, u32[]{:S(2)}) collective-permute-start(bf16[128,2048]{1,0:T(8,128)(2,1)S(1)} %shard_map.73.a0), channel_id=1, source_target_pairs={{0,1},{1,2},{2,3},{3,0},{4,5},{5,6},{6,7},{7,4},{8,9},{9,10},{10,1... | collective-permute-start | bytes 1572872 | tf_op jit(solution)/shard_map/ppermute | solution.py:321
  46.0 23.3 %collective-permute-start.3 = (bf16[128,2048]{1,0:T(8,128)(2,1)S(1)}, bf16[128,2048]{1,0:T(8,128)(2,1)}, u32[]{:S(2)}, u32[]{:S(2)}) collective-permute-start(bf16[128,2048]{1,0:T(8,128)(2,1)S(1)} %shard_map.73.a0), channel_id=1, source_target_pairs={{0,4},{4,0},{1,5},{5,1},{2,6},{6,2},{3,7},{7,3},{8,12},{12,8},{9,1... | collective-permute-start | bytes 1572872 | tf_op jit(solution)/shard_map/ppermute | solution.py:359
  54.4 10.1 %copy-start.3 = (bf16[128,2048]{1,0:T(8,128)(2,1)}, bf16[128,2048]{1,0:T(8,128)(2,1)S(1)}, u32[]{:S(2)}) copy-start(bf16[128,2048]{1,0:T(8,128)(2,1)S(1)} %collective-permute-done.2.a3) | copy-start | bytes 1572868
  54.4 40.8 %collective-permute-start.10 = (bf16[512,768]{1,0:T(8,128)(2,1)S(1)}, bf16[512,768]{1,0:T(8,128)(2,1)S(1)}, u32[]{:S(2)}, u32[]{:S(2)}) collective-permute-start(bf16[512,768]{1,0:T(8,128)(2,1)S(1)} %bitcast.22), channel_id=1, source_target_pairs={{0,64},{64,0},{1,65},{65,1},{2,66},{66,2},{3,67},{67,3},{4,68},{68... | collective-permute-start | bytes 2359304 | tf_op jit(solution)/shard_map/ppermute | solution.py:368
  59.7 36.5 %collective-permute-start.11 = (bf16[512,768]{1,0:T(8,128)(2,1)S(1)}, bf16[512,768]{1,0:T(8,128)(2,1)}, u32[]{:S(2)}, u32[]{:S(2)}) collective-permute-start(bf16[512,768]{1,0:T(8,128)(2,1)S(1)} %collective-permute-done.9.w01), channel_id=1, source_target_pairs={{0,64},{64,0},{1,65},{65,1},{2,66},{66,2},{3,67},{67,3},{4,68},{68... | collective-permute-start | bytes 2359304 | tf_op jit(solution)/shard_map/ppermute | solution.py:369
  59.7 0.9 copy-start.10
  63.5 1.0 copy-start.5
  65.2 5.0 %collective-permute-start.8 = (bf16[16,2048]{1,0:T(8,128)(2,1)S(1)}, bf16[16,2048]{1,0:T(8,128)(2,1)S(1)}, u32[]{:S(2)}, u32[]{:S(2)}) collective-permute-start(bf16[16,2048]{1,0:T(8,128)(2,1)S(1)} %shard_map.74), channel_id=1, source_target_pairs={{4,12},{12,20},{20,28},{28,36},{36,44},{44,52},{52,60},{5,13},{13,... | collective-permute-start | bytes 196616 | tf_op jit(solution)/shard_map/ppermute | solution.py:376
  65.8 7.0 %collective-permute-start.7 = (bf16[16,2048]{1,0:T(8,128)(2,1)S(1)}, bf16[16,2048]{1,0:T(8,128)(2,1)S(1)}, u32[]{:S(2)}, u32[]{:S(2)}) collective-permute-start(bf16[16,2048]{1,0:T(8,128)(2,1)S(1)} %shard_map.74), channel_id=1, source_target_pairs={{4,8},{12,16},{20,24},{28,32},{36,40},{44,48},{52,56},{5,9},{13,17... | collective-permute-start | bytes 196616 | tf_op jit(solution)/shard_map/ppermute | solution.py:376
  66.5 3.5 %copy-start.17 = (f32[32,16]{0,1:T(8,128)S(1)}, f32[32,16]{0,1:T(8,128)}, u32[]{:S(2)}) copy-start(f32[32,16]{0,1:T(8,128)} %param.12) | copy-start | bytes 6148
  66.7 3.4 %copy-start.18 = (f32[32,16]{0,1:T(8,128)S(1)}, f32[32,16]{0,1:T(8,128)}, u32[]{:S(2)}) copy-start(f32[32,16]{0,1:T(8,128)} %param.11) | copy-start | bytes 6148
  69.3 22.1 %collective-permute-start.6 = (bf16[128,2048]{1,0:T(8,128)(2,1)}, bf16[128,2048]{1,0:T(8,128)(2,1)}, u32[]{:S(2)}, u32[]{:S(2)}) collective-permute-start(bf16[128,2048]{1,0:T(8,128)(2,1)} %collective-permute-done.3.b0), channel_id=1, source_target_pairs={{0,3},{1,0},{2,1},{3,2},{4,7},{5,4},{6,5},{7,6},{8,11},{9,8},{10,9... | collective-permute-start | bytes 1572872 | tf_op jit(solution)/shard_map/ppermute | solution.py:321
  70.1 4.3 %copy-start.19 = (f32[32]{0:T(128)S(1)}, f32[32]{0:T(128)}, u32[]{:S(2)}) copy-start(f32[32]{0:T(128)} %param.13) | copy-start | bytes 388
  70.2 23.9 %collective-permute-start.5 = (bf16[128,2048]{1,0:T(8,128)(2,1)}, bf16[128,2048]{1,0:T(8,128)(2,1)}, u32[]{:S(2)}, u32[]{:S(2)}) collective-permute-start(bf16[128,2048]{1,0:T(8,128)(2,1)} %collective-permute-done.3.b0), channel_id=1, source_target_pairs={{0,2},{1,3},{2,0},{3,1},{4,6},{5,7},{6,4},{7,5},{8,10},{9,11},{10,... | collective-permute-start | bytes 1572872 | tf_op jit(solution)/shard_map/ppermute | solution.py:321
  72.8 2.2 %copy-start.15 = (bf16[16,2048]{1,0:T(8,128)(2,1)}, bf16[16,2048]{1,0:T(8,128)(2,1)S(1)}, u32[]{:S(2)}) copy-start(bf16[16,2048]{1,0:T(8,128)(2,1)S(1)} %collective-permute-done.7) | copy-start | bytes 196612
  72.8 22.4 %collective-permute-start.4 = (bf16[128,2048]{1,0:T(8,128)(2,1)}, bf16[128,2048]{1,0:T(8,128)(2,1)}, u32[]{:S(2)}, u32[]{:S(2)}) collective-permute-start(bf16[128,2048]{1,0:T(8,128)(2,1)} %collective-permute-done.3.b0), channel_id=1, source_target_pairs={{0,1},{1,2},{2,3},{3,0},{4,5},{5,6},{6,7},{7,4},{8,9},{9,10},{10,1... | collective-permute-start | bytes 1572872 | tf_op jit(solution)/shard_map/ppermute | solution.py:321
  75.0 16.2 %all-to-all-start.1 = ((f32[8,9,128]{2,1,0:T(8,128)}), f32[8,9,128]{2,1,0:T(8,128)S(1)}, u32[]{:S(2)}, u32[]{:S(2)}) async-start(f32[8,9,128]{2,1,0:T(8,128)} %broadcast_in_dim.25), calls=%async_computation.1 | async-start | bytes 131072 | tf_op jit(solution)/shard_map/all_to_all | solution.py:330
  82.9 0.8 copy-start.16
  95.2 0.9 copy-start.12
  96.1 1.0 copy-start.4
  97.2 1.0 copy-start.6
  98.2 1.0 copy-start.8
  99.3 1.1 copy-start.11
  100.4 1.1 copy-start.13
  111.9 14.2 %all-to-all-start.2 = ((f32[8,16,256]{2,1,0:T(8,128)}), f32[8,16,256]{2,1,0:T(8,128)S(1)}, u32[]{:S(2)}, u32[]{:S(2)}) async-start(f32[8,16,256]{2,1,0:T(8,128)} %broadcast_in_dim.26), calls=%async_computation.2 | async-start | bytes 262144 | tf_op jit(solution)/shard_map/all_to_all | solution.py:330
  117.3 1.0 copy-start.1
  (2 other events, 1.6 us)

commit v4 on v3

--- a/solution.py
+++ b/solution.py
@@ -21,6 +21,7 @@
 ROWS = HALO + SPAN
 D = 2048
 COLS = 3 * CH
+WIDE = 2 * CH
 MIB = 1024 * 1024
 
 
@@ -64,16 +65,7 @@
     return [t[0] * ext[j + 2] + t[1] * ext[j + 1] + t[2] * ext[j] for j in range(CHUNK)]
 
 
-def project_kernel(
-    a0, a1, a2, a3, b0, b1, b2, b3, halo, w00, w01, w10, w11,
-    taps, rates,
-    query_ref, carried_ref, chunk_ref, state_ref,
-    lhs, w, proj, decay_s, carry, sems,
-):
-    x = lax.axis_index("x")
-    yh = lax.axis_index("yh")
-    yl = lax.axis_index("yl")
-    core = lax.axis_index("co")
+def copier(sems):
     copies = []
 
     def copy(src, dst):
@@ -81,27 +73,38 @@
         c.start()
         copies.append(c)
 
+    return copies, copy
+
+
+def copy_rows(copy, pieces, halo, lhs):
+    x, yh = lax.axis_index("x"), lax.axis_index("yh")
+    copy(halo, lhs.at[pl.ds(0, HALO)])
+    for i, piece in enumerate(pieces):
+        at = lax.rem(yh + i // NX, 2) * NX + lax.rem(x + NX - i % NX, NX)
+        copy(piece, lhs.at[pl.ds(pl.multiple_of(HALO + at * HERE, 16), HERE)])
+
+
+def project_kernel(
+    a0, a1, a2, a3, b0, b1, b2, b3, halo, w00, w01, w10, w11, taps, rates,
+    carried_ref, chunk_ref, state_ref,
+    lhs, w, proj, decay_s, carry, sems,
+):
+    yl, core = lax.axis_index("yl"), lax.axis_index("co")
+    copies, copy = copier(sems)
     for r, pieces in enumerate(((w00, w01), (w10, w11))):
         for e, piece in enumerate(pieces):
             row = lax.rem(yl + e, 2) * 1024 + lax.rem(core + r, 2) * 512
             copy(piece, w.at[pl.ds(pl.multiple_of(row, 512), 512)])
-    copy(halo, lhs.at[pl.ds(0, HALO)])
-    for e, pieces in enumerate(((a0, a1, a2, a3), (b0, b1, b2, b3))):
-        for d, piece in enumerate(pieces):
-            at = lax.rem(yh + e, 2) * NX + lax.rem(x + NX - d, NX)
-            copy(piece, lhs.at[pl.ds(pl.multiple_of(HALO + at * HERE, 16), HERE)])
+    copy_rows(copy, (a0, a1, a2, a3, b0, b1, b2, b3), halo, lhs)
 
     decay_s[...] = jnp.exp(-rates[...])
     for c in copies:
         c.wait()
 
-    for s in (1, 2, 0):
+    for s in range(2):
         cols = slice(s * CH, (s + 1) * CH)
-        product = jnp.dot(lhs[...], w[:, cols], preferred_element_type=F32).astype(BF16)
-        if s == 0:
-            query_ref[...] = product
-        else:
-            proj[:, (s - 1) * CH : s * CH] = product.astype(F32)
+        product = jnp.dot(lhs[...], w[:, cols], preferred_element_type=F32)
+        proj[:, cols] = rounded(product)
 
     sub = lax.broadcasted_iota(jnp.int32, (8, LANES), 0)
 
@@ -162,29 +165,35 @@
     return pl.pallas_call(
         project_kernel,
         in_specs=[any_spec] * 13 + [vmem] * 2,
-        out_specs=[vmem] * 4,
+        out_specs=[vmem] * 3,
         out_shape=[
-            jax.ShapeDtypeStruct((ROWS, CH), BF16),
             jax.ShapeDtypeStruct((SPAN, CH), BF16),
             jax.ShapeDtypeStruct((POLES, SPAN // CHUNK, CH), F32),
             jax.ShapeDtypeStruct((POLES, CH), F32),
         ],
         scratch_shapes=[
             pltpu.VMEM((ROWS, D), BF16),
-            pltpu.VMEM((D, COLS), BF16),
-            pltpu.VMEM((ROWS, 2 * CH), F32),
+            pltpu.VMEM((D, WIDE), BF16),
+            pltpu.VMEM((ROWS, WIDE), F32),
             pltpu.VMEM((POLES, CH), F32),
             pltpu.VMEM((POLES, 8, LANES), F32),
             pltpu.SemaphoreType.DMA((13,)),
         ],
-        compiler_params=params(28),
+        compiler_params=params(50),
         cost_estimate=pl.CostEstimate(
-            flops=2 * ROWS * D * COLS, bytes_accessed=10_000_000, transcendentals=0
+            flops=2 * ROWS * D * WIDE, bytes_accessed=10_000_000, transcendentals=0
         ),
     )(*normed, halo, *weights, taps, rates)
 
 
-def direct_kernel(query, carried, taps, rates, residues, skip, gate_ref, local_ref, taps_s):
+def direct_kernel(
+    a0, a1, a2, a3, b0, b1, b2, b3, halo, wq, carried, taps, rates, residues, skip,
+    gate_ref, local_ref,
+    lhs, w, query, taps_s, sems,
+):
+    copies, copy = copier(sems)
+    copy(wq, w)
+    copy_rows(copy, (a0, a1, a2, a3, b0, b1, b2, b3), halo, lhs)
     decay = jnp.exp(-rates[...])
     power = residues[...] * jnp.sqrt(2.0 * rates[...])
     for i in range(CHUNK):
@@ -192,6 +201,9 @@
         taps_s[i : i + 1, :] = row + skip[...] if i == 0 else row
         power = power * decay
     sub = lax.broadcasted_iota(jnp.int32, (8, LANES), 0)
+    for c in copies:
+        c.wait()
+    query[...] = rounded(jnp.dot(lhs[...], w[...], preferred_element_type=F32))
 
     @pl.loop(0, CH // LANES)
     def _(l):
@@ -201,20 +213,18 @@
         def _(p):
             row0 = pl.multiple_of(p * HERE, 16)
 
-            def rows(ref, count):
-                pairs = [
-                    ref[pl.ds(pl.multiple_of(row0 + 16 * i, 16), 16), here].astype(F32)
-                    for i in range(count)
-                ]
-                return [half for pair in pairs for half in (pair[:8], pair[8:])]
-
             t = [taps[i : i + 1, here] for i in range(3)]
-            queries = filtered(rows(query, 9), t, sub)
+            ext = [query[pl.ds(row0 + 8 * i, 8), here] for i in range(2 + CHUNK)]
+            queries = filtered(ext, t, sub)
             for j in range(0, CHUNK, 2):
                 gate_ref[pl.ds(pl.multiple_of(row0 + 8 * j, 16), 16), here] = jnp.concatenate(
                     queries[j : j + 2], axis=0
                 ).astype(BF16)
-            x = rows(carried, 8)
+            pairs = [
+                carried[pl.ds(pl.multiple_of(row0 + 8 * j, 16), 16), here].astype(F32)
+                for j in range(0, CHUNK, 2)
+            ]
+            x = [half for pair in pairs for half in (pair[:8], pair[8:])]
             k = [taps_s[i : i + 1, here] for i in range(CHUNK)]
             for j in range(CHUNK):
                 acc = k[0] * x[j]
@@ -223,22 +233,29 @@
                 local_ref[pl.ds(row0 + 8 * j, 8), here] = acc
 
 
-def direct(query, carried, taps, rates, residues, skip):
+def direct(normed, halo, weight, carried, taps, rates, residues, skip):
+    any_spec = pl.BlockSpec(memory_space=pl.ANY)
     vmem = pl.BlockSpec(memory_space=pltpu.VMEM)
     return pl.pallas_call(
         direct_kernel,
-        in_specs=[vmem] * 6,
+        in_specs=[any_spec] * 10 + [vmem] * 5,
         out_specs=[vmem] * 2,
         out_shape=[
             jax.ShapeDtypeStruct((SPAN, CH), BF16),
             jax.ShapeDtypeStruct((SPAN, CH), F32),
         ],
-        scratch_shapes=[pltpu.VMEM((CHUNK, CH), F32)],
-        compiler_params=params(10),
+        scratch_shapes=[
+            pltpu.VMEM((ROWS, D), BF16),
+            pltpu.VMEM((D, CH), BF16),
+            pltpu.VMEM((ROWS, CH), F32),
+            pltpu.VMEM((CHUNK, CH), F32),
+            pltpu.SemaphoreType.DMA((10,)),
+        ],
+        compiler_params=params(50),
         cost_estimate=pl.CostEstimate(
-            flops=40 * SPAN * CH, bytes_accessed=3_000_000, transcendentals=0
+            flops=2 * ROWS * D * CH, bytes_accessed=8_000_000, transcendentals=0
         ),
-    )(query, carried, taps, rates, residues, skip)
+    )(*normed, halo, weight, carried, taps, rates, residues, skip)
 
 
 def finish_kernel(
@@ -356,18 +373,22 @@
 def body(tokens, norm_gain, in_weight, short_filter, rates, residues, skip):
     x, yh = lax.axis_index("x"), lax.axis_index("yh")
     own = normalise(tokens[0], norm_gain[None, :])
+
+    blocks = in_weight.reshape(8, 3, NZ, PIECES, 32).transpose(3, 0, 1, 2, 4)
+    unit = swap(blocks.reshape(PIECES, 8, COLS), ("yh", "x")).reshape(64, COLS)
+    own, unit = lax.optimization_barrier((own, unit))
+
     partner = lax.ppermute(own, "yh", ring(2, 1))
     own_row = along_x(own)
-
-    blocks = in_weight.reshape(8, 3, NZ, PIECES, 32).transpose(3, 0, 1, 2, 4)
-    blocks = spread(blocks.reshape(PIECES, 8, COLS)).reshape(NZ * PIECES, 8, COLS)
-    plane = swap(blocks, ("z", "yh", "x")).reshape(512, COLS)
+    plane = swap(spread(unit[:, CH:]), "z").reshape(512, WIDE)
+    query_weight = lax.all_gather(unit[:, :CH], ("yl", "co", "z"), axis=0, tiled=True)
 
     other_plane = lax.ppermute(plane, "yl", ring(2, 1))
     partner_row = along_x(partner)
     sibling = lax.ppermute(plane, "co", ring(2, 1))
     other_sibling = lax.ppermute(other_plane, "co", ring(2, 1))
     weights = [plane, other_plane, sibling, other_sibling]
+    normed = own_row + partner_row
 
     tail = last_rows(own_row)
     halo = 0
@@ -390,9 +411,11 @@
     taps = short_filter.reshape(3, 3, NZ, PIECES, 32)
     taps = lax.dynamic_index_in_dim(taps, yh * NX + x, 3, keepdims=False).reshape(3, COLS)
 
-    query, carried, chunk, state = project(own_row + partner_row, halo, weights, taps, rate_table)
+    carried, chunk, state = project(normed, halo, weights, taps, rate_table)
     states = swap(spread(state), "z")
-    gate, local = direct(query, carried, taps, rate_table, residue_table, skip_row)
+    gate, local = direct(
+        normed, halo, query_weight, carried, taps, rate_table, residue_table, skip_row
+    )
     pieces = finish(states, rate_table, residue_table, local, chunk, gate)
     return place(swap(pieces, ("yh", "x")))
 

time: 149 us -> 173 us (1.16); the launches traced: 148 us -> 170 us
  blocking collectives: 55.7 us -> 16.6 us
  waiting for transfers between devices: 35.9 us -> 58.9 us
  starting transfers between devices: 27.5 us -> 46.9 us
  between operations: 0.27 us -> 13.6 us
  Pallas kernels: 14.9 us -> 19.6 us
    all_to_all x2 -> x1, blocking collectives: 55.7 us -> 16.6 us  [swap(): return lax.all_to_all(value, axes, split_axis=0, concat_axis=0, tiled=True)]
    all_gather x0 -> x1, waiting for transfers between devices: none -> 24.8 us  [body(): lax.all_gather(unit[:, :CH], ('yl', 'co', 'z'), axis=0, tiled=True)]
    all_to_all x2 -> x4, starting transfers between devices: 13 us -> 32.8 us  [swap(): return lax.all_to_all(value, axes, split_axis=0, concat_axis=0, tiled=True)]
    all_to_all x2 -> x4, waiting for transfers between devices: 14.2 us -> 24.3 us  [swap(): return lax.all_to_all(value, axes, split_axis=0, concat_axis=0, tiled=True)]
    ppermute x1, waiting for transfers between devices: 5.27 us -> 0.01 us  [body(): other_plane = lax.ppermute(plane, 'yl', ring(2, 1))]
    pallas_call x1, Pallas kernels: 1.07 us -> 6.06 us  [direct(): pl.pallas_call(direct_kernel, in_specs=[any_spec] * 10 + [vmem] * 5, out_...]
    ppermute x6, waiting for transfers between devices: 13.9 us -> 9.71 us  [along_x(): got = {d: lax.ppermute(value, 'x', ring(NX, d)) for d in (2, 1, 3)}]
    unnamed x40 -> x32, local copies, waits for them, and re-layouts: 10.4 us -> 6.57 us
  transfers between devices with their start and end apart: 14 -> 17, of which waited for: 9 -> 7; matrix products, arithmetic and copies ran while one was open for 1% -> 3% of each run, Pallas kernels for 1% -> 9%
where the time goes in v4:
time: 173 us; the launch traced here: 170 us
  waiting for transfers between devices  58.9 us (34%)
  starting transfers between devices  46.9 us (27%)
  Pallas kernels  19.6 us (11%)
  blocking collectives  16.6 us (10%)
  between operations  13.6 us (8%)
  local copies, waits for them, and re-layouts  13.1 us (8%)
    all_to_all x4, starting transfers between devices, swap(): return lax.all_to_all(value, axes, split_axis=0, concat_axis=0, tiled=True)  32.8 us
    all_gather x1, waiting for transfers between devices, body(): lax.all_gather(unit[:, :CH], ('yl', 'co', 'z'), axis=0, tiled=True)  24.8 us
    all_to_all x4, waiting for transfers between devices, swap(): return lax.all_to_all(value, axes, split_axis=0, concat_axis=0, tiled=True)  24.3 us
    all_to_all x1, blocking collectives, swap(): return lax.all_to_all(value, axes, split_axis=0, concat_axis=0, tiled=True)  16.6 us
    ppermute x6, waiting for transfers between devices, along_x(): got = {d: lax.ppermute(value, 'x', ring(NX, d)) for d in (2, 1, 3)}  9.71 us
    ppermute x6, starting transfers between devices, along_x(): got = {d: lax.ppermute(value, 'x', ring(NX, d)) for d in (2, 1, 3)}  9.71 us
    pallas_call x1, Pallas kernels, project(): pl.pallas_call(project_kernel, in_specs=[any_spec] * 13 + [vmem] * 2, out...  8.71 us
    unnamed x32, local copies, waits for them, and re-layouts  6.57 us
  transfers between devices with their start and end apart: 17, of which 7 were waited for; matrix products, arithmetic and copies ran while one was open for 3% of the time, Pallas kernels for 9%

profile of v4, /device:TPU:2, one launch (start us, length us, event | category | flops | bytes accessed | tf_op | source)
XLA Modules:
  0.0 169.7 jit_solution(14774186106644533811)
XLA Ops:
  6.5 1.2 reshape.46
  7.8 0.9 reshape.47
  8.7 7.6 %all-to-all-start = ((bf16[8,8,768]{2,1,0:T(8,128)(2,1)}), bf16[8,8,768]{2,1,0:T(8,128)(2,1)S(1)}, u32[]{:S(2)}, u32[]{:S(2)}) async-start(bf16[8,8,768]{2,1,0:T(8,128)(2,1)} %reshape.47), calls=%async_computation | async-start | bytes 196608 | tf_op jit(solution)/shard_map/all_to_all | solution.py:347
  16.9 6.2 %all-to-all-done = bf16[8,8,768]{2,1,0:T(8,128)(2,1)S(1)} async-done(((bf16[8,8,768]{2,1,0:T(8,128)(2,1)}), bf16[8,8,768]{2,1,0:T(8,128)(2,1)S(1)}, u32[]{:S(2)}, u32[]{:S(2)}) %all-to-all-start) | async-done | bytes 98336 | tf_op jit(solution)/shard_map/all_to_all | solution.py:347
  23.1 0.8 broadcast_in_dim.9
  23.9 8.5 %all-to-all-start.1 = ((bf16[8,64,512]{2,1,0:T(8,128)(2,1)}), bf16[8,64,512]{2,1,0:T(8,128)(2,1)}, u32[]{:S(2)}, u32[]{:S(2)}) async-start(bf16[8,64,512]{2,1,0:T(8,128)(2,1)} %broadcast_in_dim.9), calls=%async_computation.1 | async-start | bytes 1048576 | tf_op jit(solution)/shard_map/all_to_all | solution.py:347
  33.5 3.0 %collective-permute-start.1 = (bf16[128,2048]{1,0:T(8,128)(2,1)S(1)}, bf16[128,2048]{1,0:T(8,128)(2,1)S(1)}, u32[]{:S(2)}, u32[]{:S(2)}) collective-permute-start(bf16[128,2048]{1,0:T(8,128)(2,1)S(1)} %shard_map.73.a0), channel_id=1, source_target_pairs={{0,2},{1,3},{2,0},{3,1},{4,6},{5,7},{6,4},{7,5},{8,10},{9,11},{10,... | collective-permute-start | bytes 1572872 | tf_op jit(solution)/shard_map/ppermute | solution.py:338
  37.1 0.7 collective-permute-start.3
  37.8 10.7 %all-to-all-done.1 = bf16[8,64,512]{2,1,0:T(8,128)(2,1)} async-done(((bf16[8,64,512]{2,1,0:T(8,128)(2,1)}), bf16[8,64,512]{2,1,0:T(8,128)(2,1)}, u32[]{:S(2)}, u32[]{:S(2)}) %all-to-all-start.1) | async-done | bytes 524320 | tf_op jit(solution)/shard_map/all_to_all | solution.py:347
  49.8 8.1 %collective-permute-done.2.a3 = bf16[128,2048]{1,0:T(8,128)(2,1)S(1)} collective-permute-done((bf16[128,2048]{1,0:T(8,128)(2,1)S(1)}, bf16[128,2048]{1,0:T(8,128)(2,1)S(1)}, u32[]{:S(2)}, u32[]{:S(2)}) %collective-permute-start.2) | collective-permute-done | bytes 524320 | tf_op jit(solution)/shard_map/ppermute | solution.py:338
  58.0 1.3 collective-permute-start.7
  59.3 1.3 collective-permute-start.8
  61.5 2.9 %collective-permute-start.5 = (bf16[128,2048]{1,0:T(8,128)(2,1)S(1)}, bf16[128,2048]{1,0:T(8,128)(2,1)}, u32[]{:S(2)}, u32[]{:S(2)}) collective-permute-start(bf16[128,2048]{1,0:T(8,128)(2,1)S(1)} %collective-permute-done.3.b0), channel_id=1, source_target_pairs={{0,2},{1,3},{2,0},{3,1},{4,6},{5,7},{6,4},{7,5},{8,10},{9,11},{10,... | collective-permute-start | bytes 1572872 | tf_op jit(solution)/shard_map/ppermute | solution.py:338
  64.6 2.0 %collective-permute-start.6 = (bf16[128,2048]{1,0:T(8,128)(2,1)S(1)}, bf16[128,2048]{1,0:T(8,128)(2,1)}, u32[]{:S(2)}, u32[]{:S(2)}) collective-permute-start(bf16[128,2048]{1,0:T(8,128)(2,1)S(1)} %collective-permute-done.3.b0), channel_id=1, source_target_pairs={{0,3},{1,0},{2,1},{3,2},{4,7},{5,4},{6,5},{7,6},{8,11},{9,8},{10,9... | collective-permute-start | bytes 1572872 | tf_op jit(solution)/shard_map/ppermute | solution.py:338
  67.8 9.8 %all-to-all-start.2 = ((f32[8,9,128]{2,1,0:T(8,128)}), f32[8,9,128]{2,1,0:T(8,128)S(1)}, u32[]{:S(2)}, u32[]{:S(2)}) async-start(f32[8,9,128]{2,1,0:T(8,128)} %broadcast_in_dim.10), calls=%async_computation.2 | async-start | bytes 131072 | tf_op jit(solution)/shard_map/all_to_all | solution.py:347
  77.6 0.9 add.12.halo
  78.5 7.4 %all-to-all-done.2 = f32[8,9,128]{2,1,0:T(8,128)S(1)} async-done(((f32[8,9,128]{2,1,0:T(8,128)}), f32[8,9,128]{2,1,0:T(8,128)S(1)}, u32[]{:S(2)}, u32[]{:S(2)}) %all-to-all-start.2) | async-done | bytes 36896 | tf_op jit(solution)/shard_map/all_to_all | solution.py:347
  86.8 0.9 collective-permute-done.6.b3
  87.8 8.7 %shard_map.75 = (bf16[1024,256]{1,0:T(8,128)(2,1)S(1)}, f32[16,64,256]{2,1,0:T(8,128)}, f32[16,256]{1,0:T(8,128)S(1)}) custom-call(bf16[128,2048]{1,0:T(8,128)(2,1)S(1)} %shard_map.73.a0, bf16[128,2048]{1,0:T(8,128)(2,1)S(1)} %collective-permute-done.a1, bf16[128,2048]{1,0:T(8,128)(2,1)S(1)} %collective-permute-done.1.a2, ...), custom_call_target="tpu_custom_call" | custom-call | flops 2181038080 | bytes 10000000 | tf_op jit(solution)/shard_map/pallas_call | solution.py:165
  96.5 0.8 copy-done.9
  98.0 6.9 %all-to-all-start.3 = ((f32[8,16,256]{2,1,0:T(8,128)}), f32[8,16,256]{2,1,0:T(8,128)S(1)}, u32[]{:S(2)}, u32[]{:S(2)}) async-start(f32[8,16,256]{2,1,0:T(8,128)} %broadcast_in_dim.11), calls=%async_computation.3 | async-start | bytes 262144 | tf_op jit(solution)/shard_map/all_to_all | solution.py:347
  105.1 0.8 slice_reduce_fusion
  106.0 24.8 %all-gather.2.cloned.1.call-done.wq = bf16[2048,256]{1,0:T(8,128)(2,1)} async-done(((bf16[64,256]{1,0:T(8,128)(2,1)}), bf16[2048,256]{1,0:T(8,128)(2,1)}) %all-gather.2.cloned.1.call-update) | async-done | bytes 1048592 | tf_op jit(solution)/shard_map/all_gather | solution.py:384
  130.8 1.0 copy-done.6
  131.8 1.0 copy-done.8
  132.9 6.1 %shard_map.76 = (bf16[1024,256]{1,0:T(8,128)(2,1)S(1)}, f32[1024,256]{1,0:T(8,128)}) custom-call(bf16[128,2048]{1,0:T(8,128)(2,1)S(1)} %shard_map.73.a0, bf16[128,2048]{1,0:T(8,128)(2,1)S(1)} %collective-permute-done.a1, bf16[128,2048]{1,0:T(8,128)(2,1)S(1)} %collective-permute-done.1.a2, bf16[128,2048]{1,0:T(8,128)(2,1)S(1)} %collective-permute-done.2.a3, ...), custom_call_target="tpu_custom_call" | custom-call | flops 1090519040 | bytes 8000000 | tf_op jit(solution)/shard_map/pallas_call | solution.py:239
  139.0 0.8 copy-done.2
  139.7 1.2 copy-done.1
  141.0 1.0 copy-done.3
  142.0 3.4 %shard_map.77 = bf16[8,256,128]{2,1,0:T(8,128)(2,1)S(1)} custom-call(f32[8,16,256]{2,1,0:T(8,128)S(1)} %all-to-all-done.3.states, f32[16,256]{1,0:T(8,128)S(1)} %reshape.56.rates, f32[16,256]{1,0:T(8,128)S(1)} %reshape.58.residues, f32[1024,256]{1,0:T(8,128)S(1)} %copy-done.1, f32[16,64,256]{2,1,0:T(8,128)S(1)} %copy-done, bf16[1024,256]{1,0:T(8,128)(2,1)S(1)} %copy-done.3), custom_call_target="tpu_custom_call" | custom-call | tf_op jit(solution)/shard_map/pallas_call | solution.py:303
  145.4 16.6 %all_to_all.25.pieces = bf16[8,256,128]{2,1,0:T(8,128)(2,1)S(1)} all-to-all(bf16[8,256,128]{2,1,0:T(8,128)(2,1)S(1)} %shard_map.77), channel_id=1, replica_groups=mesh['yl'=2,'co'=2,'z'=8,'yh'=2,'x'=4] {'yh','x'}, dimensions={0} | all-to-all | bytes 1048576 | tf_op jit(solution)/shard_map/all_to_all | solution.py:347
  162.0 0.8 shard_map.78
  (67 shorter events, 7.8 us)
Async XLA Ops:
  7.8 8.5 %copy-start.4 = (bf16[1,128,2048]{2,1,0:T(8,128)(2,1)S(1)}, bf16[1,128,2048]{2,1,0:T(8,128)(2,1)}, u32[]{:S(2)}) copy-start(bf16[1,128,2048]{2,1,0:T(8,128)(2,1)} %param.7) | copy-start | bytes 1572868
  8.7 7.6 %copy-start.10 = (f32[2048]{0:T(1024)S(1)}, f32[2048]{0:T(1024)}, u32[]{:S(2)}) copy-start(f32[2048]{0:T(1024)} %param.8) | copy-start | bytes 24580
  8.7 14.3 %all-to-all-start = ((bf16[8,8,768]{2,1,0:T(8,128)(2,1)}), bf16[8,8,768]{2,1,0:T(8,128)(2,1)S(1)}, u32[]{:S(2)}, u32[]{:S(2)}) async-start(bf16[8,8,768]{2,1,0:T(8,128)(2,1)} %reshape.47), calls=%async_computation | async-start | bytes 196608 | tf_op jit(solution)/shard_map/all_to_all | solution.py:347
  23.9 24.6 %all-to-all-start.1 = ((bf16[8,64,512]{2,1,0:T(8,128)(2,1)}), bf16[8,64,512]{2,1,0:T(8,128)(2,1)}, u32[]{:S(2)}, u32[]{:S(2)}) async-start(bf16[8,64,512]{2,1,0:T(8,128)(2,1)} %broadcast_in_dim.9), calls=%async_computation.1 | async-start | bytes 1048576 | tf_op jit(solution)/shard_map/all_to_all | solution.py:347
  32.4 98.4 %all-gather.2.cloned.1.call-start = ((), (), s32[]{:S(2)}) async-start(), calls=%async_computation.5 | async-start | bytes 1081344 | tf_op jit(solution)/shard_map/all_gather | solution.py:384
  33.1 16.1 %collective-permute-start = (bf16[128,2048]{1,0:T(8,128)(2,1)S(1)}, bf16[128,2048]{1,0:T(8,128)(2,1)S(1)}, u32[]{:S(2)}, u32[]{:S(2)}) collective-permute-start(bf16[128,2048]{1,0:T(8,128)(2,1)S(1)} %shard_map.73.a0), channel_id=1, source_target_pairs={{0,1},{1,2},{2,3},{3,0},{4,5},{5,6},{6,7},{7,4},{8,9},{9,10},{10,1... | collective-permute-start | bytes 1572872 | tf_op jit(solution)/shard_map/ppermute | solution.py:338
  33.5 16.4 %collective-permute-start.1 = (bf16[128,2048]{1,0:T(8,128)(2,1)S(1)}, bf16[128,2048]{1,0:T(8,128)(2,1)S(1)}, u32[]{:S(2)}, u32[]{:S(2)}) collective-permute-start(bf16[128,2048]{1,0:T(8,128)(2,1)S(1)} %shard_map.73.a0), channel_id=1, source_target_pairs={{0,2},{1,3},{2,0},{3,1},{4,6},{5,7},{6,4},{7,5},{8,10},{9,11},{10,... | collective-permute-start | bytes 1572872 | tf_op jit(solution)/shard_map/ppermute | solution.py:338
  36.4 21.5 %collective-permute-start.2 = (bf16[128,2048]{1,0:T(8,128)(2,1)S(1)}, bf16[128,2048]{1,0:T(8,128)(2,1)S(1)}, u32[]{:S(2)}, u32[]{:S(2)}) collective-permute-start(bf16[128,2048]{1,0:T(8,128)(2,1)S(1)} %shard_map.73.a0), channel_id=1, source_target_pairs={{0,3},{1,0},{2,1},{3,2},{4,7},{5,4},{6,5},{7,6},{8,11},{9,8},{10,9... | collective-permute-start | bytes 1572872 | tf_op jit(solution)/shard_map/ppermute | solution.py:338
  37.1 23.6 %collective-permute-start.3 = (bf16[128,2048]{1,0:T(8,128)(2,1)S(1)}, bf16[128,2048]{1,0:T(8,128)(2,1)S(1)}, u32[]{:S(2)}, u32[]{:S(2)}) collective-permute-start(bf16[128,2048]{1,0:T(8,128)(2,1)S(1)} %shard_map.73.a0), channel_id=1, source_target_pairs={{0,4},{4,0},{1,5},{5,1},{2,6},{6,2},{3,7},{7,3},{8,12},{12,8},{9,1... | collective-permute-start | bytes 1572872 | tf_op jit(solution)/shard_map/ppermute | solution.py:381
  48.5 12.1 %copy-start.12 = (f32[3,6144]{1,0:T(4,128)S(1)}, f32[3,6144]{1,0:T(4,128)}, u32[]{:S(2)}) copy-start(f32[3,6144]{1,0:T(4,128)} %param.10) | copy-start | bytes 221188
  48.5 18.1 %collective-permute-start.9 = (bf16[512,512]{1,0:T(8,128)(2,1)}, bf16[512,512]{1,0:T(8,128)(2,1)}, u32[]{:S(2)}, u32[]{:S(2)}) collective-permute-start(bf16[512,512]{1,0:T(8,128)(2,1)} %bitcast.4.w00), channel_id=1, source_target_pairs={{0,128},{128,0},{1,129},{129,1},{2,130},{130,2},{3,131},{131,3},{4... | collective-permute-start | bytes 1572872 | tf_op jit(solution)/shard_map/ppermute | solution.py:386
  58.0 6.5 %collective-permute-start.7 = (bf16[16,2048]{1,0:T(8,128)(2,1)S(1)}, bf16[16,2048]{1,0:T(8,128)(2,1)}, u32[]{:S(2)}, u32[]{:S(2)}) collective-permute-start(bf16[16,2048]{1,0:T(8,128)(2,1)S(1)} %shard_map.74), channel_id=1, source_target_pairs={{4,8},{12,16},{20,24},{28,32},{36,40},{44,48},{52,56},{5,9},{13,17... | collective-permute-start | bytes 196616 | tf_op jit(solution)/shard_map/ppermute | solution.py:397
  59.3 7.3 %collective-permute-start.8 = (bf16[16,2048]{1,0:T(8,128)(2,1)S(1)}, bf16[16,2048]{1,0:T(8,128)(2,1)}, u32[]{:S(2)}, u32[]{:S(2)}) collective-permute-start(bf16[16,2048]{1,0:T(8,128)(2,1)S(1)} %shard_map.74), channel_id=1, source_target_pairs={{4,12},{12,20},{20,28},{28,36},{36,44},{44,52},{52,60},{5,13},{13,... | collective-permute-start | bytes 196616 | tf_op jit(solution)/shard_map/ppermute | solution.py:397
  60.6 3.8 %copy-start.13 = (f32[32,16]{0,1:T(8,128)S(1)}, f32[32,16]{0,1:T(8,128)}, u32[]{:S(2)}) copy-start(f32[32,16]{0,1:T(8,128)} %param.11) | copy-start | bytes 6148
  60.7 3.7 %copy-start.14 = (f32[32,16]{0,1:T(8,128)S(1)}, f32[32,16]{0,1:T(8,128)}, u32[]{:S(2)}) copy-start(f32[32,16]{0,1:T(8,128)} %param.12) | copy-start | bytes 6148
  60.8 35.7 %copy-start.5 = (bf16[128,2048]{1,0:T(8,128)(2,1)}, bf16[128,2048]{1,0:T(8,128)(2,1)S(1)}, u32[]{:S(2)}) copy-start(bf16[128,2048]{1,0:T(8,128)(2,1)S(1)} %collective-permute-done.3.b0) | copy-start | bytes 1572868
  60.8 26.0 %collective-permute-start.4 = (bf16[128,2048]{1,0:T(8,128)(2,1)S(1)}, bf16[128,2048]{1,0:T(8,128)(2,1)S(1)}, u32[]{:S(2)}, u32[]{:S(2)}) collective-permute-start(bf16[128,2048]{1,0:T(8,128)(2,1)S(1)} %collective-permute-done.3.b0), channel_id=1, source_target_pairs={{0,1},{1,2},{2,3},{3,0},{4,5},{5,6},{6,7},{7,4},{8,9},{9,10},{10,1... | collective-permute-start | bytes 1572872 | tf_op jit(solution)/shard_map/ppermute | solution.py:338
  61.5 25.3 %collective-permute-start.5 = (bf16[128,2048]{1,0:T(8,128)(2,1)S(1)}, bf16[128,2048]{1,0:T(8,128)(2,1)}, u32[]{:S(2)}, u32[]{:S(2)}) collective-permute-start(bf16[128,2048]{1,0:T(8,128)(2,1)S(1)} %collective-permute-done.3.b0), channel_id=1, source_target_pairs={{0,2},{1,3},{2,0},{3,1},{4,6},{5,7},{6,4},{7,5},{8,10},{9,11},{10,... | collective-permute-start | bytes 1572872 | tf_op jit(solution)/shard_map/ppermute | solution.py:338
  64.5 2.7 %copy-start.15 = (f32[32]{0:T(128)S(1)}, f32[32]{0:T(128)}, u32[]{:S(2)}) copy-start(f32[32]{0:T(128)} %param.13) | copy-start | bytes 388
  64.6 23.2 %collective-permute-start.6 = (bf16[128,2048]{1,0:T(8,128)(2,1)S(1)}, bf16[128,2048]{1,0:T(8,128)(2,1)}, u32[]{:S(2)}, u32[]{:S(2)}) collective-permute-start(bf16[128,2048]{1,0:T(8,128)(2,1)S(1)} %collective-permute-done.3.b0), channel_id=1, source_target_pairs={{0,3},{1,0},{2,1},{3,2},{4,7},{5,4},{6,5},{7,6},{8,11},{9,8},{10,9... | collective-permute-start | bytes 1572872 | tf_op jit(solution)/shard_map/ppermute | solution.py:338
  66.6 21.1 %collective-permute-start.10 = (bf16[512,512]{1,0:T(8,128)(2,1)}, bf16[512,512]{1,0:T(8,128)(2,1)}, u32[]{:S(2)}, u32[]{:S(2)}) collective-permute-start(bf16[512,512]{1,0:T(8,128)(2,1)} %bitcast.4.w00), channel_id=1, source_target_pairs={{0,64},{64,0},{1,65},{65,1},{2,66},{66,2},{3,67},{67,3},{4,68},{68... | collective-permute-start | bytes 1572872 | tf_op jit(solution)/shard_map/ppermute | solution.py:388
  66.6 21.1 %collective-permute-start.11 = (bf16[512,512]{1,0:T(8,128)(2,1)}, bf16[512,512]{1,0:T(8,128)(2,1)}, u32[]{:S(2)}, u32[]{:S(2)}) collective-permute-start(bf16[512,512]{1,0:T(8,128)(2,1)} %collective-permute-done.9.w01), channel_id=1, source_target_pairs={{0,64},{64,0},{1,65},{65,1},{2,66},{66,2},{3,67},{67,3},{4,68},{68... | collective-permute-start | bytes 1572872 | tf_op jit(solution)/shard_map/ppermute | solution.py:389
  67.8 18.2 %all-to-all-start.2 = ((f32[8,9,128]{2,1,0:T(8,128)}), f32[8,9,128]{2,1,0:T(8,128)S(1)}, u32[]{:S(2)}, u32[]{:S(2)}) async-start(f32[8,9,128]{2,1,0:T(8,128)} %broadcast_in_dim.10), calls=%async_computation.2 | async-start | bytes 131072 | tf_op jit(solution)/shard_map/all_to_all | solution.py:347
  86.8 9.7 %copy-start.7 = (bf16[128,2048]{1,0:T(8,128)(2,1)}, bf16[128,2048]{1,0:T(8,128)(2,1)S(1)}, u32[]{:S(2)}) copy-start(bf16[128,2048]{1,0:T(8,128)(2,1)S(1)} %collective-permute-done.4.b1) | copy-start | bytes 1572868
  96.5 0.8 copy-start.9
  98.0 41.8 %all-to-all-start.3 = ((f32[8,16,256]{2,1,0:T(8,128)}), f32[8,16,256]{2,1,0:T(8,128)S(1)}, u32[]{:S(2)}, u32[]{:S(2)}) async-start(f32[8,16,256]{2,1,0:T(8,128)} %broadcast_in_dim.11), calls=%async_computation.3 | async-start | bytes 262144 | tf_op jit(solution)/shard_map/all_to_all | solution.py:347
  130.8 1.0 copy-start.6
  131.8 1.0 copy-start.8
  132.9 6.9 %copy-start = (f32[16,64,256]{2,1,0:T(8,128)S(1)}, f32[16,64,256]{2,1,0:T(8,128)}, u32[]{:S(2)}) copy-start(f32[16,64,256]{2,1,0:T(8,128)} %get-tuple-element.23.chunk) | copy-start | bytes 3145732
  138.9 0.8 copy-start.2
  139.7 1.2 copy-start.1
  141.0 1.0 copy-start.3
  (1 other events, 0.6 us)
Sparse Core Ops, SparseCore 0:
  35.0 95.7 all-gather.1

commit v5 on v3

--- a/solution.py
+++ b/solution.py
@@ -20,6 +20,9 @@
 SPAN = PIECES * HERE
 ROWS = HALO + SPAN
 D = 2048
+UNIT = 128
+NEAR = (0, 1, 2, 3, 5, 6, 7)
+TABLE = 16
 COLS = 3 * CH
 MIB = 1024 * 1024
 
@@ -64,37 +67,96 @@
     return [t[0] * ext[j + 2] + t[1] * ext[j + 1] + t[2] * ext[j] for j in range(CHUNK)]
 
 
+class Copier:
+    def __init__(self, sems):
+        self.sems, self.copies = sems, []
+
+    def __call__(self, src, dst):
+        c = pltpu.make_async_copy(src, dst, self.sems.at[len(self.copies)])
+        c.start()
+        self.copies.append(c)
+
+    def one_of(self, which, sources, dst):
+        sem = self.sems.at[len(self.copies)]
+        for i, src in enumerate(sources):
+            c = pltpu.make_async_copy(src, dst, sem)
+            pl.when(which == i)(c.start)
+        self.copies.append(c)
+
+    def wait(self):
+        for c in self.copies:
+            c.wait()
+
+
+HALF = HERE // 2
+PIECE_LIST = (
+    (0, 0, 0, HERE, 0, 0),
+    (0, 1, 0, HERE, 1, 0),
+    (0, 3, 0, HERE, 2, 0),
+    (1, 0, 0, HERE, 3, 0),
+    (1, 1, 0, HERE, 4, 0),
+    (0, 2, 0, HALF, 4, HERE),
+    (1, 3, 0, HERE, 5, 0),
+    (0, 2, HALF, HALF, 5, HERE),
+    (1, 2, 0, HALF, 6, 0),
+    (1, 2, HALF, HALF, 7, 0),
+)
+PIECE_ARRAYS = 8
+
+
+def copy_rows(copy, arrays, halo, lhs):
+    x, yh = lax.axis_index("x"), lax.axis_index("yh")
+    copy.one_of(yh, halo, lhs.at[pl.ds(0, HALO)])
+    for other, by, first, rows, array, at in PIECE_LIST:
+        place = lax.rem(yh + other, 2) * NX + lax.rem(x + NX - by, NX)
+        row = pl.multiple_of(HALO + place * HERE + first, 16)
+        copy(arrays[array].at[pl.ds(at, rows)], lhs.at[pl.ds(row, rows)])
+
+
+def copy_weights(copy, planes, w):
+    z, core = lax.axis_index("z"), lax.axis_index("co")
+    for r in range(2):
+        most, last = planes[2 * r], planes[2 * r + 1]
+        for i, d in enumerate(NEAR + (NZ // 2,)):
+            place = last if d == NZ // 2 else most.at[i]
+            row = lax.rem(core + r, 2) * 512 + lax.rem(z + NZ - d, NZ) * 64
+            for yl in range(2):
+                to = pl.ds(pl.multiple_of(yl * 1024 + row, 64), 64)
+                copy(place.at[pl.ds(yl * 64, 64)], w.at[to])
+
+
+def decode(blocks, out):
+    z = lax.axis_index("z")
+    halves = [jnp.zeros((TABLE, COLS), F32)] * 2
+    for i, d in enumerate(NEAR + (NZ // 2,)):
+        block = blocks[i].astype(F32)
+        low = lax.rem(z + NZ - d, NZ) < NZ // 2
+        halves[0] = halves[0] + jnp.where(low, block, 0.0)
+        halves[1] = halves[1] + jnp.where(low, 0.0, block)
+    for h, block in enumerate(halves):
+        tile = [block[:, i * LANES : (i + 1) * LANES] for i in range(6)]
+        lanes = slice(h * LANES, (h + 1) * LANES)
+        out[0:16, lanes] = tile[0] + tile[1] + tile[2]
+        out[16:32, lanes] = tile[3] + tile[4]
+        skip = tile[5][0:1] + tile[5][1:2] + tile[5][2:3]
+        out[32:40, lanes] = jnp.broadcast_to(skip, (8, LANES))
+
+
 def project_kernel(
-    a0, a1, a2, a3, b0, b1, b2, b3, halo, w00, w01, w10, w11,
-    taps, rates,
-    query_ref, carried_ref, chunk_ref, state_ref,
-    lhs, w, proj, decay_s, carry, sems,
+    *refs,
 ):
-    x = lax.axis_index("x")
-    yh = lax.axis_index("yh")
-    yl = lax.axis_index("yl")
-    core = lax.axis_index("co")
-    copies = []
-
-    def copy(src, dst):
-        c = pltpu.make_async_copy(src, dst, sems.at[len(copies)])
-        c.start()
-        copies.append(c)
-
-    for r, pieces in enumerate(((w00, w01), (w10, w11))):
-        for e, piece in enumerate(pieces):
-            row = lax.rem(yl + e, 2) * 1024 + lax.rem(core + r, 2) * 512
-            copy(piece, w.at[pl.ds(pl.multiple_of(row, 512), 512)])
-    copy(halo, lhs.at[pl.ds(0, HALO)])
-    for e, pieces in enumerate(((a0, a1, a2, a3), (b0, b1, b2, b3))):
-        for d, piece in enumerate(pieces):
-            at = lax.rem(yh + e, 2) * NX + lax.rem(x + NX - d, NX)
-            copy(piece, lhs.at[pl.ds(pl.multiple_of(HALO + at * HERE, 16), HERE)])
-
-    decay_s[...] = jnp.exp(-rates[...])
-    for c in copies:
-        c.wait()
-
+    arrays, refs = refs[:PIECE_ARRAYS], refs[PIECE_ARRAYS:]
+    halo, planes, refs = refs[:2], refs[2:6], refs[6:]
+    taps, query_ref, carried_ref, chunk_ref, state_ref, rates = refs[:6]
+    lhs, w, proj, blocks, decay_s, carry, sems = refs[6:]
+    copy = Copier(sems)
+    copy_weights(copy, planes, w)
+    copy(planes[0].at[:, pl.ds(UNIT, TABLE)], blocks.at[pl.ds(0, NZ - 1)])
+    copy(planes[1].at[pl.ds(UNIT, TABLE)], blocks.at[NZ - 1])
+    copy_rows(copy, arrays, halo, lhs)
+    copy.wait()
+    decode(blocks, rates)
+    decay_s[...] = jnp.exp(-rates[0:16, :])
     for s in (1, 2, 0):
         cols = slice(s * CH, (s + 1) * CH)
         product = jnp.dot(lhs[...], w[:, cols], preferred_element_type=F32).astype(BF16)
@@ -153,43 +215,48 @@
                 carry[m] = jnp.broadcast_to(s[7:8, :], (8, LANES))
 
         for m in range(POLES):
-            state_ref[m : m + 1, here] = carry[m, 0:1, :]
-
-
-def project(normed, halo, weights, taps, rates):
+            for i in range(NZ):
+                state_ref[i, m : m + 1, here] = carry[m, 0:1, :]
+
+
+def project(arrays, halo, weights, taps):
     any_spec = pl.BlockSpec(memory_space=pl.ANY)
     vmem = pl.BlockSpec(memory_space=pltpu.VMEM)
     return pl.pallas_call(
         project_kernel,
-        in_specs=[any_spec] * 13 + [vmem] * 2,
-        out_specs=[vmem] * 4,
+        in_specs=[any_spec] * (PIECE_ARRAYS + 6) + [vmem],
+        out_specs=[vmem] * 5,
         out_shape=[
             jax.ShapeDtypeStruct((ROWS, CH), BF16),
             jax.ShapeDtypeStruct((SPAN, CH), BF16),
             jax.ShapeDtypeStruct((POLES, SPAN // CHUNK, CH), F32),
-            jax.ShapeDtypeStruct((POLES, CH), F32),
+            jax.ShapeDtypeStruct((NZ, POLES, CH), F32),
+            jax.ShapeDtypeStruct((40, CH), F32),
         ],
         scratch_shapes=[
             pltpu.VMEM((ROWS, D), BF16),
             pltpu.VMEM((D, COLS), BF16),
             pltpu.VMEM((ROWS, 2 * CH), F32),
+            pltpu.VMEM((NZ, TABLE, COLS), BF16),
             pltpu.VMEM((POLES, CH), F32),
             pltpu.VMEM((POLES, 8, LANES), F32),
-            pltpu.SemaphoreType.DMA((13,)),
+            pltpu.SemaphoreType.DMA((len(PIECE_LIST) + 35,)),
         ],
-        compiler_params=params(28),
+        compiler_params=params(60),
         cost_estimate=pl.CostEstimate(
             flops=2 * ROWS * D * COLS, bytes_accessed=10_000_000, transcendentals=0
         ),
-    )(*normed, halo, *weights, taps, rates)
-
-
-def direct_kernel(query, carried, taps, rates, residues, skip, gate_ref, local_ref, taps_s):
-    decay = jnp.exp(-rates[...])
-    power = residues[...] * jnp.sqrt(2.0 * rates[...])
+    )(*arrays, *halo, *weights, taps)
+
+
+def direct_kernel(query, carried, taps, table, gate_ref, local_ref, taps_s):
+    rate = table[0:16, :]
+    decay = jnp.exp(-rate)
+    power = table[16:32, :] * jnp.sqrt(2.0 * rate)
+    skip = table[32:33, :]
     for i in range(CHUNK):
         row = jnp.sum(power, axis=0, keepdims=True)
-        taps_s[i : i + 1, :] = row + skip[...] if i == 0 else row
+        taps_s[i : i + 1, :] = row + skip if i == 0 else row
         power = power * decay
     sub = lax.broadcasted_iota(jnp.int32, (8, LANES), 0)
 
@@ -200,6 +267,8 @@
         @pl.loop(0, PIECES)
         def _(p):
             row0 = pl.multiple_of(p * HERE, 16)
+
+            t = [taps[i : i + 1, here] for i in range(3)]
 
             def rows(ref, count):
                 pairs = [
@@ -208,7 +277,6 @@
                 ]
                 return [half for pair in pairs for half in (pair[:8], pair[8:])]
 
-            t = [taps[i : i + 1, here] for i in range(3)]
             queries = filtered(rows(query, 9), t, sub)
             for j in range(0, CHUNK, 2):
                 gate_ref[pl.ds(pl.multiple_of(row0 + 8 * j, 16), 16), here] = jnp.concatenate(
@@ -223,11 +291,11 @@
                 local_ref[pl.ds(row0 + 8 * j, 8), here] = acc
 
 
-def direct(query, carried, taps, rates, residues, skip):
+def direct(query, carried, taps, table):
     vmem = pl.BlockSpec(memory_space=pltpu.VMEM)
     return pl.pallas_call(
         direct_kernel,
-        in_specs=[vmem] * 6,
+        in_specs=[vmem] * 4,
         out_specs=[vmem] * 2,
         out_shape=[
             jax.ShapeDtypeStruct((SPAN, CH), BF16),
@@ -238,14 +306,15 @@
         cost_estimate=pl.CostEstimate(
             flops=40 * SPAN * CH, bytes_accessed=3_000_000, transcendentals=0
         ),
-    )(query, carried, taps, rates, residues, skip)
+    )(query, carried, taps, table)
 
 
 def finish_kernel(
-    states, rates, residues, local, chunk, gate, out, scr, start_s, decay_s, weight_s
+    states, table, local, chunk, gate, out, scr, rates, start_s, decay_s, weight_s
 ):
     z = lax.axis_index("z")
-    rate = rates[...]
+    rate = table[0:16, :]
+    rates[...] = rate
     span = jnp.exp(-float(SPAN) * rate)
     total = jnp.zeros((POLES, CH), F32)
     for i in range(NZ - 1):
@@ -253,7 +322,7 @@
     start_s[...] = total
     decay = jnp.exp(-rate)
     decay_s[...] = decay
-    weight_s[...] = residues[...] * jnp.sqrt(2.0 * rate) * decay
+    weight_s[...] = table[16:32, :] * jnp.sqrt(2.0 * rate) * decay
     sub = lax.broadcasted_iota(jnp.int32, (8, LANES), 0)
 
     @pl.loop(0, PIECES)
@@ -281,11 +350,11 @@
             out[p, here, :] = scr[...].T.astype(BF16)
 
 
-def finish(states, rates, residues, local, chunk, gate):
+def finish(states, table, local, chunk, gate):
     vmem = pl.BlockSpec(memory_space=pltpu.VMEM)
     return pl.pallas_call(
         finish_kernel,
-        in_specs=[vmem] * 6,
+        in_specs=[vmem] * 5,
         out_specs=vmem,
         out_shape=jax.ShapeDtypeStruct((PIECES, CH, HERE), BF16),
         scratch_shapes=[
@@ -293,9 +362,10 @@
             pltpu.VMEM((POLES, CH), F32),
             pltpu.VMEM((POLES, CH), F32),
             pltpu.VMEM((POLES, CH), F32),
+            pltpu.VMEM((POLES, CH), F32),
         ],
         compiler_params=params(10),
-    )(states, rates, residues, local, chunk, gate)
+    )(states, table, local, chunk, gate)
 
 
 def place_kernel(pieces, out):
@@ -317,26 +387,26 @@
     return [(i, (i + by) % size) for i in range(size)]
 
 
-def along_x(value):
-    got = {d: lax.ppermute(value, "x", ring(NX, d)) for d in (2, 1, 3)}
-    return [value] + [got[d] for d in (1, 2, 3)]
-
-
-def spread(value):
-    return jnp.broadcast_to(value[None], (NZ,) + value.shape)
+def shift(value, axis, by):
+    return lax.ppermute(value, axis, ring(lax.axis_size(axis), by))
+
+
+def spread(value, count=NZ):
+    return jnp.broadcast_to(value[None], (count,) + value.shape)
 
 
 def swap(value, axes):
     return lax.all_to_all(value, axes, split_axis=0, concat_axis=0, tiled=True)
 
 
-def tail_kernel(a0, a1, a2, a3, out, sem):
-    which = lax.rem(lax.axis_index("x") + 1, NX)
-    for d, piece in enumerate((a0, a1, a2, a3)):
-
-        @pl.when(which == d)
+def tail_kernel(own, behind, ahead, mixed, out, sem):
+    x = lax.axis_index("x")
+    for at, piece in ((3, own), (0, behind), (2, ahead), (1, mixed)):
+
+        @pl.when(x == at)
         def _(piece=piece):
-            copy = pltpu.make_async_copy(piece.at[pl.ds(HERE - HALO, HALO)], out, sem)
+            rows = pl.ds(piece.shape[0] - HALO, HALO)
+            copy = pltpu.make_async_copy(piece.at[rows], out, sem)
             copy.start()
             copy.wait()
 
@@ -353,47 +423,66 @@
     )(*row)
 
 
+def coded(values, parts):
+    out = []
+    for _ in range(parts):
+        part = lax.reduce_precision(values, 8, 7)
+        out.append(part)
+        values = values - part
+    return out
+
+
 def body(tokens, norm_gain, in_weight, short_filter, rates, residues, skip):
-    x, yh = lax.axis_index("x"), lax.axis_index("yh")
-    own = normalise(tokens[0], norm_gain[None, :])
-    partner = lax.ppermute(own, "yh", ring(2, 1))
-    own_row = along_x(own)
-
-    blocks = in_weight.reshape(8, 3, NZ, PIECES, 32).transpose(3, 0, 1, 2, 4)
-    blocks = spread(blocks.reshape(PIECES, 8, COLS)).reshape(NZ * PIECES, 8, COLS)
-    plane = swap(blocks, ("z", "yh", "x")).reshape(512, COLS)
-
-    other_plane = lax.ppermute(plane, "yl", ring(2, 1))
-    partner_row = along_x(partner)
-    sibling = lax.ppermute(plane, "co", ring(2, 1))
-    other_sibling = lax.ppermute(other_plane, "co", ring(2, 1))
-    weights = [plane, other_plane, sibling, other_sibling]
-
-    tail = last_rows(own_row)
-    halo = 0
-    for to in range(2):
-        pairs = [(2 * z + 1, 2 * z + 2 + to) for z in range(NZ - 1)]
-        halo = halo + lax.ppermute(tail, ("z", "yh"), pairs)
-
-    rates, residues, skip, _ = lax.optimization_barrier((rates, residues, skip, plane))
-    mine = jnp.concatenate(
-        [
-            rates.T.reshape(4, LANES),
-            residues.T.reshape(4, LANES),
-            jnp.pad(skip, (0, LANES - 32)).reshape(1, LANES),
-        ]
-    )
-    table = swap(spread(mine), "z")
-    rate_table = table[:, 0:4].reshape(NZ, POLES, 32).transpose(1, 0, 2).reshape(POLES, CH)
-    residue_table = table[:, 4:8].reshape(NZ, POLES, 32).transpose(1, 0, 2).reshape(POLES, CH)
-    skip_row = table[:, 8, :32].reshape(1, CH)
+    x, yh, z = lax.axis_index("x"), lax.axis_index("yh"), lax.axis_index("z")
+    together = lax.optimization_barrier
+
     taps = short_filter.reshape(3, 3, NZ, PIECES, 32)
     taps = lax.dynamic_index_in_dim(taps, yh * NX + x, 3, keepdims=False).reshape(3, COLS)
-
-    query, carried, chunk, state = project(own_row + partner_row, halo, weights, taps, rate_table)
-    states = swap(spread(state), "z")
-    gate, local = direct(query, carried, taps, rate_table, residue_table, skip_row)
-    pieces = finish(states, rate_table, residue_table, local, chunk, gate)
+    skips = jnp.pad(jnp.stack(coded(skip, 3)), ((0, TABLE - 3), (0, 0)))
+    mine = jnp.stack(coded(rates.T, 3) + coded(residues.T, 2) + [skips], axis=1)
+    mine = jnp.tile(mine, (1, 1, 4)).reshape(TABLE, COLS)
+    lane = jnp.arange(COLS)[None, :] % LANES
+    mine = jnp.where(lane // 32 == z % 4, mine, 0.0).astype(BF16)
+
+    blocks = in_weight.reshape(8, 3, NZ, PIECES, 32).transpose(3, 0, 1, 2, 4)
+    blocks = spread(blocks.reshape(PIECES, 8, COLS), 2).reshape(2 * PIECES, 8, COLS)
+    tokens, blocks = together((tokens, blocks))
+    unit = swap(blocks, ("yl", "yh", "x")).reshape(UNIT, COLS)
+    unit = jnp.concatenate([unit, mine])
+    own = normalise(tokens[0], norm_gain[None, :])
+    partner = shift(own, "yh", 1)
+    own_1, own_3 = shift(own, "x", 1), shift(own, "x", -1)
+
+    def step(up, down):
+        return shift(up, "z", 1), shift(down, "z", -1)
+
+    up_1, down_1 = step(unit, unit)
+    up_1, down_1, partner, own_1, own_3, taps = together(
+        (up_1, down_1, partner, own_1, own_3, taps)
+    )
+    mixed_1 = shift(jnp.concatenate([partner, own_1[:HALF]]), "x", 1)
+    mixed_3 = shift(jnp.concatenate([partner, own_3[HALF:]]), "x", -1)
+    up_2, down_2 = step(up_1, down_1)
+    up_3, down_3 = step(up_2, down_2)
+    up_3, down_3, mixed_1, mixed_3 = together((up_3, down_3, mixed_1, mixed_3))
+    first = shift(mixed_1[:HALF], "x", 1)
+    second = shift(mixed_3[HALF:HERE], "x", -1)
+    tail = last_rows((own, own_1, own_3, mixed_3))
+    halo = [
+        lax.ppermute(tail, ("z", "yh"), [(2 * i + 1, 2 * i + 2 + to) for i in range(NZ - 1)])
+        for to in range(2)
+    ]
+    near = jnp.stack([unit, up_1, up_2, up_3, down_3, down_2, down_1])
+    last = shift(up_3, "z", 1)
+    near_sibling = shift(near, "co", 1)
+    last, first, second, near_sibling, *halo = together((last, first, second, near_sibling, *halo))
+    weights = [near, last, near_sibling, shift(last, "co", 1)]
+    arrays = [own, own_1, own_3, partner, mixed_1, mixed_3, first, second]
+
+    query, carried, chunk, state, table = project(arrays, halo, weights, taps)
+    states = swap(state, "z")
+    gate, local = direct(query, carried, taps, table)
+    pieces = finish(states, table, local, chunk, gate)
     return place(swap(pieces, ("yh", "x")))
 
 

time: 149 us -> 125 us (0.84)
  blocking collectives: 55.7 us -> 15.5 us
  starting transfers between devices: 27.5 us -> 42.2 us
  local copies, waits for them, and re-layouts: 14.2 us -> 10.2 us
  Pallas kernels: 14.9 us -> 18.7 us
    all_to_all x2 -> x1, blocking collectives: 55.7 us -> 15.5 us  [swap(): return lax.all_to_all(value, axes, split_axis=0, concat_axis=0, tiled=True)]
    ppermute x12 -> x18, starting transfers between devices: 14.5 us -> 25.2 us  [the longest x16 23.9 us: shift(): return lax.ppermute(value, axis, ring(lax.axis_size(axis), by))]
    all_to_all x2, starting transfers between devices: 13 us -> 17 us  [swap(): return lax.all_to_all(value, axes, split_axis=0, concat_axis=0, tiled=True)]
    pallas_call x3, Pallas kernels: 13.4 us -> 17.1 us  [the longest x1 12.7 us: project(): pl.pallas_call(project_kernel, in_specs=[any_spec] * (PIECE_ARRAYS + 6) +...]
    unnamed x40 -> x61, local copies, waits for them, and re-layouts: 10.4 us -> 6.9 us
    ppermute x12 -> x18, waiting for transfers between devices: 21.8 us -> 23.8 us  [the longest x16 23.8 us: shift(): return lax.ppermute(value, axis, ring(lax.axis_size(axis), by))]
  transfers between devices with their start and end apart: 14 -> 20, of which waited for: 9 -> 8; matrix products, arithmetic and copies ran while one was open for 1% -> 1% of each run, Pallas kernels for 1% -> 1%
where the time goes in v5:
time: 125 us; the launch traced here: 124 us
  starting transfers between devices  42.2 us (34%)
  waiting for transfers between devices  36.9 us (30%)
  Pallas kernels  18.7 us (15%)
  blocking collectives  15.5 us (12%)
  local copies, waits for them, and re-layouts  10.2 us (8%)
    ppermute x16, starting transfers between devices, shift(): return lax.ppermute(value, axis, ring(lax.axis_size(axis), by))  23.9 us
    ppermute x16, waiting for transfers between devices, shift(): return lax.ppermute(value, axis, ring(lax.axis_size(axis), by))  23.8 us
    all_to_all x2, starting transfers between devices, swap(): return lax.all_to_all(value, axes, split_axis=0, concat_axis=0, tiled=True)  17 us
    all_to_all x1, blocking collectives, swap(): return lax.all_to_all(value, axes, split_axis=0, concat_axis=0, tiled=True)  15.5 us
    all_to_all x2, waiting for transfers between devices, swap(): return lax.all_to_all(value, axes, split_axis=0, concat_axis=0, tiled=True)  13.1 us
    pallas_call x1, Pallas kernels, project(): pl.pallas_call(project_kernel, in_specs=[any_spec] * (PIECE_ARRAYS + 6) +...  12.7 us
    unnamed x61, local copies, waits for them, and re-layouts  6.9 us
    pallas_call x1, Pallas kernels, finish(): pl.pallas_call(finish_kernel, in_specs=[vmem] * 5, out_specs=vmem, out_sh...  3.35 us
  transfers between devices with their start and end apart: 20, of which 8 were waited for; matrix products, arithmetic and copies ran while one was open for 1% of the time, Pallas kernels for 1%

profile of v5, /device:TPU:2, one launch (start us, length us, event | category | flops | bytes accessed | tf_op | source)
XLA Modules:
  0.0 124.4 jit_solution(564866599635420888)
XLA Ops:
  0.0 1.3 %reshape.74 = bf16[8,3,8,8,32]{4,3,2,1,0:T(8,128)(2,1)S(1)} reshape(bf16[8,6144]{1,0:T(8,128)(2,1)} %param.9) | data formatting | bytes 196608 | tf_op jit(solution)/shard_map/reshape | solution.py:447
  1.6 0.7 broadcast_in_dim.24
  2.9 2.3 %collective-permute-start.4 = (bf16[128,2048]{1,0:T(8,128)(2,1)S(1)}, bf16[128,2048]{1,0:T(8,128)(2,1)S(1)}, u32[]{:S(2)}, u32[]{:S(2)}) collective-permute-start(bf16[128,2048]{1,0:T(8,128)(2,1)S(1)} %shard_map.73.own.refs_0_), channel_id=1, source_target_pairs={{0,3},{1,0},{2,1},{3,2},{4,7},{5,4},{6,5},{7,6},{8,11},{9,8},{10,9... | collective-permute-start | bytes 1572872 | tf_op jit(solution)/shard_map/ppermute | solution.py:391
  5.3 2.9 %collective-permute-start.2 = (bf16[128,2048]{1,0:T(8,128)(2,1)S(1)}, bf16[128,2048]{1,0:T(8,128)(2,1)S(1)}, u32[]{:S(2)}, u32[]{:S(2)}) collective-permute-start(bf16[128,2048]{1,0:T(8,128)(2,1)S(1)} %shard_map.73.own.refs_0_), channel_id=1, source_target_pairs={{0,4},{4,0},{1,5},{5,1},{2,6},{6,2},{3,7},{7,3},{8,12},{12,8},{9,1... | collective-permute-start | bytes 1572872 | tf_op jit(solution)/shard_map/ppermute | solution.py:391
  8.2 6.3 %all-to-all-start = ((bf16[16,8,768]{2,1,0:T(8,128)(2,1)}), bf16[16,8,768]{2,1,0:T(8,128)(2,1)S(1)}, u32[]{:S(2)}, u32[]{:S(2)}) async-start(bf16[16,8,768]{2,1,0:T(8,128)(2,1)} %bitcast.1), calls=%async_computation | async-start | bytes 393216 | tf_op jit(solution)/shard_map/all_to_all | solution.py:399
  14.8 7.7 %all-to-all-done = bf16[16,8,768]{2,1,0:T(8,128)(2,1)S(1)} async-done(((bf16[16,8,768]{2,1,0:T(8,128)(2,1)}), bf16[16,8,768]{2,1,0:T(8,128)(2,1)S(1)}, u32[]{:S(2)}, u32[]{:S(2)}) %all-to-all-start) | async-done | bytes 196640 | tf_op jit(solution)/shard_map/all_to_all | solution.py:399
  22.5 5.9 %collective-permute-start.1 = (bf16[144,768]{1,0:T(8,128)(2,1)S(1)}, bf16[144,768]{1,0:T(8,128)(2,1)S(1)}, u32[]{:S(2)}, u32[]{:S(2)}) collective-permute-start(bf16[144,768]{1,0:T(8,128)(2,1)S(1)} %pad_maximum_fusion.2), channel_id=1, source_target_pairs={{0,56},{8,0},{16,8},{24,16},{32,24},{40,32},{48,40},{56,48},{1,57}... | collective-permute-start | bytes 663560 | tf_op jit(solution)/shard_map/ppermute | solution.py:391
  28.7 0.7 reshape.78.refs_14_.taps
  29.3 2.8 %collective-permute-done.1 = bf16[144,768]{1,0:T(8,128)(2,1)S(1)} collective-permute-done((bf16[144,768]{1,0:T(8,128)(2,1)S(1)}, bf16[144,768]{1,0:T(8,128)(2,1)S(1)}, u32[]{:S(2)}, u32[]{:S(2)}) %collective-permute-start.1) | collective-permute-done | bytes 221216 | tf_op jit(solution)/shard_map/ppermute | solution.py:391
  32.2 3.5 %collective-permute-done = bf16[144,768]{1,0:T(8,128)(2,1)S(1)} collective-permute-done((bf16[144,768]{1,0:T(8,128)(2,1)S(1)}, bf16[144,768]{1,0:T(8,128)(2,1)S(1)}, u32[]{:S(2)}, u32[]{:S(2)}) %collective-permute-start) | collective-permute-done | bytes 221216 | tf_op jit(solution)/shard_map/ppermute | solution.py:391
  37.1 3.0 %collective-permute-start.10 = (bf16[192,2048]{1,0:T(8,128)(2,1)S(1)}, bf16[192,2048]{1,0:T(8,128)(2,1)S(1)}, u32[]{:S(2)}, u32[]{:S(2)}) collective-permute-start(bf16[192,2048]{1,0:T(8,128)(2,1)S(1)} %get-tuple-element.55), channel_id=1, source_target_pairs={{0,3},{1,0},{2,1},{3,2},{4,7},{5,4},{6,5},{7,6},{8,11},{9,8},{10,9... | collective-permute-start | bytes 2359304 | tf_op jit(solution)/shard_map/ppermute | solution.py:391
  40.2 3.2 %collective-permute-start.7 = (bf16[144,768]{1,0:T(8,128)(2,1)S(1)}, bf16[144,768]{1,0:T(8,128)(2,1)S(1)}, u32[]{:S(2)}, u32[]{:S(2)}) collective-permute-start(bf16[144,768]{1,0:T(8,128)(2,1)S(1)} %collective-permute-done.1), channel_id=1, source_target_pairs={{0,56},{8,0},{16,8},{24,16},{32,24},{40,32},{48,40},{56,48},{1,57}... | collective-permute-start | bytes 663560 | tf_op jit(solution)/shard_map/ppermute | solution.py:391
  43.5 5.2 %collective-permute-done.5 = bf16[144,768]{1,0:T(8,128)(2,1)S(1)} collective-permute-done((bf16[144,768]{1,0:T(8,128)(2,1)S(1)}, bf16[144,768]{1,0:T(8,128)(2,1)S(1)}, u32[]{:S(2)}, u32[]{:S(2)}) %collective-permute-start.5) | collective-permute-done | bytes 221216 | tf_op jit(solution)/shard_map/ppermute | solution.py:391
  48.7 3.5 %collective-permute-start.8 = (bf16[144,768]{1,0:T(8,128)(2,1)S(1)}, bf16[144,768]{1,0:T(8,128)(2,1)S(1)}, u32[]{:S(2)}, u32[]{:S(2)}) collective-permute-start(bf16[144,768]{1,0:T(8,128)(2,1)S(1)} %collective-permute-done.7), channel_id=1, source_target_pairs={{0,56},{8,0},{16,8},{24,16},{32,24},{40,32},{48,40},{56,48},{1,57}... | collective-permute-start | bytes 663560 | tf_op jit(solution)/shard_map/ppermute | solution.py:391
  52.3 3.6 %collective-permute-done.6 = bf16[144,768]{1,0:T(8,128)(2,1)S(1)} collective-permute-done((bf16[144,768]{1,0:T(8,128)(2,1)S(1)}, bf16[144,768]{1,0:T(8,128)(2,1)S(1)}, u32[]{:S(2)}, u32[]{:S(2)}) %collective-permute-start.6) | collective-permute-done | bytes 221216 | tf_op jit(solution)/shard_map/ppermute | solution.py:391
  56.1 2.7 %collective-permute-start.13 = (bf16[64,2048]{1,0:T(8,128)(2,1)S(1)}, bf16[64,2048]{1,0:T(8,128)(2,1)S(1)}, u32[]{:S(2)}, u32[]{:S(2)}) collective-permute-start(bf16[64,2048]{1,0:T(8,128)(2,1)S(1)} %slice.15), channel_id=1, source_target_pairs={{0,3},{1,0},{2,1},{3,2},{4,7},{5,4},{6,5},{7,6},{8,11},{9,8},{10,9... | collective-permute-start | bytes 786440 | tf_op jit(solution)/shard_map/ppermute | solution.py:391
  59.1 0.7 collective-permute-start.16
  60.4 7.2 %collective-permute-done.11.refs_11_ = bf16[144,768]{1,0:T(8,128)(2,1)S(1)} collective-permute-done((bf16[144,768]{1,0:T(8,128)(2,1)S(1)}, bf16[144,768]{1,0:T(8,128)(2,1)S(1)}, u32[]{:S(2)}, u32[]{:S(2)}) %collective-permute-start.11) | collective-permute-done | bytes 221216 | tf_op jit(solution)/shard_map/ppermute | solution.py:391
  67.7 1.2 copy-done.21
  68.8 1.5 %collective-permute-done.17.refs_13_ = bf16[144,768]{1,0:T(8,128)(2,1)S(1)} collective-permute-done((bf16[144,768]{1,0:T(8,128)(2,1)S(1)}, bf16[144,768]{1,0:T(8,128)(2,1)S(1)}, u32[]{:S(2)}, u32[]{:S(2)}) %collective-permute-start.17) | collective-permute-done | bytes 221216 | tf_op jit(solution)/shard_map/ppermute | solution.py:391
  70.3 0.7 copy-done.25
  71.0 12.7 %shard_map.75 = (bf16[1040,256]{1,0:T(8,128)(2,1)}, bf16[1024,256]{1,0:T(8,128)(2,1)}, f32[16,64,256]{2,1,0:T(8,128)}, f32[8,16,256]{2,1,0:T(8,128)}, f32[40,256]{1,0:T(8,128)}) custom-call(bf16[128,2048]{1,0:T(8,128)(2,1)} %copy-done, bf16[128,2048]{1,0:T(8,128)(2,1)} %copy-done.3, bf16[128,2048]{1,0:T(8,128)(2,1)} %copy-done.2, ...), custom_call_target="tpu_custom_call" | custom-call | flops 3271557120 | bytes 10000000 | tf_op jit(solution)/shard_map/pallas_call | solution.py:225
  83.8 10.7 %all-to-all-start.1 = ((f32[8,16,256]{2,1,0:T(8,128)}), f32[8,16,256]{2,1,0:T(8,128)S(1)}, u32[]{:S(2)}, u32[]{:S(2)}) async-start(f32[8,16,256]{2,1,0:T(8,128)} %get-tuple-element.48), calls=%async_computation.1 | async-start | bytes 262144 | tf_op jit(solution)/shard_map/all_to_all | solution.py:399
  94.5 1.0 copy-done.5
  95.6 1.0 copy-done.7
  96.6 0.8 copy-done.8
  97.4 1.1 shard_map.76
  98.5 5.4 %all-to-all-done.1.states = f32[8,16,256]{2,1,0:T(8,128)S(1)} async-done(((f32[8,16,256]{2,1,0:T(8,128)}), f32[8,16,256]{2,1,0:T(8,128)S(1)}, u32[]{:S(2)}, u32[]{:S(2)}) %all-to-all-start.1) | async-done | bytes 131104 | tf_op jit(solution)/shard_map/all_to_all | solution.py:399
  103.9 0.8 copy-done.9
  104.7 3.4 %shard_map.77 = bf16[8,256,128]{2,1,0:T(8,128)(2,1)S(1)} custom-call(f32[8,16,256]{2,1,0:T(8,128)S(1)} %all-to-all-done.1.states, f32[40,256]{1,0:T(8,128)S(1)} %copy-done.9, f32[1024,256]{1,0:T(8,128)S(1)} %get-tuple-element.52.local, f32[16,64,256]{2,1,0:T(8,128)S(1)} %copy-done.4, bf16[1024,256]{1,0:T(8,128)(2,1)S(1)} %get-tuple-element.54.gate), custom_call_target="tpu_custom_call" | custom-call | tf_op jit(solution)/shard_map/pallas_call | solution.py:355
  108.0 15.5 %all_to_all.15.pieces = bf16[8,256,128]{2,1,0:T(8,128)(2,1)S(1)} all-to-all(bf16[8,256,128]{2,1,0:T(8,128)(2,1)S(1)} %shard_map.77), channel_id=1, replica_groups=mesh['yl'=2,'co'=2,'z'=8,'yh'=2,'x'=4] {'yh','x'}, dimensions={0} | all-to-all | bytes 1048576 | tf_op jit(solution)/shard_map/all_to_all | solution.py:399
  123.5 0.8 shard_map.78
  (103 shorter events, 4.0 us)
Async XLA Ops:
  1.3 13.2 %copy-start.20 = (f32[32]{0:T(128)S(1)}, f32[32]{0:T(128)}, u32[]{:S(2)}) copy-start(f32[32]{0:T(128)} %param.13) | copy-start | bytes 388
  1.3 13.2 %copy-start.17 = (f32[32,16]{0,1:T(8,128)S(1)}, f32[32,16]{0,1:T(8,128)}, u32[]{:S(2)}) copy-start(f32[32,16]{0,1:T(8,128)} %param.11) | copy-start | bytes 6148
  1.3 13.3 %copy-start.18 = (f32[32,16]{0,1:T(8,128)S(1)}, f32[32,16]{0,1:T(8,128)}, u32[]{:S(2)}) copy-start(f32[32,16]{0,1:T(8,128)} %param.12) | copy-start | bytes 6148
  1.4 27.1 %copy-start.15 = (f32[3,6144]{1,0:T(4,128)S(1)}, f32[3,6144]{1,0:T(4,128)}, u32[]{:S(2)}) copy-start(f32[3,6144]{1,0:T(4,128)} %param.10) | copy-start | bytes 221188
  2.9 56.0 %copy-start = (bf16[128,2048]{1,0:T(8,128)(2,1)}, bf16[128,2048]{1,0:T(8,128)(2,1)S(1)}, u32[]{:S(2)}) copy-start(bf16[128,2048]{1,0:T(8,128)(2,1)S(1)} %shard_map.73.own.refs_0_) | copy-start | bytes 1572868
  2.9 32.7 %collective-permute-start.4 = (bf16[128,2048]{1,0:T(8,128)(2,1)S(1)}, bf16[128,2048]{1,0:T(8,128)(2,1)S(1)}, u32[]{:S(2)}, u32[]{:S(2)}) collective-permute-start(bf16[128,2048]{1,0:T(8,128)(2,1)S(1)} %shard_map.73.own.refs_0_), channel_id=1, source_target_pairs={{0,3},{1,0},{2,1},{3,2},{4,7},{5,4},{6,5},{7,6},{8,11},{9,8},{10,9... | collective-permute-start | bytes 1572872 | tf_op jit(solution)/shard_map/ppermute | solution.py:391
  5.2 30.4 %collective-permute-start.3 = (bf16[128,2048]{1,0:T(8,128)(2,1)S(1)}, bf16[128,2048]{1,0:T(8,128)(2,1)S(1)}, u32[]{:S(2)}, u32[]{:S(2)}) collective-permute-start(bf16[128,2048]{1,0:T(8,128)(2,1)S(1)} %shard_map.73.own.refs_0_), channel_id=1, source_target_pairs={{0,1},{1,2},{2,3},{3,0},{4,5},{5,6},{6,7},{7,4},{8,9},{9,10},{10,1... | collective-permute-start | bytes 1572872 | tf_op jit(solution)/shard_map/ppermute | solution.py:391
  5.3 30.4 %collective-permute-start.2 = (bf16[128,2048]{1,0:T(8,128)(2,1)S(1)}, bf16[128,2048]{1,0:T(8,128)(2,1)S(1)}, u32[]{:S(2)}, u32[]{:S(2)}) collective-permute-start(bf16[128,2048]{1,0:T(8,128)(2,1)S(1)} %shard_map.73.own.refs_0_), channel_id=1, source_target_pairs={{0,4},{4,0},{1,5},{5,1},{2,6},{6,2},{3,7},{7,3},{8,12},{12,8},{9,1... | collective-permute-start | bytes 1572872 | tf_op jit(solution)/shard_map/ppermute | solution.py:391
  8.2 14.3 %all-to-all-start = ((bf16[16,8,768]{2,1,0:T(8,128)(2,1)}), bf16[16,8,768]{2,1,0:T(8,128)(2,1)S(1)}, u32[]{:S(2)}, u32[]{:S(2)}) async-start(bf16[16,8,768]{2,1,0:T(8,128)(2,1)} %bitcast.1), calls=%async_computation | async-start | bytes 393216 | tf_op jit(solution)/shard_map/all_to_all | solution.py:399
  22.5 9.6 %collective-permute-start.1 = (bf16[144,768]{1,0:T(8,128)(2,1)S(1)}, bf16[144,768]{1,0:T(8,128)(2,1)S(1)}, u32[]{:S(2)}, u32[]{:S(2)}) collective-permute-start(bf16[144,768]{1,0:T(8,128)(2,1)S(1)} %pad_maximum_fusion.2), channel_id=1, source_target_pairs={{0,56},{8,0},{16,8},{24,16},{32,24},{40,32},{48,40},{56,48},{1,57}... | collective-permute-start | bytes 663560 | tf_op jit(solution)/shard_map/ppermute | solution.py:391
  28.5 7.1 %collective-permute-start = (bf16[144,768]{1,0:T(8,128)(2,1)S(1)}, bf16[144,768]{1,0:T(8,128)(2,1)S(1)}, u32[]{:S(2)}, u32[]{:S(2)}) collective-permute-start(bf16[144,768]{1,0:T(8,128)(2,1)S(1)} %pad_maximum_fusion.2), channel_id=1, source_target_pairs={{0,8},{8,16},{16,24},{24,32},{32,40},{40,48},{48,56},{56,0},{1,9},... | collective-permute-start | bytes 663560 | tf_op jit(solution)/shard_map/ppermute | solution.py:391
  35.6 23.3 %copy-start.2 = (bf16[128,2048]{1,0:T(8,128)(2,1)}, bf16[128,2048]{1,0:T(8,128)(2,1)S(1)}, u32[]{:S(2)}) copy-start(bf16[128,2048]{1,0:T(8,128)(2,1)S(1)} %collective-permute-done.4.ahead.refs_2_) | copy-start | bytes 1572868
  35.6 23.3 %copy-start.3 = (bf16[128,2048]{1,0:T(8,128)(2,1)}, bf16[128,2048]{1,0:T(8,128)(2,1)S(1)}, u32[]{:S(2)}) copy-start(bf16[128,2048]{1,0:T(8,128)(2,1)S(1)} %collective-permute-done.3.behind.refs_1_) | copy-start | bytes 1572868
  36.3 3.8 %copy-start.14 = (bf16[144,768]{1,0:T(8,128)(2,1)S(1)}, bf16[144,768]{1,0:T(8,128)(2,1)}, u32[]{:S(2)}) copy-start(bf16[144,768]{1,0:T(8,128)(2,1)} %copy-done.13) | copy-start | bytes 663556
  37.1 18.7 %collective-permute-start.10 = (bf16[192,2048]{1,0:T(8,128)(2,1)S(1)}, bf16[192,2048]{1,0:T(8,128)(2,1)S(1)}, u32[]{:S(2)}, u32[]{:S(2)}) collective-permute-start(bf16[192,2048]{1,0:T(8,128)(2,1)S(1)} %get-tuple-element.55), channel_id=1, source_target_pairs={{0,3},{1,0},{2,1},{3,2},{4,7},{5,4},{6,5},{7,6},{8,11},{9,8},{10,9... | collective-permute-start | bytes 2359304 | tf_op jit(solution)/shard_map/ppermute | solution.py:391
  40.1 15.8 %collective-permute-start.9 = (bf16[192,2048]{1,0:T(8,128)(2,1)S(1)}, bf16[192,2048]{1,0:T(8,128)(2,1)S(1)}, u32[]{:S(2)}, u32[]{:S(2)}) collective-permute-start(bf16[192,2048]{1,0:T(8,128)(2,1)S(1)} %get-tuple-element.56), channel_id=1, source_target_pairs={{0,1},{1,2},{2,3},{3,0},{4,5},{5,6},{6,7},{7,4},{8,9},{9,10},{10,1... | collective-permute-start | bytes 2359304 | tf_op jit(solution)/shard_map/ppermute | solution.py:391
  40.1 8.6 %collective-permute-start.5 = (bf16[144,768]{1,0:T(8,128)(2,1)S(1)}, bf16[144,768]{1,0:T(8,128)(2,1)S(1)}, u32[]{:S(2)}, u32[]{:S(2)}) collective-permute-start(bf16[144,768]{1,0:T(8,128)(2,1)S(1)} %copy-done.14), channel_id=1, source_target_pairs={{0,8},{8,16},{16,24},{24,32},{32,40},{40,48},{48,56},{56,0},{1,9},... | collective-permute-start | bytes 663560 | tf_op jit(solution)/shard_map/ppermute | solution.py:391
  40.2 8.5 %collective-permute-start.7 = (bf16[144,768]{1,0:T(8,128)(2,1)S(1)}, bf16[144,768]{1,0:T(8,128)(2,1)S(1)}, u32[]{:S(2)}, u32[]{:S(2)}) collective-permute-start(bf16[144,768]{1,0:T(8,128)(2,1)S(1)} %collective-permute-done.1), channel_id=1, source_target_pairs={{0,56},{8,0},{16,8},{24,16},{32,24},{40,32},{48,40},{56,48},{1,57}... | collective-permute-start | bytes 663560 | tf_op jit(solution)/shard_map/ppermute | solution.py:391
  48.7 7.1 %collective-permute-start.6 = (bf16[144,768]{1,0:T(8,128)(2,1)S(1)}, bf16[144,768]{1,0:T(8,128)(2,1)S(1)}, u32[]{:S(2)}, u32[]{:S(2)}) collective-permute-start(bf16[144,768]{1,0:T(8,128)(2,1)S(1)} %collective-permute-done.5), channel_id=1, source_target_pairs={{0,8},{8,16},{16,24},{24,32},{32,40},{40,48},{48,56},{56,0},{1,9},... | collective-permute-start | bytes 663560 | tf_op jit(solution)/shard_map/ppermute | solution.py:391
  48.7 7.1 %collective-permute-start.8 = (bf16[144,768]{1,0:T(8,128)(2,1)S(1)}, bf16[144,768]{1,0:T(8,128)(2,1)S(1)}, u32[]{:S(2)}, u32[]{:S(2)}) collective-permute-start(bf16[144,768]{1,0:T(8,128)(2,1)S(1)} %collective-permute-done.7), channel_id=1, source_target_pairs={{0,56},{8,0},{16,8},{24,16},{32,24},{40,32},{48,40},{56,48},{1,57}... | collective-permute-start | bytes 663560 | tf_op jit(solution)/shard_map/ppermute | solution.py:391
  56.0 11.7 %collective-permute-start.14 = (bf16[7,144,768]{2,1,0:T(8,128)(2,1)S(1)}, bf16[7,144,768]{2,1,0:T(8,128)(2,1)S(1)}, u32[]{:S(2)}, u32[]{:S(2)}) collective-permute-start(bf16[7,144,768]{2,1,0:T(8,128)(2,1)S(1)} %bitcast_dynamic-update-slice_fusion.refs_10_), channel_id=1, source_target_pairs={{0,64},{64,0},{1,65},{65,1},{2,66},{66,2},{3,67},{67,3},{4,68},{68... | collective-permute-start | bytes 4644872 | tf_op jit(solution)/shard_map/ppermute | solution.py:391
  56.1 11.5 %collective-permute-start.13 = (bf16[64,2048]{1,0:T(8,128)(2,1)S(1)}, bf16[64,2048]{1,0:T(8,128)(2,1)S(1)}, u32[]{:S(2)}, u32[]{:S(2)}) collective-permute-start(bf16[64,2048]{1,0:T(8,128)(2,1)S(1)} %slice.15), channel_id=1, source_target_pairs={{0,3},{1,0},{2,1},{3,2},{4,7},{5,4},{6,5},{7,6},{8,11},{9,8},{10,9... | collective-permute-start | bytes 786440 | tf_op jit(solution)/shard_map/ppermute | solution.py:391
  58.9 8.8 %collective-permute-start.12 = (bf16[64,2048]{1,0:T(8,128)(2,1)S(1)}, bf16[64,2048]{1,0:T(8,128)(2,1)S(1)}, u32[]{:S(2)}, u32[]{:S(2)}) collective-permute-start(bf16[64,2048]{1,0:T(8,128)(2,1)S(1)} %slice.14), channel_id=1, source_target_pairs={{0,1},{1,2},{2,3},{3,0},{4,5},{5,6},{6,7},{7,4},{8,9},{9,10},{10,1... | collective-permute-start | bytes 786440 | tf_op jit(solution)/shard_map/ppermute | solution.py:391
  58.9 8.8 %collective-permute-start.11 = (bf16[144,768]{1,0:T(8,128)(2,1)S(1)}, bf16[144,768]{1,0:T(8,128)(2,1)S(1)}, u32[]{:S(2)}, u32[]{:S(2)}) collective-permute-start(bf16[144,768]{1,0:T(8,128)(2,1)S(1)} %collective-permute-done.6), channel_id=1, source_target_pairs={{0,8},{8,16},{16,24},{24,32},{32,40},{40,48},{48,56},{56,0},{1,9},... | collective-permute-start | bytes 663560 | tf_op jit(solution)/shard_map/ppermute | solution.py:391
  59.0 35.5 %copy-start.10 = (f32[3,768]{1,0:T(4,128)S(1)}, f32[3,768]{1,0:T(4,128)}, u32[]{:S(2)}) copy-start(f32[3,768]{1,0:T(4,128)} %reshape.78.refs_14_.taps) | copy-start | bytes 27652
  59.1 0.7 collective-permute-start.16
  59.7 10.6 %copy-start.26 = (bf16[16,2048]{1,0:T(8,128)(2,1)}, bf16[16,2048]{1,0:T(8,128)(2,1)S(1)}, u32[]{:S(2)}) copy-start(bf16[16,2048]{1,0:T(8,128)(2,1)S(1)} %collective-permute-done.16.refs_9_) | copy-start | bytes 196612
  59.8 0.7 collective-permute-start.15
  60.4 9.9 %copy-start.27 = (bf16[16,2048]{1,0:T(8,128)(2,1)}, bf16[16,2048]{1,0:T(8,128)(2,1)S(1)}, u32[]{:S(2)}) copy-start(bf16[16,2048]{1,0:T(8,128)(2,1)S(1)} %collective-permute-done.15.refs_8_) | copy-start | bytes 196612
  68.8 1.5 %collective-permute-start.17 = (bf16[144,768]{1,0:T(8,128)(2,1)S(1)}, bf16[144,768]{1,0:T(8,128)(2,1)S(1)}, u32[]{:S(2)}, u32[]{:S(2)}) collective-permute-start(bf16[144,768]{1,0:T(8,128)(2,1)S(1)} %collective-permute-done.11.refs_11_), channel_id=1, source_target_pairs={{0,64},{64,0},{1,65},{65,1},{2,66},{66,2},{3,67},{67,3},{4,68},{68... | collective-permute-start | bytes 663560 | tf_op jit(solution)/shard_map/ppermute | solution.py:391
  83.8 20.1 %copy-start.4 = (f32[16,64,256]{2,1,0:T(8,128)S(1)}, f32[16,64,256]{2,1,0:T(8,128)}, u32[]{:S(2)}) copy-start(f32[16,64,256]{2,1,0:T(8,128)} %get-tuple-element.53.chunk) | copy-start | bytes 3145732
  83.8 20.1 %all-to-all-start.1 = ((f32[8,16,256]{2,1,0:T(8,128)}), f32[8,16,256]{2,1,0:T(8,128)S(1)}, u32[]{:S(2)}, u32[]{:S(2)}) async-start(f32[8,16,256]{2,1,0:T(8,128)} %get-tuple-element.48), calls=%async_computation.1 | async-start | bytes 262144 | tf_op jit(solution)/shard_map/all_to_all | solution.py:399
  (16 other events, 29.2 us)

commit v6 on v5

--- a/solution.py
+++ b/solution.py
@@ -21,7 +21,7 @@
 ROWS = HALO + SPAN
 D = 2048
 UNIT = 128
-NEAR = (0, 1, 2, 3, 5, 6, 7)
+PLACES = (0, 1, 2, 3, 4, 5, 6, 7)
 TABLE = 16
 COLS = 3 * CH
 MIB = 1024 * 1024
@@ -104,32 +104,35 @@
 PIECE_ARRAYS = 8
 
 
-def copy_rows(copy, arrays, halo, lhs):
+def place_rows(arrays, halo, lhs):
     x, yh = lax.axis_index("x"), lax.axis_index("yh")
-    copy.one_of(yh, halo, lhs.at[pl.ds(0, HALO)])
+    for i, source in enumerate(halo):
+
+        @pl.when(yh == i)
+        def _(source=source):
+            lhs[0:HALO, :] = source[...]
+
     for other, by, first, rows, array, at in PIECE_LIST:
         place = lax.rem(yh + other, 2) * NX + lax.rem(x + NX - by, NX)
         row = pl.multiple_of(HALO + place * HERE + first, 16)
-        copy(arrays[array].at[pl.ds(at, rows)], lhs.at[pl.ds(row, rows)])
-
-
-def copy_weights(copy, planes, w):
+        lhs[pl.ds(row, rows), :] = arrays[array][at : at + rows, :]
+
+
+def place_weights(planes, w):
     z, core = lax.axis_index("z"), lax.axis_index("co")
-    for r in range(2):
-        most, last = planes[2 * r], planes[2 * r + 1]
-        for i, d in enumerate(NEAR + (NZ // 2,)):
-            place = last if d == NZ // 2 else most.at[i]
+    for r, plane in enumerate(planes):
+        for i, d in enumerate(PLACES):
             row = lax.rem(core + r, 2) * 512 + lax.rem(z + NZ - d, NZ) * 64
             for yl in range(2):
                 to = pl.ds(pl.multiple_of(yl * 1024 + row, 64), 64)
-                copy(place.at[pl.ds(yl * 64, 64)], w.at[to])
-
-
-def decode(blocks, out):
+                w[to, :] = plane[i, yl * 64 : yl * 64 + 64, :]
+
+
+def decode(plane, out):
     z = lax.axis_index("z")
     halves = [jnp.zeros((TABLE, COLS), F32)] * 2
-    for i, d in enumerate(NEAR + (NZ // 2,)):
-        block = blocks[i].astype(F32)
+    for i, d in enumerate(PLACES):
+        block = plane[i, UNIT:, :].astype(F32)
         low = lax.rem(z + NZ - d, NZ) < NZ // 2
         halves[0] = halves[0] + jnp.where(low, block, 0.0)
         halves[1] = halves[1] + jnp.where(low, 0.0, block)
@@ -146,16 +149,12 @@
     *refs,
 ):
     arrays, refs = refs[:PIECE_ARRAYS], refs[PIECE_ARRAYS:]
-    halo, planes, refs = refs[:2], refs[2:6], refs[6:]
+    halo, planes, refs = refs[:2], refs[2:4], refs[4:]
     taps, query_ref, carried_ref, chunk_ref, state_ref, rates = refs[:6]
-    lhs, w, proj, blocks, decay_s, carry, sems = refs[6:]
-    copy = Copier(sems)
-    copy_weights(copy, planes, w)
-    copy(planes[0].at[:, pl.ds(UNIT, TABLE)], blocks.at[pl.ds(0, NZ - 1)])
-    copy(planes[1].at[pl.ds(UNIT, TABLE)], blocks.at[NZ - 1])
-    copy_rows(copy, arrays, halo, lhs)
-    copy.wait()
-    decode(blocks, rates)
+    lhs, w, proj, decay_s, carry = refs[6:]
+    place_weights(planes, w)
+    place_rows(arrays, halo, lhs)
+    decode(planes[0], rates)
     decay_s[...] = jnp.exp(-rates[0:16, :])
     for s in (1, 2, 0):
         cols = slice(s * CH, (s + 1) * CH)
@@ -220,11 +219,10 @@
 
 
 def project(arrays, halo, weights, taps):
-    any_spec = pl.BlockSpec(memory_space=pl.ANY)
     vmem = pl.BlockSpec(memory_space=pltpu.VMEM)
     return pl.pallas_call(
         project_kernel,
-        in_specs=[any_spec] * (PIECE_ARRAYS + 6) + [vmem],
+        in_specs=[vmem] * (PIECE_ARRAYS + 5),
         out_specs=[vmem] * 5,
         out_shape=[
             jax.ShapeDtypeStruct((ROWS, CH), BF16),
@@ -237,12 +235,10 @@
             pltpu.VMEM((ROWS, D), BF16),
             pltpu.VMEM((D, COLS), BF16),
             pltpu.VMEM((ROWS, 2 * CH), F32),
-            pltpu.VMEM((NZ, TABLE, COLS), BF16),
             pltpu.VMEM((POLES, CH), F32),
             pltpu.VMEM((POLES, 8, LANES), F32),
-            pltpu.SemaphoreType.DMA((len(PIECE_LIST) + 35,)),
         ],
-        compiler_params=params(60),
+        compiler_params=params(36),
         cost_estimate=pl.CostEstimate(
             flops=2 * ROWS * D * COLS, bytes_accessed=10_000_000, transcendentals=0
         ),
@@ -446,25 +442,26 @@
 
     blocks = in_weight.reshape(8, 3, NZ, PIECES, 32).transpose(3, 0, 1, 2, 4)
     blocks = spread(blocks.reshape(PIECES, 8, COLS), 2).reshape(2 * PIECES, 8, COLS)
-    tokens, blocks = together((tokens, blocks))
     unit = swap(blocks, ("yl", "yh", "x")).reshape(UNIT, COLS)
     unit = jnp.concatenate([unit, mine])
     own = normalise(tokens[0], norm_gain[None, :])
+    own, unit, taps = together((own, unit, taps))
+
+    def step(up, down):
+        return shift(up, "z", 1), shift(down, "z", -1)
+
     partner = shift(own, "yh", 1)
     own_1, own_3 = shift(own, "x", 1), shift(own, "x", -1)
-
-    def step(up, down):
-        return shift(up, "z", 1), shift(down, "z", -1)
-
     up_1, down_1 = step(unit, unit)
-    up_1, down_1, partner, own_1, own_3, taps = together(
-        (up_1, down_1, partner, own_1, own_3, taps)
-    )
+    up_1, down_1, partner, own_1, own_3 = together((up_1, down_1, partner, own_1, own_3))
+
     mixed_1 = shift(jnp.concatenate([partner, own_1[:HALF]]), "x", 1)
     mixed_3 = shift(jnp.concatenate([partner, own_3[HALF:]]), "x", -1)
     up_2, down_2 = step(up_1, down_1)
     up_3, down_3 = step(up_2, down_2)
-    up_3, down_3, mixed_1, mixed_3 = together((up_3, down_3, mixed_1, mixed_3))
+    up_4 = shift(up_3, "z", 1)
+    up_4, mixed_1, mixed_3 = together((up_4, mixed_1, mixed_3))
+
     first = shift(mixed_1[:HALF], "x", 1)
     second = shift(mixed_3[HALF:HERE], "x", -1)
     tail = last_rows((own, own_1, own_3, mixed_3))
@@ -472,11 +469,8 @@
         lax.ppermute(tail, ("z", "yh"), [(2 * i + 1, 2 * i + 2 + to) for i in range(NZ - 1)])
         for to in range(2)
     ]
-    near = jnp.stack([unit, up_1, up_2, up_3, down_3, down_2, down_1])
-    last = shift(up_3, "z", 1)
-    near_sibling = shift(near, "co", 1)
-    last, first, second, near_sibling, *halo = together((last, first, second, near_sibling, *halo))
-    weights = [near, last, near_sibling, shift(last, "co", 1)]
+    plane = jnp.stack([unit, up_1, up_2, up_3, up_4, down_3, down_2, down_1])
+    weights = [plane, shift(plane, "co", 1)]
     arrays = [own, own_1, own_3, partner, mixed_1, mixed_3, first, second]
 
     query, carried, chunk, state, table = project(arrays, halo, weights, taps)

time: 125 us -> 118 us (0.944)
  waiting for transfers between devices: 36.9 us -> 44.3 us
  local copies, waits for them, and re-layouts: 10.2 us -> 4.74 us
  Pallas kernels: 18.7 us -> 14 us
  starting transfers between devices: 42.2 us -> 38.8 us
    ppermute x16 -> x15, waiting for transfers between devices: 23.8 us -> 31.6 us  [shift(): return lax.ppermute(value, axis, ring(lax.axis_size(axis), by))]
    unnamed x61 -> x23, local copies, waits for them, and re-layouts: 6.9 us -> 1.96 us
    pallas_call x1, Pallas kernels: 12.7 us -> 8.07 us  [project(): pl.pallas_call(project_kernel, in_specs=[vmem] * (PIECE_ARRAYS + 5), out_...]
    all_to_all x2, starting transfers between devices: 17 us -> 14.9 us  [swap(): return lax.all_to_all(value, axes, split_axis=0, concat_axis=0, tiled=True)]
    ppermute x16 -> x15, starting transfers between devices: 23.9 us -> 22.5 us  [shift(): return lax.ppermute(value, axis, ring(lax.axis_size(axis), by))]
  transfers between devices with their start and end apart: 20 -> 19, of which waited for: 8 -> 9; matrix products, arithmetic and copies ran while one was open for 1% -> 1% of each run, Pallas kernels for 1% -> 1%
where the time goes in v6:
time: 118 us
  waiting for transfers between devices  44.3 us (38%)
  starting transfers between devices  38.8 us (33%)
  blocking collectives  15.4 us (13%)
  Pallas kernels  14 us (12%)
  local copies, waits for them, and re-layouts  4.74 us (4%)
    ppermute x15, waiting for transfers between devices, shift(): return lax.ppermute(value, axis, ring(lax.axis_size(axis), by))  31.6 us
    ppermute x15, starting transfers between devices, shift(): return lax.ppermute(value, axis, ring(lax.axis_size(axis), by))  22.5 us
    all_to_all x1, blocking collectives, swap(): return lax.all_to_all(value, axes, split_axis=0, concat_axis=0, tiled=True)  15.4 us
    all_to_all x2, starting transfers between devices, swap(): return lax.all_to_all(value, axes, split_axis=0, concat_axis=0, tiled=True)  14.9 us
    all_to_all x2, waiting for transfers between devices, swap(): return lax.all_to_all(value, axes, split_axis=0, concat_axis=0, tiled=True)  12.7 us
    pallas_call x1, Pallas kernels, project(): pl.pallas_call(project_kernel, in_specs=[vmem] * (PIECE_ARRAYS + 5), out_...  8.07 us
    pallas_call x1, Pallas kernels, finish(): pl.pallas_call(finish_kernel, in_specs=[vmem] * 5, out_specs=vmem, out_sh...  3.41 us
  transfers between devices with their start and end apart: 19, of which 9 were waited for; matrix products, arithmetic and copies ran while one was open for 1% of the time, Pallas kernels for 1%

profile of v6, /device:TPU:2, one launch (start us, length us, event | category | flops | bytes accessed | tf_op | source)
XLA Modules:
  0.0 117.8 jit_solution(3151626221450392966)
XLA Ops:
  0.0 1.3 %reshape.74 = bf16[8,3,8,8,32]{4,3,2,1,0:T(8,128)(2,1)S(1)} reshape(bf16[8,6144]{1,0:T(8,128)(2,1)} %param.9) | data formatting | bytes 196608 | tf_op jit(solution)/shard_map/reshape | solution.py:443
  1.6 0.7 broadcast_in_dim.25
  2.3 7.5 %all-to-all-start = ((bf16[16,8,768]{2,1,0:T(8,128)(2,1)}), bf16[16,8,768]{2,1,0:T(8,128)(2,1)S(1)}, u32[]{:S(2)}, u32[]{:S(2)}) async-start(bf16[16,8,768]{2,1,0:T(8,128)(2,1)} %bitcast.3), calls=%async_computation | async-start | bytes 393216 | tf_op jit(solution)/shard_map/all_to_all | solution.py:395
  10.4 0.6 shard_map.73.own.refs_0_
  11.0 5.8 %all-to-all-done = bf16[16,8,768]{2,1,0:T(8,128)(2,1)S(1)} async-done(((bf16[16,8,768]{2,1,0:T(8,128)(2,1)}), bf16[16,8,768]{2,1,0:T(8,128)(2,1)S(1)}, u32[]{:S(2)}, u32[]{:S(2)}) %all-to-all-start) | async-done | bytes 196640 | tf_op jit(solution)/shard_map/all_to_all | solution.py:395
  16.8 1.5 %collective-permute-start.4 = (bf16[128,2048]{1,0:T(8,128)(2,1)S(1)}, bf16[128,2048]{1,0:T(8,128)(2,1)S(1)}, u32[]{:S(2)}, u32[]{:S(2)}) collective-permute-start(bf16[128,2048]{1,0:T(8,128)(2,1)S(1)} %shard_map.73.own.refs_0_), channel_id=1, source_target_pairs={{0,3},{1,0},{2,1},{3,2},{4,7},{5,4},{6,5},{7,6},{8,11},{9,8},{10,9... | collective-permute-start | bytes 1572872 | tf_op jit(solution)/shard_map/ppermute | solution.py:387
  18.9 0.9 collective-permute-start.2
  19.8 5.9 %collective-permute-start.1 = (bf16[144,768]{1,0:T(8,128)(2,1)S(1)}, bf16[144,768]{1,0:T(8,128)(2,1)S(1)}, u32[]{:S(2)}, u32[]{:S(2)}) collective-permute-start(bf16[144,768]{1,0:T(8,128)(2,1)S(1)} %pad_maximum_fusion.2), channel_id=1, source_target_pairs={{0,56},{8,0},{16,8},{24,16},{32,24},{40,32},{48,40},{56,48},{1,57}... | collective-permute-start | bytes 663560 | tf_op jit(solution)/shard_map/ppermute | solution.py:387
  25.6 3.4 %collective-permute-done.1 = bf16[144,768]{1,0:T(8,128)(2,1)S(1)} collective-permute-done((bf16[144,768]{1,0:T(8,128)(2,1)S(1)}, bf16[144,768]{1,0:T(8,128)(2,1)S(1)}, u32[]{:S(2)}, u32[]{:S(2)}) %collective-permute-start.1) | collective-permute-done | bytes 221216 | tf_op jit(solution)/shard_map/ppermute | solution.py:387
  29.1 3.7 %collective-permute-done = bf16[144,768]{1,0:T(8,128)(2,1)S(1)} collective-permute-done((bf16[144,768]{1,0:T(8,128)(2,1)S(1)}, bf16[144,768]{1,0:T(8,128)(2,1)S(1)}, u32[]{:S(2)}, u32[]{:S(2)}) %collective-permute-start) | collective-permute-done | bytes 221216 | tf_op jit(solution)/shard_map/ppermute | solution.py:387
  33.0 1.5 %collective-permute-start.9 = (bf16[192,2048]{1,0:T(8,128)(2,1)S(1)}, bf16[192,2048]{1,0:T(8,128)(2,1)S(1)}, u32[]{:S(2)}, u32[]{:S(2)}) collective-permute-start(bf16[192,2048]{1,0:T(8,128)(2,1)S(1)} %get-tuple-element.41), channel_id=1, source_target_pairs={{0,3},{1,0},{2,1},{3,2},{4,7},{5,4},{6,5},{7,6},{8,11},{9,8},{10,9... | collective-permute-start | bytes 2359304 | tf_op jit(solution)/shard_map/ppermute | solution.py:387
  35.1 1.6 %collective-permute-start.5 = (bf16[144,768]{1,0:T(8,128)(2,1)S(1)}, bf16[144,768]{1,0:T(8,128)(2,1)S(1)}, u32[]{:S(2)}, u32[]{:S(2)}) collective-permute-start(bf16[144,768]{1,0:T(8,128)(2,1)S(1)} %collective-permute-done), channel_id=1, source_target_pairs={{0,8},{8,16},{16,24},{24,32},{32,40},{40,48},{48,56},{56,0},{1,9},... | collective-permute-start | bytes 663560 | tf_op jit(solution)/shard_map/ppermute | solution.py:387
  36.7 4.0 %collective-permute-start.14 = (bf16[144,768]{1,0:T(8,128)(2,1)S(1)}, bf16[144,768]{1,0:T(8,128)(2,1)S(1)}, u32[]{:S(2)}, u32[]{:S(2)}) collective-permute-start(bf16[144,768]{1,0:T(8,128)(2,1)S(1)} %collective-permute-done.1), channel_id=1, source_target_pairs={{0,56},{8,0},{16,8},{24,16},{32,24},{40,32},{48,40},{56,48},{1,57}... | collective-permute-start | bytes 663560 | tf_op jit(solution)/shard_map/ppermute | solution.py:387
  40.8 4.1 %collective-permute-done.5 = bf16[144,768]{1,0:T(8,128)(2,1)S(1)} collective-permute-done((bf16[144,768]{1,0:T(8,128)(2,1)S(1)}, bf16[144,768]{1,0:T(8,128)(2,1)S(1)}, u32[]{:S(2)}, u32[]{:S(2)}) %collective-permute-start.5) | collective-permute-done | bytes 221216 | tf_op jit(solution)/shard_map/ppermute | solution.py:387
  44.9 3.6 %collective-permute-start.15 = (bf16[144,768]{1,0:T(8,128)(2,1)S(1)}, bf16[144,768]{1,0:T(8,128)(2,1)S(1)}, u32[]{:S(2)}, u32[]{:S(2)}) collective-permute-start(bf16[144,768]{1,0:T(8,128)(2,1)S(1)} %collective-permute-done.14), channel_id=1, source_target_pairs={{0,56},{8,0},{16,8},{24,16},{32,24},{40,32},{48,40},{56,48},{1,57}... | collective-permute-start | bytes 663560 | tf_op jit(solution)/shard_map/ppermute | solution.py:387
  48.5 5.2 %collective-permute-done.6 = bf16[144,768]{1,0:T(8,128)(2,1)S(1)} collective-permute-done((bf16[144,768]{1,0:T(8,128)(2,1)S(1)}, bf16[144,768]{1,0:T(8,128)(2,1)S(1)}, u32[]{:S(2)}, u32[]{:S(2)}) %collective-permute-start.6) | collective-permute-done | bytes 221216 | tf_op jit(solution)/shard_map/ppermute | solution.py:387
  53.8 7.1 %collective-permute-done.7 = bf16[144,768]{1,0:T(8,128)(2,1)S(1)} collective-permute-done((bf16[144,768]{1,0:T(8,128)(2,1)S(1)}, bf16[144,768]{1,0:T(8,128)(2,1)S(1)}, u32[]{:S(2)}, u32[]{:S(2)}) %collective-permute-start.7) | collective-permute-done | bytes 221216 | tf_op jit(solution)/shard_map/ppermute | solution.py:387
  61.2 1.1 collective-permute-start.11
  62.3 1.2 %collective-permute-start.10 = (bf16[64,2048]{1,0:T(8,128)(2,1)S(1)}, bf16[64,2048]{1,0:T(8,128)(2,1)S(1)}, u32[]{:S(2)}, u32[]{:S(2)}) collective-permute-start(bf16[64,2048]{1,0:T(8,128)(2,1)S(1)} %slice.14), channel_id=1, source_target_pairs={{0,1},{1,2},{2,3},{3,0},{4,5},{5,6},{6,7},{7,4},{8,9},{9,10},{10,1... | collective-permute-start | bytes 786440 | tf_op jit(solution)/shard_map/ppermute | solution.py:387
  63.5 0.7 collective-permute-start.13
  64.2 0.7 collective-permute-start.12
  64.9 5.2 %collective-permute-done.11.refs_7_ = bf16[64,2048]{1,0:T(8,128)(2,1)S(1)} collective-permute-done((bf16[64,2048]{1,0:T(8,128)(2,1)S(1)}, bf16[64,2048]{1,0:T(8,128)(2,1)S(1)}, u32[]{:S(2)}, u32[]{:S(2)}) %collective-permute-start.11) | collective-permute-done | bytes 262176 | tf_op jit(solution)/shard_map/ppermute | solution.py:387
  70.1 2.7 %collective-permute-done.10.refs_6_ = bf16[64,2048]{1,0:T(8,128)(2,1)S(1)} collective-permute-done((bf16[64,2048]{1,0:T(8,128)(2,1)S(1)}, bf16[64,2048]{1,0:T(8,128)(2,1)S(1)}, u32[]{:S(2)}, u32[]{:S(2)}) %collective-permute-start.10) | collective-permute-done | bytes 262176 | tf_op jit(solution)/shard_map/ppermute | solution.py:387
  72.8 8.1 %shard_map.75 = (bf16[1040,256]{1,0:T(8,128)(2,1)S(1)}, bf16[1024,256]{1,0:T(8,128)(2,1)S(1)}, f32[16,64,256]{2,1,0:T(8,128)S(1)}, f32[8,16,256]{2,1,0:T(8,128)}, f32[40,256]{1,0:T(8,128)S(1)}) custom-call(bf16[128,2048]{1,0:T(8,128)(2,1)S(1)} %shard_map.73.own.refs_0_, bf16[128,2048]{1,0:T(8,128)(2,1)S(1)} %collective-permute-done.3.behind.refs_1_, ...), custom_call_target="tpu_custom_call" | custom-call | flops 3271557120 | bytes 10000000 | tf_op jit(solution)/shard_map/pallas_call | solution.py:223
  80.9 0.8 copy-done.1
  81.7 7.4 %all-to-all-start.1 = ((f32[8,16,256]{2,1,0:T(8,128)}), f32[8,16,256]{2,1,0:T(8,128)S(1)}, u32[]{:S(2)}, u32[]{:S(2)}) async-start(f32[8,16,256]{2,1,0:T(8,128)} %get-tuple-element.34), calls=%async_computation.1 | async-start | bytes 262144 | tf_op jit(solution)/shard_map/all_to_all | solution.py:395
  89.1 1.0 copy-done.2
  90.2 1.1 shard_map.76
  91.3 7.0 %all-to-all-done.1.states = f32[8,16,256]{2,1,0:T(8,128)S(1)} async-done(((f32[8,16,256]{2,1,0:T(8,128)}), f32[8,16,256]{2,1,0:T(8,128)S(1)}, u32[]{:S(2)}, u32[]{:S(2)}) %all-to-all-start.1) | async-done | bytes 131104 | tf_op jit(solution)/shard_map/all_to_all | solution.py:395
  98.2 3.4 %shard_map.77 = bf16[8,256,128]{2,1,0:T(8,128)(2,1)S(1)} custom-call(f32[8,16,256]{2,1,0:T(8,128)S(1)} %all-to-all-done.1.states, f32[40,256]{1,0:T(8,128)S(1)} %get-tuple-element.35.table, f32[1024,256]{1,0:T(8,128)S(1)} %get-tuple-element.38.local, f32[16,64,256]{2,1,0:T(8,128)S(1)} %get-tuple-element.39.chunk, bf16[1024,256]{1,0:T(8,128)(2,1)S(1)} %get-tuple-element.40.gate), custom_call_target="tpu_custom_call" | custom-call | tf_op jit(solution)/shard_map/pallas_call | solution.py:351
  101.6 15.4 %all_to_all.15.pieces = bf16[8,256,128]{2,1,0:T(8,128)(2,1)S(1)} all-to-all(bf16[8,256,128]{2,1,0:T(8,128)(2,1)S(1)} %shard_map.77), channel_id=1, replica_groups=mesh['yl'=2,'co'=2,'z'=8,'yh'=2,'x'=4] {'yh','x'}, dimensions={0} | all-to-all | bytes 1048576 | tf_op jit(solution)/shard_map/all_to_all | solution.py:395
  117.0 0.8 shard_map.78
  (62 shorter events, 2.6 us)
Async XLA Ops:
  0.0 9.8 %copy-start.7 = (f32[32]{0:T(128)S(1)}, f32[32]{0:T(128)}, u32[]{:S(2)}) copy-start(f32[32]{0:T(128)} %param.13) | copy-start | bytes 388
  0.0 9.8 %copy-start.5 = (f32[32,16]{0,1:T(8,128)S(1)}, f32[32,16]{0,1:T(8,128)}, u32[]{:S(2)}) copy-start(f32[32,16]{0,1:T(8,128)} %param.11) | copy-start | bytes 6148
  0.0 9.9 %copy-start.6 = (f32[32,16]{0,1:T(8,128)S(1)}, f32[32,16]{0,1:T(8,128)}, u32[]{:S(2)}) copy-start(f32[32,16]{0,1:T(8,128)} %param.12) | copy-start | bytes 6148
  0.0 10.1 %copy-start.4 = (f32[3,6144]{1,0:T(4,128)S(1)}, f32[3,6144]{1,0:T(4,128)}, u32[]{:S(2)}) copy-start(f32[3,6144]{1,0:T(4,128)} %param.10) | copy-start | bytes 221188
  0.0 10.4 %copy-start.3 = (f32[2048]{0:T(1024)S(1)}, f32[2048]{0:T(1024)}, u32[]{:S(2)}) copy-start(f32[2048]{0:T(1024)} %param.8) | copy-start | bytes 24580
  0.0 10.4 %copy-start = (bf16[1,128,2048]{2,1,0:T(8,128)(2,1)S(1)}, bf16[1,128,2048]{2,1,0:T(8,128)(2,1)}, u32[]{:S(2)}) copy-start(bf16[1,128,2048]{2,1,0:T(8,128)(2,1)} %param.7) | copy-start | bytes 1572868
  2.3 14.5 %all-to-all-start = ((bf16[16,8,768]{2,1,0:T(8,128)(2,1)}), bf16[16,8,768]{2,1,0:T(8,128)(2,1)S(1)}, u32[]{:S(2)}, u32[]{:S(2)}) async-start(bf16[16,8,768]{2,1,0:T(8,128)(2,1)} %bitcast.3), calls=%async_computation | async-start | bytes 393216 | tf_op jit(solution)/shard_map/all_to_all | solution.py:395
  16.8 16.0 %collective-permute-start.4 = (bf16[128,2048]{1,0:T(8,128)(2,1)S(1)}, bf16[128,2048]{1,0:T(8,128)(2,1)S(1)}, u32[]{:S(2)}, u32[]{:S(2)}) collective-permute-start(bf16[128,2048]{1,0:T(8,128)(2,1)S(1)} %shard_map.73.own.refs_0_), channel_id=1, source_target_pairs={{0,3},{1,0},{2,1},{3,2},{4,7},{5,4},{6,5},{7,6},{8,11},{9,8},{10,9... | collective-permute-start | bytes 1572872 | tf_op jit(solution)/shard_map/ppermute | solution.py:387
  18.3 14.4 %collective-permute-start.3 = (bf16[128,2048]{1,0:T(8,128)(2,1)S(1)}, bf16[128,2048]{1,0:T(8,128)(2,1)S(1)}, u32[]{:S(2)}, u32[]{:S(2)}) collective-permute-start(bf16[128,2048]{1,0:T(8,128)(2,1)S(1)} %shard_map.73.own.refs_0_), channel_id=1, source_target_pairs={{0,1},{1,2},{2,3},{3,0},{4,5},{5,6},{6,7},{7,4},{8,9},{9,10},{10,1... | collective-permute-start | bytes 1572872 | tf_op jit(solution)/shard_map/ppermute | solution.py:387
  18.9 13.9 %collective-permute-start.2 = (bf16[128,2048]{1,0:T(8,128)(2,1)S(1)}, bf16[128,2048]{1,0:T(8,128)(2,1)S(1)}, u32[]{:S(2)}, u32[]{:S(2)}) collective-permute-start(bf16[128,2048]{1,0:T(8,128)(2,1)S(1)} %shard_map.73.own.refs_0_), channel_id=1, source_target_pairs={{0,4},{4,0},{1,5},{5,1},{2,6},{6,2},{3,7},{7,3},{8,12},{12,8},{9,1... | collective-permute-start | bytes 1572872 | tf_op jit(solution)/shard_map/ppermute | solution.py:387
  19.8 9.3 %collective-permute-start.1 = (bf16[144,768]{1,0:T(8,128)(2,1)S(1)}, bf16[144,768]{1,0:T(8,128)(2,1)S(1)}, u32[]{:S(2)}, u32[]{:S(2)}) collective-permute-start(bf16[144,768]{1,0:T(8,128)(2,1)S(1)} %pad_maximum_fusion.2), channel_id=1, source_target_pairs={{0,56},{8,0},{16,8},{24,16},{32,24},{40,32},{48,40},{56,48},{1,57}... | collective-permute-start | bytes 663560 | tf_op jit(solution)/shard_map/ppermute | solution.py:387
  25.6 7.1 %collective-permute-start = (bf16[144,768]{1,0:T(8,128)(2,1)S(1)}, bf16[144,768]{1,0:T(8,128)(2,1)S(1)}, u32[]{:S(2)}, u32[]{:S(2)}) collective-permute-start(bf16[144,768]{1,0:T(8,128)(2,1)S(1)} %pad_maximum_fusion.2), channel_id=1, source_target_pairs={{0,8},{8,16},{16,24},{24,32},{32,40},{40,48},{48,56},{56,0},{1,9},... | collective-permute-start | bytes 663560 | tf_op jit(solution)/shard_map/ppermute | solution.py:387
  33.0 27.9 %collective-permute-start.9 = (bf16[192,2048]{1,0:T(8,128)(2,1)S(1)}, bf16[192,2048]{1,0:T(8,128)(2,1)S(1)}, u32[]{:S(2)}, u32[]{:S(2)}) collective-permute-start(bf16[192,2048]{1,0:T(8,128)(2,1)S(1)} %get-tuple-element.41), channel_id=1, source_target_pairs={{0,3},{1,0},{2,1},{3,2},{4,7},{5,4},{6,5},{7,6},{8,11},{9,8},{10,9... | collective-permute-start | bytes 2359304 | tf_op jit(solution)/shard_map/ppermute | solution.py:387
  34.6 26.4 %collective-permute-start.8 = (bf16[192,2048]{1,0:T(8,128)(2,1)S(1)}, bf16[192,2048]{1,0:T(8,128)(2,1)S(1)}, u32[]{:S(2)}, u32[]{:S(2)}) collective-permute-start(bf16[192,2048]{1,0:T(8,128)(2,1)S(1)} %get-tuple-element.42), channel_id=1, source_target_pairs={{0,1},{1,2},{2,3},{3,0},{4,5},{5,6},{6,7},{7,4},{8,9},{9,10},{10,1... | collective-permute-start | bytes 2359304 | tf_op jit(solution)/shard_map/ppermute | solution.py:387
  35.1 9.8 %collective-permute-start.5 = (bf16[144,768]{1,0:T(8,128)(2,1)S(1)}, bf16[144,768]{1,0:T(8,128)(2,1)S(1)}, u32[]{:S(2)}, u32[]{:S(2)}) collective-permute-start(bf16[144,768]{1,0:T(8,128)(2,1)S(1)} %collective-permute-done), channel_id=1, source_target_pairs={{0,8},{8,16},{16,24},{24,32},{32,40},{40,48},{48,56},{56,0},{1,9},... | collective-permute-start | bytes 663560 | tf_op jit(solution)/shard_map/ppermute | solution.py:387
  36.7 8.2 %collective-permute-start.14 = (bf16[144,768]{1,0:T(8,128)(2,1)S(1)}, bf16[144,768]{1,0:T(8,128)(2,1)S(1)}, u32[]{:S(2)}, u32[]{:S(2)}) collective-permute-start(bf16[144,768]{1,0:T(8,128)(2,1)S(1)} %collective-permute-done.1), channel_id=1, source_target_pairs={{0,56},{8,0},{16,8},{24,16},{32,24},{40,32},{48,40},{56,48},{1,57}... | collective-permute-start | bytes 663560 | tf_op jit(solution)/shard_map/ppermute | solution.py:387
  44.9 8.8 %collective-permute-start.6 = (bf16[144,768]{1,0:T(8,128)(2,1)S(1)}, bf16[144,768]{1,0:T(8,128)(2,1)S(1)}, u32[]{:S(2)}, u32[]{:S(2)}) collective-permute-start(bf16[144,768]{1,0:T(8,128)(2,1)S(1)} %collective-permute-done.5), channel_id=1, source_target_pairs={{0,8},{8,16},{16,24},{24,32},{32,40},{40,48},{48,56},{56,0},{1,9},... | collective-permute-start | bytes 663560 | tf_op jit(solution)/shard_map/ppermute | solution.py:387
  44.9 16.0 %collective-permute-start.15 = (bf16[144,768]{1,0:T(8,128)(2,1)S(1)}, bf16[144,768]{1,0:T(8,128)(2,1)S(1)}, u32[]{:S(2)}, u32[]{:S(2)}) collective-permute-start(bf16[144,768]{1,0:T(8,128)(2,1)S(1)} %collective-permute-done.14), channel_id=1, source_target_pairs={{0,56},{8,0},{16,8},{24,16},{32,24},{40,32},{48,40},{56,48},{1,57}... | collective-permute-start | bytes 663560 | tf_op jit(solution)/shard_map/ppermute | solution.py:387
  53.8 7.1 %collective-permute-start.7 = (bf16[144,768]{1,0:T(8,128)(2,1)S(1)}, bf16[144,768]{1,0:T(8,128)(2,1)S(1)}, u32[]{:S(2)}, u32[]{:S(2)}) collective-permute-start(bf16[144,768]{1,0:T(8,128)(2,1)S(1)} %collective-permute-done.6), channel_id=1, source_target_pairs={{0,8},{8,16},{16,24},{24,32},{32,40},{40,48},{48,56},{56,0},{1,9},... | collective-permute-start | bytes 663560 | tf_op jit(solution)/shard_map/ppermute | solution.py:387
  61.0 11.8 %collective-permute-start.16 = (bf16[8,144,768]{2,1,0:T(8,128)(2,1)S(1)}, bf16[8,144,768]{2,1,0:T(8,128)(2,1)S(1)}, u32[]{:S(2)}, u32[]{:S(2)}) collective-permute-start(bf16[8,144,768]{2,1,0:T(8,128)(2,1)S(1)} %bitcast_dynamic-update-slice_fusion.refs_10_), channel_id=1, source_target_pairs={{0,64},{64,0},{1,65},{65,1},{2,66},{66,2},{3,67},{67,3},{4,68},{68... | collective-permute-start | bytes 5308424 | tf_op jit(solution)/shard_map/ppermute | solution.py:387
  61.2 9.0 %collective-permute-start.11 = (bf16[64,2048]{1,0:T(8,128)(2,1)S(1)}, bf16[64,2048]{1,0:T(8,128)(2,1)S(1)}, u32[]{:S(2)}, u32[]{:S(2)}) collective-permute-start(bf16[64,2048]{1,0:T(8,128)(2,1)S(1)} %slice.15), channel_id=1, source_target_pairs={{0,3},{1,0},{2,1},{3,2},{4,7},{5,4},{6,5},{7,6},{8,11},{9,8},{10,9... | collective-permute-start | bytes 786440 | tf_op jit(solution)/shard_map/ppermute | solution.py:387
  62.3 10.6 %collective-permute-start.10 = (bf16[64,2048]{1,0:T(8,128)(2,1)S(1)}, bf16[64,2048]{1,0:T(8,128)(2,1)S(1)}, u32[]{:S(2)}, u32[]{:S(2)}) collective-permute-start(bf16[64,2048]{1,0:T(8,128)(2,1)S(1)} %slice.14), channel_id=1, source_target_pairs={{0,1},{1,2},{2,3},{3,0},{4,5},{5,6},{6,7},{7,4},{8,9},{9,10},{10,1... | collective-permute-start | bytes 786440 | tf_op jit(solution)/shard_map/ppermute | solution.py:387
  63.5 1.3 %collective-permute-start.13 = (bf16[16,2048]{1,0:T(8,128)(2,1)S(1)}, bf16[16,2048]{1,0:T(8,128)(2,1)S(1)}, u32[]{:S(2)}, u32[]{:S(2)}) collective-permute-start(bf16[16,2048]{1,0:T(8,128)(2,1)S(1)} %shard_map.74), channel_id=1, source_target_pairs={{4,12},{12,20},{20,28},{28,36},{36,44},{44,52},{52,60},{5,13},{13,... | collective-permute-start | bytes 196616 | tf_op jit(solution)/shard_map/ppermute | solution.py:469
  64.2 0.7 collective-permute-start.12
  80.9 0.8 copy-start.1
  81.7 16.5 %all-to-all-start.1 = ((f32[8,16,256]{2,1,0:T(8,128)}), f32[8,16,256]{2,1,0:T(8,128)S(1)}, u32[]{:S(2)}, u32[]{:S(2)}) async-start(f32[8,16,256]{2,1,0:T(8,128)} %get-tuple-element.34), calls=%async_computation.1 | async-start | bytes 262144 | tf_op jit(solution)/shard_map/all_to_all | solution.py:395
  89.1 1.0 copy-start.2

commit v7 on v6

--- a/solution.py
+++ b/solution.py
@@ -31,7 +31,25 @@
     return pltpu.CompilerParams(vmem_limit_bytes=mib * MIB)
 
 
-def norm_kernel(tok_ref, gain_ref, out_ref, scr):
+def coded(values, parts):
+    out = []
+    for _ in range(parts):
+        part = values.astype(BF16).astype(F32)
+        out.append(part)
+        values = values - part
+    return out
+
+
+def norm_kernel(tok_ref, gain_ref, rates, residues, skip, out_ref, table_ref, scr):
+    shape = (TABLE, LANES)
+    mine = lax.broadcasted_iota(jnp.int32, shape, 1) // 32 == lax.rem(lax.axis_index("z"), 4)
+    row = lax.broadcasted_iota(jnp.int32, shape, 0)
+    last = jnp.zeros(shape, F32)
+    for i, part in enumerate(coded(skip[...], 3)):
+        last = jnp.where(row == i, jnp.broadcast_to(part, shape), last)
+    tiles = coded(rates[...], 3) + coded(residues[...], 2) + [last]
+    for i, tile in enumerate(tiles):
+        table_ref[:, i * LANES : (i + 1) * LANES] = jnp.where(mine, tile, 0.0).astype(BF16)
     x = tok_ref[...].astype(F32)
     inv = lax.rsqrt(jnp.mean(x * x, axis=1, keepdims=True) + 1e-6)
     for k in range(D // LANES):
@@ -45,13 +63,44 @@
             ).astype(BF16)
 
 
-def normalise(tokens, gain):
+def normalise(tokens, gain, rates, residues, skip):
+    wide = [jnp.tile(v, (1, LANES // 32)) for v in (rates.T, residues.T, skip[None, :])]
     return pl.pallas_call(
         norm_kernel,
-        out_shape=jax.ShapeDtypeStruct((HERE, D), BF16),
+        out_shape=[
+            jax.ShapeDtypeStruct((HERE, D), BF16),
+            jax.ShapeDtypeStruct((TABLE, COLS), BF16),
+        ],
         scratch_shapes=[pltpu.VMEM((D // LANES, HERE, LANES), F32)],
         compiler_params=params(10),
-    )(tokens, gain)
+    )(tokens, gain, *wide)
+
+
+def columns_kernel(w_ref, out_ref):
+    lane = lax.broadcasted_iota(jnp.int32, (8, LANES), 1) // 32
+    for s in range(3):
+        for half in range(2):
+            to = slice(s * CH + half * LANES, s * CH + (half + 1) * LANES)
+            for high in range(2):
+                tiles = []
+                for k in range(4):
+                    first = s * NZ * CH + (4 * half + k) * CH + high * LANES
+                    tiles.append(w_ref[:, first : first + LANES].astype(F32))
+                for low in range(4):
+                    total = pltpu.roll(tiles[0], (-32 * low) % LANES, 1)
+                    for k in range(1, 4):
+                        turned = pltpu.roll(tiles[k], (32 * (k - low)) % LANES, 1)
+                        total = jnp.where(lane == k, turned, total)
+                    for yl in range(2):
+                        out_ref[yl * PIECES + 4 * high + low, :, to] = total.astype(BF16)
+
+
+def columns_by_place(weight):
+    return pl.pallas_call(
+        columns_kernel,
+        out_shape=jax.ShapeDtypeStruct((2 * PIECES, 8, COLS), BF16),
+        compiler_params=params(10),
+    )(weight)
 
 
 def rounded(v):
@@ -419,33 +468,16 @@
     )(*row)
 
 
-def coded(values, parts):
-    out = []
-    for _ in range(parts):
-        part = lax.reduce_precision(values, 8, 7)
-        out.append(part)
-        values = values - part
-    return out
-
-
 def body(tokens, norm_gain, in_weight, short_filter, rates, residues, skip):
     x, yh, z = lax.axis_index("x"), lax.axis_index("yh"), lax.axis_index("z")
     together = lax.optimization_barrier
 
     taps = short_filter.reshape(3, 3, NZ, PIECES, 32)
     taps = lax.dynamic_index_in_dim(taps, yh * NX + x, 3, keepdims=False).reshape(3, COLS)
-    skips = jnp.pad(jnp.stack(coded(skip, 3)), ((0, TABLE - 3), (0, 0)))
-    mine = jnp.stack(coded(rates.T, 3) + coded(residues.T, 2) + [skips], axis=1)
-    mine = jnp.tile(mine, (1, 1, 4)).reshape(TABLE, COLS)
-    lane = jnp.arange(COLS)[None, :] % LANES
-    mine = jnp.where(lane // 32 == z % 4, mine, 0.0).astype(BF16)
-
-    blocks = in_weight.reshape(8, 3, NZ, PIECES, 32).transpose(3, 0, 1, 2, 4)
-    blocks = spread(blocks.reshape(PIECES, 8, COLS), 2).reshape(2 * PIECES, 8, COLS)
+    blocks = columns_by_place(in_weight)
     unit = swap(blocks, ("yl", "yh", "x")).reshape(UNIT, COLS)
-    unit = jnp.concatenate([unit, mine])
-    own = normalise(tokens[0], norm_gain[None, :])
-    own, unit, taps = together((own, unit, taps))
+    own, mine = normalise(tokens[0], norm_gain[None, :], rates, residues, skip)
+    own, unit, taps = together((own, jnp.concatenate([unit, mine]), taps))
 
     def step(up, down):
         return shift(up, "z", 1), shift(down, "z", -1)
@@ -453,11 +485,11 @@
     partner = shift(own, "yh", 1)
     own_1, own_3 = shift(own, "x", 1), shift(own, "x", -1)
     up_1, down_1 = step(unit, unit)
-    up_1, down_1, partner, own_1, own_3 = together((up_1, down_1, partner, own_1, own_3))
+    up_2, down_2 = step(up_1, down_1)
+    up_2, down_2, partner, own_1, own_3 = together((up_2, down_2, partner, own_1, own_3))
 
     mixed_1 = shift(jnp.concatenate([partner, own_1[:HALF]]), "x", 1)
     mixed_3 = shift(jnp.concatenate([partner, own_3[HALF:]]), "x", -1)
-    up_2, down_2 = step(up_1, down_1)
     up_3, down_3 = step(up_2, down_2)
     up_4 = shift(up_3, "z", 1)
     up_4, mixed_1, mixed_3 = together((up_4, mixed_1, mixed_3))

time: 118 us -> 113 us (0.958)
  waiting for transfers between devices: 44.3 us -> 39.4 us
  starting transfers between devices: 38.8 us -> 35 us
  local copies, waits for them, and re-layouts: 4.74 us -> 8.12 us
    all_to_all x2, waiting for transfers between devices: 12.7 us -> 8.17 us  [swap(): return lax.all_to_all(value, axes, split_axis=0, concat_axis=0, tiled=True)]
    all_to_all x2, starting transfers between devices: 14.9 us -> 12 us  [swap(): return lax.all_to_all(value, axes, split_axis=0, concat_axis=0, tiled=True)]
    unnamed x23 -> x17, local copies, waits for them, and re-layouts: 1.96 us -> 4.57 us
    another operation x3 -> x6, local copies, waits for them, and re-layouts: 0.16 us -> 2.31 us  [normalise(): jnp.tile(v, (1, LANES // 32))]
    reshape x2 -> x0, local copies, waits for them, and re-layouts: 1.34 us -> none  [body(): blocks = in_weight.reshape(8, 3, NZ, PIECES, 32).transpose(3, 0, 1, 2, 4)]
  transfers between devices with their start and end apart: 19 -> 19, of which waited for: 9 -> 9; matrix products, arithmetic and copies ran while one was open for 1% -> 3% of each run, Pallas kernels for 1% -> 2%
where the time goes in v7:
time: 113 us
  waiting for transfers between devices  39.4 us (35%)
  starting transfers between devices  35 us (31%)
  blocking collectives  14.9 us (13%)
  Pallas kernels  14.8 us (13%)
  local copies, waits for them, and re-layouts  8.12 us (7%)
    ppermute x15, waiting for transfers between devices, shift(): return lax.ppermute(value, axis, ring(lax.axis_size(axis), by))  31.3 us
    ppermute x15, starting transfers between devices, shift(): return lax.ppermute(value, axis, ring(lax.axis_size(axis), by))  21.7 us
    all_to_all x1, blocking collectives, swap(): return lax.all_to_all(value, axes, split_axis=0, concat_axis=0, tiled=True)  14.9 us
    all_to_all x2, starting transfers between devices, swap(): return lax.all_to_all(value, axes, split_axis=0, concat_axis=0, tiled=True)  12 us
    all_to_all x2, waiting for transfers between devices, swap(): return lax.all_to_all(value, axes, split_axis=0, concat_axis=0, tiled=True)  8.17 us
    pallas_call x1, Pallas kernels, project(): pl.pallas_call(project_kernel, in_specs=[vmem] * (PIECE_ARRAYS + 5), out_...  8.07 us
    unnamed x17, local copies, waits for them, and re-layouts  4.57 us
    pallas_call x1, Pallas kernels, finish(): pl.pallas_call(finish_kernel, in_specs=[vmem] * 5, out_specs=vmem, out_sh...  3.4 us
  transfers between devices with their start and end apart: 19, of which 9 were waited for; matrix products, arithmetic and copies ran while one was open for 3% of the time, Pallas kernels for 2%

profile of v7, /device:TPU:2, one launch (start us, length us, event | category | flops | bytes accessed | tf_op | source)
XLA Modules:
  0.0 112.7 jit_solution(12770675056860887751)
XLA Ops:
  0.0 0.9 copy-done.3
  0.9 0.8 shard_map.74
  1.7 7.5 %all-to-all-start = ((bf16[16,8,768]{2,1,0:T(8,128)(2,1)}), bf16[16,8,768]{2,1,0:T(8,128)(2,1)S(1)}, u32[]{:S(2)}, u32[]{:S(2)}) async-start(bf16[16,8,768]{2,1,0:T(8,128)(2,1)} %shard_map.74), calls=%async_computation | async-start | bytes 393216 | tf_op jit(solution)/shard_map/all_to_all | solution.py:444
  9.9 0.7 tile.12
  10.7 0.7 tile.28
  11.5 1.0 reshape.28
  12.7 1.0 copy-done
  15.0 1.2 %all-to-all-done = bf16[16,8,768]{2,1,0:T(8,128)(2,1)S(1)} async-done(((bf16[16,8,768]{2,1,0:T(8,128)(2,1)}), bf16[16,8,768]{2,1,0:T(8,128)(2,1)S(1)}, u32[]{:S(2)}, u32[]{:S(2)}) %all-to-all-start) | async-done | bytes 196640 | tf_op jit(solution)/shard_map/all_to_all | solution.py:444
  16.2 1.5 %collective-permute-start.6 = (bf16[128,2048]{1,0:T(8,128)(2,1)S(1)}, bf16[128,2048]{1,0:T(8,128)(2,1)S(1)}, u32[]{:S(2)}, u32[]{:S(2)}) collective-permute-start(bf16[128,2048]{1,0:T(8,128)(2,1)S(1)} %get-tuple-element.27.own.refs_0_), channel_id=1, source_target_pairs={{0,3},{1,0},{2,1},{3,2},{4,7},{5,4},{6,5},{7,6},{8,11},{9,8},{10,9... | collective-permute-start | bytes 1572872 | tf_op jit(solution)/shard_map/ppermute | solution.py:436
  18.3 1.8 %collective-permute-start.4 = (bf16[128,2048]{1,0:T(8,128)(2,1)S(1)}, bf16[128,2048]{1,0:T(8,128)(2,1)S(1)}, u32[]{:S(2)}, u32[]{:S(2)}) collective-permute-start(bf16[128,2048]{1,0:T(8,128)(2,1)S(1)} %get-tuple-element.27.own.refs_0_), channel_id=1, source_target_pairs={{0,4},{4,0},{1,5},{5,1},{2,6},{6,2},{3,7},{7,3},{8,12},{12,8},{9,1... | collective-permute-start | bytes 1572872 | tf_op jit(solution)/shard_map/ppermute | solution.py:436
  20.1 5.9 %collective-permute-start.2 = (bf16[144,768]{1,0:T(8,128)(2,1)S(1)}, bf16[144,768]{1,0:T(8,128)(2,1)S(1)}, u32[]{:S(2)}, u32[]{:S(2)}) collective-permute-start(bf16[144,768]{1,0:T(8,128)(2,1)S(1)} %pad_maximum_fusion.2), channel_id=1, source_target_pairs={{0,56},{8,0},{16,8},{24,16},{32,24},{40,32},{48,40},{56,48},{1,57}... | collective-permute-start | bytes 663560 | tf_op jit(solution)/shard_map/ppermute | solution.py:436
  25.9 3.4 %collective-permute-done.2 = bf16[144,768]{1,0:T(8,128)(2,1)S(1)} collective-permute-done((bf16[144,768]{1,0:T(8,128)(2,1)S(1)}, bf16[144,768]{1,0:T(8,128)(2,1)S(1)}, u32[]{:S(2)}, u32[]{:S(2)}) %collective-permute-start.2) | collective-permute-done | bytes 221216 | tf_op jit(solution)/shard_map/ppermute | solution.py:436
  29.4 3.7 %collective-permute-start.3 = (bf16[144,768]{1,0:T(8,128)(2,1)S(1)}, bf16[144,768]{1,0:T(8,128)(2,1)S(1)}, u32[]{:S(2)}, u32[]{:S(2)}) collective-permute-start(bf16[144,768]{1,0:T(8,128)(2,1)S(1)} %collective-permute-done.2), channel_id=1, source_target_pairs={{0,56},{8,0},{16,8},{24,16},{32,24},{40,32},{48,40},{56,48},{1,57}... | collective-permute-start | bytes 663560 | tf_op jit(solution)/shard_map/ppermute | solution.py:436
  33.1 3.4 %collective-permute-done.3 = bf16[144,768]{1,0:T(8,128)(2,1)S(1)} collective-permute-done((bf16[144,768]{1,0:T(8,128)(2,1)S(1)}, bf16[144,768]{1,0:T(8,128)(2,1)S(1)}, u32[]{:S(2)}, u32[]{:S(2)}) %collective-permute-start.3) | collective-permute-done | bytes 221216 | tf_op jit(solution)/shard_map/ppermute | solution.py:436
  36.5 3.7 %collective-permute-done.1 = bf16[144,768]{1,0:T(8,128)(2,1)S(1)} collective-permute-done((bf16[144,768]{1,0:T(8,128)(2,1)S(1)}, bf16[144,768]{1,0:T(8,128)(2,1)S(1)}, u32[]{:S(2)}, u32[]{:S(2)}) %collective-permute-start.1) | collective-permute-done | bytes 221216 | tf_op jit(solution)/shard_map/ppermute | solution.py:436
  40.5 1.4 %collective-permute-start.10 = (bf16[192,2048]{1,0:T(8,128)(2,1)S(1)}, bf16[192,2048]{1,0:T(8,128)(2,1)S(1)}, u32[]{:S(2)}, u32[]{:S(2)}) collective-permute-start(bf16[192,2048]{1,0:T(8,128)(2,1)S(1)} %get-tuple-element.45), channel_id=1, source_target_pairs={{0,3},{1,0},{2,1},{3,2},{4,7},{5,4},{6,5},{7,6},{8,11},{9,8},{10,9... | collective-permute-start | bytes 2359304 | tf_op jit(solution)/shard_map/ppermute | solution.py:436
  41.9 0.7 collective-permute-start.9
  42.7 3.2 %collective-permute-start.15 = (bf16[144,768]{1,0:T(8,128)(2,1)S(1)}, bf16[144,768]{1,0:T(8,128)(2,1)S(1)}, u32[]{:S(2)}, u32[]{:S(2)}) collective-permute-start(bf16[144,768]{1,0:T(8,128)(2,1)S(1)} %collective-permute-done.3), channel_id=1, source_target_pairs={{0,56},{8,0},{16,8},{24,16},{32,24},{40,32},{48,40},{56,48},{1,57}... | collective-permute-start | bytes 663560 | tf_op jit(solution)/shard_map/ppermute | solution.py:436
  46.0 5.7 %collective-permute-done.7 = bf16[144,768]{1,0:T(8,128)(2,1)S(1)} collective-permute-done((bf16[144,768]{1,0:T(8,128)(2,1)S(1)}, bf16[144,768]{1,0:T(8,128)(2,1)S(1)}, u32[]{:S(2)}, u32[]{:S(2)}) %collective-permute-start.7) | collective-permute-done | bytes 221216 | tf_op jit(solution)/shard_map/ppermute | solution.py:436
  51.7 7.1 %collective-permute-done.8 = bf16[144,768]{1,0:T(8,128)(2,1)S(1)} collective-permute-done((bf16[144,768]{1,0:T(8,128)(2,1)S(1)}, bf16[144,768]{1,0:T(8,128)(2,1)S(1)}, u32[]{:S(2)}, u32[]{:S(2)}) %collective-permute-start.8) | collective-permute-done | bytes 221216 | tf_op jit(solution)/shard_map/ppermute | solution.py:436
  59.1 2.8 %collective-permute-start.12 = (bf16[64,2048]{1,0:T(8,128)(2,1)S(1)}, bf16[64,2048]{1,0:T(8,128)(2,1)S(1)}, u32[]{:S(2)}, u32[]{:S(2)}) collective-permute-start(bf16[64,2048]{1,0:T(8,128)(2,1)S(1)} %slice.15), channel_id=1, source_target_pairs={{0,3},{1,0},{2,1},{3,2},{4,7},{5,4},{6,5},{7,6},{8,11},{9,8},{10,9... | collective-permute-start | bytes 786440 | tf_op jit(solution)/shard_map/ppermute | solution.py:436
  63.3 4.8 %collective-permute-done.12.refs_7_ = bf16[64,2048]{1,0:T(8,128)(2,1)S(1)} collective-permute-done((bf16[64,2048]{1,0:T(8,128)(2,1)S(1)}, bf16[64,2048]{1,0:T(8,128)(2,1)S(1)}, u32[]{:S(2)}, u32[]{:S(2)}) %collective-permute-start.12) | collective-permute-done | bytes 262176 | tf_op jit(solution)/shard_map/ppermute | solution.py:436
  68.1 3.1 %collective-permute-done.11.refs_6_ = bf16[64,2048]{1,0:T(8,128)(2,1)S(1)} collective-permute-done((bf16[64,2048]{1,0:T(8,128)(2,1)S(1)}, bf16[64,2048]{1,0:T(8,128)(2,1)S(1)}, u32[]{:S(2)}, u32[]{:S(2)}) %collective-permute-start.11) | collective-permute-done | bytes 262176 | tf_op jit(solution)/shard_map/ppermute | solution.py:436
  71.1 8.1 %shard_map.76 = (bf16[1040,256]{1,0:T(8,128)(2,1)S(1)}, bf16[1024,256]{1,0:T(8,128)(2,1)S(1)}, f32[16,64,256]{2,1,0:T(8,128)S(1)}, f32[8,16,256]{2,1,0:T(8,128)}, f32[40,256]{1,0:T(8,128)S(1)}) custom-call(bf16[128,2048]{1,0:T(8,128)(2,1)S(1)} %get-tuple-element.27.own.refs_0_, bf16[128,2048]{1,0:T(8,128)(2,1)S(1)} %collective-permute-done.5.behind.refs_1_, ...), custom_call_target="tpu_custom_call" | custom-call | flops 3271557120 | bytes 10000000 | tf_op jit(solution)/shard_map/pallas_call | solution.py:272
  79.2 0.8 copy-done.1
  80.0 4.5 %all-to-all-start.1 = ((f32[8,16,256]{2,1,0:T(8,128)}), f32[8,16,256]{2,1,0:T(8,128)S(1)}, u32[]{:S(2)}, u32[]{:S(2)}) async-start(f32[8,16,256]{2,1,0:T(8,128)} %get-tuple-element.38), calls=%async_computation.1 | async-start | bytes 262144 | tf_op jit(solution)/shard_map/all_to_all | solution.py:444
  84.5 1.0 copy-done.2
  85.5 1.1 shard_map.77
  86.6 7.0 %all-to-all-done.1.states = f32[8,16,256]{2,1,0:T(8,128)S(1)} async-done(((f32[8,16,256]{2,1,0:T(8,128)}), f32[8,16,256]{2,1,0:T(8,128)S(1)}, u32[]{:S(2)}, u32[]{:S(2)}) %all-to-all-start.1) | async-done | bytes 131104 | tf_op jit(solution)/shard_map/all_to_all | solution.py:444
  93.6 3.4 %shard_map.78 = bf16[8,256,128]{2,1,0:T(8,128)(2,1)S(1)} custom-call(f32[8,16,256]{2,1,0:T(8,128)S(1)} %all-to-all-done.1.states, f32[40,256]{1,0:T(8,128)S(1)} %get-tuple-element.39.table, f32[1024,256]{1,0:T(8,128)S(1)} %get-tuple-element.42.local, f32[16,64,256]{2,1,0:T(8,128)S(1)} %get-tuple-element.43.chunk, bf16[1024,256]{1,0:T(8,128)(2,1)S(1)} %get-tuple-element.44.gate), custom_call_target="tpu_custom_call" | custom-call | tf_op jit(solution)/shard_map/pallas_call | solution.py:400
  97.0 14.9 %all_to_all.15.pieces = bf16[8,256,128]{2,1,0:T(8,128)(2,1)S(1)} all-to-all(bf16[8,256,128]{2,1,0:T(8,128)(2,1)S(1)} %shard_map.78), channel_id=1, replica_groups=mesh['yl'=2,'co'=2,'z'=8,'yh'=2,'x'=4] {'yh','x'}, dimensions={0} | all-to-all | bytes 1048576 | tf_op jit(solution)/shard_map/all_to_all | solution.py:444
  111.9 0.8 shard_map.79
  (47 shorter events, 4.8 us)
Async XLA Ops:
  0.0 0.9 copy-start.3
  1.7 14.5 %all-to-all-start = ((bf16[16,8,768]{2,1,0:T(8,128)(2,1)}), bf16[16,8,768]{2,1,0:T(8,128)(2,1)S(1)}, u32[]{:S(2)}, u32[]{:S(2)}) async-start(bf16[16,8,768]{2,1,0:T(8,128)(2,1)} %shard_map.74), calls=%async_computation | async-start | bytes 393216 | tf_op jit(solution)/shard_map/all_to_all | solution.py:444
  12.7 1.0 copy-start
  13.7 0.7 copy-start.4
  16.2 24.0 %collective-permute-start.6 = (bf16[128,2048]{1,0:T(8,128)(2,1)S(1)}, bf16[128,2048]{1,0:T(8,128)(2,1)S(1)}, u32[]{:S(2)}, u32[]{:S(2)}) collective-permute-start(bf16[128,2048]{1,0:T(8,128)(2,1)S(1)} %get-tuple-element.27.own.refs_0_), channel_id=1, source_target_pairs={{0,3},{1,0},{2,1},{3,2},{4,7},{5,4},{6,5},{7,6},{8,11},{9,8},{10,9... | collective-permute-start | bytes 1572872 | tf_op jit(solution)/shard_map/ppermute | solution.py:436
  17.7 22.5 %collective-permute-start.5 = (bf16[128,2048]{1,0:T(8,128)(2,1)S(1)}, bf16[128,2048]{1,0:T(8,128)(2,1)S(1)}, u32[]{:S(2)}, u32[]{:S(2)}) collective-permute-start(bf16[128,2048]{1,0:T(8,128)(2,1)S(1)} %get-tuple-element.27.own.refs_0_), channel_id=1, source_target_pairs={{0,1},{1,2},{2,3},{3,0},{4,5},{5,6},{6,7},{7,4},{8,9},{9,10},{10,1... | collective-permute-start | bytes 1572872 | tf_op jit(solution)/shard_map/ppermute | solution.py:436
  18.3 21.9 %collective-permute-start.4 = (bf16[128,2048]{1,0:T(8,128)(2,1)S(1)}, bf16[128,2048]{1,0:T(8,128)(2,1)S(1)}, u32[]{:S(2)}, u32[]{:S(2)}) collective-permute-start(bf16[128,2048]{1,0:T(8,128)(2,1)S(1)} %get-tuple-element.27.own.refs_0_), channel_id=1, source_target_pairs={{0,4},{4,0},{1,5},{5,1},{2,6},{6,2},{3,7},{7,3},{8,12},{12,8},{9,1... | collective-permute-start | bytes 1572872 | tf_op jit(solution)/shard_map/ppermute | solution.py:436
  20.1 9.3 %collective-permute-start.2 = (bf16[144,768]{1,0:T(8,128)(2,1)S(1)}, bf16[144,768]{1,0:T(8,128)(2,1)S(1)}, u32[]{:S(2)}, u32[]{:S(2)}) collective-permute-start(bf16[144,768]{1,0:T(8,128)(2,1)S(1)} %pad_maximum_fusion.2), channel_id=1, source_target_pairs={{0,56},{8,0},{16,8},{24,16},{32,24},{40,32},{48,40},{56,48},{1,57}... | collective-permute-start | bytes 663560 | tf_op jit(solution)/shard_map/ppermute | solution.py:436
  25.9 7.1 %collective-permute-start = (bf16[144,768]{1,0:T(8,128)(2,1)S(1)}, bf16[144,768]{1,0:T(8,128)(2,1)S(1)}, u32[]{:S(2)}, u32[]{:S(2)}) collective-permute-start(bf16[144,768]{1,0:T(8,128)(2,1)S(1)} %pad_maximum_fusion.2), channel_id=1, source_target_pairs={{0,8},{8,16},{16,24},{24,32},{32,40},{40,48},{48,56},{56,0},{1,9},... | collective-permute-start | bytes 663560 | tf_op jit(solution)/shard_map/ppermute | solution.py:436
  29.4 7.1 %collective-permute-start.3 = (bf16[144,768]{1,0:T(8,128)(2,1)S(1)}, bf16[144,768]{1,0:T(8,128)(2,1)S(1)}, u32[]{:S(2)}, u32[]{:S(2)}) collective-permute-start(bf16[144,768]{1,0:T(8,128)(2,1)S(1)} %collective-permute-done.2), channel_id=1, source_target_pairs={{0,56},{8,0},{16,8},{24,16},{32,24},{40,32},{48,40},{56,48},{1,57}... | collective-permute-start | bytes 663560 | tf_op jit(solution)/shard_map/ppermute | solution.py:436
  33.1 7.1 %collective-permute-start.1 = (bf16[144,768]{1,0:T(8,128)(2,1)S(1)}, bf16[144,768]{1,0:T(8,128)(2,1)S(1)}, u32[]{:S(2)}, u32[]{:S(2)}) collective-permute-start(bf16[144,768]{1,0:T(8,128)(2,1)S(1)} %collective-permute-done), channel_id=1, source_target_pairs={{0,8},{8,16},{16,24},{24,32},{32,40},{40,48},{48,56},{56,0},{1,9},... | collective-permute-start | bytes 663560 | tf_op jit(solution)/shard_map/ppermute | solution.py:436
  40.5 18.3 %collective-permute-start.10 = (bf16[192,2048]{1,0:T(8,128)(2,1)S(1)}, bf16[192,2048]{1,0:T(8,128)(2,1)S(1)}, u32[]{:S(2)}, u32[]{:S(2)}) collective-permute-start(bf16[192,2048]{1,0:T(8,128)(2,1)S(1)} %get-tuple-element.45), channel_id=1, source_target_pairs={{0,3},{1,0},{2,1},{3,2},{4,7},{5,4},{6,5},{7,6},{8,11},{9,8},{10,9... | collective-permute-start | bytes 2359304 | tf_op jit(solution)/shard_map/ppermute | solution.py:436
  41.9 16.9 %collective-permute-start.9 = (bf16[192,2048]{1,0:T(8,128)(2,1)S(1)}, bf16[192,2048]{1,0:T(8,128)(2,1)S(1)}, u32[]{:S(2)}, u32[]{:S(2)}) collective-permute-start(bf16[192,2048]{1,0:T(8,128)(2,1)S(1)} %get-tuple-element.46), channel_id=1, source_target_pairs={{0,1},{1,2},{2,3},{3,0},{4,5},{5,6},{6,7},{7,4},{8,9},{9,10},{10,1... | collective-permute-start | bytes 2359304 | tf_op jit(solution)/shard_map/ppermute | solution.py:436
  42.6 9.0 %collective-permute-start.7 = (bf16[144,768]{1,0:T(8,128)(2,1)S(1)}, bf16[144,768]{1,0:T(8,128)(2,1)S(1)}, u32[]{:S(2)}, u32[]{:S(2)}) collective-permute-start(bf16[144,768]{1,0:T(8,128)(2,1)S(1)} %collective-permute-done.1), channel_id=1, source_target_pairs={{0,8},{8,16},{16,24},{24,32},{32,40},{40,48},{48,56},{56,0},{1,9},... | collective-permute-start | bytes 663560 | tf_op jit(solution)/shard_map/ppermute | solution.py:436
  42.7 16.1 %collective-permute-start.15 = (bf16[144,768]{1,0:T(8,128)(2,1)S(1)}, bf16[144,768]{1,0:T(8,128)(2,1)S(1)}, u32[]{:S(2)}, u32[]{:S(2)}) collective-permute-start(bf16[144,768]{1,0:T(8,128)(2,1)S(1)} %collective-permute-done.3), channel_id=1, source_target_pairs={{0,56},{8,0},{16,8},{24,16},{32,24},{40,32},{48,40},{56,48},{1,57}... | collective-permute-start | bytes 663560 | tf_op jit(solution)/shard_map/ppermute | solution.py:436
  51.6 7.1 %collective-permute-start.8 = (bf16[144,768]{1,0:T(8,128)(2,1)S(1)}, bf16[144,768]{1,0:T(8,128)(2,1)S(1)}, u32[]{:S(2)}, u32[]{:S(2)}) collective-permute-start(bf16[144,768]{1,0:T(8,128)(2,1)S(1)} %collective-permute-done.7), channel_id=1, source_target_pairs={{0,8},{8,16},{16,24},{24,32},{32,40},{40,48},{48,56},{56,0},{1,9},... | collective-permute-start | bytes 663560 | tf_op jit(solution)/shard_map/ppermute | solution.py:436
  58.9 12.2 %collective-permute-start.16 = (bf16[8,144,768]{2,1,0:T(8,128)(2,1)S(1)}, bf16[8,144,768]{2,1,0:T(8,128)(2,1)S(1)}, u32[]{:S(2)}, u32[]{:S(2)}) collective-permute-start(bf16[8,144,768]{2,1,0:T(8,128)(2,1)S(1)} %bitcast_dynamic-update-slice_fusion.refs_10_), channel_id=1, source_target_pairs={{0,64},{64,0},{1,65},{65,1},{2,66},{66,2},{3,67},{67,3},{4,68},{68... | collective-permute-start | bytes 5308424 | tf_op jit(solution)/shard_map/ppermute | solution.py:436
  59.1 9.0 %collective-permute-start.12 = (bf16[64,2048]{1,0:T(8,128)(2,1)S(1)}, bf16[64,2048]{1,0:T(8,128)(2,1)S(1)}, u32[]{:S(2)}, u32[]{:S(2)}) collective-permute-start(bf16[64,2048]{1,0:T(8,128)(2,1)S(1)} %slice.15), channel_id=1, source_target_pairs={{0,3},{1,0},{2,1},{3,2},{4,7},{5,4},{6,5},{7,6},{8,11},{9,8},{10,9... | collective-permute-start | bytes 786440 | tf_op jit(solution)/shard_map/ppermute | solution.py:436
  61.9 9.3 %collective-permute-start.11 = (bf16[64,2048]{1,0:T(8,128)(2,1)S(1)}, bf16[64,2048]{1,0:T(8,128)(2,1)S(1)}, u32[]{:S(2)}, u32[]{:S(2)}) collective-permute-start(bf16[64,2048]{1,0:T(8,128)(2,1)S(1)} %slice.14), channel_id=1, source_target_pairs={{0,1},{1,2},{2,3},{3,0},{4,5},{5,6},{6,7},{7,4},{8,9},{9,10},{10,1... | collective-permute-start | bytes 786440 | tf_op jit(solution)/shard_map/ppermute | solution.py:436
  61.9 1.3 %collective-permute-start.14 = (bf16[16,2048]{1,0:T(8,128)(2,1)S(1)}, bf16[16,2048]{1,0:T(8,128)(2,1)S(1)}, u32[]{:S(2)}, u32[]{:S(2)}) collective-permute-start(bf16[16,2048]{1,0:T(8,128)(2,1)S(1)} %shard_map.75), channel_id=1, source_target_pairs={{4,12},{12,20},{20,28},{28,36},{36,44},{44,52},{52,60},{5,13},{13,... | collective-permute-start | bytes 196616 | tf_op jit(solution)/shard_map/ppermute | solution.py:501
  62.6 0.7 collective-permute-start.13
  79.2 0.8 copy-start.1
  80.0 13.6 %all-to-all-start.1 = ((f32[8,16,256]{2,1,0:T(8,128)}), f32[8,16,256]{2,1,0:T(8,128)S(1)}, u32[]{:S(2)}, u32[]{:S(2)}) async-start(f32[8,16,256]{2,1,0:T(8,128)} %get-tuple-element.38), calls=%async_computation.1 | async-start | bytes 262144 | tf_op jit(solution)/shard_map/all_to_all | solution.py:444
  84.5 1.0 copy-start.2

commit v8 on v7

--- a/solution.py
+++ b/solution.py
@@ -147,23 +147,15 @@
     (0, 2, 0, HALF, 4, HERE),
     (1, 3, 0, HERE, 5, 0),
     (0, 2, HALF, HALF, 5, HERE),
-    (1, 2, 0, HALF, 6, 0),
-    (1, 2, HALF, HALF, 7, 0),
 )
-PIECE_ARRAYS = 8
-
-
-def place_rows(arrays, halo, lhs):
+PIECE_ARRAYS = 6
+
+
+def place_rows(arrays, lhs):
     x, yh = lax.axis_index("x"), lax.axis_index("yh")
-    for i, source in enumerate(halo):
-
-        @pl.when(yh == i)
-        def _(source=source):
-            lhs[0:HALO, :] = source[...]
-
     for other, by, first, rows, array, at in PIECE_LIST:
         place = lax.rem(yh + other, 2) * NX + lax.rem(x + NX - by, NX)
-        row = pl.multiple_of(HALO + place * HERE + first, 16)
+        row = pl.multiple_of(place * HERE + first, 16)
         lhs[pl.ds(row, rows), :] = arrays[array][at : at + rows, :]
 
 
@@ -194,24 +186,66 @@
         out[32:40, lanes] = jnp.broadcast_to(skip, (8, LANES))
 
 
+def multiply_kernel(*refs):
+    arrays, refs = refs[:PIECE_ARRAYS], refs[PIECE_ARRAYS:]
+    planes, (w, proj, rates, lhs) = refs[:2], refs[2:]
+    place_weights(planes, w)
+    place_rows(arrays, lhs)
+    decode(planes[0], rates)
+    for s in range(3):
+        cols = slice(s * CH, (s + 1) * CH)
+        product = jnp.dot(lhs[...], w[:, cols], preferred_element_type=F32)
+        proj[:, cols] = product.astype(BF16)
+
+
+def multiply(arrays, weights):
+    vmem = pl.BlockSpec(memory_space=pltpu.VMEM)
+    return pl.pallas_call(
+        multiply_kernel,
+        in_specs=[vmem] * (PIECE_ARRAYS + 2),
+        out_specs=[vmem] * 3,
+        out_shape=[
+            jax.ShapeDtypeStruct((D, COLS), BF16),
+            jax.ShapeDtypeStruct((SPAN, COLS), BF16),
+            jax.ShapeDtypeStruct((40, CH), F32),
+        ],
+        scratch_shapes=[pltpu.VMEM((SPAN, D), BF16)],
+        compiler_params=params(24),
+        cost_estimate=pl.CostEstimate(
+            flops=2 * SPAN * D * COLS // 8, bytes_accessed=1_000_000, transcendentals=0
+        ),
+    )(*arrays, *weights)
+
+
 def project_kernel(
-    *refs,
+    first, second, halo_0, halo_1, w, done, taps, rates,
+    query_ref, carried_ref, chunk_ref, state_ref,
+    lhs, proj, decay_s, carry,
 ):
-    arrays, refs = refs[:PIECE_ARRAYS], refs[PIECE_ARRAYS:]
-    halo, planes, refs = refs[:2], refs[2:4], refs[4:]
-    taps, query_ref, carried_ref, chunk_ref, state_ref, rates = refs[:6]
-    lhs, w, proj, decay_s, carry = refs[6:]
-    place_weights(planes, w)
-    place_rows(arrays, halo, lhs)
-    decode(planes[0], rates)
+    x, yh = lax.axis_index("x"), lax.axis_index("yh")
+    for i, source in enumerate((halo_0, halo_1)):
+
+        @pl.when(yh == i)
+        def _(source=source):
+            lhs[0:HALO, :] = source[...]
+
+    lhs[HALO : HALO + HALF, :] = first[...]
+    lhs[HALO + HALF :, :] = second[...]
     decay_s[...] = jnp.exp(-rates[0:16, :])
-    for s in (1, 2, 0):
+    place = lax.rem(yh + 1, 2) * NX + lax.rem(x + 2, NX)
+    rows = pl.ds(pl.multiple_of(HALO + place * HERE, 16), HERE)
+    for s in range(3):
         cols = slice(s * CH, (s + 1) * CH)
-        product = jnp.dot(lhs[...], w[:, cols], preferred_element_type=F32).astype(BF16)
+        late = jnp.dot(lhs[...], w[:, cols], preferred_element_type=F32).astype(BF16)
         if s == 0:
-            query_ref[...] = product
+            query_ref[HALO:, :] = done[:, cols]
+            query_ref[0:HALO, :] = late[0:HALO]
+            query_ref[rows, :] = late[HALO:]
         else:
-            proj[:, (s - 1) * CH : s * CH] = product.astype(F32)
+            to = slice((s - 1) * CH, s * CH)
+            proj[HALO:, to] = done[:, cols].astype(F32)
+            proj[0:HALO, to] = late[0:HALO].astype(F32)
+            proj[rows, to] = late[HALO:].astype(F32)
 
     sub = lax.broadcasted_iota(jnp.int32, (8, LANES), 0)
 
@@ -267,31 +301,29 @@
                 state_ref[i, m : m + 1, here] = carry[m, 0:1, :]
 
 
-def project(arrays, halo, weights, taps):
+def project(first, second, halo, w, done, taps, rates):
     vmem = pl.BlockSpec(memory_space=pltpu.VMEM)
     return pl.pallas_call(
         project_kernel,
-        in_specs=[vmem] * (PIECE_ARRAYS + 5),
-        out_specs=[vmem] * 5,
+        in_specs=[vmem] * 8,
+        out_specs=[vmem] * 4,
         out_shape=[
             jax.ShapeDtypeStruct((ROWS, CH), BF16),
             jax.ShapeDtypeStruct((SPAN, CH), BF16),
             jax.ShapeDtypeStruct((POLES, SPAN // CHUNK, CH), F32),
             jax.ShapeDtypeStruct((NZ, POLES, CH), F32),
-            jax.ShapeDtypeStruct((40, CH), F32),
         ],
         scratch_shapes=[
-            pltpu.VMEM((ROWS, D), BF16),
-            pltpu.VMEM((D, COLS), BF16),
+            pltpu.VMEM((HALO + HERE, D), BF16),
             pltpu.VMEM((ROWS, 2 * CH), F32),
             pltpu.VMEM((POLES, CH), F32),
             pltpu.VMEM((POLES, 8, LANES), F32),
         ],
-        compiler_params=params(36),
+        compiler_params=params(20),
         cost_estimate=pl.CostEstimate(
-            flops=2 * ROWS * D * COLS, bytes_accessed=10_000_000, transcendentals=0
+            flops=2 * (HALO + HERE) * D * COLS, bytes_accessed=7_000_000, transcendentals=0
         ),
-    )(*arrays, *halo, *weights, taps)
+    )(first, second, *halo, w, done, taps, rates)
 
 
 def direct_kernel(query, carried, taps, table, gate_ref, local_ref, taps_s):
@@ -503,9 +535,10 @@
     ]
     plane = jnp.stack([unit, up_1, up_2, up_3, up_4, down_3, down_2, down_1])
     weights = [plane, shift(plane, "co", 1)]
-    arrays = [own, own_1, own_3, partner, mixed_1, mixed_3, first, second]
-
-    query, carried, chunk, state, table = project(arrays, halo, weights, taps)
+    arrays = [own, own_1, own_3, partner, mixed_1, mixed_3]
+
+    w, done, table = multiply(arrays, weights)
+    query, carried, chunk, state = project(first, second, halo, w, done, taps, table)
     states = swap(state, "z")
     gate, local = direct(query, carried, taps, table)
     pieces = finish(states, table, local, chunk, gate)

time: 113 us -> 110 us (0.973)
  waiting for transfers between devices: 39.4 us -> 30.5 us
  starting transfers between devices: 35 us -> 38.5 us
    ppermute x15, waiting for transfers between devices: 31.3 us -> 22.3 us  [shift(): return lax.ppermute(value, axis, ring(lax.axis_size(axis), by))]
    all_to_all x2, starting transfers between devices: 12 us -> 15.4 us  [swap(): return lax.all_to_all(value, axes, split_axis=0, concat_axis=0, tiled=True)]
    pallas_call x1 -> x2, Pallas kernels: 8.07 us -> 8.67 us  [the longest x1 4.79 us: project(): pl.pallas_call(project_kernel, in_specs=[vmem] * 8, out_specs=[vmem] * 4,...]
  transfers between devices with their start and end apart: 19 -> 19, of which waited for: 9 -> 9; matrix products, arithmetic and copies ran while one was open for 3% -> 3% of each run, Pallas kernels for 2% -> 5%
where the time goes in v8:
time: 110 us; the launch traced here: 109 us
  starting transfers between devices  38.5 us (35%)
  waiting for transfers between devices  30.5 us (28%)
  blocking collectives  15.9 us (14%)
  Pallas kernels  15.4 us (14%)
  local copies, waits for them, and re-layouts  8.13 us (7%)
    ppermute x15, waiting for transfers between devices, shift(): return lax.ppermute(value, axis, ring(lax.axis_size(axis), by))  22.3 us
    ppermute x15, starting transfers between devices, shift(): return lax.ppermute(value, axis, ring(lax.axis_size(axis), by))  21.7 us
    all_to_all x1, blocking collectives, swap(): return lax.all_to_all(value, axes, split_axis=0, concat_axis=0, tiled=True)  15.9 us
    all_to_all x2, starting transfers between devices, swap(): return lax.all_to_all(value, axes, split_axis=0, concat_axis=0, tiled=True)  15.4 us
    all_to_all x2, waiting for transfers between devices, swap(): return lax.all_to_all(value, axes, split_axis=0, concat_axis=0, tiled=True)  8.17 us
    pallas_call x1, Pallas kernels, project(): pl.pallas_call(project_kernel, in_specs=[vmem] * 8, out_specs=[vmem] * 4,...  4.79 us
    unnamed x17, local copies, waits for them, and re-layouts  4.57 us
    pallas_call x1, Pallas kernels, multiply(): pl.pallas_call(multiply_kernel, in_specs=[vmem] * (PIECE_ARRAYS + 2), out...  3.88 us
  transfers between devices with their start and end apart: 19, of which 9 were waited for; matrix products, arithmetic and copies ran while one was open for 3% of the time, Pallas kernels for 5%

profile of v8, /device:TPU:2, one launch (start us, length us, event | category | flops | bytes accessed | tf_op | source)
XLA Modules:
  0.0 108.8 jit_solution(6747287935804622726)
XLA Ops:
  0.0 0.9 copy-done.3
  0.9 0.8 shard_map.74
  1.7 7.5 %all-to-all-start = ((bf16[16,8,768]{2,1,0:T(8,128)(2,1)}), bf16[16,8,768]{2,1,0:T(8,128)(2,1)S(1)}, u32[]{:S(2)}, u32[]{:S(2)}) async-start(bf16[16,8,768]{2,1,0:T(8,128)(2,1)} %shard_map.74), calls=%async_computation | async-start | bytes 393216 | tf_op jit(solution)/shard_map/all_to_all | solution.py:476
  9.2 1.0 reshape.28
  10.4 0.7 tile.12
  12.7 1.0 copy-done
  15.0 1.2 %all-to-all-done = bf16[16,8,768]{2,1,0:T(8,128)(2,1)S(1)} async-done(((bf16[16,8,768]{2,1,0:T(8,128)(2,1)}), bf16[16,8,768]{2,1,0:T(8,128)(2,1)S(1)}, u32[]{:S(2)}, u32[]{:S(2)}) %all-to-all-start) | async-done | bytes 196640 | tf_op jit(solution)/shard_map/all_to_all | solution.py:476
  16.2 1.9 %collective-permute-start.4 = (bf16[128,2048]{1,0:T(8,128)(2,1)S(1)}, bf16[128,2048]{1,0:T(8,128)(2,1)S(1)}, u32[]{:S(2)}, u32[]{:S(2)}) collective-permute-start(bf16[128,2048]{1,0:T(8,128)(2,1)S(1)} %get-tuple-element.30.own.refs_0_), channel_id=1, source_target_pairs={{0,4},{4,0},{1,5},{5,1},{2,6},{6,2},{3,7},{7,3},{8,12},{12,8},{9,1... | collective-permute-start | bytes 1572872 | tf_op jit(solution)/shard_map/ppermute | solution.py:468
  18.1 1.5 %collective-permute-start.5 = (bf16[128,2048]{1,0:T(8,128)(2,1)S(1)}, bf16[128,2048]{1,0:T(8,128)(2,1)S(1)}, u32[]{:S(2)}, u32[]{:S(2)}) collective-permute-start(bf16[128,2048]{1,0:T(8,128)(2,1)S(1)} %get-tuple-element.30.own.refs_0_), channel_id=1, source_target_pairs={{0,1},{1,2},{2,3},{3,0},{4,5},{5,6},{6,7},{7,4},{8,9},{9,10},{10,1... | collective-permute-start | bytes 1572872 | tf_op jit(solution)/shard_map/ppermute | solution.py:468
  20.1 1.9 %collective-permute-start = (bf16[144,768]{1,0:T(8,128)(2,1)S(1)}, bf16[144,768]{1,0:T(8,128)(2,1)S(1)}, u32[]{:S(2)}, u32[]{:S(2)}) collective-permute-start(bf16[144,768]{1,0:T(8,128)(2,1)S(1)} %pad_maximum_fusion.2), channel_id=1, source_target_pairs={{0,8},{8,16},{16,24},{24,32},{32,40},{40,48},{48,56},{56,0},{1,9},... | collective-permute-start | bytes 663560 | tf_op jit(solution)/shard_map/ppermute | solution.py:468
  22.0 3.9 %collective-permute-start.2 = (bf16[144,768]{1,0:T(8,128)(2,1)S(1)}, bf16[144,768]{1,0:T(8,128)(2,1)S(1)}, u32[]{:S(2)}, u32[]{:S(2)}) collective-permute-start(bf16[144,768]{1,0:T(8,128)(2,1)S(1)} %pad_maximum_fusion.2), channel_id=1, source_target_pairs={{0,56},{8,0},{16,8},{24,16},{32,24},{40,32},{48,40},{56,48},{1,57}... | collective-permute-start | bytes 663560 | tf_op jit(solution)/shard_map/ppermute | solution.py:468
  25.9 4.0 %collective-permute-done = bf16[144,768]{1,0:T(8,128)(2,1)S(1)} collective-permute-done((bf16[144,768]{1,0:T(8,128)(2,1)S(1)}, bf16[144,768]{1,0:T(8,128)(2,1)S(1)}, u32[]{:S(2)}, u32[]{:S(2)}) %collective-permute-start) | collective-permute-done | bytes 221216 | tf_op jit(solution)/shard_map/ppermute | solution.py:468
  30.0 3.2 %collective-permute-start.3 = (bf16[144,768]{1,0:T(8,128)(2,1)S(1)}, bf16[144,768]{1,0:T(8,128)(2,1)S(1)}, u32[]{:S(2)}, u32[]{:S(2)}) collective-permute-start(bf16[144,768]{1,0:T(8,128)(2,1)S(1)} %collective-permute-done.2), channel_id=1, source_target_pairs={{0,56},{8,0},{16,8},{24,16},{32,24},{40,32},{48,40},{56,48},{1,57}... | collective-permute-start | bytes 663560 | tf_op jit(solution)/shard_map/ppermute | solution.py:468
  33.2 3.9 %collective-permute-done.1 = bf16[144,768]{1,0:T(8,128)(2,1)S(1)} collective-permute-done((bf16[144,768]{1,0:T(8,128)(2,1)S(1)}, bf16[144,768]{1,0:T(8,128)(2,1)S(1)}, u32[]{:S(2)}, u32[]{:S(2)}) %collective-permute-start.1) | collective-permute-done | bytes 221216 | tf_op jit(solution)/shard_map/ppermute | solution.py:468
  37.4 1.9 %collective-permute-start.10 = (bf16[192,2048]{1,0:T(8,128)(2,1)S(1)}, bf16[192,2048]{1,0:T(8,128)(2,1)S(1)}, u32[]{:S(2)}, u32[]{:S(2)}) collective-permute-start(bf16[192,2048]{1,0:T(8,128)(2,1)S(1)} %get-tuple-element.49), channel_id=1, source_target_pairs={{0,3},{1,0},{2,1},{3,2},{4,7},{5,4},{6,5},{7,6},{8,11},{9,8},{10,9... | collective-permute-start | bytes 2359304 | tf_op jit(solution)/shard_map/ppermute | solution.py:468
  39.6 3.3 %collective-permute-start.15 = (bf16[144,768]{1,0:T(8,128)(2,1)S(1)}, bf16[144,768]{1,0:T(8,128)(2,1)S(1)}, u32[]{:S(2)}, u32[]{:S(2)}) collective-permute-start(bf16[144,768]{1,0:T(8,128)(2,1)S(1)} %collective-permute-done.3), channel_id=1, source_target_pairs={{0,56},{8,0},{16,8},{24,16},{32,24},{40,32},{48,40},{56,48},{1,57}... | collective-permute-start | bytes 663560 | tf_op jit(solution)/shard_map/ppermute | solution.py:468
  42.9 4.9 %collective-permute-done.7 = bf16[144,768]{1,0:T(8,128)(2,1)S(1)} collective-permute-done((bf16[144,768]{1,0:T(8,128)(2,1)S(1)}, bf16[144,768]{1,0:T(8,128)(2,1)S(1)}, u32[]{:S(2)}, u32[]{:S(2)}) %collective-permute-start.7) | collective-permute-done | bytes 221216 | tf_op jit(solution)/shard_map/ppermute | solution.py:468
  47.9 7.0 %collective-permute-done.8 = bf16[144,768]{1,0:T(8,128)(2,1)S(1)} collective-permute-done((bf16[144,768]{1,0:T(8,128)(2,1)S(1)}, bf16[144,768]{1,0:T(8,128)(2,1)S(1)}, u32[]{:S(2)}, u32[]{:S(2)}) %collective-permute-start.8) | collective-permute-done | bytes 221216 | tf_op jit(solution)/shard_map/ppermute | solution.py:468
  55.3 1.7 %collective-permute-start.11 = (bf16[64,2048]{1,0:T(8,128)(2,1)S(1)}, bf16[64,2048]{1,0:T(8,128)(2,1)S(1)}, u32[]{:S(2)}, u32[]{:S(2)}) collective-permute-start(bf16[64,2048]{1,0:T(8,128)(2,1)S(1)} %slice.14), channel_id=1, source_target_pairs={{0,1},{1,2},{2,3},{3,0},{4,5},{5,6},{6,7},{7,4},{8,9},{9,10},{10,1... | collective-permute-start | bytes 786440 | tf_op jit(solution)/shard_map/ppermute | solution.py:468
  56.9 1.4 %collective-permute-start.12 = (bf16[64,2048]{1,0:T(8,128)(2,1)S(1)}, bf16[64,2048]{1,0:T(8,128)(2,1)S(1)}, u32[]{:S(2)}, u32[]{:S(2)}) collective-permute-start(bf16[64,2048]{1,0:T(8,128)(2,1)S(1)} %slice.15), channel_id=1, source_target_pairs={{0,3},{1,0},{2,1},{3,2},{4,7},{5,4},{6,5},{7,6},{8,11},{9,8},{10,9... | collective-permute-start | bytes 786440 | tf_op jit(solution)/shard_map/ppermute | solution.py:468
  59.7 3.9 %shard_map.76 = (bf16[2048,768]{1,0:T(8,128)(2,1)S(1)}, bf16[1024,768]{1,0:T(8,128)(2,1)S(1)}, f32[40,256]{1,0:T(8,128)S(1)}) custom-call(bf16[128,2048]{1,0:T(8,128)(2,1)S(1)} %get-tuple-element.30.own.refs_0_, bf16[128,2048]{1,0:T(8,128)(2,1)S(1)} %collective-permute-done.5.behind.refs_1_, bf16[128,2048]{1,0:T(8,128)(2,1)S(1)} %collective-permute-done.6.ahead.refs_2_, ...), custom_call_target="tpu_custom_call" | custom-call | flops 402653184 | bytes 1000000 | tf_op jit(solution)/shard_map/pallas_call | solution.py:203
  63.6 1.3 %collective-permute-done.11.first = bf16[64,2048]{1,0:T(8,128)(2,1)S(1)} collective-permute-done((bf16[64,2048]{1,0:T(8,128)(2,1)S(1)}, bf16[64,2048]{1,0:T(8,128)(2,1)S(1)}, u32[]{:S(2)}, u32[]{:S(2)}) %collective-permute-start.11) | collective-permute-done | bytes 262176 | tf_op jit(solution)/shard_map/ppermute | solution.py:468
  65.0 1.1 %collective-permute-done.12.second = bf16[64,2048]{1,0:T(8,128)(2,1)S(1)} collective-permute-done((bf16[64,2048]{1,0:T(8,128)(2,1)S(1)}, bf16[64,2048]{1,0:T(8,128)(2,1)S(1)}, u32[]{:S(2)}, u32[]{:S(2)}) %collective-permute-start.12) | collective-permute-done | bytes 262176 | tf_op jit(solution)/shard_map/ppermute | solution.py:468
  66.1 4.8 %shard_map.77 = (bf16[1040,256]{1,0:T(8,128)(2,1)S(1)}, bf16[1024,256]{1,0:T(8,128)(2,1)S(1)}, f32[16,64,256]{2,1,0:T(8,128)S(1)}, f32[8,16,256]{2,1,0:T(8,128)}) custom-call(bf16[64,2048]{1,0:T(8,128)(2,1)S(1)} %collective-permute-done.11.first, bf16[64,2048]{1,0:T(8,128)(2,1)S(1)} %collective-permute-done.12.second, ...), custom_call_target="tpu_custom_call" | custom-call | flops 452984832 | bytes 7000000 | tf_op jit(solution)/shard_map/pallas_call | solution.py:306
  70.9 0.8 copy-done.1
  71.7 7.9 %all-to-all-start.1 = ((f32[8,16,256]{2,1,0:T(8,128)}), f32[8,16,256]{2,1,0:T(8,128)S(1)}, u32[]{:S(2)}, u32[]{:S(2)}) async-start(f32[8,16,256]{2,1,0:T(8,128)} %get-tuple-element.43), calls=%async_computation.1 | async-start | bytes 262144 | tf_op jit(solution)/shard_map/all_to_all | solution.py:476
  79.6 1.0 copy-done.2
  80.6 1.1 shard_map.78
  81.7 7.0 %all-to-all-done.1.states = f32[8,16,256]{2,1,0:T(8,128)S(1)} async-done(((f32[8,16,256]{2,1,0:T(8,128)}), f32[8,16,256]{2,1,0:T(8,128)S(1)}, u32[]{:S(2)}, u32[]{:S(2)}) %all-to-all-start.1) | async-done | bytes 131104 | tf_op jit(solution)/shard_map/all_to_all | solution.py:476
  88.7 3.4 %shard_map.79 = bf16[8,256,128]{2,1,0:T(8,128)(2,1)S(1)} custom-call(f32[8,16,256]{2,1,0:T(8,128)S(1)} %all-to-all-done.1.states, f32[40,256]{1,0:T(8,128)S(1)} %get-tuple-element.42.rates.table, f32[1024,256]{1,0:T(8,128)S(1)} %get-tuple-element.46.local, f32[16,64,256]{2,1,0:T(8,128)S(1)} %get-tuple-element.47.chunk, ...), custom_call_target="tpu_custom_call" | custom-call | tf_op jit(solution)/shard_map/pallas_call | solution.py:432
  92.1 15.9 %all_to_all.15.pieces = bf16[8,256,128]{2,1,0:T(8,128)(2,1)S(1)} all-to-all(bf16[8,256,128]{2,1,0:T(8,128)(2,1)S(1)} %shard_map.79), channel_id=1, replica_groups=mesh['yl'=2,'co'=2,'z'=8,'yh'=2,'x'=4] {'yh','x'}, dimensions={0} | all-to-all | bytes 1048576 | tf_op jit(solution)/shard_map/all_to_all | solution.py:476
  108.0 0.8 shard_map.80
  (48 shorter events, 6.0 us)
Async XLA Ops:
  0.0 0.9 copy-start.3
  1.7 14.5 %all-to-all-start = ((bf16[16,8,768]{2,1,0:T(8,128)(2,1)}), bf16[16,8,768]{2,1,0:T(8,128)(2,1)S(1)}, u32[]{:S(2)}, u32[]{:S(2)}) async-start(bf16[16,8,768]{2,1,0:T(8,128)(2,1)} %shard_map.74), calls=%async_computation | async-start | bytes 393216 | tf_op jit(solution)/shard_map/all_to_all | solution.py:476
  12.7 1.0 copy-start
  13.7 0.7 copy-start.4
  16.2 20.9 %collective-permute-start.4 = (bf16[128,2048]{1,0:T(8,128)(2,1)S(1)}, bf16[128,2048]{1,0:T(8,128)(2,1)S(1)}, u32[]{:S(2)}, u32[]{:S(2)}) collective-permute-start(bf16[128,2048]{1,0:T(8,128)(2,1)S(1)} %get-tuple-element.30.own.refs_0_), channel_id=1, source_target_pairs={{0,4},{4,0},{1,5},{5,1},{2,6},{6,2},{3,7},{7,3},{8,12},{12,8},{9,1... | collective-permute-start | bytes 1572872 | tf_op jit(solution)/shard_map/ppermute | solution.py:468
  18.1 19.1 %collective-permute-start.5 = (bf16[128,2048]{1,0:T(8,128)(2,1)S(1)}, bf16[128,2048]{1,0:T(8,128)(2,1)S(1)}, u32[]{:S(2)}, u32[]{:S(2)}) collective-permute-start(bf16[128,2048]{1,0:T(8,128)(2,1)S(1)} %get-tuple-element.30.own.refs_0_), channel_id=1, source_target_pairs={{0,1},{1,2},{2,3},{3,0},{4,5},{5,6},{6,7},{7,4},{8,9},{9,10},{10,1... | collective-permute-start | bytes 1572872 | tf_op jit(solution)/shard_map/ppermute | solution.py:468
  19.5 17.6 %collective-permute-start.6 = (bf16[128,2048]{1,0:T(8,128)(2,1)S(1)}, bf16[128,2048]{1,0:T(8,128)(2,1)S(1)}, u32[]{:S(2)}, u32[]{:S(2)}) collective-permute-start(bf16[128,2048]{1,0:T(8,128)(2,1)S(1)} %get-tuple-element.30.own.refs_0_), channel_id=1, source_target_pairs={{0,3},{1,0},{2,1},{3,2},{4,7},{5,4},{6,5},{7,6},{8,11},{9,8},{10,9... | collective-permute-start | bytes 1572872 | tf_op jit(solution)/shard_map/ppermute | solution.py:468
  20.1 9.9 %collective-permute-start = (bf16[144,768]{1,0:T(8,128)(2,1)S(1)}, bf16[144,768]{1,0:T(8,128)(2,1)S(1)}, u32[]{:S(2)}, u32[]{:S(2)}) collective-permute-start(bf16[144,768]{1,0:T(8,128)(2,1)S(1)} %pad_maximum_fusion.2), channel_id=1, source_target_pairs={{0,8},{8,16},{16,24},{24,32},{32,40},{40,48},{48,56},{56,0},{1,9},... | collective-permute-start | bytes 663560 | tf_op jit(solution)/shard_map/ppermute | solution.py:468
  22.0 8.0 %collective-permute-start.2 = (bf16[144,768]{1,0:T(8,128)(2,1)S(1)}, bf16[144,768]{1,0:T(8,128)(2,1)S(1)}, u32[]{:S(2)}, u32[]{:S(2)}) collective-permute-start(bf16[144,768]{1,0:T(8,128)(2,1)S(1)} %pad_maximum_fusion.2), channel_id=1, source_target_pairs={{0,56},{8,0},{16,8},{24,16},{32,24},{40,32},{48,40},{56,48},{1,57}... | collective-permute-start | bytes 663560 | tf_op jit(solution)/shard_map/ppermute | solution.py:468
  30.0 7.1 %collective-permute-start.1 = (bf16[144,768]{1,0:T(8,128)(2,1)S(1)}, bf16[144,768]{1,0:T(8,128)(2,1)S(1)}, u32[]{:S(2)}, u32[]{:S(2)}) collective-permute-start(bf16[144,768]{1,0:T(8,128)(2,1)S(1)} %collective-permute-done), channel_id=1, source_target_pairs={{0,8},{8,16},{16,24},{24,32},{32,40},{40,48},{48,56},{56,0},{1,9},... | collective-permute-start | bytes 663560 | tf_op jit(solution)/shard_map/ppermute | solution.py:468
  30.0 7.1 %collective-permute-start.3 = (bf16[144,768]{1,0:T(8,128)(2,1)S(1)}, bf16[144,768]{1,0:T(8,128)(2,1)S(1)}, u32[]{:S(2)}, u32[]{:S(2)}) collective-permute-start(bf16[144,768]{1,0:T(8,128)(2,1)S(1)} %collective-permute-done.2), channel_id=1, source_target_pairs={{0,56},{8,0},{16,8},{24,16},{32,24},{40,32},{48,40},{56,48},{1,57}... | collective-permute-start | bytes 663560 | tf_op jit(solution)/shard_map/ppermute | solution.py:468
  37.4 17.6 %collective-permute-start.10 = (bf16[192,2048]{1,0:T(8,128)(2,1)S(1)}, bf16[192,2048]{1,0:T(8,128)(2,1)S(1)}, u32[]{:S(2)}, u32[]{:S(2)}) collective-permute-start(bf16[192,2048]{1,0:T(8,128)(2,1)S(1)} %get-tuple-element.49), channel_id=1, source_target_pairs={{0,3},{1,0},{2,1},{3,2},{4,7},{5,4},{6,5},{7,6},{8,11},{9,8},{10,9... | collective-permute-start | bytes 2359304 | tf_op jit(solution)/shard_map/ppermute | solution.py:468
  39.2 15.8 %collective-permute-start.9 = (bf16[192,2048]{1,0:T(8,128)(2,1)S(1)}, bf16[192,2048]{1,0:T(8,128)(2,1)S(1)}, u32[]{:S(2)}, u32[]{:S(2)}) collective-permute-start(bf16[192,2048]{1,0:T(8,128)(2,1)S(1)} %get-tuple-element.50), channel_id=1, source_target_pairs={{0,1},{1,2},{2,3},{3,0},{4,5},{5,6},{6,7},{7,4},{8,9},{9,10},{10,1... | collective-permute-start | bytes 2359304 | tf_op jit(solution)/shard_map/ppermute | solution.py:468
  39.5 8.3 %collective-permute-start.7 = (bf16[144,768]{1,0:T(8,128)(2,1)S(1)}, bf16[144,768]{1,0:T(8,128)(2,1)S(1)}, u32[]{:S(2)}, u32[]{:S(2)}) collective-permute-start(bf16[144,768]{1,0:T(8,128)(2,1)S(1)} %collective-permute-done.1), channel_id=1, source_target_pairs={{0,8},{8,16},{16,24},{24,32},{32,40},{40,48},{48,56},{56,0},{1,9},... | collective-permute-start | bytes 663560 | tf_op jit(solution)/shard_map/ppermute | solution.py:468
  39.6 15.4 %collective-permute-start.15 = (bf16[144,768]{1,0:T(8,128)(2,1)S(1)}, bf16[144,768]{1,0:T(8,128)(2,1)S(1)}, u32[]{:S(2)}, u32[]{:S(2)}) collective-permute-start(bf16[144,768]{1,0:T(8,128)(2,1)S(1)} %collective-permute-done.3), channel_id=1, source_target_pairs={{0,56},{8,0},{16,8},{24,16},{32,24},{40,32},{48,40},{56,48},{1,57}... | collective-permute-start | bytes 663560 | tf_op jit(solution)/shard_map/ppermute | solution.py:468
  47.8 7.1 %collective-permute-start.8 = (bf16[144,768]{1,0:T(8,128)(2,1)S(1)}, bf16[144,768]{1,0:T(8,128)(2,1)S(1)}, u32[]{:S(2)}, u32[]{:S(2)}) collective-permute-start(bf16[144,768]{1,0:T(8,128)(2,1)S(1)} %collective-permute-done.7), channel_id=1, source_target_pairs={{0,8},{8,16},{16,24},{24,32},{32,40},{40,48},{48,56},{56,0},{1,9},... | collective-permute-start | bytes 663560 | tf_op jit(solution)/shard_map/ppermute | solution.py:468
  55.1 4.6 %collective-permute-start.16 = (bf16[8,144,768]{2,1,0:T(8,128)(2,1)S(1)}, bf16[8,144,768]{2,1,0:T(8,128)(2,1)S(1)}, u32[]{:S(2)}, u32[]{:S(2)}) collective-permute-start(bf16[8,144,768]{2,1,0:T(8,128)(2,1)S(1)} %bitcast_dynamic-update-slice_fusion.refs_6_), channel_id=1, source_target_pairs={{0,64},{64,0},{1,65},{65,1},{2,66},{66,2},{3,67},{67,3},{4,68},{68... | collective-permute-start | bytes 5308424 | tf_op jit(solution)/shard_map/ppermute | solution.py:468
  55.3 9.7 %collective-permute-start.11 = (bf16[64,2048]{1,0:T(8,128)(2,1)S(1)}, bf16[64,2048]{1,0:T(8,128)(2,1)S(1)}, u32[]{:S(2)}, u32[]{:S(2)}) collective-permute-start(bf16[64,2048]{1,0:T(8,128)(2,1)S(1)} %slice.14), channel_id=1, source_target_pairs={{0,1},{1,2},{2,3},{3,0},{4,5},{5,6},{6,7},{7,4},{8,9},{9,10},{10,1... | collective-permute-start | bytes 786440 | tf_op jit(solution)/shard_map/ppermute | solution.py:468
  56.9 9.1 %collective-permute-start.12 = (bf16[64,2048]{1,0:T(8,128)(2,1)S(1)}, bf16[64,2048]{1,0:T(8,128)(2,1)S(1)}, u32[]{:S(2)}, u32[]{:S(2)}) collective-permute-start(bf16[64,2048]{1,0:T(8,128)(2,1)S(1)} %slice.15), channel_id=1, source_target_pairs={{0,3},{1,0},{2,1},{3,2},{4,7},{5,4},{6,5},{7,6},{8,11},{9,8},{10,9... | collective-permute-start | bytes 786440 | tf_op jit(solution)/shard_map/ppermute | solution.py:468
  58.4 5.2 %collective-permute-start.13 = (bf16[16,2048]{1,0:T(8,128)(2,1)S(1)}, bf16[16,2048]{1,0:T(8,128)(2,1)S(1)}, u32[]{:S(2)}, u32[]{:S(2)}) collective-permute-start(bf16[16,2048]{1,0:T(8,128)(2,1)S(1)} %shard_map.75), channel_id=1, source_target_pairs={{4,8},{12,16},{20,24},{28,32},{36,40},{44,48},{52,56},{5,9},{13,17... | collective-permute-start | bytes 196616 | tf_op jit(solution)/shard_map/ppermute | solution.py:533
  59.0 4.6 %collective-permute-start.14 = (bf16[16,2048]{1,0:T(8,128)(2,1)S(1)}, bf16[16,2048]{1,0:T(8,128)(2,1)S(1)}, u32[]{:S(2)}, u32[]{:S(2)}) collective-permute-start(bf16[16,2048]{1,0:T(8,128)(2,1)S(1)} %shard_map.75), channel_id=1, source_target_pairs={{4,12},{12,20},{20,28},{28,36},{36,44},{44,52},{52,60},{5,13},{13,... | collective-permute-start | bytes 196616 | tf_op jit(solution)/shard_map/ppermute | solution.py:533
  70.9 0.8 copy-start.1
  71.7 17.0 %all-to-all-start.1 = ((f32[8,16,256]{2,1,0:T(8,128)}), f32[8,16,256]{2,1,0:T(8,128)S(1)}, u32[]{:S(2)}, u32[]{:S(2)}) async-start(f32[8,16,256]{2,1,0:T(8,128)} %get-tuple-element.43), calls=%async_computation.1 | async-start | bytes 262144 | tf_op jit(solution)/shard_map/all_to_all | solution.py:476
  79.6 1.0 copy-start.2

commit v9 on v8

--- a/solution.py
+++ b/solution.py
@@ -220,7 +220,7 @@
 def project_kernel(
     first, second, halo_0, halo_1, w, done, taps, rates,
     query_ref, carried_ref, chunk_ref, state_ref,
-    lhs, proj, decay_s, carry,
+    lhs, proj, decay_s, carry, fade,
 ):
     x, yh = lax.axis_index("x"), lax.axis_index("yh")
     for i, source in enumerate((halo_0, halo_1)):
@@ -257,10 +257,11 @@
         lane0 = pl.multiple_of(l * LANES, LANES)
         here = pl.ds(lane0, LANES)
         carry[...] = jnp.zeros_like(carry)
-
-        @pl.loop(0, PIECES)
-        def _(p):
-            row0 = pl.multiple_of(p * HERE, 16)
+        for m in range(POLES):
+            fade[m] = jnp.exp(-float(CHUNK) * rates[m : m + 1, here] * (sub + 1).astype(F32))
+
+        for p in range(PIECES):
+            row0 = p * HERE
 
             def featured(s):
                 lanes = pl.ds(pl.multiple_of(s * CH + lane0, LANES), LANES)
@@ -271,7 +272,7 @@
             keys, values = featured(0), featured(1)
             pairs = [(a * b).astype(BF16) for a, b in zip(keys, values)]
             for j in range(0, CHUNK, 2):
-                carried_ref[pl.ds(pl.multiple_of(row0 + 8 * j, 16), 16), here] = jnp.concatenate(
+                carried_ref[pl.ds(row0 + 8 * j, 16), here] = jnp.concatenate(
                     pairs[j : j + 2], axis=0
                 )
             carried = [a.astype(F32) for a in pairs]
@@ -281,17 +282,15 @@
                 s = carried[0]
                 for j in range(1, CHUNK):
                     s = s * e + carried[j]
-                a1 = jnp.exp(-float(CHUNK) * rates[m : m + 1, here])
+                a1 = fade[m, 0:1, :]
                 a2 = a1 * a1
                 a4 = a2 * a2
                 s = s + a1 * down(s, 1)
                 s = s + a2 * down(s, 2)
                 s = s + a4 * down(s, 4)
                 start = carry[m]
-                s = s + jnp.exp(
-                    -float(CHUNK) * rates[m : m + 1, here] * (sub + 1).astype(F32)
-                ) * start
-                chunk_ref[m, pl.ds(pl.multiple_of(p * 8, 8), 8), here] = jnp.where(
+                s = s + fade[m] * start
+                chunk_ref[m, pl.ds(p * 8, 8), here] = jnp.where(
                     sub == 0, start, pltpu.roll(s, 1, 0)
                 )
                 carry[m] = jnp.broadcast_to(s[7:8, :], (8, LANES))
@@ -318,6 +317,7 @@
             pltpu.VMEM((ROWS, 2 * CH), F32),
             pltpu.VMEM((POLES, CH), F32),
             pltpu.VMEM((POLES, 8, LANES), F32),
+            pltpu.VMEM((POLES, 8, LANES), F32),
         ],
         compiler_params=params(20),
         cost_estimate=pl.CostEstimate(
@@ -387,7 +387,7 @@
 
 
 def finish_kernel(
-    states, table, local, chunk, gate, out, scr, rates, start_s, decay_s, weight_s
+    states, table, local, chunk, gate, out, scr, begun, rates, start_s, decay_s, weight_s
 ):
     z = lax.axis_index("z")
     rate = table[0:16, :]
@@ -402,29 +402,33 @@
     weight_s[...] = table[16:32, :] * jnp.sqrt(2.0 * rate) * decay
     sub = lax.broadcasted_iota(jnp.int32, (8, LANES), 0)
 
-    @pl.loop(0, PIECES)
-    def _(p):
-        @pl.loop(0, CH // LANES)
-        def _(l):
-            here = pl.ds(pl.multiple_of(l * LANES, LANES), LANES)
-            row0 = pl.multiple_of(p * HERE, 16)
-            age = -float(CHUNK) * (p * 8 + sub).astype(F32)
+    @pl.loop(0, CH // LANES)
+    def _(l):
+        here = pl.ds(pl.multiple_of(l * LANES, LANES), LANES)
+        for m in range(POLES):
+            fade = jnp.exp(-float(CHUNK) * rates[m : m + 1, here] * sub.astype(F32))
+            begun[m] = fade * (start_s[m : m + 1, here] * weight_s[m : m + 1, here])
+        for p in range(PIECES):
+            row0 = p * HERE
+            turned = scr.at[p % 2]
             v, e = [], []
             for m in range(POLES):
-                fade = jnp.exp(rates[m : m + 1, here] * age)
-                at = chunk[m, pl.ds(pl.multiple_of(p * 8, 8), 8), here]
-                v.append((at + fade * start_s[m : m + 1, here]) * weight_s[m : m + 1, here])
+                at = chunk[m, p * 8 : p * 8 + 8, here]
+                v.append(at * weight_s[m : m + 1, here] + begun[m])
                 e.append(decay_s[m : m + 1, here])
+                if p + 1 < PIECES:
+                    begun[m] = begun[m] * jnp.exp(-float(HERE) * rates[m : m + 1, here])
             for j in range(0, CHUNK, 2):
-                gates = gate[pl.ds(pl.multiple_of(row0 + 8 * j, 16), 16), here].astype(F32)
+                gates = gate[row0 + 8 * j : row0 + 8 * j + 16, here].astype(F32)
                 for i in range(2):
                     parts = list(v)
                     while len(parts) > 1:
                         parts = [a + b for a, b in zip(parts[::2], parts[1::2])]
-                    response = rounded(local[pl.ds(row0 + 8 * (j + i), 8), here] + parts[0])
-                    scr[pl.ds(j + i, 8, stride=CHUNK), :] = gates[8 * i : 8 * i + 8] * response
+                    at = row0 + 8 * (j + i)
+                    response = rounded(local[at : at + 8, here] + parts[0])
+                    turned[pl.ds(j + i, 8, stride=CHUNK), :] = gates[8 * i : 8 * i + 8] * response
                     v = [a * b for a, b in zip(v, e)]
-            out[p, here, :] = scr[...].T.astype(BF16)
+            out[p, here, :] = turned[...].T.astype(BF16)
 
 
 def finish(states, table, local, chunk, gate):
@@ -435,7 +439,8 @@
         out_specs=vmem,
         out_shape=jax.ShapeDtypeStruct((PIECES, CH, HERE), BF16),
         scratch_shapes=[
-            pltpu.VMEM((HERE, LANES), F32),
+            pltpu.VMEM((2, HERE, LANES), F32),
+            pltpu.VMEM((POLES, 8, LANES), F32),
             pltpu.VMEM((POLES, CH), F32),
             pltpu.VMEM((POLES, CH), F32),
             pltpu.VMEM((POLES, CH), F32),

time: 110 us -> 107 us (0.973)
  Pallas kernels: 15.4 us -> 12.8 us
    pallas_call x1, Pallas kernels: 3.4 us -> 1.81 us  [finish(): pl.pallas_call(finish_kernel, in_specs=[vmem] * 5, out_specs=vmem, out_sh...]
where the time goes in v9:
time: 107 us; the launch traced here: 106 us
  starting transfers between devices  38.5 us (36%)
  waiting for transfers between devices  30.5 us (29%)
  blocking collectives  15.9 us (15%)
  Pallas kernels  12.8 us (12%)
  local copies, waits for them, and re-layouts  8.13 us (8%)
    ppermute x15, waiting for transfers between devices, shift(): return lax.ppermute(value, axis, ring(lax.axis_size(axis), by))  22.3 us
    ppermute x15, starting transfers between devices, shift(): return lax.ppermute(value, axis, ring(lax.axis_size(axis), by))  21.7 us
    all_to_all x1, blocking collectives, swap(): return lax.all_to_all(value, axes, split_axis=0, concat_axis=0, tiled=True)  15.9 us
    all_to_all x2, starting transfers between devices, swap(): return lax.all_to_all(value, axes, split_axis=0, concat_axis=0, tiled=True)  15.4 us
    all_to_all x2, waiting for transfers between devices, swap(): return lax.all_to_all(value, axes, split_axis=0, concat_axis=0, tiled=True)  8.17 us
    unnamed x17, local copies, waits for them, and re-layouts  4.57 us
    pallas_call x1, Pallas kernels, multiply(): pl.pallas_call(multiply_kernel, in_specs=[vmem] * (PIECE_ARRAYS + 2), out...  3.88 us
    pallas_call x1, Pallas kernels, project(): pl.pallas_call(project_kernel, in_specs=[vmem] * 8, out_specs=[vmem] * 4,...  3.77 us
  transfers between devices with their start and end apart: 19, of which 9 were waited for; matrix products, arithmetic and copies ran while one was open for 3% of the time, Pallas kernels for 5%

profile of v9, /device:TPU:2, one launch (start us, length us, event | category | flops | bytes accessed | tf_op | source)
XLA Modules:
  0.0 106.2 jit_solution(14858384425004277270)
XLA Ops:
  0.0 0.9 copy-done.3
  0.9 0.8 shard_map.74
  1.7 7.5 %all-to-all-start = ((bf16[16,8,768]{2,1,0:T(8,128)(2,1)}), bf16[16,8,768]{2,1,0:T(8,128)(2,1)S(1)}, u32[]{:S(2)}, u32[]{:S(2)}) async-start(bf16[16,8,768]{2,1,0:T(8,128)(2,1)} %shard_map.74), calls=%async_computation | async-start | bytes 393216 | tf_op jit(solution)/shard_map/all_to_all | solution.py:481
  9.2 1.0 reshape.28
  10.4 0.7 tile.12
  12.7 1.0 copy-done
  15.0 1.2 %all-to-all-done = bf16[16,8,768]{2,1,0:T(8,128)(2,1)S(1)} async-done(((bf16[16,8,768]{2,1,0:T(8,128)(2,1)}), bf16[16,8,768]{2,1,0:T(8,128)(2,1)S(1)}, u32[]{:S(2)}, u32[]{:S(2)}) %all-to-all-start) | async-done | bytes 196640 | tf_op jit(solution)/shard_map/all_to_all | solution.py:481
  16.2 1.9 %collective-permute-start.4 = (bf16[128,2048]{1,0:T(8,128)(2,1)S(1)}, bf16[128,2048]{1,0:T(8,128)(2,1)S(1)}, u32[]{:S(2)}, u32[]{:S(2)}) collective-permute-start(bf16[128,2048]{1,0:T(8,128)(2,1)S(1)} %get-tuple-element.30.own.refs_0_), channel_id=1, source_target_pairs={{0,4},{4,0},{1,5},{5,1},{2,6},{6,2},{3,7},{7,3},{8,12},{12,8},{9,1... | collective-permute-start | bytes 1572872 | tf_op jit(solution)/shard_map/ppermute | solution.py:473
  18.1 1.5 %collective-permute-start.5 = (bf16[128,2048]{1,0:T(8,128)(2,1)S(1)}, bf16[128,2048]{1,0:T(8,128)(2,1)S(1)}, u32[]{:S(2)}, u32[]{:S(2)}) collective-permute-start(bf16[128,2048]{1,0:T(8,128)(2,1)S(1)} %get-tuple-element.30.own.refs_0_), channel_id=1, source_target_pairs={{0,1},{1,2},{2,3},{3,0},{4,5},{5,6},{6,7},{7,4},{8,9},{9,10},{10,1... | collective-permute-start | bytes 1572872 | tf_op jit(solution)/shard_map/ppermute | solution.py:473
  20.1 1.9 %collective-permute-start = (bf16[144,768]{1,0:T(8,128)(2,1)S(1)}, bf16[144,768]{1,0:T(8,128)(2,1)S(1)}, u32[]{:S(2)}, u32[]{:S(2)}) collective-permute-start(bf16[144,768]{1,0:T(8,128)(2,1)S(1)} %pad_maximum_fusion.2), channel_id=1, source_target_pairs={{0,8},{8,16},{16,24},{24,32},{32,40},{40,48},{48,56},{56,0},{1,9},... | collective-permute-start | bytes 663560 | tf_op jit(solution)/shard_map/ppermute | solution.py:473
  22.0 3.9 %collective-permute-start.2 = (bf16[144,768]{1,0:T(8,128)(2,1)S(1)}, bf16[144,768]{1,0:T(8,128)(2,1)S(1)}, u32[]{:S(2)}, u32[]{:S(2)}) collective-permute-start(bf16[144,768]{1,0:T(8,128)(2,1)S(1)} %pad_maximum_fusion.2), channel_id=1, source_target_pairs={{0,56},{8,0},{16,8},{24,16},{32,24},{40,32},{48,40},{56,48},{1,57}... | collective-permute-start | bytes 663560 | tf_op jit(solution)/shard_map/ppermute | solution.py:473
  25.9 4.0 %collective-permute-done = bf16[144,768]{1,0:T(8,128)(2,1)S(1)} collective-permute-done((bf16[144,768]{1,0:T(8,128)(2,1)S(1)}, bf16[144,768]{1,0:T(8,128)(2,1)S(1)}, u32[]{:S(2)}, u32[]{:S(2)}) %collective-permute-start) | collective-permute-done | bytes 221216 | tf_op jit(solution)/shard_map/ppermute | solution.py:473
  30.0 3.2 %collective-permute-start.3 = (bf16[144,768]{1,0:T(8,128)(2,1)S(1)}, bf16[144,768]{1,0:T(8,128)(2,1)S(1)}, u32[]{:S(2)}, u32[]{:S(2)}) collective-permute-start(bf16[144,768]{1,0:T(8,128)(2,1)S(1)} %collective-permute-done.2), channel_id=1, source_target_pairs={{0,56},{8,0},{16,8},{24,16},{32,24},{40,32},{48,40},{56,48},{1,57}... | collective-permute-start | bytes 663560 | tf_op jit(solution)/shard_map/ppermute | solution.py:473
  33.2 3.9 %collective-permute-done.1 = bf16[144,768]{1,0:T(8,128)(2,1)S(1)} collective-permute-done((bf16[144,768]{1,0:T(8,128)(2,1)S(1)}, bf16[144,768]{1,0:T(8,128)(2,1)S(1)}, u32[]{:S(2)}, u32[]{:S(2)}) %collective-permute-start.1) | collective-permute-done | bytes 221216 | tf_op jit(solution)/shard_map/ppermute | solution.py:473
  37.4 1.9 %collective-permute-start.10 = (bf16[192,2048]{1,0:T(8,128)(2,1)S(1)}, bf16[192,2048]{1,0:T(8,128)(2,1)S(1)}, u32[]{:S(2)}, u32[]{:S(2)}) collective-permute-start(bf16[192,2048]{1,0:T(8,128)(2,1)S(1)} %get-tuple-element.49), channel_id=1, source_target_pairs={{0,3},{1,0},{2,1},{3,2},{4,7},{5,4},{6,5},{7,6},{8,11},{9,8},{10,9... | collective-permute-start | bytes 2359304 | tf_op jit(solution)/shard_map/ppermute | solution.py:473
  39.6 3.3 %collective-permute-start.15 = (bf16[144,768]{1,0:T(8,128)(2,1)S(1)}, bf16[144,768]{1,0:T(8,128)(2,1)S(1)}, u32[]{:S(2)}, u32[]{:S(2)}) collective-permute-start(bf16[144,768]{1,0:T(8,128)(2,1)S(1)} %collective-permute-done.3), channel_id=1, source_target_pairs={{0,56},{8,0},{16,8},{24,16},{32,24},{40,32},{48,40},{56,48},{1,57}... | collective-permute-start | bytes 663560 | tf_op jit(solution)/shard_map/ppermute | solution.py:473
  42.9 4.9 %collective-permute-done.7 = bf16[144,768]{1,0:T(8,128)(2,1)S(1)} collective-permute-done((bf16[144,768]{1,0:T(8,128)(2,1)S(1)}, bf16[144,768]{1,0:T(8,128)(2,1)S(1)}, u32[]{:S(2)}, u32[]{:S(2)}) %collective-permute-start.7) | collective-permute-done | bytes 221216 | tf_op jit(solution)/shard_map/ppermute | solution.py:473
  47.9 7.0 %collective-permute-done.8 = bf16[144,768]{1,0:T(8,128)(2,1)S(1)} collective-permute-done((bf16[144,768]{1,0:T(8,128)(2,1)S(1)}, bf16[144,768]{1,0:T(8,128)(2,1)S(1)}, u32[]{:S(2)}, u32[]{:S(2)}) %collective-permute-start.8) | collective-permute-done | bytes 221216 | tf_op jit(solution)/shard_map/ppermute | solution.py:473
  55.3 1.7 %collective-permute-start.11 = (bf16[64,2048]{1,0:T(8,128)(2,1)S(1)}, bf16[64,2048]{1,0:T(8,128)(2,1)S(1)}, u32[]{:S(2)}, u32[]{:S(2)}) collective-permute-start(bf16[64,2048]{1,0:T(8,128)(2,1)S(1)} %slice.14), channel_id=1, source_target_pairs={{0,1},{1,2},{2,3},{3,0},{4,5},{5,6},{6,7},{7,4},{8,9},{9,10},{10,1... | collective-permute-start | bytes 786440 | tf_op jit(solution)/shard_map/ppermute | solution.py:473
  56.9 1.4 %collective-permute-start.12 = (bf16[64,2048]{1,0:T(8,128)(2,1)S(1)}, bf16[64,2048]{1,0:T(8,128)(2,1)S(1)}, u32[]{:S(2)}, u32[]{:S(2)}) collective-permute-start(bf16[64,2048]{1,0:T(8,128)(2,1)S(1)} %slice.15), channel_id=1, source_target_pairs={{0,3},{1,0},{2,1},{3,2},{4,7},{5,4},{6,5},{7,6},{8,11},{9,8},{10,9... | collective-permute-start | bytes 786440 | tf_op jit(solution)/shard_map/ppermute | solution.py:473
  59.7 3.9 %shard_map.76 = (bf16[2048,768]{1,0:T(8,128)(2,1)S(1)}, bf16[1024,768]{1,0:T(8,128)(2,1)S(1)}, f32[40,256]{1,0:T(8,128)S(1)}) custom-call(bf16[128,2048]{1,0:T(8,128)(2,1)S(1)} %get-tuple-element.30.own.refs_0_, bf16[128,2048]{1,0:T(8,128)(2,1)S(1)} %collective-permute-done.5.behind.refs_1_, bf16[128,2048]{1,0:T(8,128)(2,1)S(1)} %collective-permute-done.6.ahead.refs_2_, ...), custom_call_target="tpu_custom_call" | custom-call | flops 402653184 | bytes 1000000 | tf_op jit(solution)/shard_map/pallas_call | solution.py:203
  63.6 1.3 %collective-permute-done.11.first = bf16[64,2048]{1,0:T(8,128)(2,1)S(1)} collective-permute-done((bf16[64,2048]{1,0:T(8,128)(2,1)S(1)}, bf16[64,2048]{1,0:T(8,128)(2,1)S(1)}, u32[]{:S(2)}, u32[]{:S(2)}) %collective-permute-start.11) | collective-permute-done | bytes 262176 | tf_op jit(solution)/shard_map/ppermute | solution.py:473
  65.0 1.1 %collective-permute-done.12.second = bf16[64,2048]{1,0:T(8,128)(2,1)S(1)} collective-permute-done((bf16[64,2048]{1,0:T(8,128)(2,1)S(1)}, bf16[64,2048]{1,0:T(8,128)(2,1)S(1)}, u32[]{:S(2)}, u32[]{:S(2)}) %collective-permute-start.12) | collective-permute-done | bytes 262176 | tf_op jit(solution)/shard_map/ppermute | solution.py:473
  66.1 3.8 %shard_map.77 = (bf16[1040,256]{1,0:T(8,128)(2,1)S(1)}, bf16[1024,256]{1,0:T(8,128)(2,1)S(1)}, f32[16,64,256]{2,1,0:T(8,128)S(1)}, f32[8,16,256]{2,1,0:T(8,128)}) custom-call(bf16[64,2048]{1,0:T(8,128)(2,1)S(1)} %collective-permute-done.11.first, bf16[64,2048]{1,0:T(8,128)(2,1)S(1)} %collective-permute-done.12.second, ...), custom_call_target="tpu_custom_call" | custom-call | flops 452984832 | bytes 7000000 | tf_op jit(solution)/shard_map/pallas_call | solution.py:305
  69.8 0.8 copy-done.1
  70.6 7.9 %all-to-all-start.1 = ((f32[8,16,256]{2,1,0:T(8,128)}), f32[8,16,256]{2,1,0:T(8,128)S(1)}, u32[]{:S(2)}, u32[]{:S(2)}) async-start(f32[8,16,256]{2,1,0:T(8,128)} %get-tuple-element.43), calls=%async_computation.1 | async-start | bytes 262144 | tf_op jit(solution)/shard_map/all_to_all | solution.py:481
  78.6 1.0 copy-done.2
  79.6 1.1 %shard_map.78 = (bf16[1024,256]{1,0:T(8,128)(2,1)S(1)}, f32[1024,256]{1,0:T(8,128)S(1)}) custom-call(bf16[1040,256]{1,0:T(8,128)(2,1)S(1)} %get-tuple-element.44.query, bf16[1024,256]{1,0:T(8,128)(2,1)S(1)} %copy-done.2, f32[3,768]{1,0:T(4,128)S(1)} %reshape.29.taps, f32[40,256]{1,0:T(8,128)S(1)} %get-tuple-element.42.rates.table), custom_call_target="tpu_custom_call" | custom-call | flops 10485760 | bytes 3000000 | tf_op jit(solution)/shard_map/pallas_call | solution.py:373
  80.7 7.0 %all-to-all-done.1.states = f32[8,16,256]{2,1,0:T(8,128)S(1)} async-done(((f32[8,16,256]{2,1,0:T(8,128)}), f32[8,16,256]{2,1,0:T(8,128)S(1)}, u32[]{:S(2)}, u32[]{:S(2)}) %all-to-all-start.1) | async-done | bytes 131104 | tf_op jit(solution)/shard_map/all_to_all | solution.py:481
  87.6 1.8 %shard_map.79 = bf16[8,256,128]{2,1,0:T(8,128)(2,1)S(1)} custom-call(f32[8,16,256]{2,1,0:T(8,128)S(1)} %all-to-all-done.1.states, f32[40,256]{1,0:T(8,128)S(1)} %get-tuple-element.42.rates.table, f32[1024,256]{1,0:T(8,128)S(1)} %get-tuple-element.46.local, f32[16,64,256]{2,1,0:T(8,128)S(1)} %get-tuple-element.47.chunk, ...), custom_call_target="tpu_custom_call" | custom-call | tf_op jit(solution)/shard_map/pallas_call | solution.py:436
  89.5 15.9 %all_to_all.15.pieces = bf16[8,256,128]{2,1,0:T(8,128)(2,1)S(1)} all-to-all(bf16[8,256,128]{2,1,0:T(8,128)(2,1)S(1)} %shard_map.79), channel_id=1, replica_groups=mesh['yl'=2,'co'=2,'z'=8,'yh'=2,'x'=4] {'yh','x'}, dimensions={0} | all-to-all | bytes 1048576 | tf_op jit(solution)/shard_map/all_to_all | solution.py:481
  105.4 0.8 shard_map.80
  (48 shorter events, 6.0 us)
Async XLA Ops:
  0.0 0.9 copy-start.3
  1.7 14.5 %all-to-all-start = ((bf16[16,8,768]{2,1,0:T(8,128)(2,1)}), bf16[16,8,768]{2,1,0:T(8,128)(2,1)S(1)}, u32[]{:S(2)}, u32[]{:S(2)}) async-start(bf16[16,8,768]{2,1,0:T(8,128)(2,1)} %shard_map.74), calls=%async_computation | async-start | bytes 393216 | tf_op jit(solution)/shard_map/all_to_all | solution.py:481
  12.7 1.0 copy-start
  13.7 0.7 copy-start.4
  16.2 20.9 %collective-permute-start.4 = (bf16[128,2048]{1,0:T(8,128)(2,1)S(1)}, bf16[128,2048]{1,0:T(8,128)(2,1)S(1)}, u32[]{:S(2)}, u32[]{:S(2)}) collective-permute-start(bf16[128,2048]{1,0:T(8,128)(2,1)S(1)} %get-tuple-element.30.own.refs_0_), channel_id=1, source_target_pairs={{0,4},{4,0},{1,5},{5,1},{2,6},{6,2},{3,7},{7,3},{8,12},{12,8},{9,1... | collective-permute-start | bytes 1572872 | tf_op jit(solution)/shard_map/ppermute | solution.py:473
  18.1 19.1 %collective-permute-start.5 = (bf16[128,2048]{1,0:T(8,128)(2,1)S(1)}, bf16[128,2048]{1,0:T(8,128)(2,1)S(1)}, u32[]{:S(2)}, u32[]{:S(2)}) collective-permute-start(bf16[128,2048]{1,0:T(8,128)(2,1)S(1)} %get-tuple-element.30.own.refs_0_), channel_id=1, source_target_pairs={{0,1},{1,2},{2,3},{3,0},{4,5},{5,6},{6,7},{7,4},{8,9},{9,10},{10,1... | collective-permute-start | bytes 1572872 | tf_op jit(solution)/shard_map/ppermute | solution.py:473
  19.5 17.6 %collective-permute-start.6 = (bf16[128,2048]{1,0:T(8,128)(2,1)S(1)}, bf16[128,2048]{1,0:T(8,128)(2,1)S(1)}, u32[]{:S(2)}, u32[]{:S(2)}) collective-permute-start(bf16[128,2048]{1,0:T(8,128)(2,1)S(1)} %get-tuple-element.30.own.refs_0_), channel_id=1, source_target_pairs={{0,3},{1,0},{2,1},{3,2},{4,7},{5,4},{6,5},{7,6},{8,11},{9,8},{10,9... | collective-permute-start | bytes 1572872 | tf_op jit(solution)/shard_map/ppermute | solution.py:473
  20.1 9.9 %collective-permute-start = (bf16[144,768]{1,0:T(8,128)(2,1)S(1)}, bf16[144,768]{1,0:T(8,128)(2,1)S(1)}, u32[]{:S(2)}, u32[]{:S(2)}) collective-permute-start(bf16[144,768]{1,0:T(8,128)(2,1)S(1)} %pad_maximum_fusion.2), channel_id=1, source_target_pairs={{0,8},{8,16},{16,24},{24,32},{32,40},{40,48},{48,56},{56,0},{1,9},... | collective-permute-start | bytes 663560 | tf_op jit(solution)/shard_map/ppermute | solution.py:473
  22.0 8.0 %collective-permute-start.2 = (bf16[144,768]{1,0:T(8,128)(2,1)S(1)}, bf16[144,768]{1,0:T(8,128)(2,1)S(1)}, u32[]{:S(2)}, u32[]{:S(2)}) collective-permute-start(bf16[144,768]{1,0:T(8,128)(2,1)S(1)} %pad_maximum_fusion.2), channel_id=1, source_target_pairs={{0,56},{8,0},{16,8},{24,16},{32,24},{40,32},{48,40},{56,48},{1,57}... | collective-permute-start | bytes 663560 | tf_op jit(solution)/shard_map/ppermute | solution.py:473
  30.0 7.1 %collective-permute-start.1 = (bf16[144,768]{1,0:T(8,128)(2,1)S(1)}, bf16[144,768]{1,0:T(8,128)(2,1)S(1)}, u32[]{:S(2)}, u32[]{:S(2)}) collective-permute-start(bf16[144,768]{1,0:T(8,128)(2,1)S(1)} %collective-permute-done), channel_id=1, source_target_pairs={{0,8},{8,16},{16,24},{24,32},{32,40},{40,48},{48,56},{56,0},{1,9},... | collective-permute-start | bytes 663560 | tf_op jit(solution)/shard_map/ppermute | solution.py:473
  30.0 7.1 %collective-permute-start.3 = (bf16[144,768]{1,0:T(8,128)(2,1)S(1)}, bf16[144,768]{1,0:T(8,128)(2,1)S(1)}, u32[]{:S(2)}, u32[]{:S(2)}) collective-permute-start(bf16[144,768]{1,0:T(8,128)(2,1)S(1)} %collective-permute-done.2), channel_id=1, source_target_pairs={{0,56},{8,0},{16,8},{24,16},{32,24},{40,32},{48,40},{56,48},{1,57}... | collective-permute-start | bytes 663560 | tf_op jit(solution)/shard_map/ppermute | solution.py:473
  37.4 17.6 %collective-permute-start.10 = (bf16[192,2048]{1,0:T(8,128)(2,1)S(1)}, bf16[192,2048]{1,0:T(8,128)(2,1)S(1)}, u32[]{:S(2)}, u32[]{:S(2)}) collective-permute-start(bf16[192,2048]{1,0:T(8,128)(2,1)S(1)} %get-tuple-element.49), channel_id=1, source_target_pairs={{0,3},{1,0},{2,1},{3,2},{4,7},{5,4},{6,5},{7,6},{8,11},{9,8},{10,9... | collective-permute-start | bytes 2359304 | tf_op jit(solution)/shard_map/ppermute | solution.py:473
  39.2 15.8 %collective-permute-start.9 = (bf16[192,2048]{1,0:T(8,128)(2,1)S(1)}, bf16[192,2048]{1,0:T(8,128)(2,1)S(1)}, u32[]{:S(2)}, u32[]{:S(2)}) collective-permute-start(bf16[192,2048]{1,0:T(8,128)(2,1)S(1)} %get-tuple-element.50), channel_id=1, source_target_pairs={{0,1},{1,2},{2,3},{3,0},{4,5},{5,6},{6,7},{7,4},{8,9},{9,10},{10,1... | collective-permute-start | bytes 2359304 | tf_op jit(solution)/shard_map/ppermute | solution.py:473
  39.5 8.3 %collective-permute-start.7 = (bf16[144,768]{1,0:T(8,128)(2,1)S(1)}, bf16[144,768]{1,0:T(8,128)(2,1)S(1)}, u32[]{:S(2)}, u32[]{:S(2)}) collective-permute-start(bf16[144,768]{1,0:T(8,128)(2,1)S(1)} %collective-permute-done.1), channel_id=1, source_target_pairs={{0,8},{8,16},{16,24},{24,32},{32,40},{40,48},{48,56},{56,0},{1,9},... | collective-permute-start | bytes 663560 | tf_op jit(solution)/shard_map/ppermute | solution.py:473
  39.6 15.4 %collective-permute-start.15 = (bf16[144,768]{1,0:T(8,128)(2,1)S(1)}, bf16[144,768]{1,0:T(8,128)(2,1)S(1)}, u32[]{:S(2)}, u32[]{:S(2)}) collective-permute-start(bf16[144,768]{1,0:T(8,128)(2,1)S(1)} %collective-permute-done.3), channel_id=1, source_target_pairs={{0,56},{8,0},{16,8},{24,16},{32,24},{40,32},{48,40},{56,48},{1,57}... | collective-permute-start | bytes 663560 | tf_op jit(solution)/shard_map/ppermute | solution.py:473
  47.8 7.1 %collective-permute-start.8 = (bf16[144,768]{1,0:T(8,128)(2,1)S(1)}, bf16[144,768]{1,0:T(8,128)(2,1)S(1)}, u32[]{:S(2)}, u32[]{:S(2)}) collective-permute-start(bf16[144,768]{1,0:T(8,128)(2,1)S(1)} %collective-permute-done.7), channel_id=1, source_target_pairs={{0,8},{8,16},{16,24},{24,32},{32,40},{40,48},{48,56},{56,0},{1,9},... | collective-permute-start | bytes 663560 | tf_op jit(solution)/shard_map/ppermute | solution.py:473
  55.1 4.6 %collective-permute-start.16 = (bf16[8,144,768]{2,1,0:T(8,128)(2,1)S(1)}, bf16[8,144,768]{2,1,0:T(8,128)(2,1)S(1)}, u32[]{:S(2)}, u32[]{:S(2)}) collective-permute-start(bf16[8,144,768]{2,1,0:T(8,128)(2,1)S(1)} %bitcast_dynamic-update-slice_fusion.refs_6_), channel_id=1, source_target_pairs={{0,64},{64,0},{1,65},{65,1},{2,66},{66,2},{3,67},{67,3},{4,68},{68... | collective-permute-start | bytes 5308424 | tf_op jit(solution)/shard_map/ppermute | solution.py:473
  55.3 9.7 %collective-permute-start.11 = (bf16[64,2048]{1,0:T(8,128)(2,1)S(1)}, bf16[64,2048]{1,0:T(8,128)(2,1)S(1)}, u32[]{:S(2)}, u32[]{:S(2)}) collective-permute-start(bf16[64,2048]{1,0:T(8,128)(2,1)S(1)} %slice.14), channel_id=1, source_target_pairs={{0,1},{1,2},{2,3},{3,0},{4,5},{5,6},{6,7},{7,4},{8,9},{9,10},{10,1... | collective-permute-start | bytes 786440 | tf_op jit(solution)/shard_map/ppermute | solution.py:473
  56.9 9.1 %collective-permute-start.12 = (bf16[64,2048]{1,0:T(8,128)(2,1)S(1)}, bf16[64,2048]{1,0:T(8,128)(2,1)S(1)}, u32[]{:S(2)}, u32[]{:S(2)}) collective-permute-start(bf16[64,2048]{1,0:T(8,128)(2,1)S(1)} %slice.15), channel_id=1, source_target_pairs={{0,3},{1,0},{2,1},{3,2},{4,7},{5,4},{6,5},{7,6},{8,11},{9,8},{10,9... | collective-permute-start | bytes 786440 | tf_op jit(solution)/shard_map/ppermute | solution.py:473
  58.4 5.2 %collective-permute-start.13 = (bf16[16,2048]{1,0:T(8,128)(2,1)S(1)}, bf16[16,2048]{1,0:T(8,128)(2,1)S(1)}, u32[]{:S(2)}, u32[]{:S(2)}) collective-permute-start(bf16[16,2048]{1,0:T(8,128)(2,1)S(1)} %shard_map.75), channel_id=1, source_target_pairs={{4,8},{12,16},{20,24},{28,32},{36,40},{44,48},{52,56},{5,9},{13,17... | collective-permute-start | bytes 196616 | tf_op jit(solution)/shard_map/ppermute | solution.py:538
  59.0 4.6 %collective-permute-start.14 = (bf16[16,2048]{1,0:T(8,128)(2,1)S(1)}, bf16[16,2048]{1,0:T(8,128)(2,1)S(1)}, u32[]{:S(2)}, u32[]{:S(2)}) collective-permute-start(bf16[16,2048]{1,0:T(8,128)(2,1)S(1)} %shard_map.75), channel_id=1, source_target_pairs={{4,12},{12,20},{20,28},{28,36},{36,44},{44,52},{52,60},{5,13},{13,... | collective-permute-start | bytes 196616 | tf_op jit(solution)/shard_map/ppermute | solution.py:538
  69.8 0.8 copy-start.1
  70.6 17.0 %all-to-all-start.1 = ((f32[8,16,256]{2,1,0:T(8,128)}), f32[8,16,256]{2,1,0:T(8,128)S(1)}, u32[]{:S(2)}, u32[]{:S(2)}) async-start(f32[8,16,256]{2,1,0:T(8,128)} %get-tuple-element.43), calls=%async_computation.1 | async-start | bytes 262144 | tf_op jit(solution)/shard_map/all_to_all | solution.py:481
  78.6 1.0 copy-start.2

commit v10 on v9

--- a/solution.py
+++ b/solution.py
@@ -219,7 +219,7 @@
 
 def project_kernel(
     first, second, halo_0, halo_1, w, done, taps, rates,
-    query_ref, carried_ref, chunk_ref, state_ref,
+    both_ref, chunk_ref, state_ref,
     lhs, proj, decay_s, carry, fade,
 ):
     x, yh = lax.axis_index("x"), lax.axis_index("yh")
@@ -238,9 +238,9 @@
         cols = slice(s * CH, (s + 1) * CH)
         late = jnp.dot(lhs[...], w[:, cols], preferred_element_type=F32).astype(BF16)
         if s == 0:
-            query_ref[HALO:, :] = done[:, cols]
-            query_ref[0:HALO, :] = late[0:HALO]
-            query_ref[rows, :] = late[HALO:]
+            both_ref[HALO:ROWS, :] = done[:, cols]
+            both_ref[0:HALO, :] = late[0:HALO]
+            both_ref[rows, :] = late[HALO:]
         else:
             to = slice((s - 1) * CH, s * CH)
             proj[HALO:, to] = done[:, cols].astype(F32)
@@ -272,7 +272,7 @@
             keys, values = featured(0), featured(1)
             pairs = [(a * b).astype(BF16) for a, b in zip(keys, values)]
             for j in range(0, CHUNK, 2):
-                carried_ref[pl.ds(row0 + 8 * j, 16), here] = jnp.concatenate(
+                both_ref[pl.ds(ROWS + row0 + 8 * j, 16), here] = jnp.concatenate(
                     pairs[j : j + 2], axis=0
                 )
             carried = [a.astype(F32) for a in pairs]
@@ -305,10 +305,9 @@
     return pl.pallas_call(
         project_kernel,
         in_specs=[vmem] * 8,
-        out_specs=[vmem] * 4,
+        out_specs=[vmem] * 3,
         out_shape=[
-            jax.ShapeDtypeStruct((ROWS, CH), BF16),
-            jax.ShapeDtypeStruct((SPAN, CH), BF16),
+            jax.ShapeDtypeStruct((ROWS + SPAN, CH), BF16),
             jax.ShapeDtypeStruct((POLES, SPAN // CHUNK, CH), F32),
             jax.ShapeDtypeStruct((NZ, POLES, CH), F32),
         ],
@@ -326,7 +325,7 @@
     )(first, second, *halo, w, done, taps, rates)
 
 
-def direct_kernel(query, carried, taps, table, gate_ref, local_ref, taps_s):
+def direct_kernel(both, taps, table, gate_ref, local_ref, taps_s):
     rate = table[0:16, :]
     decay = jnp.exp(-rate)
     power = table[16:32, :] * jnp.sqrt(2.0 * rate)
@@ -347,19 +346,19 @@
 
             t = [taps[i : i + 1, here] for i in range(3)]
 
-            def rows(ref, count):
+            def rows(first, count):
                 pairs = [
-                    ref[pl.ds(pl.multiple_of(row0 + 16 * i, 16), 16), here].astype(F32)
+                    both[pl.ds(pl.multiple_of(first + row0 + 16 * i, 16), 16), here].astype(F32)
                     for i in range(count)
                 ]
                 return [half for pair in pairs for half in (pair[:8], pair[8:])]
 
-            queries = filtered(rows(query, 9), t, sub)
+            queries = filtered(rows(0, 9), t, sub)
             for j in range(0, CHUNK, 2):
                 gate_ref[pl.ds(pl.multiple_of(row0 + 8 * j, 16), 16), here] = jnp.concatenate(
                     queries[j : j + 2], axis=0
                 ).astype(BF16)
-            x = rows(carried, 8)
+            x = rows(ROWS, 8)
             k = [taps_s[i : i + 1, here] for i in range(CHUNK)]
             for j in range(CHUNK):
                 acc = k[0] * x[j]
@@ -368,11 +367,11 @@
                 local_ref[pl.ds(row0 + 8 * j, 8), here] = acc
 
 
-def direct(query, carried, taps, table):
+def direct(both, taps, table):
     vmem = pl.BlockSpec(memory_space=pltpu.VMEM)
     return pl.pallas_call(
         direct_kernel,
-        in_specs=[vmem] * 4,
+        in_specs=[vmem] * 3,
         out_specs=[vmem] * 2,
         out_shape=[
             jax.ShapeDtypeStruct((SPAN, CH), BF16),
@@ -383,12 +382,15 @@
         cost_estimate=pl.CostEstimate(
             flops=40 * SPAN * CH, bytes_accessed=3_000_000, transcendentals=0
         ),
-    )(query, carried, taps, table)
+    )(both, taps, table)
 
 
 def finish_kernel(
-    states, table, local, chunk, gate, out, scr, begun, rates, start_s, decay_s, weight_s
+    states, table, local, chunk, gate_far, out,
+    scr, begun, rates, start_s, decay_s, weight_s, gate, sem,
 ):
+    copy = pltpu.make_async_copy(gate_far, gate, sem)
+    copy.start()
     z = lax.axis_index("z")
     rate = table[0:16, :]
     rates[...] = rate
@@ -401,6 +403,8 @@
     decay_s[...] = decay
     weight_s[...] = table[16:32, :] * jnp.sqrt(2.0 * rate) * decay
     sub = lax.broadcasted_iota(jnp.int32, (8, LANES), 0)
+
+    copy.wait()
 
     @pl.loop(0, CH // LANES)
     def _(l):
@@ -435,7 +439,7 @@
     vmem = pl.BlockSpec(memory_space=pltpu.VMEM)
     return pl.pallas_call(
         finish_kernel,
-        in_specs=[vmem] * 5,
+        in_specs=[vmem] * 4 + [pl.BlockSpec(memory_space=pltpu.HBM)],
         out_specs=vmem,
         out_shape=jax.ShapeDtypeStruct((PIECES, CH, HERE), BF16),
         scratch_shapes=[
@@ -445,6 +449,8 @@
             pltpu.VMEM((POLES, CH), F32),
             pltpu.VMEM((POLES, CH), F32),
             pltpu.VMEM((POLES, CH), F32),
+            pltpu.VMEM((SPAN, CH), BF16),
+            pltpu.SemaphoreType.DMA,
         ],
         compiler_params=params(10),
     )(states, table, local, chunk, gate)
@@ -543,9 +549,9 @@
     arrays = [own, own_1, own_3, partner, mixed_1, mixed_3]
 
     w, done, table = multiply(arrays, weights)
-    query, carried, chunk, state = project(first, second, halo, w, done, taps, table)
+    both, chunk, state = project(first, second, halo, w, done, taps, table)
     states = swap(state, "z")
-    gate, local = direct(query, carried, taps, table)
+    gate, local = direct(both, taps, table)
     pieces = finish(states, table, local, chunk, gate)
     return place(swap(pieces, ("yh", "x")))
 

time: 107 us -> 107 us (level)
  no operation moved by 1% of the time
where the time goes in v10:
time: 107 us
  starting transfers between devices  38.5 us (36%)
  waiting for transfers between devices  30.7 us (29%)
  blocking collectives  15.9 us (15%)
  Pallas kernels  13 us (12%)
  local copies, waits for them, and re-layouts  8.13 us (8%)
    ppermute x15, waiting for transfers between devices, shift(): return lax.ppermute(value, axis, ring(lax.axis_size(axis), by))  22.3 us
    ppermute x15, starting transfers between devices, shift(): return lax.ppermute(value, axis, ring(lax.axis_size(axis), by))  21.7 us
    all_to_all x1, blocking collectives, swap(): return lax.all_to_all(value, axes, split_axis=0, concat_axis=0, tiled=True)  15.9 us
    all_to_all x2, starting transfers between devices, swap(): return lax.all_to_all(value, axes, split_axis=0, concat_axis=0, tiled=True)  15.4 us
    all_to_all x2, waiting for transfers between devices, swap(): return lax.all_to_all(value, axes, split_axis=0, concat_axis=0, tiled=True)  8.34 us
    unnamed x17, local copies, waits for them, and re-layouts  4.57 us
    pallas_call x1, Pallas kernels, multiply(): pl.pallas_call(multiply_kernel, in_specs=[vmem] * (PIECE_ARRAYS + 2), out...  3.88 us
    pallas_call x1, Pallas kernels, project(): pl.pallas_call(project_kernel, in_specs=[vmem] * 8, out_specs=[vmem] * 3,...  3.77 us
  transfers between devices with their start and end apart: 19, of which 9 were waited for; matrix products, arithmetic and copies ran while one was open for 3% of the time, Pallas kernels for 5%

profile of v10, /device:TPU:2, one launch (start us, length us, event | category | flops | bytes accessed | tf_op | source)
XLA Modules:
  0.0 106.5 jit_solution(5238283843831048710)
XLA Ops:
  0.0 0.9 copy-done.3
  0.9 0.8 shard_map.74
  1.7 7.5 %all-to-all-start = ((bf16[16,8,768]{2,1,0:T(8,128)(2,1)}), bf16[16,8,768]{2,1,0:T(8,128)(2,1)S(1)}, u32[]{:S(2)}, u32[]{:S(2)}) async-start(bf16[16,8,768]{2,1,0:T(8,128)(2,1)} %shard_map.74), calls=%async_computation | async-start | bytes 393216 | tf_op jit(solution)/shard_map/all_to_all | solution.py:487
  9.2 1.0 reshape.28
  10.4 0.7 tile.12
  12.7 1.0 copy-done.2
  15.0 1.2 %all-to-all-done = bf16[16,8,768]{2,1,0:T(8,128)(2,1)S(1)} async-done(((bf16[16,8,768]{2,1,0:T(8,128)(2,1)}), bf16[16,8,768]{2,1,0:T(8,128)(2,1)S(1)}, u32[]{:S(2)}, u32[]{:S(2)}) %all-to-all-start) | async-done | bytes 196640 | tf_op jit(solution)/shard_map/all_to_all | solution.py:487
  16.2 1.9 %collective-permute-start.4 = (bf16[128,2048]{1,0:T(8,128)(2,1)S(1)}, bf16[128,2048]{1,0:T(8,128)(2,1)S(1)}, u32[]{:S(2)}, u32[]{:S(2)}) collective-permute-start(bf16[128,2048]{1,0:T(8,128)(2,1)S(1)} %get-tuple-element.29.own.refs_0_), channel_id=1, source_target_pairs={{0,4},{4,0},{1,5},{5,1},{2,6},{6,2},{3,7},{7,3},{8,12},{12,8},{9,1... | collective-permute-start | bytes 1572872 | tf_op jit(solution)/shard_map/ppermute | solution.py:479
  18.1 1.5 %collective-permute-start.5 = (bf16[128,2048]{1,0:T(8,128)(2,1)S(1)}, bf16[128,2048]{1,0:T(8,128)(2,1)S(1)}, u32[]{:S(2)}, u32[]{:S(2)}) collective-permute-start(bf16[128,2048]{1,0:T(8,128)(2,1)S(1)} %get-tuple-element.29.own.refs_0_), channel_id=1, source_target_pairs={{0,1},{1,2},{2,3},{3,0},{4,5},{5,6},{6,7},{7,4},{8,9},{9,10},{10,1... | collective-permute-start | bytes 1572872 | tf_op jit(solution)/shard_map/ppermute | solution.py:479
  20.1 1.9 %collective-permute-start = (bf16[144,768]{1,0:T(8,128)(2,1)S(1)}, bf16[144,768]{1,0:T(8,128)(2,1)S(1)}, u32[]{:S(2)}, u32[]{:S(2)}) collective-permute-start(bf16[144,768]{1,0:T(8,128)(2,1)S(1)} %pad_maximum_fusion.2), channel_id=1, source_target_pairs={{0,8},{8,16},{16,24},{24,32},{32,40},{40,48},{48,56},{56,0},{1,9},... | collective-permute-start | bytes 663560 | tf_op jit(solution)/shard_map/ppermute | solution.py:479
  22.0 3.9 %collective-permute-start.2 = (bf16[144,768]{1,0:T(8,128)(2,1)S(1)}, bf16[144,768]{1,0:T(8,128)(2,1)S(1)}, u32[]{:S(2)}, u32[]{:S(2)}) collective-permute-start(bf16[144,768]{1,0:T(8,128)(2,1)S(1)} %pad_maximum_fusion.2), channel_id=1, source_target_pairs={{0,56},{8,0},{16,8},{24,16},{32,24},{40,32},{48,40},{56,48},{1,57}... | collective-permute-start | bytes 663560 | tf_op jit(solution)/shard_map/ppermute | solution.py:479
  25.9 4.0 %collective-permute-done = bf16[144,768]{1,0:T(8,128)(2,1)S(1)} collective-permute-done((bf16[144,768]{1,0:T(8,128)(2,1)S(1)}, bf16[144,768]{1,0:T(8,128)(2,1)S(1)}, u32[]{:S(2)}, u32[]{:S(2)}) %collective-permute-start) | collective-permute-done | bytes 221216 | tf_op jit(solution)/shard_map/ppermute | solution.py:479
  30.0 3.2 %collective-permute-start.3 = (bf16[144,768]{1,0:T(8,128)(2,1)S(1)}, bf16[144,768]{1,0:T(8,128)(2,1)S(1)}, u32[]{:S(2)}, u32[]{:S(2)}) collective-permute-start(bf16[144,768]{1,0:T(8,128)(2,1)S(1)} %collective-permute-done.2), channel_id=1, source_target_pairs={{0,56},{8,0},{16,8},{24,16},{32,24},{40,32},{48,40},{56,48},{1,57}... | collective-permute-start | bytes 663560 | tf_op jit(solution)/shard_map/ppermute | solution.py:479
  33.2 3.9 %collective-permute-done.1 = bf16[144,768]{1,0:T(8,128)(2,1)S(1)} collective-permute-done((bf16[144,768]{1,0:T(8,128)(2,1)S(1)}, bf16[144,768]{1,0:T(8,128)(2,1)S(1)}, u32[]{:S(2)}, u32[]{:S(2)}) %collective-permute-start.1) | collective-permute-done | bytes 221216 | tf_op jit(solution)/shard_map/ppermute | solution.py:479
  37.4 1.9 %collective-permute-start.10 = (bf16[192,2048]{1,0:T(8,128)(2,1)S(1)}, bf16[192,2048]{1,0:T(8,128)(2,1)S(1)}, u32[]{:S(2)}, u32[]{:S(2)}) collective-permute-start(bf16[192,2048]{1,0:T(8,128)(2,1)S(1)} %get-tuple-element.47), channel_id=1, source_target_pairs={{0,3},{1,0},{2,1},{3,2},{4,7},{5,4},{6,5},{7,6},{8,11},{9,8},{10,9... | collective-permute-start | bytes 2359304 | tf_op jit(solution)/shard_map/ppermute | solution.py:479
  39.6 3.3 %collective-permute-start.15 = (bf16[144,768]{1,0:T(8,128)(2,1)S(1)}, bf16[144,768]{1,0:T(8,128)(2,1)S(1)}, u32[]{:S(2)}, u32[]{:S(2)}) collective-permute-start(bf16[144,768]{1,0:T(8,128)(2,1)S(1)} %collective-permute-done.3), channel_id=1, source_target_pairs={{0,56},{8,0},{16,8},{24,16},{32,24},{40,32},{48,40},{56,48},{1,57}... | collective-permute-start | bytes 663560 | tf_op jit(solution)/shard_map/ppermute | solution.py:479
  42.9 4.9 %collective-permute-done.7 = bf16[144,768]{1,0:T(8,128)(2,1)S(1)} collective-permute-done((bf16[144,768]{1,0:T(8,128)(2,1)S(1)}, bf16[144,768]{1,0:T(8,128)(2,1)S(1)}, u32[]{:S(2)}, u32[]{:S(2)}) %collective-permute-start.7) | collective-permute-done | bytes 221216 | tf_op jit(solution)/shard_map/ppermute | solution.py:479
  47.9 7.0 %collective-permute-done.8 = bf16[144,768]{1,0:T(8,128)(2,1)S(1)} collective-permute-done((bf16[144,768]{1,0:T(8,128)(2,1)S(1)}, bf16[144,768]{1,0:T(8,128)(2,1)S(1)}, u32[]{:S(2)}, u32[]{:S(2)}) %collective-permute-start.8) | collective-permute-done | bytes 221216 | tf_op jit(solution)/shard_map/ppermute | solution.py:479
  55.3 1.7 %collective-permute-start.11 = (bf16[64,2048]{1,0:T(8,128)(2,1)S(1)}, bf16[64,2048]{1,0:T(8,128)(2,1)S(1)}, u32[]{:S(2)}, u32[]{:S(2)}) collective-permute-start(bf16[64,2048]{1,0:T(8,128)(2,1)S(1)} %slice.14), channel_id=1, source_target_pairs={{0,1},{1,2},{2,3},{3,0},{4,5},{5,6},{6,7},{7,4},{8,9},{9,10},{10,1... | collective-permute-start | bytes 786440 | tf_op jit(solution)/shard_map/ppermute | solution.py:479
  56.9 1.4 %collective-permute-start.12 = (bf16[64,2048]{1,0:T(8,128)(2,1)S(1)}, bf16[64,2048]{1,0:T(8,128)(2,1)S(1)}, u32[]{:S(2)}, u32[]{:S(2)}) collective-permute-start(bf16[64,2048]{1,0:T(8,128)(2,1)S(1)} %slice.15), channel_id=1, source_target_pairs={{0,3},{1,0},{2,1},{3,2},{4,7},{5,4},{6,5},{7,6},{8,11},{9,8},{10,9... | collective-permute-start | bytes 786440 | tf_op jit(solution)/shard_map/ppermute | solution.py:479
  59.7 3.9 %shard_map.76 = (bf16[2048,768]{1,0:T(8,128)(2,1)S(1)}, bf16[1024,768]{1,0:T(8,128)(2,1)S(1)}, f32[40,256]{1,0:T(8,128)S(1)}) custom-call(bf16[128,2048]{1,0:T(8,128)(2,1)S(1)} %get-tuple-element.29.own.refs_0_, bf16[128,2048]{1,0:T(8,128)(2,1)S(1)} %collective-permute-done.5.behind.refs_1_, bf16[128,2048]{1,0:T(8,128)(2,1)S(1)} %collective-permute-done.6.ahead.refs_2_, ...), custom_call_target="tpu_custom_call" | custom-call | flops 402653184 | bytes 1000000 | tf_op jit(solution)/shard_map/pallas_call | solution.py:203
  63.6 1.3 %collective-permute-done.11.first = bf16[64,2048]{1,0:T(8,128)(2,1)S(1)} collective-permute-done((bf16[64,2048]{1,0:T(8,128)(2,1)S(1)}, bf16[64,2048]{1,0:T(8,128)(2,1)S(1)}, u32[]{:S(2)}, u32[]{:S(2)}) %collective-permute-start.11) | collective-permute-done | bytes 262176 | tf_op jit(solution)/shard_map/ppermute | solution.py:479
  65.0 1.1 %collective-permute-done.12.second = bf16[64,2048]{1,0:T(8,128)(2,1)S(1)} collective-permute-done((bf16[64,2048]{1,0:T(8,128)(2,1)S(1)}, bf16[64,2048]{1,0:T(8,128)(2,1)S(1)}, u32[]{:S(2)}, u32[]{:S(2)}) %collective-permute-start.12) | collective-permute-done | bytes 262176 | tf_op jit(solution)/shard_map/ppermute | solution.py:479
  66.1 3.8 %shard_map.77 = (bf16[2064,256]{1,0:T(8,128)(2,1)S(1)}, f32[16,64,256]{2,1,0:T(8,128)S(1)}, f32[8,16,256]{2,1,0:T(8,128)}) custom-call(bf16[64,2048]{1,0:T(8,128)(2,1)S(1)} %collective-permute-done.11.first, bf16[64,2048]{1,0:T(8,128)(2,1)S(1)} %collective-permute-done.12.second, bf16[16,2048]{1,0:T(8,128)(2,1)S(1)} %collective-permute-done.13.halo_0, ...), custom_call_target="tpu_custom_call" | custom-call | flops 452984832 | bytes 7000000 | tf_op jit(solution)/shard_map/pallas_call | solution.py:305
  69.8 7.9 %all-to-all-start.1 = ((f32[8,16,256]{2,1,0:T(8,128)}), f32[8,16,256]{2,1,0:T(8,128)S(1)}, u32[]{:S(2)}, u32[]{:S(2)}) async-start(f32[8,16,256]{2,1,0:T(8,128)} %get-tuple-element.42), calls=%async_computation.1 | async-start | bytes 262144 | tf_op jit(solution)/shard_map/all_to_all | solution.py:487
  77.8 1.1 %shard_map.78 = (bf16[1024,256]{1,0:T(8,128)(2,1)S(1)}, f32[1024,256]{1,0:T(8,128)S(1)}) custom-call(bf16[2064,256]{1,0:T(8,128)(2,1)S(1)} %get-tuple-element.43.both, f32[3,768]{1,0:T(4,128)S(1)} %reshape.29.taps, f32[40,256]{1,0:T(8,128)S(1)} %get-tuple-element.41.rates.table), custom_call_target="tpu_custom_call" | custom-call | flops 10485760 | bytes 3000000 | tf_op jit(solution)/shard_map/pallas_call | solution.py:372
  78.9 0.8 copy-done
  79.7 7.1 %all-to-all-done.1.states = f32[8,16,256]{2,1,0:T(8,128)S(1)} async-done(((f32[8,16,256]{2,1,0:T(8,128)}), f32[8,16,256]{2,1,0:T(8,128)S(1)}, u32[]{:S(2)}, u32[]{:S(2)}) %all-to-all-start.1) | async-done | bytes 131104 | tf_op jit(solution)/shard_map/all_to_all | solution.py:487
  86.9 1.0 copy-done.1
  87.9 1.9 %shard_map.79 = bf16[8,256,128]{2,1,0:T(8,128)(2,1)S(1)} custom-call(f32[8,16,256]{2,1,0:T(8,128)S(1)} %all-to-all-done.1.states, f32[40,256]{1,0:T(8,128)S(1)} %get-tuple-element.41.rates.table, f32[1024,256]{1,0:T(8,128)S(1)} %get-tuple-element.44.local, f32[16,64,256]{2,1,0:T(8,128)S(1)} %get-tuple-element.45.chunk, bf16[1024,256]{1,0:T(8,128)(2,1)S(1)} %copy-done.1), custom_call_target="tpu_custom_call" | custom-call | tf_op jit(solution)/shard_map/pallas_call | solution.py:440
  89.8 15.9 %all_to_all.15.pieces = bf16[8,256,128]{2,1,0:T(8,128)(2,1)S(1)} all-to-all(bf16[8,256,128]{2,1,0:T(8,128)(2,1)S(1)} %shard_map.79), channel_id=1, replica_groups=mesh['yl'=2,'co'=2,'z'=8,'yh'=2,'x'=4] {'yh','x'}, dimensions={0} | all-to-all | bytes 1048576 | tf_op jit(solution)/shard_map/all_to_all | solution.py:487
  105.7 0.8 shard_map.80
  (48 shorter events, 6.0 us)
Async XLA Ops:
  0.0 0.9 copy-start.3
  1.7 14.5 %all-to-all-start = ((bf16[16,8,768]{2,1,0:T(8,128)(2,1)}), bf16[16,8,768]{2,1,0:T(8,128)(2,1)S(1)}, u32[]{:S(2)}, u32[]{:S(2)}) async-start(bf16[16,8,768]{2,1,0:T(8,128)(2,1)} %shard_map.74), calls=%async_computation | async-start | bytes 393216 | tf_op jit(solution)/shard_map/all_to_all | solution.py:487
  12.7 1.0 copy-start.2
  13.7 0.7 copy-start.4
  16.2 20.9 %collective-permute-start.4 = (bf16[128,2048]{1,0:T(8,128)(2,1)S(1)}, bf16[128,2048]{1,0:T(8,128)(2,1)S(1)}, u32[]{:S(2)}, u32[]{:S(2)}) collective-permute-start(bf16[128,2048]{1,0:T(8,128)(2,1)S(1)} %get-tuple-element.29.own.refs_0_), channel_id=1, source_target_pairs={{0,4},{4,0},{1,5},{5,1},{2,6},{6,2},{3,7},{7,3},{8,12},{12,8},{9,1... | collective-permute-start | bytes 1572872 | tf_op jit(solution)/shard_map/ppermute | solution.py:479
  18.1 19.1 %collective-permute-start.5 = (bf16[128,2048]{1,0:T(8,128)(2,1)S(1)}, bf16[128,2048]{1,0:T(8,128)(2,1)S(1)}, u32[]{:S(2)}, u32[]{:S(2)}) collective-permute-start(bf16[128,2048]{1,0:T(8,128)(2,1)S(1)} %get-tuple-element.29.own.refs_0_), channel_id=1, source_target_pairs={{0,1},{1,2},{2,3},{3,0},{4,5},{5,6},{6,7},{7,4},{8,9},{9,10},{10,1... | collective-permute-start | bytes 1572872 | tf_op jit(solution)/shard_map/ppermute | solution.py:479
  19.5 17.6 %collective-permute-start.6 = (bf16[128,2048]{1,0:T(8,128)(2,1)S(1)}, bf16[128,2048]{1,0:T(8,128)(2,1)S(1)}, u32[]{:S(2)}, u32[]{:S(2)}) collective-permute-start(bf16[128,2048]{1,0:T(8,128)(2,1)S(1)} %get-tuple-element.29.own.refs_0_), channel_id=1, source_target_pairs={{0,3},{1,0},{2,1},{3,2},{4,7},{5,4},{6,5},{7,6},{8,11},{9,8},{10,9... | collective-permute-start | bytes 1572872 | tf_op jit(solution)/shard_map/ppermute | solution.py:479
  20.1 9.9 %collective-permute-start = (bf16[144,768]{1,0:T(8,128)(2,1)S(1)}, bf16[144,768]{1,0:T(8,128)(2,1)S(1)}, u32[]{:S(2)}, u32[]{:S(2)}) collective-permute-start(bf16[144,768]{1,0:T(8,128)(2,1)S(1)} %pad_maximum_fusion.2), channel_id=1, source_target_pairs={{0,8},{8,16},{16,24},{24,32},{32,40},{40,48},{48,56},{56,0},{1,9},... | collective-permute-start | bytes 663560 | tf_op jit(solution)/shard_map/ppermute | solution.py:479
  22.0 8.0 %collective-permute-start.2 = (bf16[144,768]{1,0:T(8,128)(2,1)S(1)}, bf16[144,768]{1,0:T(8,128)(2,1)S(1)}, u32[]{:S(2)}, u32[]{:S(2)}) collective-permute-start(bf16[144,768]{1,0:T(8,128)(2,1)S(1)} %pad_maximum_fusion.2), channel_id=1, source_target_pairs={{0,56},{8,0},{16,8},{24,16},{32,24},{40,32},{48,40},{56,48},{1,57}... | collective-permute-start | bytes 663560 | tf_op jit(solution)/shard_map/ppermute | solution.py:479
  30.0 7.1 %collective-permute-start.1 = (bf16[144,768]{1,0:T(8,128)(2,1)S(1)}, bf16[144,768]{1,0:T(8,128)(2,1)S(1)}, u32[]{:S(2)}, u32[]{:S(2)}) collective-permute-start(bf16[144,768]{1,0:T(8,128)(2,1)S(1)} %collective-permute-done), channel_id=1, source_target_pairs={{0,8},{8,16},{16,24},{24,32},{32,40},{40,48},{48,56},{56,0},{1,9},... | collective-permute-start | bytes 663560 | tf_op jit(solution)/shard_map/ppermute | solution.py:479
  30.0 7.1 %collective-permute-start.3 = (bf16[144,768]{1,0:T(8,128)(2,1)S(1)}, bf16[144,768]{1,0:T(8,128)(2,1)S(1)}, u32[]{:S(2)}, u32[]{:S(2)}) collective-permute-start(bf16[144,768]{1,0:T(8,128)(2,1)S(1)} %collective-permute-done.2), channel_id=1, source_target_pairs={{0,56},{8,0},{16,8},{24,16},{32,24},{40,32},{48,40},{56,48},{1,57}... | collective-permute-start | bytes 663560 | tf_op jit(solution)/shard_map/ppermute | solution.py:479
  37.4 17.6 %collective-permute-start.10 = (bf16[192,2048]{1,0:T(8,128)(2,1)S(1)}, bf16[192,2048]{1,0:T(8,128)(2,1)S(1)}, u32[]{:S(2)}, u32[]{:S(2)}) collective-permute-start(bf16[192,2048]{1,0:T(8,128)(2,1)S(1)} %get-tuple-element.47), channel_id=1, source_target_pairs={{0,3},{1,0},{2,1},{3,2},{4,7},{5,4},{6,5},{7,6},{8,11},{9,8},{10,9... | collective-permute-start | bytes 2359304 | tf_op jit(solution)/shard_map/ppermute | solution.py:479
  39.2 15.8 %collective-permute-start.9 = (bf16[192,2048]{1,0:T(8,128)(2,1)S(1)}, bf16[192,2048]{1,0:T(8,128)(2,1)S(1)}, u32[]{:S(2)}, u32[]{:S(2)}) collective-permute-start(bf16[192,2048]{1,0:T(8,128)(2,1)S(1)} %get-tuple-element.48), channel_id=1, source_target_pairs={{0,1},{1,2},{2,3},{3,0},{4,5},{5,6},{6,7},{7,4},{8,9},{9,10},{10,1... | collective-permute-start | bytes 2359304 | tf_op jit(solution)/shard_map/ppermute | solution.py:479
  39.5 8.3 %collective-permute-start.7 = (bf16[144,768]{1,0:T(8,128)(2,1)S(1)}, bf16[144,768]{1,0:T(8,128)(2,1)S(1)}, u32[]{:S(2)}, u32[]{:S(2)}) collective-permute-start(bf16[144,768]{1,0:T(8,128)(2,1)S(1)} %collective-permute-done.1), channel_id=1, source_target_pairs={{0,8},{8,16},{16,24},{24,32},{32,40},{40,48},{48,56},{56,0},{1,9},... | collective-permute-start | bytes 663560 | tf_op jit(solution)/shard_map/ppermute | solution.py:479
  39.6 15.4 %collective-permute-start.15 = (bf16[144,768]{1,0:T(8,128)(2,1)S(1)}, bf16[144,768]{1,0:T(8,128)(2,1)S(1)}, u32[]{:S(2)}, u32[]{:S(2)}) collective-permute-start(bf16[144,768]{1,0:T(8,128)(2,1)S(1)} %collective-permute-done.3), channel_id=1, source_target_pairs={{0,56},{8,0},{16,8},{24,16},{32,24},{40,32},{48,40},{56,48},{1,57}... | collective-permute-start | bytes 663560 | tf_op jit(solution)/shard_map/ppermute | solution.py:479
  47.8 7.1 %collective-permute-start.8 = (bf16[144,768]{1,0:T(8,128)(2,1)S(1)}, bf16[144,768]{1,0:T(8,128)(2,1)S(1)}, u32[]{:S(2)}, u32[]{:S(2)}) collective-permute-start(bf16[144,768]{1,0:T(8,128)(2,1)S(1)} %collective-permute-done.7), channel_id=1, source_target_pairs={{0,8},{8,16},{16,24},{24,32},{32,40},{40,48},{48,56},{56,0},{1,9},... | collective-permute-start | bytes 663560 | tf_op jit(solution)/shard_map/ppermute | solution.py:479
  55.1 4.6 %collective-permute-start.16 = (bf16[8,144,768]{2,1,0:T(8,128)(2,1)S(1)}, bf16[8,144,768]{2,1,0:T(8,128)(2,1)S(1)}, u32[]{:S(2)}, u32[]{:S(2)}) collective-permute-start(bf16[8,144,768]{2,1,0:T(8,128)(2,1)S(1)} %bitcast_dynamic-update-slice_fusion.refs_6_), channel_id=1, source_target_pairs={{0,64},{64,0},{1,65},{65,1},{2,66},{66,2},{3,67},{67,3},{4,68},{68... | collective-permute-start | bytes 5308424 | tf_op jit(solution)/shard_map/ppermute | solution.py:479
  55.3 9.7 %collective-permute-start.11 = (bf16[64,2048]{1,0:T(8,128)(2,1)S(1)}, bf16[64,2048]{1,0:T(8,128)(2,1)S(1)}, u32[]{:S(2)}, u32[]{:S(2)}) collective-permute-start(bf16[64,2048]{1,0:T(8,128)(2,1)S(1)} %slice.14), channel_id=1, source_target_pairs={{0,1},{1,2},{2,3},{3,0},{4,5},{5,6},{6,7},{7,4},{8,9},{9,10},{10,1... | collective-permute-start | bytes 786440 | tf_op jit(solution)/shard_map/ppermute | solution.py:479
  56.9 9.1 %collective-permute-start.12 = (bf16[64,2048]{1,0:T(8,128)(2,1)S(1)}, bf16[64,2048]{1,0:T(8,128)(2,1)S(1)}, u32[]{:S(2)}, u32[]{:S(2)}) collective-permute-start(bf16[64,2048]{1,0:T(8,128)(2,1)S(1)} %slice.15), channel_id=1, source_target_pairs={{0,3},{1,0},{2,1},{3,2},{4,7},{5,4},{6,5},{7,6},{8,11},{9,8},{10,9... | collective-permute-start | bytes 786440 | tf_op jit(solution)/shard_map/ppermute | solution.py:479
  58.4 5.2 %collective-permute-start.13 = (bf16[16,2048]{1,0:T(8,128)(2,1)S(1)}, bf16[16,2048]{1,0:T(8,128)(2,1)S(1)}, u32[]{:S(2)}, u32[]{:S(2)}) collective-permute-start(bf16[16,2048]{1,0:T(8,128)(2,1)S(1)} %shard_map.75), channel_id=1, source_target_pairs={{4,8},{12,16},{20,24},{28,32},{36,40},{44,48},{52,56},{5,9},{13,17... | collective-permute-start | bytes 196616 | tf_op jit(solution)/shard_map/ppermute | solution.py:544
  59.0 4.6 %collective-permute-start.14 = (bf16[16,2048]{1,0:T(8,128)(2,1)S(1)}, bf16[16,2048]{1,0:T(8,128)(2,1)S(1)}, u32[]{:S(2)}, u32[]{:S(2)}) collective-permute-start(bf16[16,2048]{1,0:T(8,128)(2,1)S(1)} %shard_map.75), channel_id=1, source_target_pairs={{4,12},{12,20},{20,28},{28,36},{36,44},{44,52},{52,60},{5,13},{13,... | collective-permute-start | bytes 196616 | tf_op jit(solution)/shard_map/ppermute | solution.py:544
  69.8 17.0 %all-to-all-start.1 = ((f32[8,16,256]{2,1,0:T(8,128)}), f32[8,16,256]{2,1,0:T(8,128)S(1)}, u32[]{:S(2)}, u32[]{:S(2)}) async-start(f32[8,16,256]{2,1,0:T(8,128)} %get-tuple-element.42), calls=%async_computation.1 | async-start | bytes 262144 | tf_op jit(solution)/shard_map/all_to_all | solution.py:487
  78.9 0.8 copy-start
  86.9 1.0 copy-start.1
